TPU v7x, 32 devices: a whole 2x2x4 slice. The times are simulated.
32 devices in a mesh: ctx: 8 (over z, y), mp: 4 (over x, core).
Axes of the slice: x: 2, y: 2, z: 4, core: 2. Of those that a mesh axis runs over, the one named last changes fastest.
Arguments:
- block_in: bfloat16 [2048, 1024], P(('ctx', 'mp')), may hold values from -6 to 6
- attn_gain: float32 [1024], replicated, may hold values from 0.5 to 1.5
- query_weight: bfloat16 [1024, 1024], P(None, 'mp'), may hold values from -0.1875 to 0.1875
- key_weight: bfloat16 [1024, 512], P(None, 'mp'), may hold values from -0.1875 to 0.1875
- value_weight: bfloat16 [1024, 512], P(None, 'mp'), may hold values from -0.1875 to 0.1875
- out_weight: bfloat16 [1024, 1024], P('mp'), may hold values from -2.5 to 2.5
- query_gain: float32 [64], replicated, may hold values from 0.6 to 1.6
- key_gain: float32 [64], replicated, may hold values from 0.6 to 1.6
- ffn_gain: float32 [1024], replicated, may hold values from 0.5 to 1.5
- gate_weight: bfloat16 [1024, 4608], P(None, 'mp'), may hold values from -0.1875 to 0.1875
- up_weight: bfloat16 [1024, 4608], P(None, 'mp'), may hold values from -0.1875 to 0.1875
- down_weight: bfloat16 [4608, 1024], P('mp'), may hold values from -0.09375 to 0.09375
- segments: int32 [2048], replicated, may hold values from 0 to 4, as said below
- positions: int32 [2048], P('ctx'), may hold values from 0 to 1279, as said below
- cotangent: bfloat16 [2048, 1024], P(('ctx', 'mp')), may hold values from -6 to 6
Outputs:
- block_out: bfloat16 [2048, 1024], P(('ctx', 'mp'))
- grad_input: float32 [2048, 1024], P(('ctx', 'mp'))
- query_grad: float32 [1024, 1024], P('ctx', 'mp')
- key_grad: float32 [1024, 512], P('ctx', 'mp')
- value_grad: float32 [1024, 512], P('ctx', 'mp')
- out_grad: float32 [1024, 1024], P('mp', 'ctx')
- gate_grad: float32 [1024, 4608], P('ctx', 'mp')
- up_grad: float32 [1024, 4608], P('ctx', 'mp')
- down_grad: float32 [4608, 1024], P('mp', 'ctx')
- attn_gain_grad: float32 [1024], replicated
- ffn_gain_grad: float32 [1024], replicated
- query_gain_grad: float32 [64], replicated
- key_gain_grad: float32 [64], replicated
Inputs may be any that keep to these rules, and one draw needn't show every extreme that they name: `segments`: never falls from a token to the next; every document number occurs; one document holds exactly 1280 tokens, no document more. `positions`: the token's index minus the index of the first token of its document.
All inputs are finite; a program needn't handle non-finite values.
Results may differ from a plain program's by a relative error of at most 0.023.
Values may be sent and summed in bfloat16 or wider, within the bound.
No kernel may reach another device: no remote copies, remote signals or barrier semaphores. Data moves between devices by JAX's collectives and lax.ppermute only.
A program may use at most 192 MiB of HBM per device.

v0:
```python
import functools

import jax
import jax.numpy as jnp
from jax import lax
from jax.experimental import pallas as pl
from jax.experimental.pallas import tpu as pltpu
from jax.sharding import PartitionSpec as P

HEADS = 16
KV_HEADS = 8
HD = 64
EPS = 1e-05
ROPE_BASE = 1000000.0
MASKED_SCORE = -1e30
LONGEST = {2048: 1280, 8192: 4352}
BF = jnp.bfloat16
F32 = jnp.float32
ROWS = (((0,), (0,)), ((), ()))
COLS = (((1,), (1,)), ((), ()))
SCALE = HD ** (-0.5)


def dot(a, b, dims=(((1,), (0,)), ((), ()))):
    return lax.dot_general(a, b, dims, preferred_element_type=F32)


def xor(values, axis, mask):
    n = lax.axis_size(axis)
    return lax.ppermute(values, axis, [(i, i ^ mask) for i in range(n)])


def up(values, step):
    n = lax.axis_size("ctx")
    return lax.ppermute(values, "ctx", [(i, i + step) for i in range(n - step)])


def down(values, step):
    n = lax.axis_size("ctx")
    return lax.ppermute(values, "ctx", [(i, i - step) for i in range(step, n)])


def lanes(shape):
    return lax.broadcasted_iota(jnp.int32, shape, len(shape) - 1)


def group_sum(values):
    width = values.shape[-1]
    line = lax.broadcasted_iota(jnp.int32, (width, width), 0) // HD
    ones = (line == lanes((width, width)) // HD).astype(BF)
    front = values.astype(BF)
    back = (values - front.astype(F32)).astype(BF)
    return dot(front, ones) + dot(back, ones)


def partner(values):
    width = values.shape[-1]
    first = lanes(values.shape) % HD < HD // 2
    return jnp.where(
        first, pltpu.roll(values, width - HD // 2, 1), pltpu.roll(values, HD // 2, 1)
    )


def wide(table, width):
    return jnp.concatenate([table] * (width // table.shape[-1]), axis=-1)


def row_norm(values):
    return lax.rsqrt(jnp.mean(values * values, axis=-1, keepdims=True) + EPS)


def head_norm(values):
    return lax.rsqrt(group_sum(values * values) * (1.0 / HD) + EPS)


def head_norm_backward(values, gain, grads, cos, sin):
    width = values.shape[-1]
    grads = grads * wide(cos, width) - partner(grads) * wide(sin, width)
    scale = head_norm(values)
    normed = values * scale
    inner = grads * gain
    grad_in = scale * (inner - normed * (group_sum(inner * normed) * (1.0 / HD)))
    return grad_in, jnp.sum(grads * normed, axis=0, keepdims=True)


def place_of(iota, rows, rank):
    quarter = rows // 4
    part = iota // quarter
    relative = (part % 2) * 2 + part // 2
    return jnp.bitwise_xor(relative, rank) * quarter + iota % quarter


def stack(slab, kv_head):
    slab = slab.astype(F32)
    turned = pltpu.roll(slab, HD, 1)
    low = lanes(slab.shape) < HD
    if kv_head == 0:
        parts = [jnp.where(low, slab, 0.0), jnp.where(low, turned, 0.0)]
    else:
        parts = [jnp.where(low, 0.0, turned), jnp.where(low, 0.0, slab)]
    return jnp.concatenate(parts, axis=0)


def unstack(stacked, kv_head):
    rows = stacked.shape[0] // 2
    first, second = stacked[:rows], stacked[rows:]
    low = lanes(first.shape) < HD
    if kv_head == 0:
        return jnp.where(low, first, pltpu.roll(second, HD, 1))
    return jnp.where(low, pltpu.roll(first, HD, 1), second)


def qkv_kernel(
    ranks, x0, x1, x2, x3, gain, wq, wk, wv, query_gain, key_gain, cos, sin,
    act_out, select_out, pair_out, query_rot_out, query_out, key_out,
):
    x = jnp.concatenate([x0[...], x1[...], x2[...], x3[...]], axis=0).astype(F32)
    act = (x * row_norm(x) * gain[...]).astype(BF)
    act_out[...] = act
    keys = dot(act, wk[...])
    key_out[...] = keys
    width = keys.shape[-1]
    normed = keys * head_norm(keys) * key_gain[...]
    rotated = normed * cos[...] + partner(normed) * sin[...]
    pair_out[:, :width] = rotated.astype(BF)
    pair_out[:, width:] = dot(act, wv[...]).astype(BF)
    queries = dot(act, wq[...])
    query_out[...] = queries
    normed = queries * head_norm(queries) * query_gain[...]
    width = queries.shape[-1]
    rotated = normed * wide(cos[...], width) + partner(normed) * wide(sin[...], width)
    query_rot_out[...] = rotated.astype(BF)
    select_columns(ranks, act_out, select_out)


def select_columns(ranks, source, target):
    columns = target.shape[1]
    blocks = columns // 128
    if blocks != 4:
        target[...] = jnp.zeros(target.shape, target.dtype)
        return
    for b in range(blocks):
        start = pl.multiple_of((2 * b + 1 - ranks[0] % 2) * 128, 128)
        target[:, b * 128 : (b + 1) * 128] = source[:, pl.ds(start, 128)]


def attention_kernel(
    count, ranks, query_rot, first_seen, wo, *refs
):
    blocks = refs[:count]
    out_f32, out_b, sums_out, kept_out, sent_out, scores = refs[count:]
    rows = query_rot.shape[0]
    key_width = blocks[0].shape[1] // 2
    query_index = ranks[0] * rows + place_of(
        lax.broadcasted_iota(jnp.int32, (rows, 1), 0), rows, ranks[1]
    )
    key_place = place_of(lanes((1, rows)), rows, ranks[1])
    masks = []
    for d in range(count):
        key_index = (ranks[0] - d) * rows + key_place
        mask = key_index >= first_seen[...]
        if d == 0:
            mask = mask & (key_index <= query_index)
        masks.append(jnp.where(mask, 0.0, MASKED_SCORE))
    for head in range(2):
        slab = query_rot[:, head * 128 : (head + 1) * 128]
        stacked = (stack(slab, head) * SCALE).astype(BF)
        top = jnp.full((2 * rows, 1), MASKED_SCORE, F32)
        for d in range(count):
            block = dot(stacked, blocks[d][:, :key_width], COLS)
            block = block + jnp.concatenate([masks[d], masks[d]], axis=0)
            scores[:, d * rows : (d + 1) * rows] = block
            top = jnp.maximum(top, jnp.max(block, axis=-1, keepdims=True))
        total = jnp.zeros((2 * rows, 1), F32)
        mixed = jnp.zeros((2 * rows, key_width), F32)
        for d in range(count):
            weights = jnp.exp(scores[:, d * rows : (d + 1) * rows] - top)
            total = total + jnp.sum(weights, axis=-1, keepdims=True)
            mixed = mixed + dot(weights.astype(BF), blocks[d][:, key_width:])
        sums = jnp.broadcast_to(top + jnp.log(total), (2 * rows, 128))
        sums_out[head : head + 1, :] = jnp.transpose(sums)[:1]
        out_f32[:, head * 128 : (head + 1) * 128] = unstack(mixed / total, head)
    attn_b = out_f32[...].astype(BF)
    out_b[...] = attn_b
    half = rows // 2
    kept_out[...] = dot(attn_b[:half], wo[...])
    sent_out[...] = dot(attn_b[half:], wo[...]).astype(BF)


def ffn_forward_kernel(
    ranks, x0, x1, x2, x3, half0, half1, gain, wg, wu, cot,
    resid_out, act_out, select_out, cot_select_out, gate_out, up_out, hidden_out,
):
    x = jnp.concatenate([x0[...], x1[...], x2[...], x3[...]], axis=0).astype(F32)
    resid = x + jnp.concatenate([half0[...], half1[...]], axis=0).astype(F32)
    resid_out[...] = resid
    act = (resid * row_norm(resid) * gain[...]).astype(BF)
    act_out[...] = act
    gate = dot(act, wg[...])
    upper = dot(act, wu[...])
    gate_out[...] = gate
    up_out[...] = upper
    hidden_out[...] = (gate * jax.nn.sigmoid(gate) * upper).astype(BF)
    select_columns(ranks, act_out, select_out)
    select_columns(ranks, cot, cot_select_out)


def ffn_backward_kernel(
    gate, upper, grad_hidden, wg, wu, grad_gate_out, grad_up_out, kept_out, sent_out
):
    grads = grad_hidden[...]
    values = gate[...]
    sigmoid = jax.nn.sigmoid(values)
    grad_gate = (grads * upper[...] * sigmoid * (1.0 + values * (1.0 - sigmoid))).astype(BF)
    grad_up = (grads * values * sigmoid).astype(BF)
    grad_gate_out[...] = grad_gate
    grad_up_out[...] = grad_up
    half = values.shape[0] // 2
    sent_out[...] = (
        dot(grad_gate[half:], wg[...], COLS) + dot(grad_up[half:], wu[...], COLS)
    ).astype(BF)
    kept_out[...] = dot(grad_gate[:half], wg[...], COLS) + dot(grad_up[:half], wu[...], COLS)


def attention_backward_kernel(
    count, ranks, cot, resid, half0, half1, gain, wo, attn, sums, query_rot, first_row, *refs
):
    blocks = refs[:count]
    grad_own_out, grad_b_out, select_out, gain_out, grad_query_out = refs[count : count + 5]
    terms = refs[count + 5 :]
    rows = query_rot.shape[0]
    key_width = blocks[0].shape[1] // 2
    values = resid[...]
    scale = row_norm(values)
    normed = values * scale
    grads = jnp.concatenate([half0[...], half1[...]], axis=0).astype(F32)
    inner = grads * gain[...]
    grad_in = scale * (inner - normed * jnp.mean(inner * normed, axis=-1, keepdims=True))
    grad_resid = cot[...].astype(F32) + grad_in
    own = rows // 4
    grad_own_out[...] = grad_resid[:own]
    gain_out[...] = jnp.sum(grads[:own] * normed[:own], axis=0, keepdims=True)
    grad_resid_b = grad_resid.astype(BF)
    grad_b_out[...] = grad_resid_b
    select_columns(ranks, grad_b_out, select_out)
    grad_attn = dot(grad_resid_b, wo[...], COLS)
    delta = jnp.transpose(group_sum(grad_attn * attn[...]))
    grad_attn_b = grad_attn.astype(BF)

    query_index = ranks[0] * rows + place_of(lanes((1, rows)), rows, ranks[1])
    key_place = place_of(lax.broadcasted_iota(jnp.int32, (rows, 1), 0), rows, ranks[1])
    stacked = [stack(query_rot[:, h * 128 : (h + 1) * 128], h) for h in range(2)]
    stacked_b = [s.astype(BF) for s in stacked]
    scaled = [(s * SCALE).astype(BF) for s in stacked]
    grads_b = [
        stack(grad_attn_b[:, h * 128 : (h + 1) * 128], h).astype(BF) for h in range(2)
    ]
    deltas = [
        jnp.concatenate(
            [delta[2 * h * HD : 2 * h * HD + 1], delta[(2 * h + 1) * HD : (2 * h + 1) * HD + 1]],
            axis=1,
        )
        for h in range(2)
    ]
    grad_query = [jnp.zeros((2 * rows, key_width), F32) for _ in range(2)]
    for d in range(count - 1, -1, -1):
        key_index = (ranks[0] - d) * rows + key_place
        mask = key_index >= first_row[...]
        if d == 0:
            mask = mask & (key_index <= query_index)
        mask = jnp.where(mask, 0.0, MASKED_SCORE)
        mask = jnp.concatenate([mask, mask], axis=1)
        key_block = blocks[d][:, :key_width]
        value_block = blocks[d][:, key_width:]
        key_term = jnp.zeros((rows, key_width), F32)
        value_term = jnp.zeros((rows, key_width), F32)
        for h in range(2):
            scores = dot(key_block, scaled[h], COLS) + mask
            probs = jnp.exp(scores - sums[h : h + 1, :])
            grad_probs = dot(value_block, grads_b[h], COLS)
            grad_scores = (probs * (grad_probs - deltas[h]) * SCALE).astype(BF)
            key_term = key_term + dot(grad_scores, stacked_b[h])
            value_term = value_term + dot(probs.astype(BF), grads_b[h])
            grad_query[h] = grad_query[h] + dot(grad_scores, key_block, ROWS)
        terms[d][:, :key_width] = key_term.astype(terms[d].dtype)
        terms[d][:, key_width:] = value_term.astype(terms[d].dtype)
    for h in range(2):
        grad_query_out[:, h * 128 : (h + 1) * 128] = unstack(grad_query[h], h)


def query_backward_kernel(
    queries, gain, grads, cos, sin, wq, grad_out, gain_out, partial_out
):
    grad_in, gain_terms = head_norm_backward(queries[...], gain[...], grads[...], cos[...], sin[...])
    grad_b = grad_in.astype(BF)
    grad_out[...] = grad_b
    gain_out[...] = gain_terms
    partial_out[...] = dot(grad_b, wq[...], COLS)


def key_backward_kernel(
    keys, gain, grads, cos, sin, wk, wv, query_partial, x0, x1, x2, x3,
    grad_out, gain_out, attn_gain_out, kept_out, sent_out,
):
    width = keys.shape[-1]
    grad_in, gain_terms = head_norm_backward(
        keys[...], gain[...], grads[:, :width], cos[...], sin[...]
    )
    grad_b = grad_in.astype(BF)
    value_b = grads[:, width:].astype(BF)
    grad_out[:, :width] = grad_b
    grad_out[:, width:] = value_b
    gain_out[...] = gain_terms
    partial = query_partial[...] + dot(grad_b, wk[...], COLS) + dot(value_b, wv[...], COLS)
    x = jnp.concatenate([x0[...], x1[...], x2[...], x3[...]], axis=0).astype(F32)
    attn_gain_out[...] = jnp.sum(partial * (x * row_norm(x)), axis=0, keepdims=True)
    half = partial.shape[0] // 2
    kept_out[...] = partial[:half]
    sent_out[...] = partial[half:].astype(BF)


def weight_grad_kernel(ranks, act, arrived_act, grads, arrived_grads, kept_out, sent_out):
    parity = ranks[0] % 2
    mine = ranks[0] // 2
    for lo in range(2):
        for hi in range(2):
            block = jnp.bitwise_xor(mine, lo + 2 * hi)
            start = pl.multiple_of((2 * block + parity) * 128, 128)
            there = pl.multiple_of(block * 128, 128)
            total = dot(act[:, pl.ds(start, 128)], grads[...], ROWS) + dot(
                arrived_act[:, pl.ds(there, 128)], arrived_grads[...], ROWS
            )
            target = sent_out if lo else kept_out
            target[hi * 128 : (hi + 1) * 128, :] = total.astype(target.dtype)


def shape(dims, dtype):
    return jax.ShapeDtypeStruct(dims, dtype)


def launch(kernel, outs, args, scratch=(), name=None):
    nbytes = sum(a.size * a.dtype.itemsize for a in list(args) + list(outs))
    nbytes += sum(s.shape[0] * s.shape[1] * 4 for s in scratch)
    specs = [
        pl.BlockSpec(memory_space=pltpu.SMEM if a.shape == (2,) else pltpu.VMEM) for a in args
    ]
    return pl.pallas_call(
        kernel,
        out_shape=outs,
        in_specs=specs,
        out_specs=[pl.BlockSpec(memory_space=pltpu.VMEM) for _ in outs],
        scratch_shapes=list(scratch),
        compiler_params=pltpu.CompilerParams(
            vmem_limit_bytes=min(2 * nbytes + (8 << 20), 56 << 20)
        ),
        name=name,
    )(*args)


def mp_order(values):
    rank = lax.axis_index("mp")
    parts = values.reshape(2, 2, -1)
    parts = jnp.swapaxes(parts, 0, 1)
    parts = jnp.where(rank % 2 == 1, parts[::-1], parts)
    parts = jnp.where(rank // 2 == 1, parts[:, ::-1], parts)
    return parts.reshape(values.shape)


def mp_gather(values):
    other = xor(values, "mp", 2)
    core = xor(values, "mp", 1)
    return values, other, core, xor(other, "mp", 1)


def mp_reduce(kept, sent):
    kept = kept + xor(sent, "mp", 1).astype(F32)
    own = kept.shape[0] // 2
    return kept[:own] + xor(kept[own:].astype(BF), "mp", 2).astype(F32)


def mp_allreduce(kept, sent):
    kept = (kept + xor(sent, "mp", 1).astype(F32)).astype(BF)
    other = xor(kept, "mp", 2)
    own = kept.shape[0] // 2
    other = jnp.concatenate([other[own:], other[:own]], axis=0)
    both = (kept.astype(F32) + other.astype(F32)).astype(BF)
    return both, xor(both, "mp", 1)


def split_columns(values):
    n = lax.axis_size("ctx")
    index = lax.axis_index("ctx")
    rows, columns = values.shape
    bits = n.bit_length() - 1
    parts = values.reshape((rows,) + (2,) * bits + (columns // n,))
    for bit in range(bits):
        parts = jnp.where((index >> bit) % 2 == 1, jnp.flip(parts, bits - bit), parts)
    order = [0] + [bits - b for b in range(bits)] + [bits + 1]
    parts = jnp.transpose(parts, order).reshape(rows, 2, columns // 2)
    return parts[:, 0], parts[:, 1]


def weight_grad(ranks, act, arrived_act, grads, arrived_grads, name):
    n = lax.axis_size("ctx")
    columns = grads.shape[1]
    half = act.shape[1] // 4
    if n == 8 and act.shape[1] == 1024:
        kept, sent = launch(
            weight_grad_kernel,
            [shape((half, columns), F32), shape((half, columns), BF)],
            [ranks, act, arrived_act, grads, arrived_grads],
            name=name,
        )
    else:
        own, other = split_columns(act)
        both = jnp.concatenate([own, xor(other, "ctx", 1)], axis=0)
        both_grads = jnp.concatenate([grads, arrived_grads], axis=0)
        total = dot(both, both_grads, ROWS)
        kept, sent = total[:half], total[half:].astype(BF)
    total = kept + xor(sent, "ctx", 2).astype(F32)
    mask = 4
    while mask < n:
        half = total.shape[0] // 2
        total = total[:half] + xor(total[half:].astype(BF), "ctx", mask).astype(F32)
        mask *= 2
    return total


def body(
    block_in,
    attn_gain,
    query_weight,
    key_weight,
    value_weight,
    out_weight,
    query_gain,
    key_gain,
    ffn_gain,
    gate_weight,
    up_weight,
    down_weight,
    segments,
    positions,
    cotangent,
):
    width = block_in.shape[1]
    key_width = key_weight.shape[1]
    query_width = query_weight.shape[1]
    hidden_width = gate_weight.shape[1]
    n_ctx = lax.axis_size("ctx")
    ctx_rank = lax.axis_index("ctx")
    own_rows = block_in.shape[0]
    rows = positions.shape[0]
    total_tokens = rows * n_ctx
    longest = LONGEST.get(total_tokens, total_tokens)
    window = min(n_ctx - 1, -(-(longest - 1) // rows))
    slots = (window + 1) // 2
    count = window + 1
    half = rows // 2
    ranks = jnp.stack([ctx_rank, lax.axis_index("mp")]).astype(jnp.int32)

    x = mp_gather(block_in)
    place = mp_order(jnp.arange(rows, dtype=jnp.int32))
    positions = mp_order(positions)
    first_seen = ctx_rank * rows + place - positions
    lane = jnp.arange(128, dtype=jnp.int32)
    freqs = ROPE_BASE ** (-2.0 * (lane % (HD // 2)).astype(F32) / HD)
    angles = positions.astype(F32)[:, None] * freqs[None, :]
    cos = jnp.cos(angles)
    sin = jnp.sin(angles) * jnp.where(lane % HD < HD // 2, -1.0, 1.0)[None, :]
    query_gain_row = jnp.tile(query_gain, query_width // HD).reshape(1, -1)
    key_gain_row = jnp.tile(key_gain, key_width // HD).reshape(1, -1)
    attn_gain_row = attn_gain.reshape(1, -1)
    ffn_gain_row = ffn_gain.reshape(1, -1)

    act_attn, act_attn_select, pair, query_rot, queries, keys_pre = launch(
        qkv_kernel,
        [
            shape((rows, width), BF),
            shape((rows, width // 2), BF),
            shape((rows, 2 * key_width), BF),
            shape((rows, query_width), BF),
            shape((rows, query_width), F32),
            shape((rows, key_width), F32),
        ],
        [ranks, *x, attn_gain_row, query_weight, key_weight, value_weight,
         query_gain_row, key_gain_row, cos, sin],
        name="qkv",
    )

    odd_rank = ctx_rank % 2 == 1
    items = [pair] + [up(pair, 2 * k) for k in range(1, slots + 1) if 2 * k < n_ctx]
    while len(items) < slots + 1:
        items.append(jnp.zeros_like(pair))
    blocks = {0: pair}
    for k in range(1, slots + 1):
        if 2 * k <= window:
            blocks[2 * k] = items[k]
    for j in range(slots):
        blocks[2 * j + 1] = xor(jnp.where(odd_rank, items[j + 1], items[j]), "ctx", 1)
    blocks = [blocks[d] for d in range(count)]

    cot = jnp.concatenate(mp_gather(cotangent), axis=0)
    grad_hidden = dot(cot, down_weight, COLS)

    attn_rows, attn_b, log_sums, kept, sent = launch(
        functools.partial(attention_kernel, count),
        [
            shape((rows, query_width), F32),
            shape((rows, query_width), BF),
            shape((2, 2 * rows), F32),
            shape((half, width), F32),
            shape((half, width), BF),
        ],
        [ranks, query_rot, first_seen.reshape(-1, 1), out_weight, *blocks],
        scratch=[pltpu.VMEM((2 * rows, count * rows), F32)],
        name="attention",
    )
    resid_halves = mp_allreduce(kept, sent)
    early = xor(jnp.concatenate([act_attn_select, attn_b], axis=1), "ctx", 1)
    act_attn_there = early[:, : width // 2]
    attn_there = early[:, width // 2 :]

    resid, act_ffn, act_select, cot_select, gate_pre, up_proj, hidden = launch(
        ffn_forward_kernel,
        [
            shape((rows, width), F32),
            shape((rows, width), BF),
            shape((rows, width // 2), BF),
            shape((rows, width // 2), BF),
            shape((rows, hidden_width), F32),
            shape((rows, hidden_width), F32),
            shape((rows, hidden_width), BF),
        ],
        [ranks, *x, *resid_halves, ffn_gain_row, gate_weight, up_weight, cot],
        name="ffn_forward",
    )
    hidden_there = xor(hidden, "ctx", 1)
    cot_there = xor(cot_select, "ctx", 1)
    grad_gate, grad_up, kept, sent = launch(
        ffn_backward_kernel,
        [
            shape((rows, hidden_width), BF),
            shape((rows, hidden_width), BF),
            shape((half, width), F32),
            shape((half, width), BF),
        ],
        [gate_pre, up_proj, grad_hidden, gate_weight, up_weight],
        name="ffn_backward",
    )
    grad_act_halves = mp_allreduce(kept, sent)
    act_there = xor(act_select, "ctx", 1)
    gate_there = xor(grad_gate, "ctx", 1)
    up_there = xor(grad_up, "ctx", 1)

    outs = launch(
        functools.partial(attention_backward_kernel, count),
        [
            shape((own_rows, width), F32),
            shape((rows, width), BF),
            shape((rows, width // 2), BF),
            shape((1, width), F32),
            shape((rows, query_width), F32),
        ]
        + [shape((rows, 2 * key_width), BF if d else F32) for d in range(count)],
        [ranks, cot, resid, *grad_act_halves, ffn_gain_row, out_weight, attn_rows, log_sums,
         query_rot, first_seen.reshape(1, -1), *blocks],
        name="attention_backward",
    )
    grad_resid, grad_resid_b, grad_select, ffn_gain_part, grad_query = outs[:5]
    terms = outs[5:]

    sums = [terms[2 * k].astype(F32) if 2 * k <= window else 0.0 for k in range(slots + 1)]
    for j in range(slots - 1, -1, -1):
        arrived = xor(terms[2 * j + 1], "ctx", 1).astype(F32)
        sums[j] = sums[j] + jnp.where(odd_rank, 0.0, arrived)
        sums[j + 1] = sums[j + 1] + jnp.where(odd_rank, arrived, 0.0)
    pair_grad = sums[0]
    for k in range(slots, 0, -1):
        if 2 * k < n_ctx:
            pair_grad = pair_grad + down(sums[k].astype(BF), 2 * k).astype(F32)

    grad_query_b, query_gain_part, query_partial = launch(
        query_backward_kernel,
        [
            shape((rows, query_width), BF),
            shape((1, query_width), F32),
            shape((rows, width), F32),
        ],
        [queries, query_gain_row, grad_query, cos, sin, query_weight],
        name="query_backward",
    )
    late = xor(jnp.concatenate([grad_select, grad_query_b], axis=1), "ctx", 1)
    grad_there = late[:, : width // 2]
    query_there = late[:, width // 2 :]

    down_grad = weight_grad(ranks, cot, cot_there, hidden, hidden_there, "down_grad")
    gate_grad = weight_grad(ranks, act_ffn, act_there, grad_gate, gate_there, "gate_grad")
    up_grad = weight_grad(ranks, act_ffn, act_there, grad_up, up_there, "up_grad")
    out_grad = weight_grad(ranks, grad_resid_b, grad_there, attn_b, attn_there, "out_grad")
    query_grad = weight_grad(
        ranks, act_attn, act_attn_there, grad_query_b, query_there, "query_grad"
    )

    pair_b, key_gain_part, attn_gain_part, kept, sent = launch(
        key_backward_kernel,
        [
            shape((rows, 2 * key_width), BF),
            shape((1, key_width), F32),
            shape((1, width), F32),
            shape((half, width), F32),
            shape((half, width), BF),
        ],
        [keys_pre, key_gain_row, pair_grad, cos, sin, key_weight, value_weight,
         query_partial, *x],
        name="key_backward",
    )
    pair_there = xor(pair_b, "ctx", 1)
    pair_weight_grad = weight_grad(
        ranks, act_attn, act_attn_there, pair_b, pair_there, "key_value_grad"
    )
    grad_act_attn = mp_reduce(kept, sent)
    inputs = block_in.astype(F32)
    scale = row_norm(inputs)
    normed = inputs * scale
    inner = grad_act_attn * attn_gain
    grad_input = grad_resid + scale * (
        inner - normed * jnp.mean(inner * normed, axis=-1, keepdims=True)
    )

    block_out = dot(hidden, down_weight)
    block_out = (
        resid[:own_rows] + mp_reduce(block_out[:half], block_out[half:].astype(BF))
    ).astype(BF)

    gains = jnp.concatenate(
        [
            attn_gain_part.reshape(-1),
            ffn_gain_part.reshape(-1),
            jnp.sum(query_gain_part.reshape(-1, HD), axis=0),
            jnp.sum(key_gain_part.reshape(-1, HD), axis=0),
        ]
    ).reshape(-1, 128)
    for axis in ("mp", "ctx"):
        mask = 1
        while mask < lax.axis_size(axis):
            gains = gains + xor(gains, axis, mask)
            mask *= 2
    gains = gains.reshape(-1)
    return (
        block_out,
        grad_input,
        query_grad,
        pair_weight_grad[:, :key_width],
        pair_weight_grad[:, key_width:],
        jnp.transpose(out_grad),
        gate_grad,
        up_grad,
        jnp.transpose(down_grad),
        gains[:width],
        gains[width : 2 * width],
        gains[2 * width : 2 * width + HD],
        gains[2 * width + HD :],
    )


def solution(mesh):
    in_specs = (
        P(("ctx", "mp"), None),
        P(),
        P(None, "mp"),
        P(None, "mp"),
        P(None, "mp"),
        P("mp", None),
        P(),
        P(),
        P(),
        P(None, "mp"),
        P(None, "mp"),
        P("mp", None),
        P(),
        P("ctx"),
        P(("ctx", "mp"), None),
    )
    out_specs = (
        P(("ctx", "mp"), None),
        P(("ctx", "mp"), None),
        P("ctx", "mp"),
        P("ctx", "mp"),
        P("ctx", "mp"),
        P("mp", "ctx"),
        P("ctx", "mp"),
        P("ctx", "mp"),
        P("mp", "ctx"),
        P(),
        P(),
        P(),
        P(),
    )
    return jax.shard_map(body, mesh=mesh, in_specs=in_specs, out_specs=out_specs, check_vma=False)
```

profile of v0, /device:TPU:0, one launch (start us, length us, event | category | flops | bytes accessed | tf_op | source)
XLA Modules:
  0.0 326.1 jit_solution(2084880885348253278)
XLA Ops:
  0.7 3.0 collective-permute-start
  4.6 2.7 collective-permute-done.x1
  14.2 2.3 qkv.1
  20.0 4.4 %collective-permute-start.3 = (bf16[256,256]{1,0:T(8,128)(2,1)}, bf16[256,256]{1,0:T(8,128)(2,1)}, u32[]{:S(2)}, u32[]{:S(2)}) collective-permute-start(bf16[256,256]{1,0:T(8,128)(2,1)} %get-tuple-element.67.refs_0_), channel_id=1, source_target_pairs={{0,8},{4,12},{8,16},{12,20},{16,24},{20,28},{1,9},{5,13},{9,17},{1... | collective-permute-start | bytes 393224 | tf_op jit(solution)/shard_map/ppermute | solution.py:35
  24.4 4.5 %collective-permute-start.5 = (bf16[256,256]{1,0:T(8,128)(2,1)}, bf16[256,256]{1,0:T(8,128)(2,1)}, u32[]{:S(2)}, u32[]{:S(2)}) collective-permute-start(bf16[256,256]{1,0:T(8,128)(2,1)} %get-tuple-element.67.refs_0_), channel_id=1, source_target_pairs={{0,16},{4,20},{8,24},{12,28},{1,17},{5,21},{9,25},{13,29},{2,18},{... | collective-permute-start | bytes 393224 | tf_op jit(solution)/shard_map/ppermute | solution.py:35
  28.9 1.9 collective-permute-start.7
  30.9 1.6 collective-permute-done.5.refs_4_
  32.5 2.1 collective-permute-done.7
  34.6 1.8 broadcast_select_fusion
  36.4 1.6 collective-permute-start.4
  40.2 2.9 collective-permute-done.4.refs_1_
  43.1 2.6 collective-permute-done.6.refs_3_
  48.1 4.4 %attention.1 = (f32[256,256]{1,0:T(8,128)S(1)}, bf16[256,256]{1,0:T(8,128)(2,1)S(1)}, f32[2,512]{1,0:T(2,128)S(1)}, f32[128,1024]{1,0:T(8,128)S(1)}, bf16[128,1024]{1,0:T(8,128)(2,1)S(1)}) custom-call(s32[2]{0:T(128)S(1)} %pad_add_fusion.ranks, bf16[256,256]{1,0:T(8,128)(2,1)S(1)} %copy-done.42, s32[256,1]{1,0:T(8,128)S(1)} %sub.36.first_seen, ...), custom_call_target="tpu_custom_call" | custom-call | tf_op jit(solution)/shard_map/attention/pallas_call | solution.py:347
  54.3 4.2 %collective-permute-done.12 = bf16[64,1024]{1,0:T(8,128)(2,1)S(1)} collective-permute-done((bf16[64,1024]{1,0:T(8,128)(2,1)S(1)}, bf16[64,1024]{1,0:T(8,128)(2,1)S(1)}, u32[]{:S(2)}, u32[]{:S(2)}) %collective-permute-start.12) | collective-permute-done | bytes 131104 | tf_op jit(solution)/shard_map/ppermute | solution.py:30
  60.2 7.2 %collective-permute-done.10 = bf16[128,1024]{1,0:T(8,128)(2,1)S(1)} collective-permute-done((bf16[128,1024]{1,0:T(8,128)(2,1)S(1)}, bf16[128,1024]{1,0:T(8,128)(2,1)S(1)}, u32[]{:S(2)}, u32[]{:S(2)}) %collective-permute-start.10) | collective-permute-done | bytes 262176 | tf_op jit(solution)/shard_map/ppermute | solution.py:30
  70.0 2.5 ffn_forward.1
  72.5 3.2 ffn_backward.1
  79.1 6.9 %collective-permute-done.18 = bf16[128,1024]{1,0:T(8,128)(2,1)S(1)} collective-permute-done((bf16[128,1024]{1,0:T(8,128)(2,1)S(1)}, bf16[128,1024]{1,0:T(8,128)(2,1)S(1)}, u32[]{:S(2)}, u32[]{:S(2)}) %collective-permute-start.18) | collective-permute-done | bytes 262176 | tf_op jit(solution)/shard_map/ppermute | solution.py:30
  96.1 7.8 %attention_backward.1 = (f32[64,1024]{1,0:T(8,128)S(1)}, bf16[256,1024]{1,0:T(8,128)(2,1)S(1)}, bf16[256,512]{1,0:T(8,128)(2,1)S(1)}, f32[1,1024]{1,0:T(1,128)S(...) custom-call(s32[2]{0:T(128)S(1)} %pad_add_fusion.ranks, ...), custom_call_target="tpu_custom_call" | custom-call | tf_op jit(solution)/shard_map/attention_backward/pallas_call | solution.py:347
  104.0 1.6 collective-permute-start.20
  108.2 2.2 collective-permute-done.20
  110.4 2.8 collective-permute-done.21
  113.2 2.0 collective-permute-done.23
  125.9 1.8 collective-permute-done.22
  127.7 4.5 %collective-permute-done.24 = bf16[256,256]{1,0:T(8,128)(2,1)} collective-permute-done((bf16[256,256]{1,0:T(8,128)(2,1)}, bf16[256,256]{1,0:T(8,128)(2,1)}, u32[]{:S(2)}, u32[]{:S(2)}) %collective-permute-start.24) | collective-permute-done | bytes 131104 | tf_op jit(solution)/shard_map/ppermute | solution.py:40
  149.4 1.6 collective-permute-start.28
  159.5 1.9 collective-permute-done.28
  162.9 16.8 %collective-permute-done.44.arrived_act = bf16[256,512]{1,0:T(8,128)(2,1)S(1)} collective-permute-done((bf16[256,512]{1,0:T(8,128)(2,1)}, bf16[256,512]{1,0:T(8,128)(2,1)S(1)}, u32[]{:S(2)}, u32[]{:S(2)}) %collective-permute-start.44) | collective-permute-done | bytes 262176 | tf_op jit(solution)/shard_map/ppermute | solution.py:30
  184.2 26.2 %collective-permute-done.50 = f32[17,128]{1,0:T(8,128)S(1)} collective-permute-done((f32[17,128]{1,0:T(8,128)S(1)}, f32[17,128]{1,0:T(8,128)S(1)}, u32[]{:S(2)}, u32[]{:S(2)}) %collective-permute-start.50) | collective-permute-done | bytes 8736 | tf_op jit(solution)/shard_map/ppermute | solution.py:30
  210.4 2.1 collective-permute-start.46
  212.6 1.6 fusion.21
  215.7 2.0 collective-permute-start.42
  219.3 7.6 %collective-permute-done.51 = f32[17,128]{1,0:T(8,128)S(1)} collective-permute-done((f32[17,128]{1,0:T(8,128)S(1)}, f32[17,128]{1,0:T(8,128)S(1)}, u32[]{:S(2)}, u32[]{:S(2)}) %collective-permute-start.51) | collective-permute-done | bytes 8736 | tf_op jit(solution)/shard_map/ppermute | solution.py:30
  228.0 1.6 collective-permute-start.29
  229.6 21.2 %collective-permute-done.52 = f32[17,128]{1,0:T(8,128)S(1)} collective-permute-done((f32[17,128]{1,0:T(8,128)S(1)}, f32[17,128]{1,0:T(8,128)S(1)}, u32[]{:S(2)}, u32[]{:S(2)}) %collective-permute-start.52) | collective-permute-done | bytes 8736 | tf_op jit(solution)/shard_map/ppermute | solution.py:30
  258.5 3.4 %collective-permute-start.47 = (bf16[128,1152]{1,0:T(8,128)(2,1)}, bf16[128,1152]{1,0:T(8,128)(2,1)}, u32[]{:S(2)}, u32[]{:S(2)}) collective-permute-start(bf16[128,1152]{1,0:T(8,128)(2,1)} %slice.216), channel_id=1, source_target_pairs={{0,16},{4,20},{8,24},{12,28},{16,0},{20,4},{24,8},{28,12},{1,17},{... | collective-permute-start | bytes 884744 | tf_op jit(solution)/shard_map/ppermute | solution.py:30
  265.4 2.2 collective-permute-start.40
  268.3 1.7 collective-permute-start.36
  270.7 14.6 %collective-permute-done.33 = bf16[256,256]{1,0:T(8,128)(2,1)S(1)} collective-permute-done((bf16[256,256]{1,0:T(8,128)(2,1)S(1)}, bf16[256,256]{1,0:T(8,128)(2,1)S(1)}, u32[]{:S(2)}, u32[]{:S(2)}) %collective-permute-start.33) | collective-permute-done | bytes 131104 | tf_op jit(solution)/shard_map/ppermute | solution.py:30
  285.3 4.4 %collective-permute-start.31 = (bf16[128,256]{1,0:T(8,128)(2,1)S(1)}, bf16[128,256]{1,0:T(8,128)(2,1)S(1)}, u32[]{:S(2)}, u32[]{:S(2)}) collective-permute-start(bf16[128,256]{1,0:T(8,128)(2,1)S(1)} %slice.224), channel_id=1, source_target_pairs={{0,16},{4,20},{8,24},{12,28},{16,0},{20,4},{24,8},{28,12},{1,17},{... | collective-permute-start | bytes 196616 | tf_op jit(solution)/shard_map/ppermute | solution.py:30
  290.4 15.4 %collective-permute-done.36 = bf16[128,256]{1,0:T(8,128)(2,1)S(1)} collective-permute-done((bf16[128,256]{1,0:T(8,128)(2,1)S(1)}, bf16[128,256]{1,0:T(8,128)(2,1)S(1)}, u32[]{:S(2)}, u32[]{:S(2)}) %collective-permute-start.36) | collective-permute-done | bytes 65568 | tf_op jit(solution)/shard_map/ppermute | solution.py:30
  308.7 1.7 copy.38
  310.4 3.4 %collective-permute-done.34 = bf16[128,256]{1,0:T(8,128)(2,1)} collective-permute-done((bf16[128,256]{1,0:T(8,128)(2,1)}, bf16[128,256]{1,0:T(8,128)(2,1)}, u32[]{:S(2)}, u32[]{:S(2)}) %collective-permute-start.34) | collective-permute-done | bytes 65568 | tf_op jit(solution)/shard_map/ppermute | solution.py:30
  316.5 1.7 fusion.6
  318.2 1.9 fusion
  320.2 2.1 copy.39
  322.3 1.9 slice_add_fusion.1
  324.2 1.8 slice_add_fusion.2
  (353 shorter events, 102.9 us)
Async XLA Ops:
  0.7 6.7 %collective-permute-start = (bf16[64,1024]{1,0:T(8,128)(2,1)}, bf16[64,1024]{1,0:T(8,128)(2,1)S(1)}, u32[]{:S(2)}, u32[]{:S(2)}) collective-permute-start(bf16[64,1024]{1,0:T(8,128)(2,1)} %x0.5), channel_id=1, source_target_pairs={{0,2},{1,3},{2,0},{3,1},{4,6},{5,7},{6,4},{7,5},{8,10},{9,11},{10,... | collective-permute-start | bytes 393224 | tf_op jit(solution)/shard_map/ppermute | solution.py:30
  3.7 5.9 %collective-permute-start.1 = (bf16[64,1024]{1,0:T(8,128)(2,1)}, bf16[64,1024]{1,0:T(8,128)(2,1)S(1)}, u32[]{:S(2)}, u32[]{:S(2)}) collective-permute-start(bf16[64,1024]{1,0:T(8,128)(2,1)} %x0.5), channel_id=1, source_target_pairs={{0,1},{1,0},{2,3},{3,2},{4,5},{5,4},{6,7},{7,6},{8,9},{9,8},{10,11... | collective-permute-start | bytes 393224 | tf_op jit(solution)/shard_map/ppermute | solution.py:30
  20.0 10.8 %collective-permute-start.3 = (bf16[256,256]{1,0:T(8,128)(2,1)}, bf16[256,256]{1,0:T(8,128)(2,1)}, u32[]{:S(2)}, u32[]{:S(2)}) collective-permute-start(bf16[256,256]{1,0:T(8,128)(2,1)} %get-tuple-element.67.refs_0_), channel_id=1, source_target_pairs={{0,8},{4,12},{8,16},{12,20},{16,24},{20,28},{1,9},{5,13},{9,17},{1... | collective-permute-start | bytes 393224 | tf_op jit(solution)/shard_map/ppermute | solution.py:35
  24.4 8.0 %collective-permute-start.5 = (bf16[256,256]{1,0:T(8,128)(2,1)}, bf16[256,256]{1,0:T(8,128)(2,1)}, u32[]{:S(2)}, u32[]{:S(2)}) collective-permute-start(bf16[256,256]{1,0:T(8,128)(2,1)} %get-tuple-element.67.refs_0_), channel_id=1, source_target_pairs={{0,16},{4,20},{8,24},{12,28},{1,17},{5,21},{9,25},{13,29},{2,18},{... | collective-permute-start | bytes 393224 | tf_op jit(solution)/shard_map/ppermute | solution.py:35
  28.9 5.7 %collective-permute-start.7 = (bf16[256,256]{1,0:T(8,128)(2,1)}, bf16[256,256]{1,0:T(8,128)(2,1)}, u32[]{:S(2)}, u32[]{:S(2)}) collective-permute-start(bf16[256,256]{1,0:T(8,128)(2,1)} %get-tuple-element.67.refs_0_), channel_id=1, source_target_pairs={{0,24},{4,28},{1,25},{5,29},{2,26},{6,30},{3,27},{7,31}} | collective-permute-start | bytes 393224 | tf_op jit(solution)/shard_map/ppermute | solution.py:35
  36.4 6.7 %collective-permute-start.4 = (bf16[256,256]{1,0:T(8,128)(2,1)}, bf16[256,256]{1,0:T(8,128)(2,1)S(1)}, u32[]{:S(2)}, u32[]{:S(2)}) collective-permute-start(bf16[256,256]{1,0:T(8,128)(2,1)} %get-tuple-element.169), channel_id=1, source_target_pairs={{0,4},{4,0},{8,12},{12,8},{16,20},{20,16},{24,28},{28,24},{1,5},{5... | collective-permute-start | bytes 393224 | tf_op jit(solution)/shard_map/ppermute | solution.py:30
  38.0 7.7 %collective-permute-start.6 = (bf16[256,256]{1,0:T(8,128)(2,1)}, bf16[256,256]{1,0:T(8,128)(2,1)S(1)}, u32[]{:S(2)}, u32[]{:S(2)}) collective-permute-start(bf16[256,256]{1,0:T(8,128)(2,1)} %get-tuple-element.168), channel_id=1, source_target_pairs={{0,4},{4,0},{8,12},{12,8},{16,20},{20,16},{24,28},{28,24},{1,5},{5... | collective-permute-start | bytes 393224 | tf_op jit(solution)/shard_map/ppermute | solution.py:30
  38.5 8.6 %collective-permute-start.8 = (bf16[256,256]{1,0:T(8,128)(2,1)}, bf16[256,256]{1,0:T(8,128)(2,1)S(1)}, u32[]{:S(2)}, u32[]{:S(2)}) collective-permute-start(bf16[256,256]{1,0:T(8,128)(2,1)} %get-tuple-element.167), channel_id=1, source_target_pairs={{0,4},{4,0},{8,12},{12,8},{16,20},{20,16},{24,28},{28,24},{1,5},{5... | collective-permute-start | bytes 393224 | tf_op jit(solution)/shard_map/ppermute | solution.py:30
  52.5 6.0 %collective-permute-start.9 = (bf16[128,1024]{1,0:T(8,128)(2,1)S(1)}, bf16[128,1024]{1,0:T(8,128)(2,1)S(1)}, u32[]{:S(2)}, u32[]{:S(2)}) collective-permute-start(bf16[128,1024]{1,0:T(8,128)(2,1)S(1)} %get-tuple-element.69), channel_id=1, source_target_pairs={{0,1},{1,0},{2,3},{3,2},{4,5},{5,4},{6,7},{7,6},{8,9},{9,8},{10,11... | collective-permute-start | bytes 786440 | tf_op jit(solution)/shard_map/ppermute | solution.py:30
  52.6 5.9 %collective-permute-start.12 = (bf16[64,1024]{1,0:T(8,128)(2,1)S(1)}, bf16[64,1024]{1,0:T(8,128)(2,1)S(1)}, u32[]{:S(2)}, u32[]{:S(2)}) collective-permute-start(bf16[64,1024]{1,0:T(8,128)(2,1)S(1)} %copy-done.94), channel_id=1, source_target_pairs={{0,2},{1,3},{2,0},{3,1},{4,6},{5,7},{6,4},{7,5},{8,10},{9,11},{10,... | collective-permute-start | bytes 393224 | tf_op jit(solution)/shard_map/ppermute | solution.py:30
  54.1 6.0 %collective-permute-start.13 = (bf16[64,1024]{1,0:T(8,128)(2,1)S(1)}, bf16[64,1024]{1,0:T(8,128)(2,1)S(1)}, u32[]{:S(2)}, u32[]{:S(2)}) collective-permute-start(bf16[64,1024]{1,0:T(8,128)(2,1)S(1)} %copy-done.94), channel_id=1, source_target_pairs={{0,1},{1,0},{2,3},{3,2},{4,5},{5,4},{6,7},{7,6},{8,9},{9,8},{10,11... | collective-permute-start | bytes 393224 | tf_op jit(solution)/shard_map/ppermute | solution.py:30
  58.6 8.8 %collective-permute-start.10 = (bf16[128,1024]{1,0:T(8,128)(2,1)S(1)}, bf16[128,1024]{1,0:T(8,128)(2,1)S(1)}, u32[]{:S(2)}, u32[]{:S(2)}) collective-permute-start(bf16[128,1024]{1,0:T(8,128)(2,1)S(1)} %add_convert_fusion.3), channel_id=1, source_target_pairs={{0,2},{1,3},{2,0},{3,1},{4,6},{5,7},{6,4},{7,5},{8,10},{9,11},{10,... | collective-permute-start | bytes 786440 | tf_op jit(solution)/shard_map/ppermute | solution.py:30
  77.5 8.4 %collective-permute-start.18 = (bf16[128,1024]{1,0:T(8,128)(2,1)S(1)}, bf16[128,1024]{1,0:T(8,128)(2,1)S(1)}, u32[]{:S(2)}, u32[]{:S(2)}) collective-permute-start(bf16[128,1024]{1,0:T(8,128)(2,1)S(1)} %add_convert_fusion.1), channel_id=1, source_target_pairs={{0,2},{1,3},{2,0},{3,1},{4,6},{5,7},{6,4},{7,5},{8,10},{9,11},{10,... | collective-permute-start | bytes 786440 | tf_op jit(solution)/shard_map/ppermute | solution.py:30
  104.0 6.4 %collective-permute-start.20 = (bf16[256,256]{1,0:T(8,128)(2,1)S(1)}, bf16[256,256]{1,0:T(8,128)(2,1)S(1)}, u32[]{:S(2)}, u32[]{:S(2)}) collective-permute-start(bf16[256,256]{1,0:T(8,128)(2,1)S(1)} %get-tuple-element.81), channel_id=1, source_target_pairs={{0,4},{4,0},{8,12},{12,8},{16,20},{20,16},{24,28},{28,24},{1,5},{5... | collective-permute-start | bytes 393224 | tf_op jit(solution)/shard_map/ppermute | solution.py:30
  105.5 7.6 %collective-permute-start.21 = (bf16[256,256]{1,0:T(8,128)(2,1)S(1)}, bf16[256,256]{1,0:T(8,128)(2,1)S(1)}, u32[]{:S(2)}, u32[]{:S(2)}) collective-permute-start(bf16[256,256]{1,0:T(8,128)(2,1)S(1)} %get-tuple-element.82), channel_id=1, source_target_pairs={{0,4},{4,0},{8,12},{12,8},{16,20},{20,16},{24,28},{28,24},{1,5},{5... | collective-permute-start | bytes 393224 | tf_op jit(solution)/shard_map/ppermute | solution.py:30
  106.1 9.1 %collective-permute-start.23 = (bf16[256,256]{1,0:T(8,128)(2,1)S(1)}, bf16[256,256]{1,0:T(8,128)(2,1)S(1)}, u32[]{:S(2)}, u32[]{:S(2)}) collective-permute-start(bf16[256,256]{1,0:T(8,128)(2,1)S(1)} %get-tuple-element.84), channel_id=1, source_target_pairs={{0,4},{4,0},{8,12},{12,8},{16,20},{20,16},{24,28},{28,24},{1,5},{5... | collective-permute-start | bytes 393224 | tf_op jit(solution)/shard_map/ppermute | solution.py:30
  116.1 11.7 %collective-permute-start.22 = (bf16[256,256]{1,0:T(8,128)(2,1)}, bf16[256,256]{1,0:T(8,128)(2,1)}, u32[]{:S(2)}, u32[]{:S(2)}) collective-permute-start(bf16[256,256]{1,0:T(8,128)(2,1)} %get-tuple-element.164), channel_id=1, source_target_pairs={{24,0},{28,4},{25,1},{29,5},{26,2},{30,6},{27,3},{31,7}} | collective-permute-start | bytes 393224 | tf_op jit(solution)/shard_map/ppermute | solution.py:40
  117.4 14.8 %collective-permute-start.24 = (bf16[256,256]{1,0:T(8,128)(2,1)}, bf16[256,256]{1,0:T(8,128)(2,1)}, u32[]{:S(2)}, u32[]{:S(2)}) collective-permute-start(bf16[256,256]{1,0:T(8,128)(2,1)} %get-tuple-element.165), channel_id=1, source_target_pairs={{16,0},{20,4},{24,8},{28,12},{17,1},{21,5},{25,9},{29,13},{18,2},{... | collective-permute-start | bytes 393224 | tf_op jit(solution)/shard_map/ppermute | solution.py:40
  118.7 13.5 %collective-permute-start.25 = (bf16[256,256]{1,0:T(8,128)(2,1)}, bf16[256,256]{1,0:T(8,128)(2,1)}, u32[]{:S(2)}, u32[]{:S(2)}) collective-permute-start(bf16[256,256]{1,0:T(8,128)(2,1)} %get-tuple-element.166), channel_id=1, source_target_pairs={{8,0},{12,4},{16,8},{20,12},{24,16},{28,20},{9,1},{13,5},{17,9},{2... | collective-permute-start | bytes 393224 | tf_op jit(solution)/shard_map/ppermute | solution.py:40
  121.7 32.5 %collective-permute-start.15 = (bf16[128,1024]{1,0:T(8,128)(2,1)}, bf16[128,1024]{1,0:T(8,128)(2,1)}, u32[]{:S(2)}, u32[]{:S(2)}) collective-permute-start(bf16[128,1024]{1,0:T(8,128)(2,1)} %slice.219), channel_id=1, source_target_pairs={{0,1},{1,0},{2,3},{3,2},{4,5},{5,4},{6,7},{7,6},{8,9},{9,8},{10,11... | collective-permute-start | bytes 786440 | tf_op jit(solution)/shard_map/ppermute | solution.py:30
  148.3 4.7 %collective-permute-start.48 = (f32[17,128]{1,0:T(8,128)}, f32[17,128]{1,0:T(8,128)S(1)}, u32[]{:S(2)}, u32[]{:S(2)}) collective-permute-start(f32[17,128]{1,0:T(8,128)} %bitcast.30), channel_id=1, source_target_pairs={{0,1},{1,0},{2,3},{3,2},{4,5},{5,4},{6,7},{7,6},{8,9},{9,8},{10,11... | collective-permute-start | bytes 26120 | tf_op jit(solution)/shard_map/ppermute | solution.py:30
  149.4 12.0 %collective-permute-start.28 = (bf16[256,768]{1,0:T(8,128)(2,1)S(1)}, bf16[256,768]{1,0:T(8,128)(2,1)S(1)}, u32[]{:S(2)}, u32[]{:S(2)}) collective-permute-start(bf16[256,768]{1,0:T(8,128)(2,1)S(1)} %pad_maximum_fusion), channel_id=1, source_target_pairs={{0,4},{4,0},{8,12},{12,8},{16,20},{20,16},{24,28},{28,24},{1,5},{5... | collective-permute-start | bytes 1179656 | tf_op jit(solution)/shard_map/ppermute | solution.py:30
  151.0 30.2 %collective-permute-start.45 = (bf16[256,1152]{1,0:T(8,128)(2,1)}, bf16[256,1152]{1,0:T(8,128)(2,1)S(1)}, u32[]{:S(2)}, u32[]{:S(2)}) collective-permute-start(bf16[256,1152]{1,0:T(8,128)(2,1)} %copy-done.5), channel_id=1, source_target_pairs={{0,4},{4,0},{8,12},{12,8},{16,20},{20,16},{24,28},{28,24},{1,5},{5... | collective-permute-start | bytes 1769480 | tf_op jit(solution)/shard_map/ppermute | solution.py:30
  151.5 28.1 %collective-permute-start.44 = (bf16[256,512]{1,0:T(8,128)(2,1)}, bf16[256,512]{1,0:T(8,128)(2,1)S(1)}, u32[]{:S(2)}, u32[]{:S(2)}) collective-permute-start(bf16[256,512]{1,0:T(8,128)(2,1)} %copy-done.84), channel_id=1, source_target_pairs={{0,4},{4,0},{8,12},{12,8},{16,20},{20,16},{24,28},{28,24},{1,5},{5... | collective-permute-start | bytes 786440 | tf_op jit(solution)/shard_map/ppermute | solution.py:30
  153.0 61.2 %collective-permute-start.41 = (bf16[256,1152]{1,0:T(8,128)(2,1)}, bf16[256,1152]{1,0:T(8,128)(2,1)S(1)}, u32[]{:S(2)}, u32[]{:S(2)}) collective-permute-start(bf16[256,1152]{1,0:T(8,128)(2,1)} %copy-done.39), channel_id=1, source_target_pairs={{0,4},{4,0},{8,12},{12,8},{16,20},{20,16},{24,28},{28,24},{1,5},{5... | collective-permute-start | bytes 1769480 | tf_op jit(solution)/shard_map/ppermute | solution.py:30
  154.3 3.8 %collective-permute-start.49 = (f32[17,128]{1,0:T(8,128)S(1)}, f32[17,128]{1,0:T(8,128)S(1)}, u32[]{:S(2)}, u32[]{:S(2)}) collective-permute-start(f32[17,128]{1,0:T(8,128)S(1)} %bitcast_add_fusion), channel_id=1, source_target_pairs={{0,2},{1,3},{2,0},{3,1},{4,6},{5,7},{6,4},{7,5},{8,10},{9,11},{10,... | collective-permute-start | bytes 26120 | tf_op jit(solution)/shard_map/ppermute | solution.py:30
  158.0 59.7 %collective-permute-start.38 = (bf16[256,1152]{1,0:T(8,128)(2,1)S(1)}, bf16[256,1152]{1,0:T(8,128)(2,1)S(1)}, u32[]{:S(2)}, u32[]{:S(2)}) collective-permute-start(bf16[256,1152]{1,0:T(8,128)(2,1)S(1)} %copy-done.38), channel_id=1, source_target_pairs={{0,4},{4,0},{8,12},{12,8},{16,20},{20,16},{24,28},{28,24},{1,5},{5... | collective-permute-start | bytes 1769480 | tf_op jit(solution)/shard_map/ppermute | solution.py:30
  161.4 52.8 %collective-permute-start.37 = (bf16[256,512]{1,0:T(8,128)(2,1)S(1)}, bf16[256,512]{1,0:T(8,128)(2,1)S(1)}, u32[]{:S(2)}, u32[]{:S(2)}) collective-permute-start(bf16[256,512]{1,0:T(8,128)(2,1)S(1)} %copy-done.83), channel_id=1, source_target_pairs={{0,4},{4,0},{8,12},{12,8},{16,20},{20,16},{24,28},{28,24},{1,5},{5... | collective-permute-start | bytes 786440 | tf_op jit(solution)/shard_map/ppermute | solution.py:30
  179.7 32.8 %collective-permute-start.16 = (bf16[64,1024]{1,0:T(8,128)(2,1)S(1)}, bf16[64,1024]{1,0:T(8,128)(2,1)S(1)}, u32[]{:S(2)}, u32[]{:S(2)}) collective-permute-start(bf16[64,1024]{1,0:T(8,128)(2,1)S(1)} %slice.221), channel_id=1, source_target_pairs={{0,2},{1,3},{2,0},{3,1},{4,6},{5,7},{6,4},{7,5},{8,10},{9,11},{10,... | collective-permute-start | bytes 393224 | tf_op jit(solution)/shard_map/ppermute | solution.py:30
  181.1 29.3 %collective-permute-start.50 = (f32[17,128]{1,0:T(8,128)S(1)}, f32[17,128]{1,0:T(8,128)S(1)}, u32[]{:S(2)}, u32[]{:S(2)}) collective-permute-start(f32[17,128]{1,0:T(8,128)S(1)} %fusion.40), channel_id=1, source_target_pairs={{0,4},{4,0},{8,12},{12,8},{16,20},{20,16},{24,28},{28,24},{1,5},{5... | collective-permute-start | bytes 26120 | tf_op jit(solution)/shard_map/ppermute | solution.py:30
  210.4 44.9 %collective-permute-start.46 = (bf16[256,1152]{1,0:T(8,128)(2,1)S(1)}, bf16[256,1152]{1,0:T(8,128)(2,1)S(1)}, u32[]{:S(2)}, u32[]{:S(2)}) collective-permute-start(bf16[256,1152]{1,0:T(8,128)(2,1)S(1)} %get-tuple-element.114), channel_id=1, source_target_pairs={{0,8},{4,12},{8,0},{12,4},{16,24},{20,28},{24,16},{28,20},{1,9},{5... | collective-permute-start | bytes 1769480 | tf_op jit(solution)/shard_map/ppermute | solution.py:30
  212.5 14.4 %collective-permute-start.51 = (f32[17,128]{1,0:T(8,128)S(1)}, f32[17,128]{1,0:T(8,128)S(1)}, u32[]{:S(2)}, u32[]{:S(2)}) collective-permute-start(f32[17,128]{1,0:T(8,128)S(1)} %add.209), channel_id=1, source_target_pairs={{0,8},{4,12},{8,0},{12,4},{16,24},{20,28},{24,16},{28,20},{1,9},{5... | collective-permute-start | bytes 26120 | tf_op jit(solution)/shard_map/ppermute | solution.py:30
  215.7 42.1 %collective-permute-start.42 = (bf16[256,1152]{1,0:T(8,128)(2,1)S(1)}, bf16[256,1152]{1,0:T(8,128)(2,1)S(1)}, u32[]{:S(2)}, u32[]{:S(2)}) collective-permute-start(bf16[256,1152]{1,0:T(8,128)(2,1)S(1)} %get-tuple-element.111), channel_id=1, source_target_pairs={{0,8},{4,12},{8,0},{12,4},{16,24},{20,28},{24,16},{28,20},{1,9},{5... | collective-permute-start | bytes 1769480 | tf_op jit(solution)/shard_map/ppermute | solution.py:30
  219.2 39.3 %collective-permute-start.39 = (bf16[256,1152]{1,0:T(8,128)(2,1)S(1)}, bf16[256,1152]{1,0:T(8,128)(2,1)S(1)}, u32[]{:S(2)}, u32[]{:S(2)}) collective-permute-start(bf16[256,1152]{1,0:T(8,128)(2,1)S(1)} %get-tuple-element.108), channel_id=1, source_target_pairs={{0,8},{4,12},{8,0},{12,4},{16,24},{20,28},{24,16},{28,20},{1,9},{5... | collective-permute-start | bytes 1769480 | tf_op jit(solution)/shard_map/ppermute | solution.py:30
  226.9 23.8 %collective-permute-start.52 = (f32[17,128]{1,0:T(8,128)S(1)}, f32[17,128]{1,0:T(8,128)S(1)}, u32[]{:S(2)}, u32[]{:S(2)}) collective-permute-start(f32[17,128]{1,0:T(8,128)S(1)} %add.210), channel_id=1, source_target_pairs={{0,16},{4,20},{8,24},{12,28},{16,0},{20,4},{24,8},{28,12},{1,17},{... | collective-permute-start | bytes 26120 | tf_op jit(solution)/shard_map/ppermute | solution.py:30
  228.0 25.4 %collective-permute-start.29 = (bf16[256,768]{1,0:T(8,128)(2,1)S(1)}, bf16[256,768]{1,0:T(8,128)(2,1)S(1)}, u32[]{:S(2)}, u32[]{:S(2)}) collective-permute-start(bf16[256,768]{1,0:T(8,128)(2,1)S(1)} %pad_maximum_fusion.1), channel_id=1, source_target_pairs={{0,4},{4,0},{8,12},{12,8},{16,20},{20,16},{24,28},{28,24},{1,5},{5... | collective-permute-start | bytes 1179656 | tf_op jit(solution)/shard_map/ppermute | solution.py:30
  250.8 12.9 %collective-permute-start.32 = (bf16[256,256]{1,0:T(8,128)(2,1)S(1)}, bf16[256,256]{1,0:T(8,128)(2,1)S(1)}, u32[]{:S(2)}, u32[]{:S(2)}) collective-permute-start(bf16[256,256]{1,0:T(8,128)(2,1)S(1)} %copy-done.71), channel_id=1, source_target_pairs={{0,4},{4,0},{8,12},{12,8},{16,20},{20,16},{24,28},{28,24},{1,5},{5... | collective-permute-start | bytes 393224 | tf_op jit(solution)/shard_map/ppermute | solution.py:30
  253.5 14.8 %collective-permute-start.26 = (bf16[128,1024]{1,0:T(8,128)(2,1)S(1)}, bf16[128,1024]{1,0:T(8,128)(2,1)S(1)}, u32[]{:S(2)}, u32[]{:S(2)}) collective-permute-start(bf16[128,1024]{1,0:T(8,128)(2,1)S(1)} %copy-done.81), channel_id=1, source_target_pairs={{0,1},{1,0},{2,3},{3,2},{4,5},{5,4},{6,7},{7,6},{8,9},{9,8},{10,11... | collective-permute-start | bytes 786440 | tf_op jit(solution)/shard_map/ppermute | solution.py:30
  255.4 10.0 %collective-permute-start.35 = (bf16[256,256]{1,0:T(8,128)(2,1)S(1)}, bf16[256,256]{1,0:T(8,128)(2,1)S(1)}, u32[]{:S(2)}, u32[]{:S(2)}) collective-permute-start(bf16[256,256]{1,0:T(8,128)(2,1)S(1)} %get-tuple-element.103), channel_id=1, source_target_pairs={{0,8},{4,12},{8,0},{12,4},{16,24},{20,28},{24,16},{28,20},{1,9},{5... | collective-permute-start | bytes 393224 | tf_op jit(solution)/shard_map/ppermute | solution.py:30
  257.8 10.4 %collective-permute-start.30 = (bf16[256,256]{1,0:T(8,128)(2,1)S(1)}, bf16[256,256]{1,0:T(8,128)(2,1)S(1)}, u32[]{:S(2)}, u32[]{:S(2)}) collective-permute-start(bf16[256,256]{1,0:T(8,128)(2,1)S(1)} %get-tuple-element.97), channel_id=1, source_target_pairs={{0,8},{4,12},{8,0},{12,4},{16,24},{20,28},{24,16},{28,20},{1,9},{5... | collective-permute-start | bytes 393224 | tf_op jit(solution)/shard_map/ppermute | solution.py:30
  258.5 59.7 %collective-permute-start.47 = (bf16[128,1152]{1,0:T(8,128)(2,1)}, bf16[128,1152]{1,0:T(8,128)(2,1)}, u32[]{:S(2)}, u32[]{:S(2)}) collective-permute-start(bf16[128,1152]{1,0:T(8,128)(2,1)} %slice.216), channel_id=1, source_target_pairs={{0,16},{4,20},{8,24},{12,28},{16,0},{20,4},{24,8},{28,12},{1,17},{... | collective-permute-start | bytes 884744 | tf_op jit(solution)/shard_map/ppermute | solution.py:30
  263.7 58.6 %collective-permute-start.43 = (bf16[128,1152]{1,0:T(8,128)(2,1)}, bf16[128,1152]{1,0:T(8,128)(2,1)}, u32[]{:S(2)}, u32[]{:S(2)}) collective-permute-start(bf16[128,1152]{1,0:T(8,128)(2,1)} %slice.217), channel_id=1, source_target_pairs={{0,16},{4,20},{8,24},{12,28},{16,0},{20,4},{24,8},{28,12},{1,17},{... | collective-permute-start | bytes 884744 | tf_op jit(solution)/shard_map/ppermute | solution.py:30
  265.4 58.8 %collective-permute-start.40 = (bf16[128,1152]{1,0:T(8,128)(2,1)}, bf16[128,1152]{1,0:T(8,128)(2,1)}, u32[]{:S(2)}, u32[]{:S(2)}) collective-permute-start(bf16[128,1152]{1,0:T(8,128)(2,1)} %slice.218), channel_id=1, source_target_pairs={{0,16},{4,20},{8,24},{12,28},{16,0},{20,4},{24,8},{28,12},{1,17},{... | collective-permute-start | bytes 884744 | tf_op jit(solution)/shard_map/ppermute | solution.py:30
  268.2 17.1 %collective-permute-start.33 = (bf16[256,256]{1,0:T(8,128)(2,1)S(1)}, bf16[256,256]{1,0:T(8,128)(2,1)S(1)}, u32[]{:S(2)}, u32[]{:S(2)}) collective-permute-start(bf16[256,256]{1,0:T(8,128)(2,1)S(1)} %get-tuple-element.100), channel_id=1, source_target_pairs={{0,8},{4,12},{8,0},{12,4},{16,24},{20,28},{24,16},{28,20},{1,9},{5... | collective-permute-start | bytes 393224 | tf_op jit(solution)/shard_map/ppermute | solution.py:30
  268.3 37.6 %collective-permute-start.36 = (bf16[128,256]{1,0:T(8,128)(2,1)S(1)}, bf16[128,256]{1,0:T(8,128)(2,1)S(1)}, u32[]{:S(2)}, u32[]{:S(2)}) collective-permute-start(bf16[128,256]{1,0:T(8,128)(2,1)S(1)} %slice.222), channel_id=1, source_target_pairs={{0,16},{4,20},{8,24},{12,28},{16,0},{20,4},{24,8},{28,12},{1,17},{... | collective-permute-start | bytes 196616 | tf_op jit(solution)/shard_map/ppermute | solution.py:30
  285.3 22.7 %collective-permute-start.31 = (bf16[128,256]{1,0:T(8,128)(2,1)S(1)}, bf16[128,256]{1,0:T(8,128)(2,1)S(1)}, u32[]{:S(2)}, u32[]{:S(2)}) collective-permute-start(bf16[128,256]{1,0:T(8,128)(2,1)S(1)} %slice.224), channel_id=1, source_target_pairs={{0,16},{4,20},{8,24},{12,28},{16,0},{20,4},{24,8},{28,12},{1,17},{... | collective-permute-start | bytes 196616 | tf_op jit(solution)/shard_map/ppermute | solution.py:30
  305.9 9.5 %collective-permute-start.27 = (bf16[64,1024]{1,0:T(8,128)(2,1)}, bf16[64,1024]{1,0:T(8,128)(2,1)}, u32[]{:S(2)}, u32[]{:S(2)}) collective-permute-start(bf16[64,1024]{1,0:T(8,128)(2,1)} %slice.220), channel_id=1, source_target_pairs={{0,2},{1,3},{2,0},{3,1},{4,6},{5,7},{6,4},{7,5},{8,10},{9,11},{10,... | collective-permute-start | bytes 393224 | tf_op jit(solution)/shard_map/ppermute | solution.py:30
  308.1 5.7 %collective-permute-start.34 = (bf16[128,256]{1,0:T(8,128)(2,1)}, bf16[128,256]{1,0:T(8,128)(2,1)}, u32[]{:S(2)}, u32[]{:S(2)}) collective-permute-start(bf16[128,256]{1,0:T(8,128)(2,1)} %slice.223), channel_id=1, source_target_pairs={{0,16},{4,20},{8,24},{12,28},{16,0},{20,4},{24,8},{28,12},{1,17},{... | collective-permute-start | bytes 196616 | tf_op jit(solution)/shard_map/ppermute | solution.py:30
  (103 other events, 1004.7 us)
where the time goes:
time: 327 us; the launch traced here: 326 us
  waiting for transfers between devices  156 us (48%)
  starting transfers between devices  66.1 us (20%)
  local copies, waits for them, and re-layouts  46 us (14%)
  Pallas kernels  28.8 us (9%)
  other arithmetic  25.2 us (8%)
    ppermute x47, waiting for transfers between devices, xor(): return lax.ppermute(values, axis, [(i, i ^ mask) for i in range(n)])  146 us
    ppermute x47, starting transfers between devices, xor(): return lax.ppermute(values, axis, [(i, i ^ mask) for i in range(n)])  51.5 us
    unnamed x201, local copies, waits for them, and re-layouts  33.1 us
    pallas_call x13, Pallas kernels, launch(): pl.pallas_call(kernel, out_shape=outs, in_specs=specs, out_specs=[pl.Bloc...  28.8 us
    ppermute x3, starting transfers between devices, up(): return lax.ppermute(values, 'ctx', [(i, i + step) for i in range(n - step)])  10.8 us
  transfers between devices with their start and end apart: 53, of which 27 were waited for; matrix products, arithmetic and copies ran while one was open for 12% of the time, Pallas kernels for 3%

commit v1 on v0

--- a/solution.py
+++ b/solution.py
@@ -144,21 +144,36 @@
         target[:, b * 128 : (b + 1) * 128] = source[:, pl.ds(start, 128)]
 
 
-def attention_kernel(
-    count, ranks, query_rot, first_seen, wo, *refs
-):
-    blocks = refs[:count]
-    out_f32, out_b, sums_out, kept_out, sent_out, scores = refs[count:]
+def cotangent_kernel(ranks, c0, c1, c2, c3, wd, cot_out, select_out, grad_hidden_out):
+    cot = jnp.concatenate([c0[...], c1[...], c2[...], c3[...]], axis=0)
+    cot_out[...] = cot
+    select_columns(ranks, cot_out, select_out)
+    grad_hidden_out[...] = dot(cot, wd[...], COLS)
+
+
+def attention_kernel(count, ranks, query_rot, positions, wo, act_select, *refs):
+    slots = count // 2
+    even = refs[:slots]
+    low_odd, high_odd = refs[slots : 2 * slots], refs[2 * slots : 3 * slots]
+    out_f32, early_out, sums_out, kept_out, sent_out = refs[3 * slots : 3 * slots + 5]
+    odd = refs[3 * slots + 5 : -1]
+    scores = refs[-1]
     rows = query_rot.shape[0]
-    key_width = blocks[0].shape[1] // 2
+    key_width = even[0].shape[1] // 2
+    for j in range(slots):
+        odd[j][...] = jnp.where(
+            ranks[0] % 2 == 1, low_odd[j][...].astype(F32), high_odd[j][...].astype(F32)
+        ).astype(BF)
+    blocks = [(even, odd)[d % 2][d // 2] for d in range(count)]
     query_index = ranks[0] * rows + place_of(
         lax.broadcasted_iota(jnp.int32, (rows, 1), 0), rows, ranks[1]
     )
+    first_seen = query_index - positions[...]
     key_place = place_of(lanes((1, rows)), rows, ranks[1])
     masks = []
     for d in range(count):
         key_index = (ranks[0] - d) * rows + key_place
-        mask = key_index >= first_seen[...]
+        mask = key_index >= first_seen
         if d == 0:
             mask = mask & (key_index <= query_index)
         masks.append(jnp.where(mask, 0.0, MASKED_SCORE))
@@ -181,15 +196,76 @@
         sums_out[head : head + 1, :] = jnp.transpose(sums)[:1]
         out_f32[:, head * 128 : (head + 1) * 128] = unstack(mixed / total, head)
     attn_b = out_f32[...].astype(BF)
-    out_b[...] = attn_b
+    chosen = act_select.shape[1]
+    early_out[:, :chosen] = act_select[...]
+    early_out[:, chosen:] = attn_b
     half = rows // 2
     kept_out[...] = dot(attn_b[:half], wo[...])
     sent_out[...] = dot(attn_b[half:], wo[...]).astype(BF)
 
 
+def add_kernel(kept, arrived, out):
+    out[...] = (kept[...].astype(F32) + arrived[...].astype(F32)).astype(out.dtype)
+
+
+def flipped_add_kernel(kept, arrived, out):
+    half = kept.shape[0] // 2
+    for a, b in ((0, half), (half, 0)):
+        total = kept[a : a + half, :].astype(F32) + arrived[b : b + half, :].astype(F32)
+        out[a : a + half, :] = total.astype(out.dtype)
+
+
+def fold_kernel(kept, arrived, front_out, back_out):
+    half = front_out.shape[0]
+    front_out[...] = kept[:half, :] + arrived[:half, :].astype(F32)
+    back_out[...] = (kept[half:, :] + arrived[half:, :].astype(F32)).astype(BF)
+
+
+def turned_add_kernel(kept, arrived, out):
+    out[...] = jnp.transpose(kept[...] + arrived[...].astype(F32))
+
+
+def split_add_kernel(kept, arrived, first_out, second_out):
+    total = kept[...] + arrived[...].astype(F32)
+    width = first_out.shape[1]
+    first_out[...] = total[:, :width]
+    second_out[...] = total[:, width:]
+
+
+def pair_sum_kernel(ranks, term, if_odd, if_even, out):
+    odd = ranks[0] % 2 == 1
+    out[...] = (
+        term[...].astype(F32)
+        + jnp.where(odd, if_odd[...].astype(F32), if_even[...].astype(F32))
+    ).astype(BF)
+
+
+def down_kernel(hidden, wd, kept_out, sent_out):
+    half = hidden.shape[0] // 2
+    sent_out[...] = dot(hidden[half:, :], wd[...]).astype(BF)
+    kept_out[...] = dot(hidden[:half, :], wd[...])
+
+
+def block_out_kernel(resid, kept, arrived, out):
+    own = out.shape[0]
+    out[...] = (resid[:own, :] + kept[:own, :] + arrived[...].astype(F32)).astype(BF)
+
+
+def grad_input_kernel(x, gain, grad_resid, kept, arrived, out):
+    own = out.shape[0]
+    grads = kept[:own, :] + arrived[...].astype(F32)
+    values = x[...].astype(F32)
+    scale = row_norm(values)
+    normed = values * scale
+    inner = grads * gain[...]
+    out[...] = grad_resid[...] + scale * (
+        inner - normed * jnp.mean(inner * normed, axis=-1, keepdims=True)
+    )
+
+
 def ffn_forward_kernel(
-    ranks, x0, x1, x2, x3, half0, half1, gain, wg, wu, cot,
-    resid_out, act_out, select_out, cot_select_out, gate_out, up_out, hidden_out,
+    ranks, x0, x1, x2, x3, half0, half1, gain, wg, wu,
+    resid_out, act_out, select_out, gate_out, up_out, hidden_out,
 ):
     x = jnp.concatenate([x0[...], x1[...], x2[...], x3[...]], axis=0).astype(F32)
     resid = x + jnp.concatenate([half0[...], half1[...]], axis=0).astype(F32)
@@ -202,18 +278,19 @@
     up_out[...] = upper
     hidden_out[...] = (gate * jax.nn.sigmoid(gate) * upper).astype(BF)
     select_columns(ranks, act_out, select_out)
-    select_columns(ranks, cot, cot_select_out)
 
 
 def ffn_backward_kernel(
-    gate, upper, grad_hidden, wg, wu, grad_gate_out, grad_up_out, kept_out, sent_out
+    gate, upper, grad_hidden, wg, wu, select, gate_packet, grad_up_out, kept_out, sent_out
 ):
     grads = grad_hidden[...]
     values = gate[...]
     sigmoid = jax.nn.sigmoid(values)
     grad_gate = (grads * upper[...] * sigmoid * (1.0 + values * (1.0 - sigmoid))).astype(BF)
     grad_up = (grads * values * sigmoid).astype(BF)
-    grad_gate_out[...] = grad_gate
+    chosen = select.shape[1]
+    gate_packet[:, :chosen] = select[...]
+    gate_packet[:, chosen:] = grad_gate
     grad_up_out[...] = grad_up
     half = values.shape[0] // 2
     sent_out[...] = (
@@ -223,7 +300,7 @@
 
 
 def attention_backward_kernel(
-    count, ranks, cot, resid, half0, half1, gain, wo, attn, sums, query_rot, first_row, *refs
+    count, ranks, cot, resid, half0, half1, gain, wo, attn, sums, query_rot, positions, *refs
 ):
     blocks = refs[:count]
     grad_own_out, grad_b_out, select_out, gain_out, grad_query_out = refs[count : count + 5]
@@ -248,6 +325,7 @@
     grad_attn_b = grad_attn.astype(BF)
 
     query_index = ranks[0] * rows + place_of(lanes((1, rows)), rows, ranks[1])
+    first_row = query_index - positions[...]
     key_place = place_of(lax.broadcasted_iota(jnp.int32, (rows, 1), 0), rows, ranks[1])
     stacked = [stack(query_rot[:, h * 128 : (h + 1) * 128], h) for h in range(2)]
     stacked_b = [s.astype(BF) for s in stacked]
@@ -265,7 +343,7 @@
     grad_query = [jnp.zeros((2 * rows, key_width), F32) for _ in range(2)]
     for d in range(count - 1, -1, -1):
         key_index = (ranks[0] - d) * rows + key_place
-        mask = key_index >= first_row[...]
+        mask = key_index >= first_row
         if d == 0:
             mask = mask & (key_index <= query_index)
         mask = jnp.where(mask, 0.0, MASKED_SCORE)
@@ -289,20 +367,27 @@
 
 
 def query_backward_kernel(
-    queries, gain, grads, cos, sin, wq, grad_out, gain_out, partial_out
+    queries, gain, grads, cos, sin, wq, select, late_out, gain_out, partial_out
 ):
     grad_in, gain_terms = head_norm_backward(queries[...], gain[...], grads[...], cos[...], sin[...])
     grad_b = grad_in.astype(BF)
-    grad_out[...] = grad_b
+    chosen = select.shape[1]
+    late_out[:, :chosen] = select[...]
+    late_out[:, chosen:] = grad_b
     gain_out[...] = gain_terms
     partial_out[...] = dot(grad_b, wq[...], COLS)
 
 
 def key_backward_kernel(
-    keys, gain, grads, cos, sin, wk, wv, query_partial, x0, x1, x2, x3,
-    grad_out, gain_out, attn_gain_out, kept_out, sent_out,
+    ranks, keys, gain, cos, sin, wk, wv, query_partial, x0, x1, x2, x3,
+    ffn_gain_part, query_gain_part, term, arrived, *refs,
 ):
+    shifted = refs[:-4]
+    grad_out, gains_out, kept_out, sent_out = refs[-4:]
     width = keys.shape[-1]
+    grads = term[...] + jnp.where(ranks[0] % 2 == 1, 0.0, arrived[...].astype(F32))
+    for other in shifted:
+        grads = grads + other[...].astype(F32)
     grad_in, gain_terms = head_norm_backward(
         keys[...], gain[...], grads[:, :width], cos[...], sin[...]
     )
@@ -310,25 +395,43 @@
     value_b = grads[:, width:].astype(BF)
     grad_out[:, :width] = grad_b
     grad_out[:, width:] = value_b
-    gain_out[...] = gain_terms
     partial = query_partial[...] + dot(grad_b, wk[...], COLS) + dot(value_b, wv[...], COLS)
-    x = jnp.concatenate([x0[...], x1[...], x2[...], x3[...]], axis=0).astype(F32)
-    attn_gain_out[...] = jnp.sum(partial * (x * row_norm(x)), axis=0, keepdims=True)
     half = partial.shape[0] // 2
     kept_out[...] = partial[:half]
     sent_out[...] = partial[half:].astype(BF)
-
-
-def weight_grad_kernel(ranks, act, arrived_act, grads, arrived_grads, kept_out, sent_out):
+    x = jnp.concatenate([x0[...], x1[...], x2[...], x3[...]], axis=0).astype(F32)
+    features = x.shape[1]
+    parts = [
+        jnp.sum(partial * (x * row_norm(x)), axis=0, keepdims=True),
+        ffn_gain_part[...],
+    ]
+    row = 0
+    for part in parts:
+        for c in range(features // 128):
+            gains_out[row : row + 1, :] = part[:, c * 128 : (c + 1) * 128]
+            row += 1
+    queries = query_gain_part[...]
+    queries = sum(queries[:, c * 128 : (c + 1) * 128] for c in range(queries.shape[1] // 128))
+    gains_out[row : row + 1, :] = queries
+    gains_out[row + 1 : row + 2, :] = gain_terms
+
+
+def weight_grad_kernel(
+    offsets, ranks, act, arrived_act, grads, arrived_grads, kept_out, sent_out
+):
     parity = ranks[0] % 2
     mine = ranks[0] // 2
-    for lo in range(2):
+    own, there_at = offsets
+    width = kept_out.shape[1]
+    mine_grads = grads[:, own : own + width]
+    other_grads = arrived_grads[:, there_at : there_at + width]
+    for lo in (1, 0):
         for hi in range(2):
             block = jnp.bitwise_xor(mine, lo + 2 * hi)
             start = pl.multiple_of((2 * block + parity) * 128, 128)
             there = pl.multiple_of(block * 128, 128)
-            total = dot(act[:, pl.ds(start, 128)], grads[...], ROWS) + dot(
-                arrived_act[:, pl.ds(there, 128)], arrived_grads[...], ROWS
+            total = dot(act[:, pl.ds(start, 128)], mine_grads, ROWS) + dot(
+                arrived_act[:, pl.ds(there, 128)], other_grads, ROWS
             )
             target = sent_out if lo else kept_out
             target[hi * 128 : (hi + 1) * 128, :] = total.astype(target.dtype)
@@ -338,23 +441,29 @@
     return jax.ShapeDtypeStruct(dims, dtype)
 
 
-def launch(kernel, outs, args, scratch=(), name=None):
-    nbytes = sum(a.size * a.dtype.itemsize for a in list(args) + list(outs))
-    nbytes += sum(s.shape[0] * s.shape[1] * 4 for s in scratch)
-    specs = [
-        pl.BlockSpec(memory_space=pltpu.SMEM if a.shape == (2,) else pltpu.VMEM) for a in args
-    ]
+def launch(kernel, outs, args, scratch=(), name=None, after=()):
+    nbytes = sum(s.shape[0] * s.shape[1] * 4 for s in scratch)
+    n_in, n_after = len(args), len(after)
+
+    def run(*refs):
+        kernel(*refs[:n_in], *refs[n_in + n_after :])
+
     return pl.pallas_call(
-        kernel,
+        run,
         out_shape=outs,
-        in_specs=specs,
+        in_specs=[
+            pl.BlockSpec(memory_space=pltpu.SMEM if a.shape == (2,) else pltpu.VMEM) for a in args
+        ]
+        + [pl.BlockSpec(memory_space=pl.ANY)] * n_after,
         out_specs=[pl.BlockSpec(memory_space=pltpu.VMEM) for _ in outs],
         scratch_shapes=list(scratch),
-        compiler_params=pltpu.CompilerParams(
-            vmem_limit_bytes=min(2 * nbytes + (8 << 20), 56 << 20)
-        ),
+        compiler_params=pltpu.CompilerParams(vmem_limit_bytes=nbytes + (12 << 20)),
         name=name,
-    )(*args)
+    )(*args, *after)
+
+
+def add(kept, arrived, dtype, name, kernel=add_kernel, after=()):
+    return launch(kernel, [shape(kept.shape, dtype)], [kept, arrived], name=name, after=after)[0]
 
 
 def mp_order(values):
@@ -372,18 +481,20 @@
     return values, other, core, xor(other, "mp", 1)
 
 
-def mp_reduce(kept, sent):
-    kept = kept + xor(sent, "mp", 1).astype(F32)
+def mp_reduce_start(kept, sent, name):
     own = kept.shape[0] // 2
-    return kept[:own] + xor(kept[own:].astype(BF), "mp", 2).astype(F32)
-
-
-def mp_allreduce(kept, sent):
-    kept = (kept + xor(sent, "mp", 1).astype(F32)).astype(BF)
-    other = xor(kept, "mp", 2)
-    own = kept.shape[0] // 2
-    other = jnp.concatenate([other[own:], other[:own]], axis=0)
-    both = (kept.astype(F32) + other.astype(F32)).astype(BF)
+    kept, back = launch(
+        fold_kernel,
+        [shape((own, kept.shape[1]), F32), shape((own, kept.shape[1]), BF)],
+        [kept, xor(sent, "mp", 1)],
+        name=name,
+    )
+    return kept, xor(back, "mp", 2)
+
+
+def mp_allreduce(kept, sent, name):
+    kept = add(kept, xor(sent, "mp", 1), BF, name + "_core")
+    both = add(kept, xor(kept, "mp", 2), BF, name + "_chip", kernel=flipped_add_kernel)
     return both, xor(both, "mp", 1)
 
 
@@ -400,30 +511,41 @@
     return parts[:, 0], parts[:, 1]
 
 
-def weight_grad(ranks, act, arrived_act, grads, arrived_grads, name):
+def weight_grad(ranks, act, arrived_act, grads, arrived_grads, offsets, columns, name, after=()):
     n = lax.axis_size("ctx")
-    columns = grads.shape[1]
     half = act.shape[1] // 4
     if n == 8 and act.shape[1] == 1024:
-        kept, sent = launch(
-            weight_grad_kernel,
+        return launch(
+            functools.partial(weight_grad_kernel, offsets),
             [shape((half, columns), F32), shape((half, columns), BF)],
             [ranks, act, arrived_act, grads, arrived_grads],
             name=name,
+            after=after,
         )
-    else:
-        own, other = split_columns(act)
-        both = jnp.concatenate([own, xor(other, "ctx", 1)], axis=0)
-        both_grads = jnp.concatenate([grads, arrived_grads], axis=0)
-        total = dot(both, both_grads, ROWS)
-        kept, sent = total[:half], total[half:].astype(BF)
-    total = kept + xor(sent, "ctx", 2).astype(F32)
+    own, other = split_columns(act)
+    grads = grads[:, offsets[0] : offsets[0] + columns]
+    arrived_grads = arrived_grads[:, offsets[1] : offsets[1] + columns]
+    both = jnp.concatenate([own, xor(other, "ctx", 1)], axis=0)
+    total = dot(both, jnp.concatenate([grads, arrived_grads], axis=0), ROWS)
+    return total[:half], total[half:].astype(BF)
+
+
+def halve(kept, sent, name, after=()):
+    n = lax.axis_size("ctx")
+    arrived = xor(sent, "ctx", 2)
     mask = 4
     while mask < n:
-        half = total.shape[0] // 2
-        total = total[:half] + xor(total[half:].astype(BF), "ctx", mask).astype(F32)
+        half, columns = kept.shape[0] // 2, kept.shape[1]
+        kept, back = launch(
+            fold_kernel,
+            [shape((half, columns), F32), shape((half, columns), BF)],
+            [kept, arrived],
+            name=name + "_fold",
+            after=after,
+        )
+        arrived = xor(back, "ctx", mask)
         mask *= 2
-    return total
+    return kept, arrived
 
 
 def body(
@@ -460,9 +582,7 @@
     ranks = jnp.stack([ctx_rank, lax.axis_index("mp")]).astype(jnp.int32)
 
     x = mp_gather(block_in)
-    place = mp_order(jnp.arange(rows, dtype=jnp.int32))
     positions = mp_order(positions)
-    first_seen = ctx_rank * rows + place - positions
     lane = jnp.arange(128, dtype=jnp.int32)
     freqs = ROPE_BASE ** (-2.0 * (lane % (HD // 2)).astype(F32) / HD)
     angles = positions.astype(F32)[:, None] * freqs[None, :]
@@ -472,6 +592,8 @@
     key_gain_row = jnp.tile(key_gain, key_width // HD).reshape(1, -1)
     attn_gain_row = attn_gain.reshape(1, -1)
     ffn_gain_row = ffn_gain.reshape(1, -1)
+    position_column = positions.reshape(-1, 1)
+    position_row = positions.reshape(1, -1)
 
     act_attn, act_attn_select, pair, query_rot, queries, keys_pre = launch(
         qkv_kernel,
@@ -486,72 +608,92 @@
         [ranks, *x, attn_gain_row, query_weight, key_weight, value_weight,
          query_gain_row, key_gain_row, cos, sin],
         name="qkv",
-    )
-
-    odd_rank = ctx_rank % 2 == 1
-    items = [pair] + [up(pair, 2 * k) for k in range(1, slots + 1) if 2 * k < n_ctx]
-    while len(items) < slots + 1:
-        items.append(jnp.zeros_like(pair))
-    blocks = {0: pair}
-    for k in range(1, slots + 1):
-        if 2 * k <= window:
-            blocks[2 * k] = items[k]
-    for j in range(slots):
-        blocks[2 * j + 1] = xor(jnp.where(odd_rank, items[j + 1], items[j]), "ctx", 1)
-    blocks = [blocks[d] for d in range(count)]
-
-    cot = jnp.concatenate(mp_gather(cotangent), axis=0)
-    grad_hidden = dot(cot, down_weight, COLS)
-
-    attn_rows, attn_b, log_sums, kept, sent = launch(
+        after=[position_column, position_row],
+    )
+
+    def cross(values, odd):
+        return lax.ppermute(values, "ctx", [(i, i ^ 1) for i in range(odd, n_ctx, 2)])
+
+    def climb(step):
+        if step >= n_ctx:
+            return jnp.zeros_like(pair)
+        only_odd = step > window
+        pairs = [(i, i + step) for i in range(n_ctx - step) if i % 2 == 1 or not only_odd]
+        return lax.ppermute(pair, "ctx", pairs)
+
+    items = [pair] + [climb(2 * k) for k in range(1, slots + 1)]
+    low_odd = [cross(items[j], 0) for j in range(slots)]
+    high_odd = [cross(items[j + 1], 1) for j in range(slots)]
+    even = items[:slots]
+
+    cot, cot_select, grad_hidden = launch(
+        cotangent_kernel,
+        [
+            shape((rows, width), BF),
+            shape((rows, width // 2), BF),
+            shape((rows, hidden_width), F32),
+        ],
+        [ranks, *mp_gather(cotangent), down_weight],
+        name="cotangent",
+    )
+    cot_there = xor(cot_select, "ctx", 1)
+
+    outs = launch(
         functools.partial(attention_kernel, count),
         [
             shape((rows, query_width), F32),
-            shape((rows, query_width), BF),
+            shape((rows, width // 2 + query_width), BF),
             shape((2, 2 * rows), F32),
             shape((half, width), F32),
             shape((half, width), BF),
-        ],
-        [ranks, query_rot, first_seen.reshape(-1, 1), out_weight, *blocks],
+        ]
+        + [shape((rows, 2 * key_width), BF) for _ in range(slots)],
+        [ranks, query_rot, position_column, out_weight, act_attn_select,
+         *even, *low_odd, *high_odd],
         scratch=[pltpu.VMEM((2 * rows, count * rows), F32)],
         name="attention",
-    )
-    resid_halves = mp_allreduce(kept, sent)
-    early = xor(jnp.concatenate([act_attn_select, attn_b], axis=1), "ctx", 1)
-    act_attn_there = early[:, : width // 2]
-    attn_there = early[:, width // 2 :]
-
-    resid, act_ffn, act_select, cot_select, gate_pre, up_proj, hidden = launch(
+        after=[grad_hidden],
+    )
+    attn_rows, early, log_sums, kept, sent = outs[:5]
+    blocks = [(even, outs[5:])[d % 2][d // 2] for d in range(count)]
+    resid_halves = mp_allreduce(kept, sent, "resid")
+    early_there = xor(early, "ctx", 1)
+    chosen = width // 2
+
+    resid, act_ffn, act_select, gate_pre, up_proj, hidden = launch(
         ffn_forward_kernel,
         [
             shape((rows, width), F32),
             shape((rows, width), BF),
             shape((rows, width // 2), BF),
-            shape((rows, width // 2), BF),
             shape((rows, hidden_width), F32),
             shape((rows, hidden_width), F32),
             shape((rows, hidden_width), BF),
         ],
-        [ranks, *x, *resid_halves, ffn_gain_row, gate_weight, up_weight, cot],
+        [ranks, *x, *resid_halves, ffn_gain_row, gate_weight, up_weight],
         name="ffn_forward",
     )
     hidden_there = xor(hidden, "ctx", 1)
-    cot_there = xor(cot_select, "ctx", 1)
-    grad_gate, grad_up, kept, sent = launch(
+    gate_packet, grad_up, kept, sent = launch(
         ffn_backward_kernel,
         [
-            shape((rows, hidden_width), BF),
+            shape((rows, chosen + hidden_width), BF),
             shape((rows, hidden_width), BF),
             shape((half, width), F32),
             shape((half, width), BF),
         ],
-        [gate_pre, up_proj, grad_hidden, gate_weight, up_weight],
+        [gate_pre, up_proj, grad_hidden, gate_weight, up_weight, act_select],
         name="ffn_backward",
-    )
-    grad_act_halves = mp_allreduce(kept, sent)
-    act_there = xor(act_select, "ctx", 1)
-    gate_there = xor(grad_gate, "ctx", 1)
+        after=[early_there, cot_there],
+    )
+    grad_act_halves = mp_allreduce(kept, sent, "grad_act")
+    gate_there = xor(gate_packet, "ctx", 1)
     up_there = xor(grad_up, "ctx", 1)
+
+    down_kept, down_sent = weight_grad(
+        ranks, cot, cot_there, hidden, hidden_there, (0, 0), hidden_width, "down_grad",
+        after=[grad_act_halves[1]],
+    )
 
     outs = launch(
         functools.partial(attention_backward_kernel, count),
@@ -564,103 +706,136 @@
         ]
         + [shape((rows, 2 * key_width), BF if d else F32) for d in range(count)],
         [ranks, cot, resid, *grad_act_halves, ffn_gain_row, out_weight, attn_rows, log_sums,
-         query_rot, first_seen.reshape(1, -1), *blocks],
+         query_rot, position_row, *blocks],
         name="attention_backward",
+        after=[down_sent],
     )
     grad_resid, grad_resid_b, grad_select, ffn_gain_part, grad_query = outs[:5]
     terms = outs[5:]
 
-    sums = [terms[2 * k].astype(F32) if 2 * k <= window else 0.0 for k in range(slots + 1)]
-    for j in range(slots - 1, -1, -1):
-        arrived = xor(terms[2 * j + 1], "ctx", 1).astype(F32)
-        sums[j] = sums[j] + jnp.where(odd_rank, 0.0, arrived)
-        sums[j + 1] = sums[j + 1] + jnp.where(odd_rank, arrived, 0.0)
-    pair_grad = sums[0]
-    for k in range(slots, 0, -1):
-        if 2 * k < n_ctx:
-            pair_grad = pair_grad + down(sums[k].astype(BF), 2 * k).astype(F32)
-
-    grad_query_b, query_gain_part, query_partial = launch(
+    arrived = [xor(terms[2 * j + 1], "ctx", 1) for j in range(slots)]
+    shifted = []
+    if 2 * slots < n_ctx:
+        pairs = [(i, i - 2 * slots) for i in range(2 * slots, n_ctx) if i % 2 == 1]
+        shifted.append(lax.ppermute(arrived[slots - 1], "ctx", pairs))
+    for k in range(slots - 1, 0, -1):
+        total = launch(
+            pair_sum_kernel,
+            [shape(terms[0].shape, BF)],
+            [ranks, terms[2 * k], arrived[k - 1], arrived[k]],
+            name="pair_sum",
+        )[0]
+        shifted.append(down(total, 2 * k))
+
+    late, query_gain_part, query_partial = launch(
         query_backward_kernel,
         [
-            shape((rows, query_width), BF),
+            shape((rows, chosen + query_width), BF),
             shape((1, query_width), F32),
             shape((rows, width), F32),
         ],
-        [queries, query_gain_row, grad_query, cos, sin, query_weight],
+        [queries, query_gain_row, grad_query, cos, sin, query_weight, grad_select],
         name="query_backward",
-    )
-    late = xor(jnp.concatenate([grad_select, grad_query_b], axis=1), "ctx", 1)
-    grad_there = late[:, : width // 2]
-    query_there = late[:, width // 2 :]
-
-    down_grad = weight_grad(ranks, cot, cot_there, hidden, hidden_there, "down_grad")
-    gate_grad = weight_grad(ranks, act_ffn, act_there, grad_gate, gate_there, "gate_grad")
-    up_grad = weight_grad(ranks, act_ffn, act_there, grad_up, up_there, "up_grad")
-    out_grad = weight_grad(ranks, grad_resid_b, grad_there, attn_b, attn_there, "out_grad")
-    query_grad = weight_grad(
-        ranks, act_attn, act_attn_there, grad_query_b, query_there, "query_grad"
-    )
-
-    pair_b, key_gain_part, attn_gain_part, kept, sent = launch(
+        after=[total],
+    )
+    late_there = xor(late, "ctx", 1)
+    out_kept, out_sent = launch(
+        down_kernel,
+        [shape((half, width), F32), shape((half, width), BF)],
+        [hidden, down_weight],
+        name="down",
+        after=[query_partial],
+    )
+    gate_kept, gate_sent = weight_grad(
+        ranks, act_ffn, gate_there, gate_packet, gate_there, (chosen, chosen), hidden_width,
+        "gate_grad", after=[query_partial],
+    )
+    pair_b, gains, kept, sent = launch(
         key_backward_kernel,
         [
             shape((rows, 2 * key_width), BF),
-            shape((1, key_width), F32),
-            shape((1, width), F32),
+            shape((2 * width // 128 + 2, 128), F32),
             shape((half, width), F32),
             shape((half, width), BF),
         ],
-        [keys_pre, key_gain_row, pair_grad, cos, sin, key_weight, value_weight,
-         query_partial, *x],
+        [ranks, keys_pre, key_gain_row, cos, sin, key_weight, value_weight, query_partial, *x,
+         ffn_gain_part, query_gain_part, terms[0], arrived[0], *shifted],
         name="key_backward",
+        after=[gate_sent, out_sent],
     )
     pair_there = xor(pair_b, "ctx", 1)
-    pair_weight_grad = weight_grad(
-        ranks, act_attn, act_attn_there, pair_b, pair_there, "key_value_grad"
-    )
-    grad_act_attn = mp_reduce(kept, sent)
-    inputs = block_in.astype(F32)
-    scale = row_norm(inputs)
-    normed = inputs * scale
-    inner = grad_act_attn * attn_gain
-    grad_input = grad_resid + scale * (
-        inner - normed * jnp.mean(inner * normed, axis=-1, keepdims=True)
-    )
-
-    block_out = dot(hidden, down_weight)
-    block_out = (
-        resid[:own_rows] + mp_reduce(block_out[:half], block_out[half:].astype(BF))
-    ).astype(BF)
-
-    gains = jnp.concatenate(
-        [
-            attn_gain_part.reshape(-1),
-            ffn_gain_part.reshape(-1),
-            jnp.sum(query_gain_part.reshape(-1, HD), axis=0),
-            jnp.sum(key_gain_part.reshape(-1, HD), axis=0),
-        ]
-    ).reshape(-1, 128)
+    kept, across = mp_reduce_start(kept, sent, "grad_input_core")
+    grad_input = launch(
+        grad_input_kernel,
+        [shape((own_rows, width), F32)],
+        [x[0], attn_gain_row, grad_resid, kept, across],
+        name="grad_input",
+    )[0]
+    up_kept, up_sent = weight_grad(
+        ranks, act_ffn, gate_there, grad_up, up_there, (0, 0), hidden_width, "up_grad",
+        after=[kept],
+    )
+    out_w_kept, out_w_sent = weight_grad(
+        ranks, grad_resid_b, late_there, early, early_there, (chosen, chosen), query_width,
+        "out_grad", after=[kept],
+    )
+    query_kept, query_sent = weight_grad(
+        ranks, act_attn, early_there, late, late_there, (chosen, chosen), query_width,
+        "query_grad", after=[kept],
+    )
+    pair_kept, pair_sent = weight_grad(
+        ranks, act_attn, early_there, pair_b, pair_there, (0, 0), 2 * key_width,
+        "key_value_grad", after=[query_sent],
+    )
+
+    def finish(halves, name, kernel=add_kernel, turned=False):
+        kept, arrived = halves
+        dims = kept.shape[::-1] if turned else kept.shape
+        return launch(kernel, [shape(dims, F32)], [kept, arrived], name=name)[0]
+
+    down_grad = finish(halve(down_kept, down_sent, "down"), "down_last", turned_add_kernel, True)
+    gate_grad = finish(halve(gate_kept, gate_sent, "gate"), "gate_last")
+    up_grad = finish(halve(up_kept, up_sent, "up"), "up_last")
+    out_grad = finish(halve(out_w_kept, out_w_sent, "out"), "out_last", turned_add_kernel, True)
+    query_grad = finish(halve(query_kept, query_sent, "query"), "query_last")
+    pair_kept, pair_arrived = halve(pair_kept, pair_sent, "key_value")
+    key_grad, value_grad = launch(
+        split_add_kernel,
+        [shape((pair_kept.shape[0], key_width), F32)] * 2,
+        [pair_kept, pair_arrived],
+        name="key_value_last",
+    )
+
+    out_kept, out_across = mp_reduce_start(out_kept, out_sent, "block_out_core")
+    block_out = launch(
+        block_out_kernel,
+        [shape((own_rows, width), BF)],
+        [resid, out_kept, out_across],
+        name="block_out",
+    )[0]
+
     for axis in ("mp", "ctx"):
         mask = 1
         while mask < lax.axis_size(axis):
-            gains = gains + xor(gains, axis, mask)
+            gains = add(gains, xor(gains, axis, mask), F32, "gains")
             mask *= 2
     gains = gains.reshape(-1)
+    heads = gains[2 * width :].reshape(2, -1, HD).sum(axis=1)
+    query_gains, key_gains = heads[0], heads[1]
     return (
         block_out,
         grad_input,
         query_grad,
-        pair_weight_grad[:, :key_width],
-        pair_weight_grad[:, key_width:],
-        jnp.transpose(out_grad),
+        key_grad,
+        value_grad,
+        out_grad,
         gate_grad,
         up_grad,
-        jnp.transpose(down_grad),
+        down_grad,
         gains[:width],
         gains[width : 2 * width],
-        gains[2 * width : 2 * width + HD],
-        gains[2 * width + HD :],
+        query_gains,
+        key_gains,
     )
 
 

time: 327 us -> 254 us (0.78)
  local copies, waits for them, and re-layouts: 46 us -> 16.3 us
  waiting for transfers between devices: 156 us -> 129 us
  other arithmetic: 25.2 us -> 0.65 us
  Pallas kernels: 28.8 us -> 44.1 us
  starting transfers between devices: 66.1 us -> 61.5 us
    ppermute x47 -> x43, waiting for transfers between devices: 146 us -> 120 us  [xor(): return lax.ppermute(values, axis, [(i, i ^ mask) for i in range(n)])]
    unnamed x201 -> x82, local copies, waits for them, and re-layouts: 33.1 us -> 12.5 us
    ppermute x47 -> x43, starting transfers between devices: 51.5 us -> 35.1 us  [xor(): return lax.ppermute(values, axis, [(i, i ^ mask) for i in range(n)])]
    pallas_call x13 -> x42, Pallas kernels: 28.8 us -> 44.1 us  [launch(): pl.pallas_call(run, out_shape=outs, in_specs=[pl.BlockSpec(memory_space=p...]
    ppermute x3 -> x10, starting transfers between devices: 10.8 us -> 23.8 us  [the longest x6 14 us: cross(): lax.ppermute(values, 'ctx', [(i, i ^ 1) for i in range(odd, n_ctx, 2)])]
    add x19 -> x0, other arithmetic: 10.6 us -> none  [the longest x4 5.29 us: weight_grad(): total = total[:half] + xor(total[half:].astype(BF), 'ctx', mask).astype(F32)]
    slice x17 -> x1, local copies, waits for them, and re-layouts: 5.85 us -> 0.01 us  [body(): heads = gains[2 * width:].reshape(2, -1, HD).sum(axis=1)]
    convert_element_type x6 -> x1, other arithmetic: 3.51 us -> 0.01 us  [body(): angles = positions.astype(F32)[:, None] * freqs[None, :]]
  transfers between devices with their start and end apart: 53 -> 55, of which waited for: 27 -> 22; matrix products, arithmetic and copies ran while one was open for 12% -> 2% of each run, Pallas kernels for 3% -> 14%
where the time goes in v1:
time: 254 us; the launch traced here: 253 us
  waiting for transfers between devices  129 us (51%)
  starting transfers between devices  61.5 us (24%)
  Pallas kernels  44.1 us (17%)
  local copies, waits for them, and re-layouts  16.3 us (6%)
    ppermute x43, waiting for transfers between devices, xor(): return lax.ppermute(values, axis, [(i, i ^ mask) for i in range(n)])  120 us
    pallas_call x42, Pallas kernels, launch(): pl.pallas_call(run, out_shape=outs, in_specs=[pl.BlockSpec(memory_space=p...  44.1 us
    ppermute x43, starting transfers between devices, xor(): return lax.ppermute(values, axis, [(i, i ^ mask) for i in range(n)])  35.1 us
    ppermute x6, starting transfers between devices, cross(): lax.ppermute(values, 'ctx', [(i, i ^ 1) for i in range(odd, n_ctx, 2)])  14 us
    unnamed x82, local copies, waits for them, and re-layouts  12.5 us
    ppermute x3, starting transfers between devices, climb(): return lax.ppermute(pair, 'ctx', pairs)  9.15 us
  transfers between devices with their start and end apart: 55, of which 22 were waited for; matrix products, arithmetic and copies ran while one was open for 2% of the time, Pallas kernels for 14%

profile of v1, /device:TPU:0, one launch (start us, length us, event | category | flops | bytes accessed | tf_op | source)
XLA Modules:
  0.0 253.1 jit_solution(14755335348852463747)
XLA Ops:
  0.6 3.0 %collective-permute-start = (bf16[64,1024]{1,0:T(8,128)(2,1)}, bf16[64,1024]{1,0:T(8,128)(2,1)S(1)}, u32[]{:S(2)}, u32[]{:S(2)}) collective-permute-start(bf16[64,1024]{1,0:T(8,128)(2,1)} %refs_0_.1), channel_id=1, source_target_pairs={{0,2},{1,3},{2,0},{3,1},{4,6},{5,7},{6,4},{7,5},{8,10},{9,11},{10,... | collective-permute-start | bytes 393224 | tf_op jit(solution)/shard_map/ppermute | solution.py:30
  5.1 2.8 %collective-permute-done.refs_2_.refs_9_ = bf16[64,1024]{1,0:T(8,128)(2,1)S(1)} collective-permute-done((bf16[64,1024]{1,0:T(8,128)(2,1)}, bf16[64,1024]{1,0:T(8,128)(2,1)S(1)}, u32[]{:S(2)}, u32[]{:S(2)}) %collective-permute-start) | collective-permute-done | bytes 131104 | tf_op jit(solution)/shard_map/ppermute | solution.py:30
  14.9 1.8 qkv.1
  16.7 4.0 %collective-permute-start.3 = (bf16[256,256]{1,0:T(8,128)(2,1)S(1)}, bf16[256,256]{1,0:T(8,128)(2,1)S(1)}, u32[]{:S(2)}, u32[]{:S(2)}) collective-permute-start(bf16[256,256]{1,0:T(8,128)(2,1)S(1)} %get-tuple-element.92.refs_5_.refs_11_), channel_id=1, source_target_pairs={{0,8},{4,12},{8,16},{12,20},{16,24},{20,28},{1,9},{5,13},{9,17},{1... | collective-permute-start | bytes 393224 | tf_op jit(solution)/shard_map/ppermute | solution.py:622
  21.0 4.5 %collective-permute-start.4 = (bf16[256,256]{1,0:T(8,128)(2,1)S(1)}, bf16[256,256]{1,0:T(8,128)(2,1)S(1)}, u32[]{:S(2)}, u32[]{:S(2)}) collective-permute-start(bf16[256,256]{1,0:T(8,128)(2,1)S(1)} %get-tuple-element.92.refs_5_.refs_11_), channel_id=1, source_target_pairs={{0,16},{4,20},{8,24},{12,28},{1,17},{5,21},{9,25},{13,29},{2,18},{... | collective-permute-start | bytes 393224 | tf_op jit(solution)/shard_map/ppermute | solution.py:622
  25.5 3.4 %collective-permute-start.5 = (bf16[256,256]{1,0:T(8,128)(2,1)S(1)}, bf16[256,256]{1,0:T(8,128)(2,1)S(1)}, u32[]{:S(2)}, u32[]{:S(2)}) collective-permute-start(bf16[256,256]{1,0:T(8,128)(2,1)S(1)} %get-tuple-element.92.refs_5_.refs_11_), channel_id=1, source_target_pairs={{0,4},{8,12},{16,20},{24,28},{1,5},{9,13},{17,21},{25,29},{2,6},{1... | collective-permute-start | bytes 393224 | tf_op jit(solution)/shard_map/ppermute | solution.py:615
  29.6 1.9 collective-permute-start.6
  32.9 4.6 %collective-permute-start.7 = (bf16[256,256]{1,0:T(8,128)(2,1)S(1)}, bf16[256,256]{1,0:T(8,128)(2,1)S(1)}, u32[]{:S(2)}, u32[]{:S(2)}) collective-permute-start(bf16[256,256]{1,0:T(8,128)(2,1)S(1)} %collective-permute-done.4.refs_7_.refs_15_), channel_id=1, source_target_pairs={{0,4},{8,12},{16,20},{24,28},{1,5},{9,13},{17,21},{25,29},{2,6},{1... | collective-permute-start | bytes 393224 | tf_op jit(solution)/shard_map/ppermute | solution.py:615
  38.8 1.5 collective-permute-start.11
  41.2 1.8 cotangent.1
  43.1 2.3 collective-permute-done.9.refs_12_
  45.4 1.4 collective-permute-done.11.refs_13_
  46.8 3.9 %attention.1 = (f32[256,256]{1,0:T(8,128)S(1)}, bf16[256,768]{1,0:T(8,128)(2,1)S(1)}, f32[2,512]{1,0:T(2,128)S(1)}, f32[128,1024]{1,0:T(8,128)S(1)}, bf16[128,10...) custom-call(s32[2]{0:T(128)S(1)} %pad_add_fusion.refs_0_, ...), custom_call_target="tpu_custom_call" | custom-call | tf_op jit(solution)/shard_map/attention/pallas_call | solution.py:451
  50.8 1.5 collective-permute-done.15.refs_1_
  52.4 2.1 collective-permute-start.16
  54.5 6.6 %collective-permute-done.16.refs_1_ = bf16[128,1024]{1,0:T(8,128)(2,1)S(1)} collective-permute-done((bf16[128,1024]{1,0:T(8,128)(2,1)S(1)}, bf16[128,1024]{1,0:T(8,128)(2,1)S(1)}, u32[]{:S(2)}, u32[]{:S(2)}) %collective-permute-start.16) | collective-permute-done | bytes 262176 | tf_op jit(solution)/shard_map/ppermute | solution.py:30
  61.3 1.4 collective-permute-done.17.refs_6_
  62.8 2.4 ffn_forward.1
  65.2 5.7 %collective-permute-done.19.refs_7_.refs_2_ = bf16[256,512]{1,0:T(8,128)(2,1)S(1)} collective-permute-done((bf16[256,512]{1,0:T(8,128)(2,1)S(1)}, bf16[256,512]{1,0:T(8,128)(2,1)S(1)}, u32[]{:S(2)}, u32[]{:S(2)}) %collective-permute-start.19) | collective-permute-done | bytes 262176 | tf_op jit(solution)/shard_map/ppermute | solution.py:30
  71.0 3.3 %ffn_backward.1 = (bf16[256,1664]{1,0:T(8,128)(2,1)S(1)}, bf16[256,1152]{1,0:T(8,128)(2,1)S(1)}, f32[128,1024]{1,0:T(8,128)S(1)}, bf16[128,1024]{1,0:T(8,128)(2,1)S(1)}) custom-call(f32[256,1152]{1,0:T(8,128)S(1)} %get-tuple-element.100.refs_0_, f32[256,1152]{1,0:T(8,128)S(1)} %get-tuple-element.101.refs_1_, ...), custom_call_target="tpu_custom_call" | custom-call | tf_op jit(solution)/shard_map/ffn_backward/pallas_call | solution.py:451
  74.7 1.7 collective-permute-start.32
  77.3 7.4 %collective-permute-done.21.refs_1_ = bf16[128,1024]{1,0:T(8,128)(2,1)S(1)} collective-permute-done((bf16[128,1024]{1,0:T(8,128)(2,1)S(1)}, bf16[128,1024]{1,0:T(8,128)(2,1)S(1)}, u32[]{:S(2)}, u32[]{:S(2)}) %collective-permute-start.21) | collective-permute-done | bytes 262176 | tf_op jit(solution)/shard_map/ppermute | solution.py:30
  85.1 5.4 %collective-permute-done.23.refs_4_ = bf16[256,1152]{1,0:T(8,128)(2,1)S(1)} collective-permute-done((bf16[256,1152]{1,0:T(8,128)(2,1)S(1)}, bf16[256,1152]{1,0:T(8,128)(2,1)S(1)}, u32[]{:S(2)}, u32[]{:S(2)}) %collective-permute-start.23) | collective-permute-done | bytes 589856 | tf_op jit(solution)/shard_map/ppermute | solution.py:30
  90.5 1.4 down_grad.1
  92.0 7.1 %attention_backward.1 = (f32[64,1024]{1,0:T(8,128)S(1)}, bf16[256,1024]{1,0:T(8,128)(2,1)S(1)}, bf16[256,512]{1,0:T(8,128)(2,1)S(1)}, f32[1,1024]{1,0:T(1,128)S(...) custom-call(s32[2]{0:T(128)S(1)} %pad_add_fusion.refs_0_, ...), custom_call_target="tpu_custom_call" | custom-call | tf_op jit(solution)/shard_map/attention_backward/pallas_call | solution.py:451
  99.4 1.7 collective-permute-start.28
  101.5 22.7 %collective-permute-done.25.refs_3_.refs_2_ = bf16[256,256]{1,0:T(8,128)(2,1)S(1)} collective-permute-done((bf16[256,256]{1,0:T(8,128)(2,1)S(1)}, bf16[256,256]{1,0:T(8,128)(2,1)S(1)}, u32[]{:S(2)}, u32[]{:S(2)}) %collective-permute-start.25) | collective-permute-done | bytes 131104 | tf_op jit(solution)/shard_map/ppermute | solution.py:30
  124.2 2.8 %collective-permute-done.28.refs_3_ = bf16[256,256]{1,0:T(8,128)(2,1)S(1)} collective-permute-done((bf16[256,256]{1,0:T(8,128)(2,1)S(1)}, bf16[256,256]{1,0:T(8,128)(2,1)S(1)}, u32[]{:S(2)}, u32[]{:S(2)}) %collective-permute-start.28) | collective-permute-done | bytes 131104 | tf_op jit(solution)/shard_map/ppermute | solution.py:30
  133.2 1.5 gate_grad.1
  134.7 3.1 %collective-permute-done.30.refs_17_ = bf16[256,256]{1,0:T(8,128)(2,1)S(1)} collective-permute-done((bf16[256,256]{1,0:T(8,128)(2,1)S(1)}, bf16[256,256]{1,0:T(8,128)(2,1)S(1)}, u32[]{:S(2)}, u32[]{:S(2)}) %collective-permute-start.30) | collective-permute-done | bytes 131104 | tf_op jit(solution)/shard_map/ppermute | solution.py:40
  137.8 1.9 collective-permute-done.31.refs_18_
  139.6 1.4 key_backward.1
  141.1 1.5 collective-permute-start.48
  142.6 3.1 %collective-permute-start.35 = (bf16[256,768]{1,0:T(8,128)(2,1)S(1)}, bf16[256,768]{1,0:T(8,128)(2,1)S(1)}, u32[]{:S(2)}, u32[]{:S(2)}) collective-permute-start(bf16[256,768]{1,0:T(8,128)(2,1)S(1)} %get-tuple-element.138.refs_3_), channel_id=1, source_target_pairs={{0,4},{4,0},{8,12},{12,8},{16,20},{20,16},{24,28},{28,24},{1,5},{5... | collective-permute-start | bytes 1179656 | tf_op jit(solution)/shard_map/ppermute | solution.py:30
  147.3 1.5 up_grad.1
  151.8 3.0 %collective-permute-done.51.refs_1_ = f32[18,128]{1,0:T(8,128)S(1)} collective-permute-done((f32[18,128]{1,0:T(8,128)S(1)}, f32[18,128]{1,0:T(8,128)S(1)}, u32[]{:S(2)}, u32[]{:S(2)}) %collective-permute-start.51) | collective-permute-done | bytes 9248 | tf_op jit(solution)/shard_map/ppermute | solution.py:30
  154.8 3.7 %collective-permute-done.52.refs_1_ = f32[18,128]{1,0:T(8,128)S(1)} collective-permute-done((f32[18,128]{1,0:T(8,128)S(1)}, f32[18,128]{1,0:T(8,128)S(1)}, u32[]{:S(2)}, u32[]{:S(2)}) %collective-permute-start.52) | collective-permute-done | bytes 9248 | tf_op jit(solution)/shard_map/ppermute | solution.py:30
  159.5 22.9 %collective-permute-done.53.refs_1_ = f32[18,128]{1,0:T(8,128)S(1)} collective-permute-done((f32[18,128]{1,0:T(8,128)S(1)}, f32[18,128]{1,0:T(8,128)S(1)}, u32[]{:S(2)}, u32[]{:S(2)}) %collective-permute-start.53) | collective-permute-done | bytes 9248 | tf_op jit(solution)/shard_map/ppermute | solution.py:30
  182.4 3.4 %collective-permute-start.38 = (bf16[256,256]{1,0:T(8,128)(2,1)S(1)}, bf16[256,256]{1,0:T(8,128)(2,1)S(1)}, u32[]{:S(2)}, u32[]{:S(2)}) collective-permute-start(bf16[256,256]{1,0:T(8,128)(2,1)S(1)} %get-tuple-element.143.refs_3_), channel_id=1, source_target_pairs={{0,4},{4,0},{8,12},{12,8},{16,20},{20,16},{24,28},{28,24},{1,5},{5... | collective-permute-start | bytes 393224 | tf_op jit(solution)/shard_map/ppermute | solution.py:30
  187.9 2.1 collective-permute-done.38.refs_4_
  192.0 2.6 %collective-permute-done.54.refs_1_ = f32[18,128]{1,0:T(8,128)S(1)} collective-permute-done((f32[18,128]{1,0:T(8,128)S(1)}, f32[18,128]{1,0:T(8,128)S(1)}, u32[]{:S(2)}, u32[]{:S(2)}) %collective-permute-start.54) | collective-permute-done | bytes 9248 | tf_op jit(solution)/shard_map/ppermute | solution.py:30
  199.6 1.3 collective-permute-start.34
  202.9 2.6 %collective-permute-start.37 = (bf16[128,256]{1,0:T(8,128)(2,1)}, bf16[128,256]{1,0:T(8,128)(2,1)}, u32[]{:S(2)}, u32[]{:S(2)}) collective-permute-start(bf16[128,256]{1,0:T(8,128)(2,1)} %get-tuple-element.142), channel_id=1, source_target_pairs={{0,16},{4,20},{8,24},{12,28},{16,0},{20,4},{24,8},{28,12},{1,17},{... | collective-permute-start | bytes 196616 | tf_op jit(solution)/shard_map/ppermute | solution.py:30
  207.2 2.6 %collective-permute-start.47 = (bf16[128,1152]{1,0:T(8,128)(2,1)}, bf16[128,1152]{1,0:T(8,128)(2,1)S(1)}, u32[]{:S(2)}, u32[]{:S(2)}) collective-permute-start(bf16[128,1152]{1,0:T(8,128)(2,1)} %get-tuple-element.162), channel_id=1, source_target_pairs={{0,16},{4,20},{8,24},{12,28},{16,0},{20,4},{24,8},{28,12},{1,17},{... | collective-permute-start | bytes 884744 | tf_op jit(solution)/shard_map/ppermute | solution.py:30
  214.7 18.7 %collective-permute-done.37.refs_1_ = bf16[128,256]{1,0:T(8,128)(2,1)} collective-permute-done((bf16[128,256]{1,0:T(8,128)(2,1)}, bf16[128,256]{1,0:T(8,128)(2,1)}, u32[]{:S(2)}, u32[]{:S(2)}) %collective-permute-start.37) | collective-permute-done | bytes 65568 | tf_op jit(solution)/shard_map/ppermute | solution.py:30
  235.6 1.9 grad_input.1
  237.5 1.5 query_last.1
  239.0 9.7 %collective-permute-done.40.refs_1_ = bf16[128,256]{1,0:T(8,128)(2,1)S(1)} collective-permute-done((bf16[128,256]{1,0:T(8,128)(2,1)S(1)}, bf16[128,256]{1,0:T(8,128)(2,1)S(1)}, u32[]{:S(2)}, u32[]{:S(2)}) %collective-permute-start.40) | collective-permute-done | bytes 65568 | tf_op jit(solution)/shard_map/ppermute | solution.py:30
  (207 shorter events, 51.4 us)
Async XLA Ops:
  0.6 7.2 %collective-permute-start = (bf16[64,1024]{1,0:T(8,128)(2,1)}, bf16[64,1024]{1,0:T(8,128)(2,1)S(1)}, u32[]{:S(2)}, u32[]{:S(2)}) collective-permute-start(bf16[64,1024]{1,0:T(8,128)(2,1)} %refs_0_.1), channel_id=1, source_target_pairs={{0,2},{1,3},{2,0},{3,1},{4,6},{5,7},{6,4},{7,5},{8,10},{9,11},{10,... | collective-permute-start | bytes 393224 | tf_op jit(solution)/shard_map/ppermute | solution.py:30
  3.6 6.6 %collective-permute-start.1 = (bf16[64,1024]{1,0:T(8,128)(2,1)}, bf16[64,1024]{1,0:T(8,128)(2,1)S(1)}, u32[]{:S(2)}, u32[]{:S(2)}) collective-permute-start(bf16[64,1024]{1,0:T(8,128)(2,1)} %refs_0_.1), channel_id=1, source_target_pairs={{0,1},{1,0},{2,3},{3,2},{4,5},{5,4},{6,7},{7,6},{8,9},{9,8},{10,11... | collective-permute-start | bytes 393224 | tf_op jit(solution)/shard_map/ppermute | solution.py:30
  3.7 17.1 %collective-permute-start.12 = (bf16[64,1024]{1,0:T(8,128)(2,1)}, bf16[64,1024]{1,0:T(8,128)(2,1)S(1)}, u32[]{:S(2)}, u32[]{:S(2)}) collective-permute-start(bf16[64,1024]{1,0:T(8,128)(2,1)} %refs_1_.5), channel_id=1, source_target_pairs={{0,2},{1,3},{2,0},{3,1},{4,6},{5,7},{6,4},{7,5},{8,10},{9,11},{10,... | collective-permute-start | bytes 393224 | tf_op jit(solution)/shard_map/ppermute | solution.py:30
  3.8 25.1 %collective-permute-start.13 = (bf16[64,1024]{1,0:T(8,128)(2,1)}, bf16[64,1024]{1,0:T(8,128)(2,1)}, u32[]{:S(2)}, u32[]{:S(2)}) collective-permute-start(bf16[64,1024]{1,0:T(8,128)(2,1)} %refs_1_.5), channel_id=1, source_target_pairs={{0,1},{1,0},{2,3},{3,2},{4,5},{5,4},{6,7},{7,6},{8,9},{9,8},{10,11... | collective-permute-start | bytes 393224 | tf_op jit(solution)/shard_map/ppermute | solution.py:30
  16.7 12.9 %collective-permute-start.3 = (bf16[256,256]{1,0:T(8,128)(2,1)S(1)}, bf16[256,256]{1,0:T(8,128)(2,1)S(1)}, u32[]{:S(2)}, u32[]{:S(2)}) collective-permute-start(bf16[256,256]{1,0:T(8,128)(2,1)S(1)} %get-tuple-element.92.refs_5_.refs_11_), channel_id=1, source_target_pairs={{0,8},{4,12},{8,16},{12,20},{16,24},{20,28},{1,9},{5,13},{9,17},{1... | collective-permute-start | bytes 393224 | tf_op jit(solution)/shard_map/ppermute | solution.py:622
  20.7 10.8 %collective-permute-start.14 = (bf16[64,1024]{1,0:T(8,128)(2,1)S(1)}, bf16[64,1024]{1,0:T(8,128)(2,1)S(1)}, u32[]{:S(2)}, u32[]{:S(2)}) collective-permute-start(bf16[64,1024]{1,0:T(8,128)(2,1)S(1)} %collective-permute-done.12.refs_2_), channel_id=1, source_target_pairs={{0,1},{1,0},{2,3},{3,2},{4,5},{5,4},{6,7},{7,6},{8,9},{9,8},{10,11... | collective-permute-start | bytes 393224 | tf_op jit(solution)/shard_map/ppermute | solution.py:30
  21.0 11.9 %collective-permute-start.4 = (bf16[256,256]{1,0:T(8,128)(2,1)S(1)}, bf16[256,256]{1,0:T(8,128)(2,1)S(1)}, u32[]{:S(2)}, u32[]{:S(2)}) collective-permute-start(bf16[256,256]{1,0:T(8,128)(2,1)S(1)} %get-tuple-element.92.refs_5_.refs_11_), channel_id=1, source_target_pairs={{0,16},{4,20},{8,24},{12,28},{1,17},{5,21},{9,25},{13,29},{2,18},{... | collective-permute-start | bytes 393224 | tf_op jit(solution)/shard_map/ppermute | solution.py:622
  25.5 12.0 %collective-permute-start.5 = (bf16[256,256]{1,0:T(8,128)(2,1)S(1)}, bf16[256,256]{1,0:T(8,128)(2,1)S(1)}, u32[]{:S(2)}, u32[]{:S(2)}) collective-permute-start(bf16[256,256]{1,0:T(8,128)(2,1)S(1)} %get-tuple-element.92.refs_5_.refs_11_), channel_id=1, source_target_pairs={{0,4},{8,12},{16,20},{24,28},{1,5},{9,13},{17,21},{25,29},{2,6},{1... | collective-permute-start | bytes 393224 | tf_op jit(solution)/shard_map/ppermute | solution.py:615
  28.9 9.8 %collective-permute-start.10 = (bf16[256,256]{1,0:T(8,128)(2,1)S(1)}, bf16[256,256]{1,0:T(8,128)(2,1)S(1)}, u32[]{:S(2)}, u32[]{:S(2)}) collective-permute-start(bf16[256,256]{1,0:T(8,128)(2,1)S(1)} %get-tuple-element.92.refs_5_.refs_11_), channel_id=1, source_target_pairs={{4,28},{5,29},{6,30},{7,31}} | collective-permute-start | bytes 393224 | tf_op jit(solution)/shard_map/ppermute | solution.py:622
  29.6 13.4 %collective-permute-start.6 = (bf16[256,256]{1,0:T(8,128)(2,1)S(1)}, bf16[256,256]{1,0:T(8,128)(2,1)S(1)}, u32[]{:S(2)}, u32[]{:S(2)}) collective-permute-start(bf16[256,256]{1,0:T(8,128)(2,1)S(1)} %collective-permute-done.3.refs_6_.refs_13_), channel_id=1, source_target_pairs={{0,4},{8,12},{16,20},{24,28},{1,5},{9,13},{17,21},{25,29},{2,6},{1... | collective-permute-start | bytes 393224 | tf_op jit(solution)/shard_map/ppermute | solution.py:615
  31.6 11.5 %collective-permute-start.8 = (bf16[256,256]{1,0:T(8,128)(2,1)S(1)}, bf16[256,256]{1,0:T(8,128)(2,1)S(1)}, u32[]{:S(2)}, u32[]{:S(2)}) collective-permute-start(bf16[256,256]{1,0:T(8,128)(2,1)S(1)} %collective-permute-done.3.refs_6_.refs_13_), channel_id=1, source_target_pairs={{4,0},{12,8},{20,16},{28,24},{5,1},{13,9},{21,17},{29,25},{6,2},{1... | collective-permute-start | bytes 393224 | tf_op jit(solution)/shard_map/ppermute | solution.py:615
  32.9 10.2 %collective-permute-start.7 = (bf16[256,256]{1,0:T(8,128)(2,1)S(1)}, bf16[256,256]{1,0:T(8,128)(2,1)S(1)}, u32[]{:S(2)}, u32[]{:S(2)}) collective-permute-start(bf16[256,256]{1,0:T(8,128)(2,1)S(1)} %collective-permute-done.4.refs_7_.refs_15_), channel_id=1, source_target_pairs={{0,4},{8,12},{16,20},{24,28},{1,5},{9,13},{17,21},{25,29},{2,6},{1... | collective-permute-start | bytes 393224 | tf_op jit(solution)/shard_map/ppermute | solution.py:615
  37.5 7.9 %collective-permute-start.9 = (bf16[256,256]{1,0:T(8,128)(2,1)S(1)}, bf16[256,256]{1,0:T(8,128)(2,1)S(1)}, u32[]{:S(2)}, u32[]{:S(2)}) collective-permute-start(bf16[256,256]{1,0:T(8,128)(2,1)S(1)} %collective-permute-done.4.refs_7_.refs_15_), channel_id=1, source_target_pairs={{4,0},{12,8},{20,16},{28,24},{5,1},{13,9},{21,17},{29,25},{6,2},{1... | collective-permute-start | bytes 393224 | tf_op jit(solution)/shard_map/ppermute | solution.py:615
  38.8 8.0 %collective-permute-start.11 = (bf16[256,256]{1,0:T(8,128)(2,1)S(1)}, bf16[256,256]{1,0:T(8,128)(2,1)S(1)}, u32[]{:S(2)}, u32[]{:S(2)}) collective-permute-start(bf16[256,256]{1,0:T(8,128)(2,1)S(1)} %collective-permute-done.10), channel_id=1, source_target_pairs={{4,0},{12,8},{20,16},{28,24},{5,1},{13,9},{21,17},{29,25},{6,2},{1... | collective-permute-start | bytes 393224 | tf_op jit(solution)/shard_map/ppermute | solution.py:615
  52.4 8.7 %collective-permute-start.16 = (bf16[128,1024]{1,0:T(8,128)(2,1)S(1)}, bf16[128,1024]{1,0:T(8,128)(2,1)S(1)}, u32[]{:S(2)}, u32[]{:S(2)}) collective-permute-start(bf16[128,1024]{1,0:T(8,128)(2,1)S(1)} %resid_core.1.refs_0_), channel_id=1, source_target_pairs={{0,2},{1,3},{2,0},{3,1},{4,6},{5,7},{6,4},{7,5},{8,10},{9,11},{10,... | collective-permute-start | bytes 786440 | tf_op jit(solution)/shard_map/ppermute | solution.py:30
  54.5 16.5 %collective-permute-start.18 = (bf16[256,768]{1,0:T(8,128)(2,1)S(1)}, bf16[256,768]{1,0:T(8,128)(2,1)S(1)}, u32[]{:S(2)}, u32[]{:S(2)}) collective-permute-start(bf16[256,768]{1,0:T(8,128)(2,1)S(1)} %get-tuple-element.103.refs_3_), channel_id=1, source_target_pairs={{0,4},{4,0},{8,12},{12,8},{16,20},{20,16},{24,28},{28,24},{1,5},{5... | collective-permute-start | bytes 1179656 | tf_op jit(solution)/shard_map/ppermute | solution.py:30
  61.2 9.7 %collective-permute-start.19 = (bf16[256,512]{1,0:T(8,128)(2,1)S(1)}, bf16[256,512]{1,0:T(8,128)(2,1)S(1)}, u32[]{:S(2)}, u32[]{:S(2)}) collective-permute-start(bf16[256,512]{1,0:T(8,128)(2,1)S(1)} %get-tuple-element.104), channel_id=1, source_target_pairs={{0,4},{4,0},{8,12},{12,8},{16,20},{20,16},{24,28},{28,24},{1,5},{5... | collective-permute-start | bytes 786440 | tf_op jit(solution)/shard_map/ppermute | solution.py:30
  74.3 16.2 %collective-permute-start.23 = (bf16[256,1152]{1,0:T(8,128)(2,1)S(1)}, bf16[256,1152]{1,0:T(8,128)(2,1)S(1)}, u32[]{:S(2)}, u32[]{:S(2)}) collective-permute-start(bf16[256,1152]{1,0:T(8,128)(2,1)S(1)} %get-tuple-element.97.refs_3_.refs_0_), channel_id=1, source_target_pairs={{0,4},{4,0},{8,12},{12,8},{16,20},{20,16},{24,28},{28,24},{1,5},{5... | collective-permute-start | bytes 1769480 | tf_op jit(solution)/shard_map/ppermute | solution.py:30
  74.7 58.5 %collective-permute-start.32 = (bf16[256,1664]{1,0:T(8,128)(2,1)S(1)}, bf16[256,1664]{1,0:T(8,128)(2,1)S(1)}, u32[]{:S(2)}, u32[]{:S(2)}) collective-permute-start(bf16[256,1664]{1,0:T(8,128)(2,1)S(1)} %get-tuple-element.131.refs_3_), channel_id=1, source_target_pairs={{0,4},{4,0},{8,12},{12,8},{16,20},{20,16},{24,28},{28,24},{1,5},{5... | collective-permute-start | bytes 2555912 | tf_op jit(solution)/shard_map/ppermute | solution.py:30
  76.5 8.2 %collective-permute-start.21 = (bf16[128,1024]{1,0:T(8,128)(2,1)S(1)}, bf16[128,1024]{1,0:T(8,128)(2,1)S(1)}, u32[]{:S(2)}, u32[]{:S(2)}) collective-permute-start(bf16[128,1024]{1,0:T(8,128)(2,1)S(1)} %grad_act_core.1.refs_0_), channel_id=1, source_target_pairs={{0,2},{1,3},{2,0},{3,1},{4,6},{5,7},{6,4},{7,5},{8,10},{9,11},{10,... | collective-permute-start | bytes 786440 | tf_op jit(solution)/shard_map/ppermute | solution.py:30
  84.7 5.8 %collective-permute-start.22 = (bf16[128,1024]{1,0:T(8,128)(2,1)S(1)}, bf16[128,1024]{1,0:T(8,128)(2,1)S(1)}, u32[]{:S(2)}, u32[]{:S(2)}) collective-permute-start(bf16[128,1024]{1,0:T(8,128)(2,1)S(1)} %grad_act_chip.1.refs_3_), channel_id=1, source_target_pairs={{0,1},{1,0},{2,3},{3,2},{4,5},{5,4},{6,7},{7,6},{8,9},{9,8},{10,11... | collective-permute-start | bytes 786440 | tf_op jit(solution)/shard_map/ppermute | solution.py:30
  84.8 62.5 %collective-permute-start.45 = (bf16[256,1152]{1,0:T(8,128)(2,1)S(1)}, bf16[256,1152]{1,0:T(8,128)(2,1)S(1)}, u32[]{:S(2)}, u32[]{:S(2)}) collective-permute-start(bf16[256,1152]{1,0:T(8,128)(2,1)S(1)} %get-tuple-element.158.refs_3_), channel_id=1, source_target_pairs={{0,4},{4,0},{8,12},{12,8},{16,20},{20,16},{24,28},{28,24},{1,5},{5... | collective-permute-start | bytes 1769480 | tf_op jit(solution)/shard_map/ppermute | solution.py:30
  99.1 25.1 %collective-permute-start.25 = (bf16[256,256]{1,0:T(8,128)(2,1)S(1)}, bf16[256,256]{1,0:T(8,128)(2,1)S(1)}, u32[]{:S(2)}, u32[]{:S(2)}) collective-permute-start(bf16[256,256]{1,0:T(8,128)(2,1)S(1)} %get-tuple-element.117), channel_id=1, source_target_pairs={{0,4},{4,0},{8,12},{12,8},{16,20},{20,16},{24,28},{28,24},{1,5},{5... | collective-permute-start | bytes 393224 | tf_op jit(solution)/shard_map/ppermute | solution.py:30
  99.4 27.6 %collective-permute-start.28 = (bf16[256,256]{1,0:T(8,128)(2,1)S(1)}, bf16[256,256]{1,0:T(8,128)(2,1)S(1)}, u32[]{:S(2)}, u32[]{:S(2)}) collective-permute-start(bf16[256,256]{1,0:T(8,128)(2,1)S(1)} %get-tuple-element.128), channel_id=1, source_target_pairs={{0,4},{4,0},{8,12},{12,8},{16,20},{20,16},{24,28},{28,24},{1,5},{5... | collective-permute-start | bytes 393224 | tf_op jit(solution)/shard_map/ppermute | solution.py:30
  101.2 28.4 %collective-permute-start.24 = (bf16[256,256]{1,0:T(8,128)(2,1)S(1)}, bf16[256,256]{1,0:T(8,128)(2,1)S(1)}, u32[]{:S(2)}, u32[]{:S(2)}) collective-permute-start(bf16[256,256]{1,0:T(8,128)(2,1)S(1)} %get-tuple-element.116), channel_id=1, source_target_pairs={{0,4},{4,0},{8,12},{12,8},{16,20},{20,16},{24,28},{28,24},{1,5},{5... | collective-permute-start | bytes 393224 | tf_op jit(solution)/shard_map/ppermute | solution.py:30
  127.6 10.1 %collective-permute-start.30 = (bf16[256,256]{1,0:T(8,128)(2,1)S(1)}, bf16[256,256]{1,0:T(8,128)(2,1)S(1)}, u32[]{:S(2)}, u32[]{:S(2)}) collective-permute-start(bf16[256,256]{1,0:T(8,128)(2,1)S(1)} %pair_sum.3), channel_id=1, source_target_pairs={{16,0},{20,4},{24,8},{28,12},{17,1},{21,5},{25,9},{29,13},{18,2},{... | collective-permute-start | bytes 393224 | tf_op jit(solution)/shard_map/ppermute | solution.py:40
  128.9 5.7 %collective-permute-start.29 = (bf16[256,256]{1,0:T(8,128)(2,1)S(1)}, bf16[256,256]{1,0:T(8,128)(2,1)S(1)}, u32[]{:S(2)}, u32[]{:S(2)}) collective-permute-start(bf16[256,256]{1,0:T(8,128)(2,1)S(1)} %collective-permute-done.28.refs_3_), channel_id=1, source_target_pairs={{28,4},{29,5},{30,6},{31,7}} | collective-permute-start | bytes 393224 | tf_op jit(solution)/shard_map/ppermute | solution.py:720
  130.2 9.4 %collective-permute-start.31 = (bf16[256,256]{1,0:T(8,128)(2,1)S(1)}, bf16[256,256]{1,0:T(8,128)(2,1)S(1)}, u32[]{:S(2)}, u32[]{:S(2)}) collective-permute-start(bf16[256,256]{1,0:T(8,128)(2,1)S(1)} %pair_sum.2.refs_7_), channel_id=1, source_target_pairs={{8,0},{12,4},{16,8},{20,12},{24,16},{28,20},{9,1},{13,5},{17,9},{2... | collective-permute-start | bytes 393224 | tf_op jit(solution)/shard_map/ppermute | solution.py:40
  141.0 5.6 %collective-permute-start.33 = (bf16[128,1024]{1,0:T(8,128)(2,1)S(1)}, bf16[128,1024]{1,0:T(8,128)(2,1)S(1)}, u32[]{:S(2)}, u32[]{:S(2)}) collective-permute-start(bf16[128,1024]{1,0:T(8,128)(2,1)S(1)} %get-tuple-element.134), channel_id=1, source_target_pairs={{0,1},{1,0},{2,3},{3,2},{4,5},{5,4},{6,7},{7,6},{8,9},{9,8},{10,11... | collective-permute-start | bytes 786440 | tf_op jit(solution)/shard_map/ppermute | solution.py:30
  141.1 54.2 %collective-permute-start.48 = (bf16[256,1152]{1,0:T(8,128)(2,1)S(1)}, bf16[256,1152]{1,0:T(8,128)(2,1)S(1)}, u32[]{:S(2)}, u32[]{:S(2)}) collective-permute-start(bf16[256,1152]{1,0:T(8,128)(2,1)S(1)} %get-tuple-element.112.refs_17_), channel_id=1, source_target_pairs={{0,8},{4,12},{8,0},{12,4},{16,24},{20,28},{24,16},{28,20},{1,9},{5... | collective-permute-start | bytes 1769480 | tf_op jit(solution)/shard_map/ppermute | solution.py:30
  142.6 39.8 %collective-permute-start.35 = (bf16[256,768]{1,0:T(8,128)(2,1)S(1)}, bf16[256,768]{1,0:T(8,128)(2,1)S(1)}, u32[]{:S(2)}, u32[]{:S(2)}) collective-permute-start(bf16[256,768]{1,0:T(8,128)(2,1)S(1)} %get-tuple-element.138.refs_3_), channel_id=1, source_target_pairs={{0,4},{4,0},{8,12},{12,8},{16,20},{20,16},{24,28},{28,24},{1,5},{5... | collective-permute-start | bytes 1179656 | tf_op jit(solution)/shard_map/ppermute | solution.py:30
  145.6 54.0 %collective-permute-start.43 = (bf16[256,1152]{1,0:T(8,128)(2,1)S(1)}, bf16[256,1152]{1,0:T(8,128)(2,1)S(1)}, u32[]{:S(2)}, u32[]{:S(2)}) collective-permute-start(bf16[256,1152]{1,0:T(8,128)(2,1)S(1)} %get-tuple-element.132.refs_19_), channel_id=1, source_target_pairs={{0,8},{4,12},{8,0},{12,4},{16,24},{20,28},{24,16},{28,20},{1,9},{5... | collective-permute-start | bytes 1769480 | tf_op jit(solution)/shard_map/ppermute | solution.py:30
  148.8 53.0 %collective-permute-start.46 = (bf16[256,1152]{1,0:T(8,128)(2,1)S(1)}, bf16[256,1152]{1,0:T(8,128)(2,1)S(1)}, u32[]{:S(2)}, u32[]{:S(2)}) collective-permute-start(bf16[256,1152]{1,0:T(8,128)(2,1)S(1)} %get-tuple-element.160), channel_id=1, source_target_pairs={{0,8},{4,12},{8,0},{12,4},{16,24},{20,28},{24,16},{28,20},{1,9},{5... | collective-permute-start | bytes 1769480 | tf_op jit(solution)/shard_map/ppermute | solution.py:30
  158.5 23.9 %collective-permute-start.53 = (f32[18,128]{1,0:T(8,128)S(1)}, f32[18,128]{1,0:T(8,128)S(1)}, u32[]{:S(2)}, u32[]{:S(2)}) collective-permute-start(f32[18,128]{1,0:T(8,128)S(1)} %gains.7.refs_0_), channel_id=1, source_target_pairs={{0,8},{4,12},{8,0},{12,4},{16,24},{20,28},{24,16},{28,20},{1,9},{5... | collective-permute-start | bytes 27656 | tf_op jit(solution)/shard_map/ppermute | solution.py:30
  182.4 4.3 %collective-permute-start.26 = (bf16[128,1024]{1,0:T(8,128)(2,1)S(1)}, bf16[128,1024]{1,0:T(8,128)(2,1)S(1)}, u32[]{:S(2)}, u32[]{:S(2)}) collective-permute-start(bf16[128,1024]{1,0:T(8,128)(2,1)S(1)} %get-tuple-element.120.refs_20_), channel_id=1, source_target_pairs={{0,1},{1,0},{2,3},{3,2},{4,5},{5,4},{6,7},{7,6},{8,9},{9,8},{10,11... | collective-permute-start | bytes 786440 | tf_op jit(solution)/shard_map/ppermute | solution.py:30
  182.4 7.6 %collective-permute-start.38 = (bf16[256,256]{1,0:T(8,128)(2,1)S(1)}, bf16[256,256]{1,0:T(8,128)(2,1)S(1)}, u32[]{:S(2)}, u32[]{:S(2)}) collective-permute-start(bf16[256,256]{1,0:T(8,128)(2,1)S(1)} %get-tuple-element.143.refs_3_), channel_id=1, source_target_pairs={{0,4},{4,0},{8,12},{12,8},{16,20},{20,16},{24,28},{28,24},{1,5},{5... | collective-permute-start | bytes 393224 | tf_op jit(solution)/shard_map/ppermute | solution.py:30
  186.7 9.6 %collective-permute-start.36 = (bf16[256,256]{1,0:T(8,128)(2,1)S(1)}, bf16[256,256]{1,0:T(8,128)(2,1)S(1)}, u32[]{:S(2)}, u32[]{:S(2)}) collective-permute-start(bf16[256,256]{1,0:T(8,128)(2,1)S(1)} %get-tuple-element.140.refs_5_), channel_id=1, source_target_pairs={{0,8},{4,12},{8,0},{12,4},{16,24},{20,28},{24,16},{28,20},{1,9},{5... | collective-permute-start | bytes 393224 | tf_op jit(solution)/shard_map/ppermute | solution.py:30
  190.0 4.6 %collective-permute-start.54 = (f32[18,128]{1,0:T(8,128)S(1)}, f32[18,128]{1,0:T(8,128)S(1)}, u32[]{:S(2)}, u32[]{:S(2)}) collective-permute-start(f32[18,128]{1,0:T(8,128)S(1)} %gains.8.refs_0_), channel_id=1, source_target_pairs={{0,16},{4,20},{8,24},{12,28},{16,0},{20,4},{24,8},{28,12},{1,17},{... | collective-permute-start | bytes 27656 | tf_op jit(solution)/shard_map/ppermute | solution.py:30
  194.6 8.4 %collective-permute-start.27 = (bf16[64,1024]{1,0:T(8,128)(2,1)S(1)}, bf16[64,1024]{1,0:T(8,128)(2,1)S(1)}, u32[]{:S(2)}, u32[]{:S(2)}) collective-permute-start(bf16[64,1024]{1,0:T(8,128)(2,1)S(1)} %get-tuple-element.122), channel_id=1, source_target_pairs={{0,2},{1,3},{2,0},{3,1},{4,6},{5,7},{6,4},{7,5},{8,10},{9,11},{10,... | collective-permute-start | bytes 393224 | tf_op jit(solution)/shard_map/ppermute | solution.py:30
  195.3 10.2 %collective-permute-start.39 = (bf16[256,256]{1,0:T(8,128)(2,1)S(1)}, bf16[256,256]{1,0:T(8,128)(2,1)S(1)}, u32[]{:S(2)}, u32[]{:S(2)}) collective-permute-start(bf16[256,256]{1,0:T(8,128)(2,1)S(1)} %get-tuple-element.145), channel_id=1, source_target_pairs={{0,8},{4,12},{8,0},{12,4},{16,24},{20,28},{24,16},{28,20},{1,9},{5... | collective-permute-start | bytes 393224 | tf_op jit(solution)/shard_map/ppermute | solution.py:30
  196.4 10.2 %collective-permute-start.41 = (bf16[256,256]{1,0:T(8,128)(2,1)S(1)}, bf16[256,256]{1,0:T(8,128)(2,1)S(1)}, u32[]{:S(2)}, u32[]{:S(2)}) collective-permute-start(bf16[256,256]{1,0:T(8,128)(2,1)S(1)} %get-tuple-element.152), channel_id=1, source_target_pairs={{0,8},{4,12},{8,0},{12,4},{16,24},{20,28},{24,16},{28,20},{1,9},{5... | collective-permute-start | bytes 393224 | tf_op jit(solution)/shard_map/ppermute | solution.py:30
  199.6 14.7 %collective-permute-start.34 = (bf16[64,1024]{1,0:T(8,128)(2,1)}, bf16[64,1024]{1,0:T(8,128)(2,1)}, u32[]{:S(2)}, u32[]{:S(2)}) collective-permute-start(bf16[64,1024]{1,0:T(8,128)(2,1)} %get-tuple-element.136), channel_id=1, source_target_pairs={{0,2},{1,3},{2,0},{3,1},{4,6},{5,7},{6,4},{7,5},{8,10},{9,11},{10,... | collective-permute-start | bytes 393224 | tf_op jit(solution)/shard_map/ppermute | solution.py:30
  201.8 48.5 %collective-permute-start.49 = (bf16[128,1152]{1,0:T(8,128)(2,1)}, bf16[128,1152]{1,0:T(8,128)(2,1)S(1)}, u32[]{:S(2)}, u32[]{:S(2)}) collective-permute-start(bf16[128,1152]{1,0:T(8,128)(2,1)} %get-tuple-element.165), channel_id=1, source_target_pairs={{0,16},{4,20},{8,24},{12,28},{16,0},{20,4},{24,8},{28,12},{1,17},{... | collective-permute-start | bytes 884744 | tf_op jit(solution)/shard_map/ppermute | solution.py:30
  202.9 30.4 %collective-permute-start.37 = (bf16[128,256]{1,0:T(8,128)(2,1)}, bf16[128,256]{1,0:T(8,128)(2,1)}, u32[]{:S(2)}, u32[]{:S(2)}) collective-permute-start(bf16[128,256]{1,0:T(8,128)(2,1)} %get-tuple-element.142), channel_id=1, source_target_pairs={{0,16},{4,20},{8,24},{12,28},{16,0},{20,4},{24,8},{28,12},{1,17},{... | collective-permute-start | bytes 196616 | tf_op jit(solution)/shard_map/ppermute | solution.py:30
  206.2 45.1 %collective-permute-start.44 = (bf16[128,1152]{1,0:T(8,128)(2,1)}, bf16[128,1152]{1,0:T(8,128)(2,1)S(1)}, u32[]{:S(2)}, u32[]{:S(2)}) collective-permute-start(bf16[128,1152]{1,0:T(8,128)(2,1)} %get-tuple-element.157), channel_id=1, source_target_pairs={{0,16},{4,20},{8,24},{12,28},{16,0},{20,4},{24,8},{28,12},{1,17},{... | collective-permute-start | bytes 884744 | tf_op jit(solution)/shard_map/ppermute | solution.py:30
  207.2 45.0 %collective-permute-start.47 = (bf16[128,1152]{1,0:T(8,128)(2,1)}, bf16[128,1152]{1,0:T(8,128)(2,1)S(1)}, u32[]{:S(2)}, u32[]{:S(2)}) collective-permute-start(bf16[128,1152]{1,0:T(8,128)(2,1)} %get-tuple-element.162), channel_id=1, source_target_pairs={{0,16},{4,20},{8,24},{12,28},{16,0},{20,4},{24,8},{28,12},{1,17},{... | collective-permute-start | bytes 884744 | tf_op jit(solution)/shard_map/ppermute | solution.py:30
  214.3 34.4 %collective-permute-start.40 = (bf16[128,256]{1,0:T(8,128)(2,1)S(1)}, bf16[128,256]{1,0:T(8,128)(2,1)S(1)}, u32[]{:S(2)}, u32[]{:S(2)}) collective-permute-start(bf16[128,256]{1,0:T(8,128)(2,1)S(1)} %get-tuple-element.147), channel_id=1, source_target_pairs={{0,16},{4,20},{8,24},{12,28},{16,0},{20,4},{24,8},{28,12},{1,17},{... | collective-permute-start | bytes 196616 | tf_op jit(solution)/shard_map/ppermute | solution.py:30
  233.4 16.1 %collective-permute-start.42 = (bf16[128,256]{1,0:T(8,128)(2,1)S(1)}, bf16[128,256]{1,0:T(8,128)(2,1)S(1)}, u32[]{:S(2)}, u32[]{:S(2)}) collective-permute-start(bf16[128,256]{1,0:T(8,128)(2,1)S(1)} %get-tuple-element.154), channel_id=1, source_target_pairs={{0,16},{4,20},{8,24},{12,28},{16,0},{20,4},{24,8},{28,12},{1,17},{... | collective-permute-start | bytes 196616 | tf_op jit(solution)/shard_map/ppermute | solution.py:30
  (48 other events, 517.1 us)

commit v2 on v1

--- a/solution.py
+++ b/solution.py
@@ -1,4 +1,5 @@
 import functools
+import math
 
 import jax
 import jax.numpy as jnp
@@ -111,24 +112,42 @@
 
 
 def qkv_kernel(
-    ranks, x0, x1, x2, x3, gain, wq, wk, wv, query_gain, key_gain, cos, sin,
+    ranks, x0, x1, x2, x3, gain, wq, wk, wv, query_gain, key_gain, positions,
     act_out, select_out, pair_out, query_rot_out, query_out, key_out,
+    cos_out, sin_out, column_out, row_out,
 ):
+    rows = act_out.shape[0]
+    line = lax.broadcasted_iota(jnp.int32, (rows, rows), 0)
+    picked = place_of(line, rows, ranks[1]) == lanes((rows, rows))
+    column = jnp.sum(
+        jnp.where(picked, positions[...].astype(F32), 0.0), axis=1, keepdims=True
+    )
+    column_out[...] = column.astype(jnp.int32)
+    row = jnp.sum(jnp.where(line == lanes((rows, rows)), column, 0.0), axis=0, keepdims=True)
+    row_out[...] = row.astype(jnp.int32)
+    lane = lanes((1, 128))
+    power = (lane % (HD // 2)).astype(F32) * (-2.0 / HD)
+    angles = column * jnp.exp(power * math.log(ROPE_BASE))
+    cos = jnp.cos(angles)
+    sin = jnp.sin(angles) * jnp.where(lane % HD < HD // 2, -1.0, 1.0)
+    cos_out[...] = cos
+    sin_out[...] = sin
+
     x = jnp.concatenate([x0[...], x1[...], x2[...], x3[...]], axis=0).astype(F32)
     act = (x * row_norm(x) * gain[...]).astype(BF)
     act_out[...] = act
     keys = dot(act, wk[...])
     key_out[...] = keys
     width = keys.shape[-1]
-    normed = keys * head_norm(keys) * key_gain[...]
-    rotated = normed * cos[...] + partner(normed) * sin[...]
+    normed = keys * head_norm(keys) * wide(key_gain[...], width)
+    rotated = normed * wide(cos, width) + partner(normed) * wide(sin, width)
     pair_out[:, :width] = rotated.astype(BF)
     pair_out[:, width:] = dot(act, wv[...]).astype(BF)
     queries = dot(act, wq[...])
     query_out[...] = queries
-    normed = queries * head_norm(queries) * query_gain[...]
     width = queries.shape[-1]
-    rotated = normed * wide(cos[...], width) + partner(normed) * wide(sin[...], width)
+    normed = queries * head_norm(queries) * wide(query_gain[...], width)
+    rotated = normed * wide(cos, width) + partner(normed) * wide(sin, width)
     query_rot_out[...] = rotated.astype(BF)
     select_columns(ranks, act_out, select_out)
 
@@ -225,11 +244,15 @@
     out[...] = jnp.transpose(kept[...] + arrived[...].astype(F32))
 
 
-def split_add_kernel(kept, arrived, first_out, second_out):
+def attention_last_kernel(kept, arrived, out_grad, query_grad, key_grad, value_grad):
     total = kept[...] + arrived[...].astype(F32)
-    width = first_out.shape[1]
-    first_out[...] = total[:, :width]
-    second_out[...] = total[:, width:]
+    turned = out_grad.shape[0]
+    out_grad[...] = jnp.transpose(total[:, :turned])
+    start = turned
+    for out in (query_grad, key_grad, value_grad):
+        width = out.shape[1]
+        out[...] = total[:, start : start + width]
+        start += width
 
 
 def pair_sum_kernel(ranks, term, if_odd, if_even, out):
@@ -369,7 +392,7 @@
 def query_backward_kernel(
     queries, gain, grads, cos, sin, wq, select, late_out, gain_out, partial_out
 ):
-    grad_in, gain_terms = head_norm_backward(queries[...], gain[...], grads[...], cos[...], sin[...])
+    grad_in, gain_terms = head_norm_backward(queries[...], wide(gain[...], queries.shape[-1]), grads[...], cos[...], sin[...])
     grad_b = grad_in.astype(BF)
     chosen = select.shape[1]
     late_out[:, :chosen] = select[...]
@@ -389,7 +412,7 @@
     for other in shifted:
         grads = grads + other[...].astype(F32)
     grad_in, gain_terms = head_norm_backward(
-        keys[...], gain[...], grads[:, :width], cos[...], sin[...]
+        keys[...], wide(gain[...], width), grads[:, :width], cos[...], sin[...]
     )
     grad_b = grad_in.astype(BF)
     value_b = grads[:, width:].astype(BF)
@@ -416,63 +439,63 @@
     gains_out[row + 1 : row + 2, :] = gain_terms
 
 
-def weight_grad_kernel(
-    offsets, ranks, act, arrived_act, grads, arrived_grads, kept_out, sent_out
-):
+def weight_grad_kernel(parts, ranks, *refs):
+    kept_out, sent_out = refs[-2:]
     parity = ranks[0] % 2
     mine = ranks[0] // 2
-    own, there_at = offsets
-    width = kept_out.shape[1]
-    mine_grads = grads[:, own : own + width]
-    other_grads = arrived_grads[:, there_at : there_at + width]
-    for lo in (1, 0):
-        for hi in range(2):
-            block = jnp.bitwise_xor(mine, lo + 2 * hi)
-            start = pl.multiple_of((2 * block + parity) * 128, 128)
-            there = pl.multiple_of(block * 128, 128)
-            total = dot(act[:, pl.ds(start, 128)], mine_grads, ROWS) + dot(
-                arrived_act[:, pl.ds(there, 128)], other_grads, ROWS
-            )
-            target = sent_out if lo else kept_out
-            target[hi * 128 : (hi + 1) * 128, :] = total.astype(target.dtype)
+    place = 0
+    for p, (own, there_at, width) in enumerate(parts):
+        act, arrived_act, grads, arrived_grads = refs[4 * p : 4 * p + 4]
+        mine_grads = grads[:, own : own + width]
+        other_grads = arrived_grads[:, there_at : there_at + width]
+        for lo in (1, 0):
+            for hi in range(2):
+                block = jnp.bitwise_xor(mine, lo + 2 * hi)
+                start = pl.multiple_of((2 * block + parity) * 128, 128)
+                there = pl.multiple_of(block * 128, 128)
+                total = dot(act[:, pl.ds(start, 128)], mine_grads, ROWS) + dot(
+                    arrived_act[:, pl.ds(there, 128)], other_grads, ROWS
+                )
+                target = sent_out if lo else kept_out
+                target[hi * 128 : (hi + 1) * 128, place : place + width] = total.astype(
+                    target.dtype
+                )
+        place += width
 
 
 def shape(dims, dtype):
     return jax.ShapeDtypeStruct(dims, dtype)
 
 
-def launch(kernel, outs, args, scratch=(), name=None, after=()):
+def launch(kernel, outs, args, scratch=(), name=None, after=(), carry=()):
     nbytes = sum(s.shape[0] * s.shape[1] * 4 for s in scratch)
-    n_in, n_after = len(args), len(after)
+    n_in, n_out, n_unused = len(args), len(outs), len(after) + len(carry)
 
     def run(*refs):
-        kernel(*refs[:n_in], *refs[n_in + n_after :])
-
+        results = refs[n_in + n_unused :]
+        kernel(*refs[:n_in], *results[:n_out], *results[n_out + len(carry) :])
+
+    any_spec = pl.BlockSpec(memory_space=pl.ANY)
     return pl.pallas_call(
         run,
-        out_shape=outs,
+        out_shape=list(outs) + [shape(c.shape, c.dtype) for c in carry],
         in_specs=[
             pl.BlockSpec(memory_space=pltpu.SMEM if a.shape == (2,) else pltpu.VMEM) for a in args
         ]
-        + [pl.BlockSpec(memory_space=pl.ANY)] * n_after,
-        out_specs=[pl.BlockSpec(memory_space=pltpu.VMEM) for _ in outs],
+        + [any_spec] * n_unused,
+        out_specs=[pl.BlockSpec(memory_space=pltpu.VMEM) for _ in outs] + [any_spec] * len(carry),
         scratch_shapes=list(scratch),
+        input_output_aliases={n_in + len(after) + i: n_out + i for i in range(len(carry))},
         compiler_params=pltpu.CompilerParams(vmem_limit_bytes=nbytes + (12 << 20)),
         name=name,
-    )(*args, *after)
-
-
-def add(kept, arrived, dtype, name, kernel=add_kernel, after=()):
-    return launch(kernel, [shape(kept.shape, dtype)], [kept, arrived], name=name, after=after)[0]
-
-
-def mp_order(values):
-    rank = lax.axis_index("mp")
-    parts = values.reshape(2, 2, -1)
-    parts = jnp.swapaxes(parts, 0, 1)
-    parts = jnp.where(rank % 2 == 1, parts[::-1], parts)
-    parts = jnp.where(rank // 2 == 1, parts[:, ::-1], parts)
-    return parts.reshape(values.shape)
+    )(*args, *after, *carry)
+
+
+def add(kept, arrived, dtype, name, kernel=add_kernel, after=(), carry=()):
+    out = launch(
+        kernel, [shape(kept.shape, dtype)], [kept, arrived], name=name, after=after, carry=carry
+    )
+    return out if carry else out[0]
 
 
 def mp_gather(values):
@@ -481,21 +504,16 @@
     return values, other, core, xor(other, "mp", 1)
 
 
-def mp_reduce_start(kept, sent, name):
+def mp_reduce_start(kept, sent, name, after=()):
     own = kept.shape[0] // 2
     kept, back = launch(
         fold_kernel,
         [shape((own, kept.shape[1]), F32), shape((own, kept.shape[1]), BF)],
         [kept, xor(sent, "mp", 1)],
         name=name,
+        after=after,
     )
     return kept, xor(back, "mp", 2)
-
-
-def mp_allreduce(kept, sent, name):
-    kept = add(kept, xor(sent, "mp", 1), BF, name + "_core")
-    both = add(kept, xor(kept, "mp", 2), BF, name + "_chip", kernel=flipped_add_kernel)
-    return both, xor(both, "mp", 1)
 
 
 def split_columns(values):
@@ -511,28 +529,32 @@
     return parts[:, 0], parts[:, 1]
 
 
-def weight_grad(ranks, act, arrived_act, grads, arrived_grads, offsets, columns, name, after=()):
+def weight_grad(ranks, parts, name, after=()):
     n = lax.axis_size("ctx")
+    act = parts[0][0]
     half = act.shape[1] // 4
+    columns = sum(part[5] for part in parts)
     if n == 8 and act.shape[1] == 1024:
         return launch(
-            functools.partial(weight_grad_kernel, offsets),
+            functools.partial(weight_grad_kernel, [part[4] + (part[5],) for part in parts]),
             [shape((half, columns), F32), shape((half, columns), BF)],
-            [ranks, act, arrived_act, grads, arrived_grads],
+            [ranks] + [a for part in parts for a in part[:4]],
             name=name,
             after=after,
         )
-    own, other = split_columns(act)
-    grads = grads[:, offsets[0] : offsets[0] + columns]
-    arrived_grads = arrived_grads[:, offsets[1] : offsets[1] + columns]
-    both = jnp.concatenate([own, xor(other, "ctx", 1)], axis=0)
-    total = dot(both, jnp.concatenate([grads, arrived_grads], axis=0), ROWS)
+    totals = []
+    for act, _, grads, arrived_grads, offsets, width in parts:
+        own, other = split_columns(act)
+        grads = grads[:, offsets[0] : offsets[0] + width]
+        arrived_grads = arrived_grads[:, offsets[1] : offsets[1] + width]
+        both = jnp.concatenate([own, xor(other, "ctx", 1)], axis=0)
+        totals.append(dot(both, jnp.concatenate([grads, arrived_grads], axis=0), ROWS))
+    total = jnp.concatenate(totals, axis=1)
     return total[:half], total[half:].astype(BF)
 
 
-def halve(kept, sent, name, after=()):
+def halve(kept, arrived, name, after=()):
     n = lax.axis_size("ctx")
-    arrived = xor(sent, "ctx", 2)
     mask = 4
     while mask < n:
         half, columns = kept.shape[0] // 2, kept.shape[1]
@@ -540,12 +562,12 @@
             fold_kernel,
             [shape((half, columns), F32), shape((half, columns), BF)],
             [kept, arrived],
-            name=name + "_fold",
+            name=name,
             after=after,
         )
         arrived = xor(back, "ctx", mask)
         mask *= 2
-    return kept, arrived
+    return kept, arrived, back
 
 
 def body(
@@ -582,20 +604,15 @@
     ranks = jnp.stack([ctx_rank, lax.axis_index("mp")]).astype(jnp.int32)
 
     x = mp_gather(block_in)
-    positions = mp_order(positions)
-    lane = jnp.arange(128, dtype=jnp.int32)
-    freqs = ROPE_BASE ** (-2.0 * (lane % (HD // 2)).astype(F32) / HD)
-    angles = positions.astype(F32)[:, None] * freqs[None, :]
-    cos = jnp.cos(angles)
-    sin = jnp.sin(angles) * jnp.where(lane % HD < HD // 2, -1.0, 1.0)[None, :]
-    query_gain_row = jnp.tile(query_gain, query_width // HD).reshape(1, -1)
-    key_gain_row = jnp.tile(key_gain, key_width // HD).reshape(1, -1)
+    query_gain_row = query_gain.reshape(1, -1)
+    key_gain_row = key_gain.reshape(1, -1)
     attn_gain_row = attn_gain.reshape(1, -1)
     ffn_gain_row = ffn_gain.reshape(1, -1)
-    position_column = positions.reshape(-1, 1)
-    position_row = positions.reshape(1, -1)
-
-    act_attn, act_attn_select, pair, query_rot, queries, keys_pre = launch(
+
+    (
+        act_attn, act_attn_select, pair, query_rot, queries, keys_pre,
+        cos, sin, position_column, position_row,
+    ) = launch(
         qkv_kernel,
         [
             shape((rows, width), BF),
@@ -604,11 +621,14 @@
             shape((rows, query_width), BF),
             shape((rows, query_width), F32),
             shape((rows, key_width), F32),
+            shape((rows, 128), F32),
+            shape((rows, 128), F32),
+            shape((rows, 1), jnp.int32),
+            shape((1, rows), jnp.int32),
         ],
         [ranks, *x, attn_gain_row, query_weight, key_weight, value_weight,
-         query_gain_row, key_gain_row, cos, sin],
+         query_gain_row, key_gain_row, positions.reshape(1, -1)],
         name="qkv",
-        after=[position_column, position_row],
     )
 
     def cross(values, odd):
@@ -625,18 +645,6 @@
     low_odd = [cross(items[j], 0) for j in range(slots)]
     high_odd = [cross(items[j + 1], 1) for j in range(slots)]
     even = items[:slots]
-
-    cot, cot_select, grad_hidden = launch(
-        cotangent_kernel,
-        [
-            shape((rows, width), BF),
-            shape((rows, width // 2), BF),
-            shape((rows, hidden_width), F32),
-        ],
-        [ranks, *mp_gather(cotangent), down_weight],
-        name="cotangent",
-    )
-    cot_there = xor(cot_select, "ctx", 1)
 
     outs = launch(
         functools.partial(attention_kernel, count),
@@ -652,25 +660,40 @@
          *even, *low_odd, *high_odd],
         scratch=[pltpu.VMEM((2 * rows, count * rows), F32)],
         name="attention",
-        after=[grad_hidden],
     )
     attn_rows, early, log_sums, kept, sent = outs[:5]
     blocks = [(even, outs[5:])[d % 2][d // 2] for d in range(count)]
-    resid_halves = mp_allreduce(kept, sent, "resid")
+    chosen = width // 2
+
+    kept = add(kept, xor(sent, "mp", 1), BF, "resid_core")
+    cot, cot_select, grad_hidden = launch(
+        cotangent_kernel,
+        [
+            shape((rows, width), BF),
+            shape((rows, chosen), BF),
+            shape((rows, hidden_width), F32),
+        ],
+        [ranks, *mp_gather(cotangent), down_weight],
+        name="cotangent",
+        after=[kept],
+    )
+    both = add(
+        kept, xor(kept, "mp", 2), BF, "resid_chip", kernel=flipped_add_kernel, after=[grad_hidden]
+    )
     early_there = xor(early, "ctx", 1)
-    chosen = width // 2
+    cot_there = xor(cot_select, "ctx", 1)
 
     resid, act_ffn, act_select, gate_pre, up_proj, hidden = launch(
         ffn_forward_kernel,
         [
             shape((rows, width), F32),
             shape((rows, width), BF),
-            shape((rows, width // 2), BF),
+            shape((rows, chosen), BF),
             shape((rows, hidden_width), F32),
             shape((rows, hidden_width), F32),
             shape((rows, hidden_width), BF),
         ],
-        [ranks, *x, *resid_halves, ffn_gain_row, gate_weight, up_weight],
+        [ranks, *x, both, xor(both, "mp", 1), ffn_gain_row, gate_weight, up_weight],
         name="ffn_forward",
     )
     hidden_there = xor(hidden, "ctx", 1)
@@ -684,15 +707,13 @@
         ],
         [gate_pre, up_proj, grad_hidden, gate_weight, up_weight, act_select],
         name="ffn_backward",
-        after=[early_there, cot_there],
-    )
-    grad_act_halves = mp_allreduce(kept, sent, "grad_act")
+    )
+    kept, gate_packet = add(kept, xor(sent, "mp", 1), BF, "grad_act_core", carry=[gate_packet])
     gate_there = xor(gate_packet, "ctx", 1)
-    up_there = xor(grad_up, "ctx", 1)
-
+    both = add(kept, xor(kept, "mp", 2), BF, "grad_act_chip", kernel=flipped_add_kernel)
     down_kept, down_sent = weight_grad(
-        ranks, cot, cot_there, hidden, hidden_there, (0, 0), hidden_width, "down_grad",
-        after=[grad_act_halves[1]],
+        ranks, [(cot, cot_there, hidden, hidden_there, (0, 0), hidden_width)], "down_grad",
+        after=[both],
     )
 
     outs = launch(
@@ -700,13 +721,13 @@
         [
             shape((own_rows, width), F32),
             shape((rows, width), BF),
-            shape((rows, width // 2), BF),
+            shape((rows, chosen), BF),
             shape((1, width), F32),
             shape((rows, query_width), F32),
         ]
         + [shape((rows, 2 * key_width), BF if d else F32) for d in range(count)],
-        [ranks, cot, resid, *grad_act_halves, ffn_gain_row, out_weight, attn_rows, log_sums,
-         query_rot, position_row, *blocks],
+        [ranks, cot, resid, both, xor(both, "mp", 1), ffn_gain_row, out_weight, attn_rows,
+         log_sums, query_rot, position_row, *blocks],
         name="attention_backward",
         after=[down_sent],
     )
@@ -714,18 +735,33 @@
     terms = outs[5:]
 
     arrived = [xor(terms[2 * j + 1], "ctx", 1) for j in range(slots)]
+    gate_kept, gate_sent = weight_grad(
+        ranks,
+        [(act_ffn, gate_there, gate_packet, gate_there, (chosen, chosen), hidden_width)],
+        "gate_grad",
+        after=[grad_query],
+    )
+    down_kept, down_arrived, back = halve(
+        down_kept, xor(down_sent, "ctx", 2), "down_fold", after=[gate_sent]
+    )
     shifted = []
     if 2 * slots < n_ctx:
         pairs = [(i, i - 2 * slots) for i in range(2 * slots, n_ctx) if i % 2 == 1]
         shifted.append(lax.ppermute(arrived[slots - 1], "ctx", pairs))
     for k in range(slots - 1, 0, -1):
+        carried = [grad_up] if k == 1 else []
         total = launch(
             pair_sum_kernel,
             [shape(terms[0].shape, BF)],
             [ranks, terms[2 * k], arrived[k - 1], arrived[k]],
             name="pair_sum",
-        )[0]
-        shifted.append(down(total, 2 * k))
+            after=[back],
+            carry=carried,
+        )
+        if carried:
+            grad_up = total[1]
+        shifted.append(down(total[0], 2 * k))
+    up_there = xor(grad_up, "ctx", 1)
 
     late, query_gain_part, query_partial = launch(
         query_backward_kernel,
@@ -736,7 +772,7 @@
         ],
         [queries, query_gain_row, grad_query, cos, sin, query_weight, grad_select],
         name="query_backward",
-        after=[total],
+        after=[grad_up],
     )
     late_there = xor(late, "ctx", 1)
     out_kept, out_sent = launch(
@@ -746,9 +782,9 @@
         name="down",
         after=[query_partial],
     )
-    gate_kept, gate_sent = weight_grad(
-        ranks, act_ffn, gate_there, gate_packet, gate_there, (chosen, chosen), hidden_width,
-        "gate_grad", after=[query_partial],
+    up_kept, up_sent = weight_grad(
+        ranks, [(act_ffn, gate_there, grad_up, up_there, (0, 0), hidden_width)], "up_grad",
+        after=[out_sent],
     )
     pair_b, gains, kept, sent = launch(
         key_backward_kernel,
@@ -761,64 +797,69 @@
         [ranks, keys_pre, key_gain_row, cos, sin, key_weight, value_weight, query_partial, *x,
          ffn_gain_part, query_gain_part, terms[0], arrived[0], *shifted],
         name="key_backward",
-        after=[gate_sent, out_sent],
+        after=[up_sent],
     )
     pair_there = xor(pair_b, "ctx", 1)
-    kept, across = mp_reduce_start(kept, sent, "grad_input_core")
+    gate_kept, gate_arrived, back = halve(
+        gate_kept, xor(gate_sent, "ctx", 2), "gate_fold", after=[kept]
+    )
+    gains = add(gains, xor(gains, "mp", 1), F32, "gains", after=[back])
+    kept, across = mp_reduce_start(kept, sent, "grad_input_core", after=[gains])
+    gains = add(gains, xor(gains, "mp", 2), F32, "gains", after=[kept])
+    attn_kept, attn_sent = weight_grad(
+        ranks,
+        [
+            (grad_resid_b, late_there, early, early_there, (chosen, chosen), query_width),
+            (act_attn, early_there, late, late_there, (chosen, chosen), query_width),
+            (act_attn, early_there, pair_b, pair_there, (0, 0), 2 * key_width),
+        ],
+        "attention_grads",
+        after=[gains],
+    )
+    gains = add(gains, xor(gains, "ctx", 1), F32, "gains", after=[attn_sent])
+    up_kept, up_arrived, back = halve(
+        up_kept, xor(up_sent, "ctx", 2), "up_fold", after=[gains]
+    )
+    out_kept, out_across = mp_reduce_start(out_kept, out_sent, "block_out_core", after=[back])
     grad_input = launch(
         grad_input_kernel,
         [shape((own_rows, width), F32)],
         [x[0], attn_gain_row, grad_resid, kept, across],
         name="grad_input",
+        after=[out_kept],
     )[0]
-    up_kept, up_sent = weight_grad(
-        ranks, act_ffn, gate_there, grad_up, up_there, (0, 0), hidden_width, "up_grad",
-        after=[kept],
-    )
-    out_w_kept, out_w_sent = weight_grad(
-        ranks, grad_resid_b, late_there, early, early_there, (chosen, chosen), query_width,
-        "out_grad", after=[kept],
-    )
-    query_kept, query_sent = weight_grad(
-        ranks, act_attn, early_there, late, late_there, (chosen, chosen), query_width,
-        "query_grad", after=[kept],
-    )
-    pair_kept, pair_sent = weight_grad(
-        ranks, act_attn, early_there, pair_b, pair_there, (0, 0), 2 * key_width,
-        "key_value_grad", after=[query_sent],
-    )
-
-    def finish(halves, name, kernel=add_kernel, turned=False):
-        kept, arrived = halves
-        dims = kept.shape[::-1] if turned else kept.shape
-        return launch(kernel, [shape(dims, F32)], [kept, arrived], name=name)[0]
-
-    down_grad = finish(halve(down_kept, down_sent, "down"), "down_last", turned_add_kernel, True)
-    gate_grad = finish(halve(gate_kept, gate_sent, "gate"), "gate_last")
-    up_grad = finish(halve(up_kept, up_sent, "up"), "up_last")
-    out_grad = finish(halve(out_w_kept, out_w_sent, "out"), "out_last", turned_add_kernel, True)
-    query_grad = finish(halve(query_kept, query_sent, "query"), "query_last")
-    pair_kept, pair_arrived = halve(pair_kept, pair_sent, "key_value")
-    key_grad, value_grad = launch(
-        split_add_kernel,
-        [shape((pair_kept.shape[0], key_width), F32)] * 2,
-        [pair_kept, pair_arrived],
-        name="key_value_last",
-    )
-
-    out_kept, out_across = mp_reduce_start(out_kept, out_sent, "block_out_core")
     block_out = launch(
         block_out_kernel,
         [shape((own_rows, width), BF)],
         [resid, out_kept, out_across],
         name="block_out",
+        after=[grad_input],
     )[0]
 
-    for axis in ("mp", "ctx"):
-        mask = 1
-        while mask < lax.axis_size(axis):
-            gains = add(gains, xor(gains, axis, mask), F32, "gains")
-            mask *= 2
+    def finish(kept, arrived, name, after, kernel=add_kernel, turned=False):
+        dims = kept.shape[::-1] if turned else kept.shape
+        return launch(kernel, [shape(dims, F32)], [kept, arrived], name=name, after=after)[0]
+
+    down_grad = finish(
+        down_kept, down_arrived, "down_last", [block_out], turned_add_kernel, True
+    )
+    gate_grad = finish(gate_kept, gate_arrived, "gate_last", [down_grad])
+    attn_kept, attn_arrived, back = halve(
+        attn_kept, xor(attn_sent, "ctx", 2), "attention_fold", after=[gate_grad]
+    )
+    mask = 2
+    while mask < n_ctx:
+        gains = add(gains, xor(gains, "ctx", mask), F32, "gains", after=[back])
+        mask *= 2
+    up_grad = finish(up_kept, up_arrived, "up_last", [gains])
+    out_grad, query_grad, key_grad, value_grad = launch(
+        attention_last_kernel,
+        [shape((query_width, attn_kept.shape[0]), F32)]
+        + [shape((attn_kept.shape[0], w), F32) for w in (query_width, key_width, key_width)],
+        [attn_kept, attn_arrived],
+        name="attention_last",
+        after=[up_grad],
+    )
     gains = gains.reshape(-1)
     heads = gains[2 * width :].reshape(2, -1, HD).sum(axis=1)
     query_gains, key_gains = heads[0], heads[1]

time: 254 us -> 215 us (0.85)
  waiting for transfers between devices: 129 us -> 98.9 us
  Pallas kernels: 44.1 us -> 36 us
  local copies, waits for them, and re-layouts: 16.3 us -> 12.8 us
  starting transfers between devices: 61.5 us -> 64.9 us
    ppermute x43 -> x39, waiting for transfers between devices: 120 us -> 92.8 us  [xor(): return lax.ppermute(values, axis, [(i, i ^ mask) for i in range(n)])]
    pallas_call x42 -> x36, Pallas kernels: 44.1 us -> 36 us  [launch(): pl.pallas_call(run, out_shape=list(outs) + [shape(c.shape, c.dtype) for c...]
    ppermute x2, waiting for transfers between devices: 4.99 us -> 0.01 us  [down(): return lax.ppermute(values, 'ctx', [(i, i - step) for i in range(step, n)])]
    ppermute x43 -> x39, starting transfers between devices: 35.1 us -> 38.7 us  [xor(): return lax.ppermute(values, axis, [(i, i ^ mask) for i in range(n)])]
    unnamed x82 -> x52, local copies, waits for them, and re-layouts: 12.5 us -> 11.6 us
  transfers between devices with their start and end apart: 55 -> 51, of which waited for: 22 -> 27; matrix products, arithmetic and copies ran while one was open for 2% -> 1% of each run, Pallas kernels for 14% -> 12%
where the time goes in v2:
time: 215 us; the launch traced here: 214 us
  waiting for transfers between devices  98.9 us (46%)
  starting transfers between devices  64.9 us (30%)
  Pallas kernels  36 us (17%)
  local copies, waits for them, and re-layouts  12.8 us (6%)
    ppermute x39, waiting for transfers between devices, xor(): return lax.ppermute(values, axis, [(i, i ^ mask) for i in range(n)])  92.8 us
    ppermute x39, starting transfers between devices, xor(): return lax.ppermute(values, axis, [(i, i ^ mask) for i in range(n)])  38.7 us
    pallas_call x36, Pallas kernels, launch(): pl.pallas_call(run, out_shape=list(outs) + [shape(c.shape, c.dtype) for c...  36 us
    ppermute x6, starting transfers between devices, cross(): lax.ppermute(values, 'ctx', [(i, i ^ 1) for i in range(odd, n_ctx, 2)])  14 us
    unnamed x52, local copies, waits for them, and re-layouts  11.6 us
    ppermute x3, starting transfers between devices, climb(): return lax.ppermute(pair, 'ctx', pairs)  9.03 us
    ppermute x6, waiting for transfers between devices, cross(): lax.ppermute(values, 'ctx', [(i, i ^ 1) for i in range(odd, n_ctx, 2)])  6.04 us
  transfers between devices with their start and end apart: 51, of which 27 were waited for; matrix products, arithmetic and copies ran while one was open for 1% of the time, Pallas kernels for 12%

profile of v2, /device:TPU:0, one launch (start us, length us, event | category | flops | bytes accessed | tf_op | source)
XLA Modules:
  0.0 214.0 jit_solution(17449793424955461100)
XLA Ops:
  0.7 3.0 %collective-permute-start = (bf16[64,1024]{1,0:T(8,128)(2,1)}, bf16[64,1024]{1,0:T(8,128)(2,1)S(1)}, u32[]{:S(2)}, u32[]{:S(2)}) collective-permute-start(bf16[64,1024]{1,0:T(8,128)(2,1)} %refs_0_.1), channel_id=1, source_target_pairs={{0,2},{1,3},{2,0},{3,1},{4,6},{5,7},{6,4},{7,5},{8,10},{9,11},{10,... | collective-permute-start | bytes 393224 | tf_op jit(solution)/shard_map/ppermute | solution.py:31
  3.7 3.7 %collective-permute-done.refs_2_.refs_9_ = bf16[64,1024]{1,0:T(8,128)(2,1)S(1)} collective-permute-done((bf16[64,1024]{1,0:T(8,128)(2,1)}, bf16[64,1024]{1,0:T(8,128)(2,1)S(1)}, u32[]{:S(2)}, u32[]{:S(2)}) %collective-permute-start) | collective-permute-done | bytes 131104 | tf_op jit(solution)/shard_map/ppermute | solution.py:31
  15.2 2.2 %qkv.1 = (bf16[256,1024]{1,0:T(8,128)(2,1)S(1)}, bf16[256,512]{1,0:T(8,128)(2,1)S(1)}, bf16[256,256]{1,0:T(8,128)(2,1)S(1)}, bf16[256,256]{1,0:T(8,128)(2,1)S(1)...) custom-call(s32[2]{0:T(128)S(1)} %pad_add_fusion.refs_0_, ...), custom_call_target="tpu_custom_call" | custom-call | tf_op jit(solution)/shard_map/qkv/pallas_call | solution.py:479
  17.5 3.9 %collective-permute-start.3 = (bf16[256,256]{1,0:T(8,128)(2,1)S(1)}, bf16[256,256]{1,0:T(8,128)(2,1)S(1)}, u32[]{:S(2)}, u32[]{:S(2)}) collective-permute-start(bf16[256,256]{1,0:T(8,128)(2,1)S(1)} %get-tuple-element.95.refs_5_.refs_11_), channel_id=1, source_target_pairs={{0,8},{4,12},{8,16},{12,20},{16,24},{20,28},{1,9},{5,13},{9,17},{1... | collective-permute-start | bytes 393224 | tf_op jit(solution)/shard_map/ppermute | solution.py:642
  21.4 4.5 %collective-permute-start.4 = (bf16[256,256]{1,0:T(8,128)(2,1)S(1)}, bf16[256,256]{1,0:T(8,128)(2,1)S(1)}, u32[]{:S(2)}, u32[]{:S(2)}) collective-permute-start(bf16[256,256]{1,0:T(8,128)(2,1)S(1)} %get-tuple-element.95.refs_5_.refs_11_), channel_id=1, source_target_pairs={{0,16},{4,20},{8,24},{12,28},{1,17},{5,21},{9,25},{13,29},{2,18},{... | collective-permute-start | bytes 393224 | tf_op jit(solution)/shard_map/ppermute | solution.py:642
  26.5 4.1 %collective-permute-start.5 = (bf16[256,256]{1,0:T(8,128)(2,1)S(1)}, bf16[256,256]{1,0:T(8,128)(2,1)S(1)}, u32[]{:S(2)}, u32[]{:S(2)}) collective-permute-start(bf16[256,256]{1,0:T(8,128)(2,1)S(1)} %get-tuple-element.95.refs_5_.refs_11_), channel_id=1, source_target_pairs={{0,4},{8,12},{16,20},{24,28},{1,5},{9,13},{17,21},{25,29},{2,6},{1... | collective-permute-start | bytes 393224 | tf_op jit(solution)/shard_map/ppermute | solution.py:635
  33.2 4.6 %collective-permute-start.7 = (bf16[256,256]{1,0:T(8,128)(2,1)S(1)}, bf16[256,256]{1,0:T(8,128)(2,1)S(1)}, u32[]{:S(2)}, u32[]{:S(2)}) collective-permute-start(bf16[256,256]{1,0:T(8,128)(2,1)S(1)} %collective-permute-done.4.refs_7_.refs_15_), channel_id=1, source_target_pairs={{0,4},{8,12},{16,20},{24,28},{1,5},{9,13},{17,21},{25,29},{2,6},{1... | collective-permute-start | bytes 393224 | tf_op jit(solution)/shard_map/ppermute | solution.py:635
  39.1 1.5 collective-permute-start.11
  40.6 4.6 %collective-permute-done.9.refs_12_ = bf16[256,256]{1,0:T(8,128)(2,1)S(1)} collective-permute-done((bf16[256,256]{1,0:T(8,128)(2,1)S(1)}, bf16[256,256]{1,0:T(8,128)(2,1)S(1)}, u32[]{:S(2)}, u32[]{:S(2)}) %collective-permute-start.9) | collective-permute-done | bytes 131104 | tf_op jit(solution)/shard_map/ppermute | solution.py:635
  45.3 1.4 collective-permute-done.11.refs_13_
  46.7 3.9 %attention.1 = (f32[256,256]{1,0:T(8,128)S(1)}, bf16[256,768]{1,0:T(8,128)(2,1)S(1)}, f32[2,512]{1,0:T(2,128)S(1)}, f32[128,1024]{1,0:T(8,128)S(1)}, bf16[128,10...) custom-call(s32[2]{0:T(128)S(1)} %pad_add_fusion.refs_0_, ...), custom_call_target="tpu_custom_call" | custom-call | tf_op jit(solution)/shard_map/attention/pallas_call | solution.py:479
  50.7 1.6 collective-permute-start.14
  52.3 1.5 collective-permute-start.13
  53.8 3.2 %collective-permute-done.14.refs_2_ = bf16[64,1024]{1,0:T(8,128)(2,1)S(1)} collective-permute-done((bf16[64,1024]{1,0:T(8,128)(2,1)S(1)}, bf16[64,1024]{1,0:T(8,128)(2,1)S(1)}, u32[]{:S(2)}, u32[]{:S(2)}) %collective-permute-start.14) | collective-permute-done | bytes 131104 | tf_op jit(solution)/shard_map/ppermute | solution.py:31
  58.4 1.5 cotangent.1
  59.9 2.3 %collective-permute-done.13.refs_1_ = bf16[128,1024]{1,0:T(8,128)(2,1)S(1)} collective-permute-done((bf16[128,1024]{1,0:T(8,128)(2,1)S(1)}, bf16[128,1024]{1,0:T(8,128)(2,1)S(1)}, u32[]{:S(2)}, u32[]{:S(2)}) %collective-permute-start.13) | collective-permute-done | bytes 262176 | tf_op jit(solution)/shard_map/ppermute | solution.py:31
  62.3 1.5 collective-permute-done.17.refs_6_
  63.9 2.4 %ffn_forward.1 = (f32[256,1024]{1,0:T(8,128)S(1)}, bf16[256,1024]{1,0:T(8,128)(2,1)S(1)}, bf16[256,512]{1,0:T(8,128)(2,1)S(1)}, f32[256,1152]{1,0:T(8,128)S(1)},...) custom-call(s32[2]{0:T(128)S(1)} %pad_add_fusion.refs_0_, bf16[64,1024]{1,0:T(8,128)(2,1)S(1)} %copy-done.10, ...), custom_call_target="tpu_custom_call" | custom-call | tf_op jit(solution)/shard_map/ffn_forward/pallas_call | solution.py:479
  66.4 3.2 %ffn_backward.1 = (bf16[256,1664]{1,0:T(8,128)(2,1)S(1)}, bf16[256,1152]{1,0:T(8,128)(2,1)S(1)}, f32[128,1024]{1,0:T(8,128)S(1)}, bf16[128,1024]{1,0:T(8,128)(2,1)S(1)}) custom-call(f32[256,1152]{1,0:T(8,128)S(1)} %get-tuple-element.103.refs_0_, f32[256,1152]{1,0:T(8,128)S(1)} %get-tuple-element.104.refs_1_, f32[256,1152]{1,0:T(8,128)S(1)} %get-tuple-element.98.refs_2_, ...), custom_call_target="tpu_custom_call" | custom-call | tf_op jit(solution)/shard_map/ffn_backward/pallas_call | solution.py:479
  71.2 1.6 collective-permute-start.19
  72.8 2.0 collective-permute-start.21
  74.8 4.8 %collective-permute-done.19.refs_1_ = bf16[128,1024]{1,0:T(8,128)(2,1)S(1)} collective-permute-done((bf16[128,1024]{1,0:T(8,128)(2,1)S(1)}, bf16[128,1024]{1,0:T(8,128)(2,1)S(1)}, u32[]{:S(2)}, u32[]{:S(2)}) %collective-permute-start.19) | collective-permute-done | bytes 262176 | tf_op jit(solution)/shard_map/ppermute | solution.py:31
  79.7 8.5 %collective-permute-done.21.refs_2_ = bf16[256,512]{1,0:T(8,128)(2,1)S(1)} collective-permute-done((bf16[256,512]{1,0:T(8,128)(2,1)S(1)}, bf16[256,512]{1,0:T(8,128)(2,1)S(1)}, u32[]{:S(2)}, u32[]{:S(2)}) %collective-permute-start.21) | collective-permute-done | bytes 262176 | tf_op jit(solution)/shard_map/ppermute | solution.py:31
  88.2 1.4 down_grad.1
  90.4 1.5 collective-permute-done.20.refs_4_
  91.9 7.1 %attention_backward.1 = (f32[64,1024]{1,0:T(8,128)S(1)}, bf16[256,1024]{1,0:T(8,128)(2,1)S(1)}, bf16[256,512]{1,0:T(8,128)(2,1)S(1)}, f32[1,1024]{1,0:T(1,128)S(...) custom-call(s32[2]{0:T(128)S(1)} %pad_add_fusion.refs_0_, ...), custom_call_target="tpu_custom_call" | custom-call | tf_op jit(solution)/shard_map/attention_backward/pallas_call | solution.py:479
  99.1 2.0 collective-permute-start.23
  101.1 5.3 %collective-permute-done.26.refs_2_.refs_4_ = bf16[256,1664]{1,0:T(8,128)(2,1)S(1)} collective-permute-done((bf16[256,1664]{1,0:T(8,128)(2,1)S(1)}, bf16[256,1664]{1,0:T(8,128)(2,1)S(1)}, u32[]{:S(2)}, u32[]{:S(2)}) %collective-permute-start.26) | collective-permute-done | bytes 852000 | tf_op jit(solution)/shard_map/ppermute | solution.py:31
  106.4 1.5 gate_grad.1
  109.2 2.0 collective-permute-done.23.refs_2_.refs_15_
  112.9 1.7 collective-permute-start.30
  114.7 14.6 %collective-permute-done.30.refs_3_ = bf16[256,256]{1,0:T(8,128)(2,1)S(1)} collective-permute-done((bf16[256,256]{1,0:T(8,128)(2,1)S(1)}, bf16[256,256]{1,0:T(8,128)(2,1)S(1)}, u32[]{:S(2)}, u32[]{:S(2)}) %collective-permute-start.30) | collective-permute-done | bytes 131104 | tf_op jit(solution)/shard_map/ppermute | solution.py:31
  133.9 6.1 %collective-permute-start.40 = (bf16[256,768]{1,0:T(8,128)(2,1)S(1)}, bf16[256,768]{1,0:T(8,128)(2,1)S(1)}, u32[]{:S(2)}, u32[]{:S(2)}) collective-permute-start(bf16[256,768]{1,0:T(8,128)(2,1)S(1)} %get-tuple-element.152.refs_3_), channel_id=1, source_target_pairs={{0,4},{4,0},{8,12},{12,8},{16,20},{20,16},{24,28},{28,24},{1,5},{5... | collective-permute-start | bytes 1179656 | tf_op jit(solution)/shard_map/ppermute | solution.py:31
  141.0 1.5 up_grad.1
  146.9 2.3 %collective-permute-done.36.refs_1_ = f32[18,128]{1,0:T(8,128)S(1)} collective-permute-done((f32[18,128]{1,0:T(8,128)S(1)}, f32[18,128]{1,0:T(8,128)S(1)}, u32[]{:S(2)}, u32[]{:S(2)}) %collective-permute-start.36) | collective-permute-done | bytes 9248 | tf_op jit(solution)/shard_map/ppermute | solution.py:31
  149.3 2.0 collective-permute-start.41
  151.3 3.9 %collective-permute-done.39.refs_2_.refs_8_ = bf16[256,768]{1,0:T(8,128)(2,1)S(1)} collective-permute-done((bf16[256,768]{1,0:T(8,128)(2,1)S(1)}, bf16[256,768]{1,0:T(8,128)(2,1)S(1)}, u32[]{:S(2)}, u32[]{:S(2)}) %collective-permute-start.39) | collective-permute-done | bytes 393248 | tf_op jit(solution)/shard_map/ppermute | solution.py:31
  155.3 1.4 collective-permute-done.41.refs_12_
  158.3 1.6 collective-permute-start.38
  159.8 3.3 %collective-permute-start.46 = (bf16[128,1152]{1,0:T(8,128)(2,1)S(1)}, bf16[128,1152]{1,0:T(8,128)(2,1)S(1)}, u32[]{:S(2)}, u32[]{:S(2)}) collective-permute-start(bf16[128,1152]{1,0:T(8,128)(2,1)S(1)} %get-tuple-element.129.refs_4_), channel_id=1, source_target_pairs={{0,16},{4,20},{8,24},{12,28},{16,0},{20,4},{24,8},{28,12},{1,17},{... | collective-permute-start | bytes 884744 | tf_op jit(solution)/shard_map/ppermute | solution.py:31
  163.1 2.1 collective-permute-start.45
  165.2 1.4 collective-permute-start.43
  167.5 2.7 %collective-permute-done.43.refs_4_ = bf16[64,1024]{1,0:T(8,128)(2,1)S(1)} collective-permute-done((bf16[64,1024]{1,0:T(8,128)(2,1)S(1)}, bf16[64,1024]{1,0:T(8,128)(2,1)S(1)}, u32[]{:S(2)}, u32[]{:S(2)}) %collective-permute-start.43) | collective-permute-done | bytes 131104 | tf_op jit(solution)/shard_map/ppermute | solution.py:31
  173.6 10.1 %collective-permute-done.46.refs_1_ = bf16[128,1152]{1,0:T(8,128)(2,1)S(1)} collective-permute-done((bf16[128,1152]{1,0:T(8,128)(2,1)S(1)}, bf16[128,1152]{1,0:T(8,128)(2,1)S(1)}, u32[]{:S(2)}, u32[]{:S(2)}) %collective-permute-start.46) | collective-permute-done | bytes 294944 | tf_op jit(solution)/shard_map/ppermute | solution.py:31
  190.1 2.9 %collective-permute-start.48 = (bf16[128,1152]{1,0:T(8,128)(2,1)S(1)}, bf16[128,1152]{1,0:T(8,128)(2,1)S(1)}, u32[]{:S(2)}, u32[]{:S(2)}) collective-permute-start(bf16[128,1152]{1,0:T(8,128)(2,1)S(1)} %get-tuple-element.156.refs_2_), channel_id=1, source_target_pairs={{0,16},{4,20},{8,24},{12,28},{16,0},{20,4},{24,8},{28,12},{1,17},{... | collective-permute-start | bytes 884744 | tf_op jit(solution)/shard_map/ppermute | solution.py:31
  193.1 9.1 %collective-permute-done.50.refs_1_ = f32[18,128]{1,0:T(8,128)S(1)} collective-permute-done((f32[18,128]{1,0:T(8,128)S(1)}, f32[18,128]{1,0:T(8,128)S(1)}, u32[]{:S(2)}, u32[]{:S(2)}) %collective-permute-start.50) | collective-permute-done | bytes 9248 | tf_op jit(solution)/shard_map/ppermute | solution.py:31
  203.4 5.1 %collective-permute-done.48.refs_1_ = bf16[128,1152]{1,0:T(8,128)(2,1)S(1)} collective-permute-done((bf16[128,1152]{1,0:T(8,128)(2,1)S(1)}, bf16[128,1152]{1,0:T(8,128)(2,1)S(1)}, u32[]{:S(2)}, u32[]{:S(2)}) %collective-permute-start.48) | collective-permute-done | bytes 294944 | tf_op jit(solution)/shard_map/ppermute | solution.py:31
  209.3 2.8 %collective-permute-done.47.refs_1_ = bf16[128,768]{1,0:T(8,128)(2,1)S(1)} collective-permute-done((bf16[128,768]{1,0:T(8,128)(2,1)S(1)}, bf16[128,768]{1,0:T(8,128)(2,1)S(1)}, u32[]{:S(2)}, u32[]{:S(2)}) %collective-permute-start.47) | collective-permute-done | bytes 196640 | tf_op jit(solution)/shard_map/ppermute | solution.py:31
  (148 shorter events, 45.9 us)
Async XLA Ops:
  0.7 6.7 %collective-permute-start = (bf16[64,1024]{1,0:T(8,128)(2,1)}, bf16[64,1024]{1,0:T(8,128)(2,1)S(1)}, u32[]{:S(2)}, u32[]{:S(2)}) collective-permute-start(bf16[64,1024]{1,0:T(8,128)(2,1)} %refs_0_.1), channel_id=1, source_target_pairs={{0,2},{1,3},{2,0},{3,1},{4,6},{5,7},{6,4},{7,5},{8,10},{9,11},{10,... | collective-permute-start | bytes 393224 | tf_op jit(solution)/shard_map/ppermute | solution.py:31
  3.7 3.8 %collective-permute-start.1 = (bf16[64,1024]{1,0:T(8,128)(2,1)}, bf16[64,1024]{1,0:T(8,128)(2,1)S(1)}, u32[]{:S(2)}, u32[]{:S(2)}) collective-permute-start(bf16[64,1024]{1,0:T(8,128)(2,1)} %refs_0_.1), channel_id=1, source_target_pairs={{0,1},{1,0},{2,3},{3,2},{4,5},{5,4},{6,7},{7,6},{8,9},{9,8},{10,11... | collective-permute-start | bytes 393224 | tf_op jit(solution)/shard_map/ppermute | solution.py:31
  17.5 13.1 %collective-permute-start.3 = (bf16[256,256]{1,0:T(8,128)(2,1)S(1)}, bf16[256,256]{1,0:T(8,128)(2,1)S(1)}, u32[]{:S(2)}, u32[]{:S(2)}) collective-permute-start(bf16[256,256]{1,0:T(8,128)(2,1)S(1)} %get-tuple-element.95.refs_5_.refs_11_), channel_id=1, source_target_pairs={{0,8},{4,12},{8,16},{12,20},{16,24},{20,28},{1,9},{5,13},{9,17},{1... | collective-permute-start | bytes 393224 | tf_op jit(solution)/shard_map/ppermute | solution.py:642
  21.4 11.9 %collective-permute-start.4 = (bf16[256,256]{1,0:T(8,128)(2,1)S(1)}, bf16[256,256]{1,0:T(8,128)(2,1)S(1)}, u32[]{:S(2)}, u32[]{:S(2)}) collective-permute-start(bf16[256,256]{1,0:T(8,128)(2,1)S(1)} %get-tuple-element.95.refs_5_.refs_11_), channel_id=1, source_target_pairs={{0,16},{4,20},{8,24},{12,28},{1,17},{5,21},{9,25},{13,29},{2,18},{... | collective-permute-start | bytes 393224 | tf_op jit(solution)/shard_map/ppermute | solution.py:642
  25.9 11.9 %collective-permute-start.10 = (bf16[256,256]{1,0:T(8,128)(2,1)S(1)}, bf16[256,256]{1,0:T(8,128)(2,1)S(1)}, u32[]{:S(2)}, u32[]{:S(2)}) collective-permute-start(bf16[256,256]{1,0:T(8,128)(2,1)S(1)} %get-tuple-element.95.refs_5_.refs_11_), channel_id=1, source_target_pairs={{4,28},{5,29},{6,30},{7,31}} | collective-permute-start | bytes 393224 | tf_op jit(solution)/shard_map/ppermute | solution.py:642
  26.5 12.6 %collective-permute-start.5 = (bf16[256,256]{1,0:T(8,128)(2,1)S(1)}, bf16[256,256]{1,0:T(8,128)(2,1)S(1)}, u32[]{:S(2)}, u32[]{:S(2)}) collective-permute-start(bf16[256,256]{1,0:T(8,128)(2,1)S(1)} %get-tuple-element.95.refs_5_.refs_11_), channel_id=1, source_target_pairs={{0,4},{8,12},{16,20},{24,28},{1,5},{9,13},{17,21},{25,29},{2,6},{1... | collective-permute-start | bytes 393224 | tf_op jit(solution)/shard_map/ppermute | solution.py:635
  30.6 10.0 %collective-permute-start.6 = (bf16[256,256]{1,0:T(8,128)(2,1)S(1)}, bf16[256,256]{1,0:T(8,128)(2,1)S(1)}, u32[]{:S(2)}, u32[]{:S(2)}) collective-permute-start(bf16[256,256]{1,0:T(8,128)(2,1)S(1)} %collective-permute-done.3.refs_6_.refs_13_), channel_id=1, source_target_pairs={{0,4},{8,12},{16,20},{24,28},{1,5},{9,13},{17,21},{25,29},{2,6},{1... | collective-permute-start | bytes 393224 | tf_op jit(solution)/shard_map/ppermute | solution.py:635
  31.9 8.7 %collective-permute-start.8 = (bf16[256,256]{1,0:T(8,128)(2,1)S(1)}, bf16[256,256]{1,0:T(8,128)(2,1)S(1)}, u32[]{:S(2)}, u32[]{:S(2)}) collective-permute-start(bf16[256,256]{1,0:T(8,128)(2,1)S(1)} %collective-permute-done.3.refs_6_.refs_13_), channel_id=1, source_target_pairs={{4,0},{12,8},{20,16},{28,24},{5,1},{13,9},{21,17},{29,25},{6,2},{1... | collective-permute-start | bytes 393224 | tf_op jit(solution)/shard_map/ppermute | solution.py:635
  33.2 7.4 %collective-permute-start.7 = (bf16[256,256]{1,0:T(8,128)(2,1)S(1)}, bf16[256,256]{1,0:T(8,128)(2,1)S(1)}, u32[]{:S(2)}, u32[]{:S(2)}) collective-permute-start(bf16[256,256]{1,0:T(8,128)(2,1)S(1)} %collective-permute-done.4.refs_7_.refs_15_), channel_id=1, source_target_pairs={{0,4},{8,12},{16,20},{24,28},{1,5},{9,13},{17,21},{25,29},{2,6},{1... | collective-permute-start | bytes 393224 | tf_op jit(solution)/shard_map/ppermute | solution.py:635
  37.8 7.4 %collective-permute-start.9 = (bf16[256,256]{1,0:T(8,128)(2,1)S(1)}, bf16[256,256]{1,0:T(8,128)(2,1)S(1)}, u32[]{:S(2)}, u32[]{:S(2)}) collective-permute-start(bf16[256,256]{1,0:T(8,128)(2,1)S(1)} %collective-permute-done.4.refs_7_.refs_15_), channel_id=1, source_target_pairs={{4,0},{12,8},{20,16},{28,24},{5,1},{13,9},{21,17},{29,25},{6,2},{1... | collective-permute-start | bytes 393224 | tf_op jit(solution)/shard_map/ppermute | solution.py:635
  39.1 7.5 %collective-permute-start.11 = (bf16[256,256]{1,0:T(8,128)(2,1)S(1)}, bf16[256,256]{1,0:T(8,128)(2,1)S(1)}, u32[]{:S(2)}, u32[]{:S(2)}) collective-permute-start(bf16[256,256]{1,0:T(8,128)(2,1)S(1)} %collective-permute-done.10), channel_id=1, source_target_pairs={{4,0},{12,8},{20,16},{28,24},{5,1},{13,9},{21,17},{29,25},{6,2},{1... | collective-permute-start | bytes 393224 | tf_op jit(solution)/shard_map/ppermute | solution.py:635
  50.6 1.6 collective-permute-start.12
  50.7 6.4 %collective-permute-start.14 = (bf16[64,1024]{1,0:T(8,128)(2,1)S(1)}, bf16[64,1024]{1,0:T(8,128)(2,1)S(1)}, u32[]{:S(2)}, u32[]{:S(2)}) collective-permute-start(bf16[64,1024]{1,0:T(8,128)(2,1)S(1)} %copy-done.17), channel_id=1, source_target_pairs={{0,2},{1,3},{2,0},{3,1},{4,6},{5,7},{6,4},{7,5},{8,10},{9,11},{10,... | collective-permute-start | bytes 393224 | tf_op jit(solution)/shard_map/ppermute | solution.py:31
  52.3 9.9 %collective-permute-start.13 = (bf16[128,1024]{1,0:T(8,128)(2,1)S(1)}, bf16[128,1024]{1,0:T(8,128)(2,1)S(1)}, u32[]{:S(2)}, u32[]{:S(2)}) collective-permute-start(bf16[128,1024]{1,0:T(8,128)(2,1)S(1)} %resid_core.1.refs_6_.refs_0_), channel_id=1, source_target_pairs={{0,2},{1,3},{2,0},{3,1},{4,6},{5,7},{6,4},{7,5},{8,10},{9,11},{10,... | collective-permute-start | bytes 786440 | tf_op jit(solution)/shard_map/ppermute | solution.py:31
  53.8 3.2 %collective-permute-start.15 = (bf16[64,1024]{1,0:T(8,128)(2,1)S(1)}, bf16[64,1024]{1,0:T(8,128)(2,1)S(1)}, u32[]{:S(2)}, u32[]{:S(2)}) collective-permute-start(bf16[64,1024]{1,0:T(8,128)(2,1)S(1)} %copy-done.17), channel_id=1, source_target_pairs={{0,1},{1,0},{2,3},{3,2},{4,5},{5,4},{6,7},{7,6},{8,9},{9,8},{10,11... | collective-permute-start | bytes 393224 | tf_op jit(solution)/shard_map/ppermute | solution.py:31
  62.3 1.6 collective-permute-start.17
  66.3 21.9 %collective-permute-start.22 = (bf16[256,1152]{1,0:T(8,128)(2,1)S(1)}, bf16[256,1152]{1,0:T(8,128)(2,1)S(1)}, u32[]{:S(2)}, u32[]{:S(2)}) collective-permute-start(bf16[256,1152]{1,0:T(8,128)(2,1)S(1)} %get-tuple-element.100.refs_3_.refs_0_), channel_id=1, source_target_pairs={{0,4},{4,0},{8,12},{12,8},{16,20},{20,16},{24,28},{28,24},{1,5},{5... | collective-permute-start | bytes 1769480 | tf_op jit(solution)/shard_map/ppermute | solution.py:31
  69.6 1.6 collective-permute-start.18
  71.2 8.4 %collective-permute-start.19 = (bf16[128,1024]{1,0:T(8,128)(2,1)S(1)}, bf16[128,1024]{1,0:T(8,128)(2,1)S(1)}, u32[]{:S(2)}, u32[]{:S(2)}) collective-permute-start(bf16[128,1024]{1,0:T(8,128)(2,1)S(1)} %get-tuple-element.109.refs_0_), channel_id=1, source_target_pairs={{0,2},{1,3},{2,0},{3,1},{4,6},{5,7},{6,4},{7,5},{8,10},{9,11},{10,... | collective-permute-start | bytes 786440 | tf_op jit(solution)/shard_map/ppermute | solution.py:31
  72.8 15.4 %collective-permute-start.21 = (bf16[256,512]{1,0:T(8,128)(2,1)S(1)}, bf16[256,512]{1,0:T(8,128)(2,1)S(1)}, u32[]{:S(2)}, u32[]{:S(2)}) collective-permute-start(bf16[256,512]{1,0:T(8,128)(2,1)S(1)} %get-tuple-element.116), channel_id=1, source_target_pairs={{0,4},{4,0},{8,12},{12,8},{16,20},{20,16},{24,28},{28,24},{1,5},{5... | collective-permute-start | bytes 786440 | tf_op jit(solution)/shard_map/ppermute | solution.py:31
  74.8 31.6 %collective-permute-start.26 = (bf16[256,1664]{1,0:T(8,128)(2,1)S(1)}, bf16[256,1664]{1,0:T(8,128)(2,1)S(1)}, u32[]{:S(2)}, u32[]{:S(2)}) collective-permute-start(bf16[256,1664]{1,0:T(8,128)(2,1)S(1)} %get-tuple-element.127.refs_3_), channel_id=1, source_target_pairs={{0,4},{4,0},{8,12},{12,8},{16,20},{20,16},{24,28},{28,24},{1,5},{5... | collective-permute-start | bytes 2555912 | tf_op jit(solution)/shard_map/ppermute | solution.py:31
  89.6 18.3 %collective-permute-start.25 = (bf16[256,1152]{1,0:T(8,128)(2,1)S(1)}, bf16[256,1152]{1,0:T(8,128)(2,1)S(1)}, u32[]{:S(2)}, u32[]{:S(2)}) collective-permute-start(bf16[256,1152]{1,0:T(8,128)(2,1)S(1)} %get-tuple-element.117.refs_17_), channel_id=1, source_target_pairs={{0,8},{4,12},{8,0},{12,4},{16,24},{20,28},{24,16},{28,20},{1,9},{5... | collective-permute-start | bytes 1769480 | tf_op jit(solution)/shard_map/ppermute | solution.py:31
  90.4 1.5 collective-permute-start.20
  99.0 10.2 %collective-permute-start.24 = (bf16[256,256]{1,0:T(8,128)(2,1)S(1)}, bf16[256,256]{1,0:T(8,128)(2,1)S(1)}, u32[]{:S(2)}, u32[]{:S(2)}) collective-permute-start(bf16[256,256]{1,0:T(8,128)(2,1)S(1)} %get-tuple-element.124), channel_id=1, source_target_pairs={{0,4},{4,0},{8,12},{12,8},{16,20},{20,16},{24,28},{28,24},{1,5},{5... | collective-permute-start | bytes 393224 | tf_op jit(solution)/shard_map/ppermute | solution.py:31
  99.1 12.2 %collective-permute-start.23 = (bf16[256,256]{1,0:T(8,128)(2,1)S(1)}, bf16[256,256]{1,0:T(8,128)(2,1)S(1)}, u32[]{:S(2)}, u32[]{:S(2)}) collective-permute-start(bf16[256,256]{1,0:T(8,128)(2,1)S(1)} %get-tuple-element.123), channel_id=1, source_target_pairs={{0,4},{4,0},{8,12},{12,8},{16,20},{20,16},{24,28},{28,24},{1,5},{5... | collective-permute-start | bytes 393224 | tf_op jit(solution)/shard_map/ppermute | solution.py:31
  111.9 28.2 %collective-permute-start.28 = (bf16[256,1152]{1,0:T(8,128)(2,1)S(1)}, bf16[256,1152]{1,0:T(8,128)(2,1)S(1)}, u32[]{:S(2)}, u32[]{:S(2)}) collective-permute-start(bf16[256,1152]{1,0:T(8,128)(2,1)S(1)} %get-tuple-element.131.refs_7_.refs_3_), channel_id=1, source_target_pairs={{0,4},{4,0},{8,12},{12,8},{16,20},{20,16},{24,28},{28,24},{1,5},{5... | collective-permute-start | bytes 1769480 | tf_op jit(solution)/shard_map/ppermute | solution.py:31
  112.2 31.8 %collective-permute-start.35 = (bf16[256,1152]{1,0:T(8,128)(2,1)S(1)}, bf16[256,1152]{1,0:T(8,128)(2,1)S(1)}, u32[]{:S(2)}, u32[]{:S(2)}) collective-permute-start(bf16[256,1152]{1,0:T(8,128)(2,1)S(1)} %get-tuple-element.128.refs_2_), channel_id=1, source_target_pairs={{0,8},{4,12},{8,0},{12,4},{16,24},{20,28},{24,16},{28,20},{1,9},{5... | collective-permute-start | bytes 1769480 | tf_op jit(solution)/shard_map/ppermute | solution.py:31
  112.9 16.4 %collective-permute-start.30 = (bf16[256,256]{1,0:T(8,128)(2,1)S(1)}, bf16[256,256]{1,0:T(8,128)(2,1)S(1)}, u32[]{:S(2)}, u32[]{:S(2)}) collective-permute-start(bf16[256,256]{1,0:T(8,128)(2,1)S(1)} %get-tuple-element.141), channel_id=1, source_target_pairs={{0,4},{4,0},{8,12},{12,8},{16,20},{20,16},{24,28},{28,24},{1,5},{5... | collective-permute-start | bytes 393224 | tf_op jit(solution)/shard_map/ppermute | solution.py:31
  129.3 4.6 %collective-permute-start.31 = (bf16[256,256]{1,0:T(8,128)(2,1)S(1)}, bf16[256,256]{1,0:T(8,128)(2,1)S(1)}, u32[]{:S(2)}, u32[]{:S(2)}) collective-permute-start(bf16[256,256]{1,0:T(8,128)(2,1)S(1)} %collective-permute-done.30.refs_3_), channel_id=1, source_target_pairs={{28,4},{29,5},{30,6},{31,7}} | collective-permute-start | bytes 393224 | tf_op jit(solution)/shard_map/ppermute | solution.py:750
  130.6 11.9 %collective-permute-start.32 = (bf16[256,256]{1,0:T(8,128)(2,1)S(1)}, bf16[256,256]{1,0:T(8,128)(2,1)S(1)}, u32[]{:S(2)}, u32[]{:S(2)}) collective-permute-start(bf16[256,256]{1,0:T(8,128)(2,1)S(1)} %pair_sum.3), channel_id=1, source_target_pairs={{16,0},{20,4},{24,8},{28,12},{17,1},{21,5},{25,9},{29,13},{18,2},{... | collective-permute-start | bytes 393224 | tf_op jit(solution)/shard_map/ppermute | solution.py:41
  131.8 10.7 %collective-permute-start.33 = (bf16[256,256]{1,0:T(8,128)(2,1)S(1)}, bf16[256,256]{1,0:T(8,128)(2,1)S(1)}, u32[]{:S(2)}, u32[]{:S(2)}) collective-permute-start(bf16[256,256]{1,0:T(8,128)(2,1)S(1)} %get-tuple-element.143), channel_id=1, source_target_pairs={{8,0},{12,4},{16,8},{20,12},{24,16},{28,20},{9,1},{13,5},{17,9},{2... | collective-permute-start | bytes 393224 | tf_op jit(solution)/shard_map/ppermute | solution.py:41
  133.9 17.4 %collective-permute-start.40 = (bf16[256,768]{1,0:T(8,128)(2,1)S(1)}, bf16[256,768]{1,0:T(8,128)(2,1)S(1)}, u32[]{:S(2)}, u32[]{:S(2)}) collective-permute-start(bf16[256,768]{1,0:T(8,128)(2,1)S(1)} %get-tuple-element.152.refs_3_), channel_id=1, source_target_pairs={{0,4},{4,0},{8,12},{12,8},{16,20},{20,16},{24,28},{28,24},{1,5},{5... | collective-permute-start | bytes 1179656 | tf_op jit(solution)/shard_map/ppermute | solution.py:31
  140.0 15.2 %collective-permute-start.39 = (bf16[256,768]{1,0:T(8,128)(2,1)S(1)}, bf16[256,768]{1,0:T(8,128)(2,1)S(1)}, u32[]{:S(2)}, u32[]{:S(2)}) collective-permute-start(bf16[256,768]{1,0:T(8,128)(2,1)S(1)} %get-tuple-element.151.refs_7_), channel_id=1, source_target_pairs={{0,4},{4,0},{8,12},{12,8},{16,20},{20,16},{24,28},{28,24},{1,5},{5... | collective-permute-start | bytes 1179656 | tf_op jit(solution)/shard_map/ppermute | solution.py:31
  142.4 22.8 %collective-permute-start.29 = (bf16[256,1152]{1,0:T(8,128)(2,1)S(1)}, bf16[256,1152]{1,0:T(8,128)(2,1)S(1)}, u32[]{:S(2)}, u32[]{:S(2)}) collective-permute-start(bf16[256,1152]{1,0:T(8,128)(2,1)S(1)} %get-tuple-element.136.refs_19_), channel_id=1, source_target_pairs={{0,8},{4,12},{8,0},{12,4},{16,24},{20,28},{24,16},{28,20},{1,9},{5... | collective-permute-start | bytes 1769480 | tf_op jit(solution)/shard_map/ppermute | solution.py:31
  143.9 7.3 %collective-permute-start.37 = (bf16[128,1024]{1,0:T(8,128)(2,1)S(1)}, bf16[128,1024]{1,0:T(8,128)(2,1)S(1)}, u32[]{:S(2)}, u32[]{:S(2)}) collective-permute-start(bf16[128,1024]{1,0:T(8,128)(2,1)S(1)} %get-tuple-element.148), channel_id=1, source_target_pairs={{0,1},{1,0},{2,3},{3,2},{4,5},{5,4},{6,7},{7,6},{8,9},{9,8},{10,11... | collective-permute-start | bytes 786440 | tf_op jit(solution)/shard_map/ppermute | solution.py:31
  145.6 3.7 %collective-permute-start.36 = (f32[18,128]{1,0:T(8,128)S(1)}, f32[18,128]{1,0:T(8,128)S(1)}, u32[]{:S(2)}, u32[]{:S(2)}) collective-permute-start(f32[18,128]{1,0:T(8,128)S(1)} %gains.5.refs_2_.refs_0_), channel_id=1, source_target_pairs={{0,2},{1,3},{2,0},{3,1},{4,6},{5,7},{6,4},{7,5},{8,10},{9,11},{10,... | collective-permute-start | bytes 27656 | tf_op jit(solution)/shard_map/ppermute | solution.py:31
  149.3 7.4 %collective-permute-start.41 = (bf16[256,256]{1,0:T(8,128)(2,1)S(1)}, bf16[256,256]{1,0:T(8,128)(2,1)S(1)}, u32[]{:S(2)}, u32[]{:S(2)}) collective-permute-start(bf16[256,256]{1,0:T(8,128)(2,1)S(1)} %get-tuple-element.154.refs_11_), channel_id=1, source_target_pairs={{0,4},{4,0},{8,12},{12,8},{16,20},{20,16},{24,28},{28,24},{1,5},{5... | collective-permute-start | bytes 393224 | tf_op jit(solution)/shard_map/ppermute | solution.py:31
  151.3 15.6 %collective-permute-start.27 = (bf16[128,1024]{1,0:T(8,128)(2,1)S(1)}, bf16[128,1024]{1,0:T(8,128)(2,1)S(1)}, u32[]{:S(2)}, u32[]{:S(2)}) collective-permute-start(bf16[128,1024]{1,0:T(8,128)(2,1)S(1)} %get-tuple-element.134.refs_5_), channel_id=1, source_target_pairs={{0,1},{1,0},{2,3},{3,2},{4,5},{5,4},{6,7},{7,6},{8,9},{9,8},{10,11... | collective-permute-start | bytes 786440 | tf_op jit(solution)/shard_map/ppermute | solution.py:31
  157.9 31.0 %collective-permute-start.44 = (bf16[256,768]{1,0:T(8,128)(2,1)S(1)}, bf16[256,768]{1,0:T(8,128)(2,1)S(1)}, u32[]{:S(2)}, u32[]{:S(2)}) collective-permute-start(bf16[256,768]{1,0:T(8,128)(2,1)S(1)} %get-tuple-element.155.refs_2_), channel_id=1, source_target_pairs={{0,8},{4,12},{8,0},{12,4},{16,24},{20,28},{24,16},{28,20},{1,9},{5... | collective-permute-start | bytes 1179656 | tf_op jit(solution)/shard_map/ppermute | solution.py:31
  158.3 4.8 %collective-permute-start.38 = (f32[18,128]{1,0:T(8,128)S(1)}, f32[18,128]{1,0:T(8,128)S(1)}, u32[]{:S(2)}, u32[]{:S(2)}) collective-permute-start(f32[18,128]{1,0:T(8,128)S(1)} %gains.6.refs_13_.refs_0_), channel_id=1, source_target_pairs={{0,4},{4,0},{8,12},{12,8},{16,20},{20,16},{24,28},{28,24},{1,5},{5... | collective-permute-start | bytes 27656 | tf_op jit(solution)/shard_map/ppermute | solution.py:31
  159.8 23.8 %collective-permute-start.46 = (bf16[128,1152]{1,0:T(8,128)(2,1)S(1)}, bf16[128,1152]{1,0:T(8,128)(2,1)S(1)}, u32[]{:S(2)}, u32[]{:S(2)}) collective-permute-start(bf16[128,1152]{1,0:T(8,128)(2,1)S(1)} %get-tuple-element.129.refs_4_), channel_id=1, source_target_pairs={{0,16},{4,20},{8,24},{12,28},{16,0},{20,4},{24,8},{28,12},{1,17},{... | collective-permute-start | bytes 884744 | tf_op jit(solution)/shard_map/ppermute | solution.py:31
  163.1 23.8 %collective-permute-start.45 = (bf16[128,1152]{1,0:T(8,128)(2,1)S(1)}, bf16[128,1152]{1,0:T(8,128)(2,1)S(1)}, u32[]{:S(2)}, u32[]{:S(2)}) collective-permute-start(bf16[128,1152]{1,0:T(8,128)(2,1)S(1)} %get-tuple-element.147.refs_2_), channel_id=1, source_target_pairs={{0,16},{4,20},{8,24},{12,28},{16,0},{20,4},{24,8},{28,12},{1,17},{... | collective-permute-start | bytes 884744 | tf_op jit(solution)/shard_map/ppermute | solution.py:31
  165.2 5.0 %collective-permute-start.43 = (bf16[64,1024]{1,0:T(8,128)(2,1)S(1)}, bf16[64,1024]{1,0:T(8,128)(2,1)S(1)}, u32[]{:S(2)}, u32[]{:S(2)}) collective-permute-start(bf16[64,1024]{1,0:T(8,128)(2,1)S(1)} %get-tuple-element.160), channel_id=1, source_target_pairs={{0,2},{1,3},{2,0},{3,1},{4,6},{5,7},{6,4},{7,5},{8,10},{9,11},{10,... | collective-permute-start | bytes 393224 | tf_op jit(solution)/shard_map/ppermute | solution.py:31
  166.9 5.0 %collective-permute-start.42 = (bf16[64,1024]{1,0:T(8,128)(2,1)S(1)}, bf16[64,1024]{1,0:T(8,128)(2,1)S(1)}, u32[]{:S(2)}, u32[]{:S(2)}) collective-permute-start(bf16[64,1024]{1,0:T(8,128)(2,1)S(1)} %get-tuple-element.158), channel_id=1, source_target_pairs={{0,2},{1,3},{2,0},{3,1},{4,6},{5,7},{6,4},{7,5},{8,10},{9,11},{10,... | collective-permute-start | bytes 393224 | tf_op jit(solution)/shard_map/ppermute | solution.py:31
  170.2 19.8 %collective-permute-start.49 = (f32[18,128]{1,0:T(8,128)S(1)}, f32[18,128]{1,0:T(8,128)S(1)}, u32[]{:S(2)}, u32[]{:S(2)}) collective-permute-start(f32[18,128]{1,0:T(8,128)S(1)} %gains.7.refs_2_.refs_0_), channel_id=1, source_target_pairs={{0,8},{4,12},{8,0},{12,4},{16,24},{20,28},{24,16},{28,20},{1,9},{5... | collective-permute-start | bytes 27656 | tf_op jit(solution)/shard_map/ppermute | solution.py:31
  190.0 12.1 %collective-permute-start.50 = (f32[18,128]{1,0:T(8,128)S(1)}, f32[18,128]{1,0:T(8,128)S(1)}, u32[]{:S(2)}, u32[]{:S(2)}) collective-permute-start(f32[18,128]{1,0:T(8,128)S(1)} %gains.8.refs_0_), channel_id=1, source_target_pairs={{0,16},{4,20},{8,24},{12,28},{16,0},{20,4},{24,8},{28,12},{1,17},{... | collective-permute-start | bytes 27656 | tf_op jit(solution)/shard_map/ppermute | solution.py:31
  190.1 18.4 %collective-permute-start.48 = (bf16[128,1152]{1,0:T(8,128)(2,1)S(1)}, bf16[128,1152]{1,0:T(8,128)(2,1)S(1)}, u32[]{:S(2)}, u32[]{:S(2)}) collective-permute-start(bf16[128,1152]{1,0:T(8,128)(2,1)S(1)} %get-tuple-element.156.refs_2_), channel_id=1, source_target_pairs={{0,16},{4,20},{8,24},{12,28},{16,0},{20,4},{24,8},{28,12},{1,17},{... | collective-permute-start | bytes 884744 | tf_op jit(solution)/shard_map/ppermute | solution.py:31
  193.0 19.1 %collective-permute-start.47 = (bf16[128,768]{1,0:T(8,128)(2,1)S(1)}, bf16[128,768]{1,0:T(8,128)(2,1)S(1)}, u32[]{:S(2)}, u32[]{:S(2)}) collective-permute-start(bf16[128,768]{1,0:T(8,128)(2,1)S(1)} %get-tuple-element.165.refs_2_), channel_id=1, source_target_pairs={{0,16},{4,20},{8,24},{12,28},{16,0},{20,4},{24,8},{28,12},{1,17},{... | collective-permute-start | bytes 589832 | tf_op jit(solution)/shard_map/ppermute | solution.py:31
  (29 other events, 184.5 us)

commit v3 on v2

--- a/solution.py
+++ b/solution.py
@@ -20,6 +20,7 @@
 ROWS = (((0,), (0,)), ((), ()))
 COLS = (((1,), (1,)), ((), ()))
 SCALE = HD ** (-0.5)
+RANKS = "ranks"
 
 
 def dot(a, b, dims=(((1,), (0,)), ((), ()))):
@@ -112,10 +113,22 @@
 
 
 def qkv_kernel(
-    ranks, x0, x1, x2, x3, gain, wq, wk, wv, query_gain, key_gain, positions,
+    x1, x2, x3, x0, gain, positions, wk, wv, key_gain, wq, query_gain,
     act_out, select_out, pair_out, query_rot_out, query_out, key_out,
-    cos_out, sin_out, column_out, row_out,
+    cos_out, sin_out, column_out, row_out, *scratch,
 ):
+    sources = (x0, gain, positions, wk, wv, key_gain, wq, query_gain)
+    buffers, sems = scratch[:-1], scratch[-1]
+    copies = [
+        pltpu.make_async_copy(source, buffer, sems.at[i])
+        for i, (source, buffer) in enumerate(zip(sources, buffers, strict=True))
+    ]
+    for copy in copies:
+        copy.start()
+    for copy in copies:
+        copy.wait()
+    x0, gain, positions, wk, wv, key_gain, wq, query_gain = buffers
+    ranks = (lax.axis_index("ctx"), lax.axis_index("mp"))
     rows = act_out.shape[0]
     line = lax.broadcasted_iota(jnp.int32, (rows, rows), 0)
     picked = place_of(line, rows, ranks[1]) == lanes((rows, rows))
@@ -163,18 +176,23 @@
         target[:, b * 128 : (b + 1) * 128] = source[:, pl.ds(start, 128)]
 
 
-def cotangent_kernel(ranks, c0, c1, c2, c3, wd, cot_out, select_out, grad_hidden_out):
+def cotangent_kernel(
+    ranks, c0, c1, c2, c3, wd, act_select, attn_b, cot_out, packet_out, grad_hidden_out
+):
     cot = jnp.concatenate([c0[...], c1[...], c2[...], c3[...]], axis=0)
     cot_out[...] = cot
-    select_columns(ranks, cot_out, select_out)
+    chosen = act_select.shape[1]
+    select_columns(ranks, cot_out, packet_out.at[:, :chosen])
+    packet_out[:, chosen : 2 * chosen] = act_select[...]
+    packet_out[:, 2 * chosen :] = attn_b[...]
     grad_hidden_out[...] = dot(cot, wd[...], COLS)
 
 
-def attention_kernel(count, ranks, query_rot, positions, wo, act_select, *refs):
+def attention_kernel(count, ranks, query_rot, positions, wo, *refs):
     slots = count // 2
     even = refs[:slots]
     low_odd, high_odd = refs[slots : 2 * slots], refs[2 * slots : 3 * slots]
-    out_f32, early_out, sums_out, kept_out, sent_out = refs[3 * slots : 3 * slots + 5]
+    out_f32, out_b, sums_out, kept_out, sent_out = refs[3 * slots : 3 * slots + 5]
     odd = refs[3 * slots + 5 : -1]
     scores = refs[-1]
     rows = query_rot.shape[0]
@@ -215,9 +233,7 @@
         sums_out[head : head + 1, :] = jnp.transpose(sums)[:1]
         out_f32[:, head * 128 : (head + 1) * 128] = unstack(mixed / total, head)
     attn_b = out_f32[...].astype(BF)
-    chosen = act_select.shape[1]
-    early_out[:, :chosen] = act_select[...]
-    early_out[:, chosen:] = attn_b
+    out_b[...] = attn_b
     half = rows // 2
     kept_out[...] = dot(attn_b[:half], wo[...])
     sent_out[...] = dot(attn_b[half:], wo[...]).astype(BF)
@@ -234,14 +250,64 @@
         out[a : a + half, :] = total.astype(out.dtype)
 
 
-def fold_kernel(kept, arrived, front_out, back_out):
-    half = front_out.shape[0]
-    front_out[...] = kept[:half, :] + arrived[:half, :].astype(F32)
-    back_out[...] = (kept[half:, :] + arrived[half:, :].astype(F32)).astype(BF)
-
-
-def turned_add_kernel(kept, arrived, out):
-    out[...] = jnp.transpose(kept[...] + arrived[...].astype(F32))
+def fold_kernel(*refs):
+    count = (len(refs) - 1) // 3
+    back_out = refs[-1]
+    place = 0
+    for p in range(count):
+        kept, arrived, front_out = refs[2 * p], refs[2 * p + 1], refs[2 * count + p]
+        half, width = front_out.shape
+        front_out[...] = kept[:half, :] + arrived[:half, :].astype(F32)
+        back_out[:, place : place + width] = (
+            kept[half:, :] + arrived[half:, :].astype(F32)
+        ).astype(BF)
+        place += width
+
+
+def mp_fold_kernel(input_kept, out_kept, gains, arrived, input_front, out_front, gains_out, back):
+    half = input_kept.shape[0]
+    own = half // 2
+    came = arrived[...].astype(F32)
+    for place, kept, front in ((0, input_kept, input_front), (1, out_kept, out_front)):
+        total = kept[...] + came[place * half : (place + 1) * half]
+        front[...] = total[:own]
+        back[place * own : (place + 1) * own, :] = total[own:].astype(BF)
+    gains_out[...] = gains[...] + unpack(came[2 * half :], gains.shape[0])
+    pack(gains_out[...], back, 2 * own)
+
+
+def pack(values, target, start):
+    count = values.shape[0]
+    target[start : start + 16, :] = jnp.zeros((16, target.shape[1]), BF)
+    front = values.astype(BF)
+    for part, piece in enumerate((front.astype(F32), values - front.astype(F32))):
+        for g in range(-(-count // 16)):
+            rows = piece[16 * g : 16 * g + 16]
+            if rows.shape[0] < 16:
+                rows = jnp.concatenate([rows, jnp.zeros((16 - rows.shape[0], 128), F32)], axis=0)
+            column = (2 * g + part) * 128
+            target[start : start + 16, column : column + 128] = rows.astype(BF)
+
+
+def unpack(values, count):
+    pieces = []
+    for g in range(-(-count // 16)):
+        column = 2 * g * 128
+        total = values[:, column : column + 128] + values[:, column + 128 : column + 256]
+        pieces.append(total[: min(16, count - 16 * g)])
+    return jnp.concatenate(pieces, axis=0)
+
+
+def last_kernel(turned, *refs):
+    count = len(turned)
+    arrived, outs, token = refs[count], refs[count + 1 : -1], refs[-1]
+    place = 0
+    for p in range(count):
+        width = refs[p].shape[1]
+        total = refs[p][...] + arrived[:, place : place + width].astype(F32)
+        outs[p][...] = jnp.transpose(total) if turned[p] else total
+        place += width
+    token[...] = jnp.zeros(token.shape, F32)
 
 
 def attention_last_kernel(kept, arrived, out_grad, query_grad, key_grad, value_grad):
@@ -255,12 +321,18 @@
         start += width
 
 
-def pair_sum_kernel(ranks, term, if_odd, if_even, out):
+def pair_sum_kernel(slots, ranks, *refs):
     odd = ranks[0] % 2 == 1
-    out[...] = (
-        term[...].astype(F32)
-        + jnp.where(odd, if_odd[...].astype(F32), if_even[...].astype(F32))
-    ).astype(BF)
+    terms, arrived = refs[:slots], refs[slots]
+    outs = refs[slots + 1 :]
+    rows = terms[0].shape[0]
+    came = [arrived[j * rows : (j + 1) * rows, :].astype(F32) for j in range(slots)]
+    outs[0][...] = terms[0][...] + jnp.where(odd, 0.0, came[0])
+    for k in range(1, slots):
+        outs[k][...] = (
+            terms[k][...].astype(F32) + jnp.where(odd, came[k - 1], came[k])
+        ).astype(BF)
+    outs[slots][...] = came[slots - 1].astype(BF)
 
 
 def down_kernel(hidden, wd, kept_out, sent_out):
@@ -269,19 +341,20 @@
     kept_out[...] = dot(hidden[:half, :], wd[...])
 
 
-def block_out_kernel(resid, kept, arrived, out):
-    own = out.shape[0]
-    out[...] = (resid[:own, :] + kept[:own, :] + arrived[...].astype(F32)).astype(BF)
-
-
-def grad_input_kernel(x, gain, grad_resid, kept, arrived, out):
-    own = out.shape[0]
-    grads = kept[:own, :] + arrived[...].astype(F32)
+def outputs_kernel(
+    x, gain, grad_resid, resid, input_kept, out_kept, gains, arrived,
+    grad_input_out, block_out, gains_out,
+):
+    own = block_out.shape[0]
+    came = arrived[...].astype(F32)
+    block_out[...] = (resid[:own, :] + out_kept[...] + came[own : 2 * own]).astype(BF)
+    gains_out[...] = gains[...] + unpack(came[2 * own :], gains.shape[0])
+    grads = input_kept[...] + came[:own]
     values = x[...].astype(F32)
     scale = row_norm(values)
     normed = values * scale
     inner = grads * gain[...]
-    out[...] = grad_resid[...] + scale * (
+    grad_input_out[...] = grad_resid[...] + scale * (
         inner - normed * jnp.mean(inner * normed, axis=-1, keepdims=True)
     )
 
@@ -327,8 +400,12 @@
 ):
     blocks = refs[:count]
     grad_own_out, grad_b_out, select_out, gain_out, grad_query_out = refs[count : count + 5]
-    terms = refs[count + 5 :]
+    even, odd = refs[count + 5 : -1], refs[-1]
     rows = query_rot.shape[0]
+    terms = [
+        even[d // 2] if d % 2 == 0 else odd.at[d // 2 * rows : (d // 2 + 1) * rows]
+        for d in range(count)
+    ]
     key_width = blocks[0].shape[1] // 2
     values = resid[...]
     scale = row_norm(values)
@@ -390,25 +467,23 @@
 
 
 def query_backward_kernel(
-    queries, gain, grads, cos, sin, wq, select, late_out, gain_out, partial_out
+    queries, gain, grads, cos, sin, wq, grad_out, gain_out, partial_out
 ):
     grad_in, gain_terms = head_norm_backward(queries[...], wide(gain[...], queries.shape[-1]), grads[...], cos[...], sin[...])
     grad_b = grad_in.astype(BF)
-    chosen = select.shape[1]
-    late_out[:, :chosen] = select[...]
-    late_out[:, chosen:] = grad_b
+    grad_out[...] = grad_b
     gain_out[...] = gain_terms
     partial_out[...] = dot(grad_b, wq[...], COLS)
 
 
 def key_backward_kernel(
-    ranks, keys, gain, cos, sin, wk, wv, query_partial, x0, x1, x2, x3,
-    ffn_gain_part, query_gain_part, term, arrived, *refs,
+    keys, gain, cos, sin, wk, wv, query_partial, x0, x1, x2, x3,
+    ffn_gain_part, query_gain_part, out_sent, select, grad_query_b, term, *refs,
 ):
     shifted = refs[:-4]
-    grad_out, gains_out, kept_out, sent_out = refs[-4:]
+    late_out, gains_out, kept_out, sent_out = refs[-4:]
     width = keys.shape[-1]
-    grads = term[...] + jnp.where(ranks[0] % 2 == 1, 0.0, arrived[...].astype(F32))
+    grads = term[...]
     for other in shifted:
         grads = grads + other[...].astype(F32)
     grad_in, gain_terms = head_norm_backward(
@@ -416,12 +491,15 @@
     )
     grad_b = grad_in.astype(BF)
     value_b = grads[:, width:].astype(BF)
-    grad_out[:, :width] = grad_b
-    grad_out[:, width:] = value_b
+    place = 0
+    for piece in (select[...], grad_query_b[...], grad_b, value_b):
+        late_out[:, place : place + piece.shape[1]] = piece
+        place += piece.shape[1]
     partial = query_partial[...] + dot(grad_b, wk[...], COLS) + dot(value_b, wv[...], COLS)
     half = partial.shape[0] // 2
     kept_out[...] = partial[:half]
-    sent_out[...] = partial[half:].astype(BF)
+    sent_out[:half, :] = partial[half:].astype(BF)
+    sent_out[half : 2 * half, :] = out_sent[...]
     x = jnp.concatenate([x0[...], x1[...], x2[...], x3[...]], axis=0).astype(F32)
     features = x.shape[1]
     parts = [
@@ -437,6 +515,7 @@
     queries = sum(queries[:, c * 128 : (c + 1) * 128] for c in range(queries.shape[1] // 128))
     gains_out[row : row + 1, :] = queries
     gains_out[row + 1 : row + 2, :] = gain_terms
+    pack(gains_out[...], sent_out, 2 * half)
 
 
 def weight_grad_kernel(parts, ranks, *refs):
@@ -444,7 +523,7 @@
     parity = ranks[0] % 2
     mine = ranks[0] // 2
     place = 0
-    for p, (own, there_at, width) in enumerate(parts):
+    for p, (own, there_at, act_at, width) in enumerate(parts):
         act, arrived_act, grads, arrived_grads = refs[4 * p : 4 * p + 4]
         mine_grads = grads[:, own : own + width]
         other_grads = arrived_grads[:, there_at : there_at + width]
@@ -452,7 +531,7 @@
             for hi in range(2):
                 block = jnp.bitwise_xor(mine, lo + 2 * hi)
                 start = pl.multiple_of((2 * block + parity) * 128, 128)
-                there = pl.multiple_of(block * 128, 128)
+                there = pl.multiple_of(act_at + block * 128, 128)
                 total = dot(act[:, pl.ds(start, 128)], mine_grads, ROWS) + dot(
                     arrived_act[:, pl.ds(there, 128)], other_grads, ROWS
                 )
@@ -469,20 +548,20 @@
 
 def launch(kernel, outs, args, scratch=(), name=None, after=(), carry=()):
     nbytes = sum(s.shape[0] * s.shape[1] * 4 for s in scratch)
+    ranked = args[0] is RANKS
+    args = list(args[ranked:])
     n_in, n_out, n_unused = len(args), len(outs), len(after) + len(carry)
 
     def run(*refs):
         results = refs[n_in + n_unused :]
-        kernel(*refs[:n_in], *results[:n_out], *results[n_out + len(carry) :])
+        ranks = [(lax.axis_index("ctx"), lax.axis_index("mp"))] if ranked else []
+        kernel(*ranks, *refs[:n_in], *results[:n_out], *results[n_out + len(carry) :])
 
     any_spec = pl.BlockSpec(memory_space=pl.ANY)
     return pl.pallas_call(
         run,
         out_shape=list(outs) + [shape(c.shape, c.dtype) for c in carry],
-        in_specs=[
-            pl.BlockSpec(memory_space=pltpu.SMEM if a.shape == (2,) else pltpu.VMEM) for a in args
-        ]
-        + [any_spec] * n_unused,
+        in_specs=[pl.BlockSpec(memory_space=pltpu.VMEM)] * n_in + [any_spec] * n_unused,
         out_specs=[pl.BlockSpec(memory_space=pltpu.VMEM) for _ in outs] + [any_spec] * len(carry),
         scratch_shapes=list(scratch),
         input_output_aliases={n_in + len(after) + i: n_out + i for i in range(len(carry))},
@@ -502,18 +581,6 @@
     other = xor(values, "mp", 2)
     core = xor(values, "mp", 1)
     return values, other, core, xor(other, "mp", 1)
-
-
-def mp_reduce_start(kept, sent, name, after=()):
-    own = kept.shape[0] // 2
-    kept, back = launch(
-        fold_kernel,
-        [shape((own, kept.shape[1]), F32), shape((own, kept.shape[1]), BF)],
-        [kept, xor(sent, "mp", 1)],
-        name=name,
-        after=after,
-    )
-    return kept, xor(back, "mp", 2)
 
 
 def split_columns(values):
@@ -529,21 +596,21 @@
     return parts[:, 0], parts[:, 1]
 
 
-def weight_grad(ranks, parts, name, after=()):
+def weight_grad(parts, name, after=()):
     n = lax.axis_size("ctx")
     act = parts[0][0]
     half = act.shape[1] // 4
-    columns = sum(part[5] for part in parts)
+    columns = sum(part[6] for part in parts)
     if n == 8 and act.shape[1] == 1024:
         return launch(
-            functools.partial(weight_grad_kernel, [part[4] + (part[5],) for part in parts]),
+            functools.partial(weight_grad_kernel, [part[4] + part[5:] for part in parts]),
             [shape((half, columns), F32), shape((half, columns), BF)],
-            [ranks] + [a for part in parts for a in part[:4]],
+            [RANKS] + [a for part in parts for a in part[:4]],
             name=name,
             after=after,
         )
     totals = []
-    for act, _, grads, arrived_grads, offsets, width in parts:
+    for act, _, grads, arrived_grads, offsets, _, width in parts:
         own, other = split_columns(act)
         grads = grads[:, offsets[0] : offsets[0] + width]
         arrived_grads = arrived_grads[:, offsets[1] : offsets[1] + width]
@@ -553,21 +620,31 @@
     return total[:half], total[half:].astype(BF)
 
 
-def halve(kept, arrived, name, after=()):
+def fold(pairs, name, after=()):
     n = lax.axis_size("ctx")
+    kept = [p[0] for p in pairs]
+    arrived = [p[1] for p in pairs]
     mask = 4
     while mask < n:
-        half, columns = kept.shape[0] // 2, kept.shape[1]
-        kept, back = launch(
+        half = kept[0].shape[0] // 2
+        widths = [k.shape[1] for k in kept]
+        outs = launch(
             fold_kernel,
-            [shape((half, columns), F32), shape((half, columns), BF)],
-            [kept, arrived],
+            [shape((half, w), F32) for w in widths] + [shape((half, sum(widths)), BF)],
+            [a for pair in zip(kept, arrived, strict=True) for a in pair],
             name=name,
             after=after,
         )
-        arrived = xor(back, "ctx", mask)
+        kept, back = outs[:-1], outs[-1]
+        came = xor(back, "ctx", mask)
         mask *= 2
-    return kept, arrived, back
+        if mask >= n:
+            return kept, came, back
+        arrived = []
+        for w in widths:
+            start = sum(a.shape[1] for a in arrived)
+            arrived.append(came[:, start : start + w])
+    return kept, came, back
 
 
 def body(
@@ -601,7 +678,6 @@
     slots = (window + 1) // 2
     count = window + 1
     half = rows // 2
-    ranks = jnp.stack([ctx_rank, lax.axis_index("mp")]).astype(jnp.int32)
 
     x = mp_gather(block_in)
     query_gain_row = query_gain.reshape(1, -1)
@@ -609,79 +685,88 @@
     attn_gain_row = attn_gain.reshape(1, -1)
     ffn_gain_row = ffn_gain.reshape(1, -1)
 
+    outs = [
+        shape((rows, width), BF),
+        shape((rows, width // 2), BF),
+        shape((rows, 2 * key_width), BF),
+        shape((rows, query_width), BF),
+        shape((rows, query_width), F32),
+        shape((rows, key_width), F32),
+        shape((rows, 128), F32),
+        shape((rows, 128), F32),
+        shape((rows, 1), jnp.int32),
+        shape((1, rows), jnp.int32),
+    ]
+    copied = [block_in, attn_gain_row, positions.reshape(1, -1), key_weight, value_weight,
+              key_gain_row, query_weight, query_gain_row]
     (
         act_attn, act_attn_select, pair, query_rot, queries, keys_pre,
         cos, sin, position_column, position_row,
-    ) = launch(
+    ) = pl.pallas_call(
         qkv_kernel,
-        [
-            shape((rows, width), BF),
-            shape((rows, width // 2), BF),
-            shape((rows, 2 * key_width), BF),
-            shape((rows, query_width), BF),
-            shape((rows, query_width), F32),
-            shape((rows, key_width), F32),
-            shape((rows, 128), F32),
-            shape((rows, 128), F32),
-            shape((rows, 1), jnp.int32),
-            shape((1, rows), jnp.int32),
-        ],
-        [ranks, *x, attn_gain_row, query_weight, key_weight, value_weight,
-         query_gain_row, key_gain_row, positions.reshape(1, -1)],
+        out_shape=outs,
+        in_specs=[pl.BlockSpec(memory_space=pltpu.VMEM)] * 3
+        + [pl.BlockSpec(memory_space=pl.ANY)] * len(copied),
+        out_specs=[pl.BlockSpec(memory_space=pltpu.VMEM)] * len(outs),
+        scratch_shapes=[pltpu.VMEM(a.shape, a.dtype) for a in copied]
+        + [pltpu.SemaphoreType.DMA((len(copied),))],
+        compiler_params=pltpu.CompilerParams(vmem_limit_bytes=52 << 20),
         name="qkv",
-    )
+    )(*x[1:], *copied)
 
     def cross(values, odd):
         return lax.ppermute(values, "ctx", [(i, i ^ 1) for i in range(odd, n_ctx, 2)])
 
-    def climb(step):
-        if step >= n_ctx:
-            return jnp.zeros_like(pair)
-        only_odd = step > window
-        pairs = [(i, i + step) for i in range(n_ctx - step) if i % 2 == 1 or not only_odd]
-        return lax.ppermute(pair, "ctx", pairs)
-
-    items = [pair] + [climb(2 * k) for k in range(1, slots + 1)]
+    def climb(step, pairs):
+        pairs = [(i, i + step) for i in pairs if i + step < n_ctx]
+        return lax.ppermute(pair, "ctx", pairs) if pairs else jnp.zeros_like(pair)
+
+    items = [pair] + [climb(2 * k, range(n_ctx)) for k in range(1, slots)]
+    farthest = climb(2 * slots - 1, range(1, n_ctx, 2))
     low_odd = [cross(items[j], 0) for j in range(slots)]
-    high_odd = [cross(items[j + 1], 1) for j in range(slots)]
+    high_odd = [cross(items[j + 1], 1) for j in range(slots - 1)] + [farthest]
     even = items[:slots]
+    cot_chip = xor(cotangent, "mp", 2)
+    cot_core = xor(cotangent, "mp", 1)
 
     outs = launch(
         functools.partial(attention_kernel, count),
         [
             shape((rows, query_width), F32),
-            shape((rows, width // 2 + query_width), BF),
+            shape((rows, query_width), BF),
             shape((2, 2 * rows), F32),
             shape((half, width), F32),
             shape((half, width), BF),
         ]
         + [shape((rows, 2 * key_width), BF) for _ in range(slots)],
-        [ranks, query_rot, position_column, out_weight, act_attn_select,
+        [RANKS, query_rot, position_column, out_weight,
          *even, *low_odd, *high_odd],
         scratch=[pltpu.VMEM((2 * rows, count * rows), F32)],
         name="attention",
-    )
-    attn_rows, early, log_sums, kept, sent = outs[:5]
+        after=[cot_chip, cot_core],
+    )
+    attn_rows, attn_b, log_sums, kept, sent = outs[:5]
     blocks = [(even, outs[5:])[d % 2][d // 2] for d in range(count)]
     chosen = width // 2
 
     kept = add(kept, xor(sent, "mp", 1), BF, "resid_core")
-    cot, cot_select, grad_hidden = launch(
+    cot, packet, grad_hidden = launch(
         cotangent_kernel,
         [
             shape((rows, width), BF),
-            shape((rows, chosen), BF),
+            shape((rows, 2 * chosen + query_width), BF),
             shape((rows, hidden_width), F32),
         ],
-        [ranks, *mp_gather(cotangent), down_weight],
+        [RANKS, cotangent, cot_chip, cot_core, xor(cot_chip, "mp", 1), down_weight,
+         act_attn_select, attn_b],
         name="cotangent",
         after=[kept],
     )
+    there = xor(packet, "ctx", 1)
     both = add(
-        kept, xor(kept, "mp", 2), BF, "resid_chip", kernel=flipped_add_kernel, after=[grad_hidden]
-    )
-    early_there = xor(early, "ctx", 1)
-    cot_there = xor(cot_select, "ctx", 1)
+        kept, xor(kept, "mp", 2), BF, "resid_chip", kernel=flipped_add_kernel,
+        after=[grad_hidden],
+    )
 
     resid, act_ffn, act_select, gate_pre, up_proj, hidden = launch(
         ffn_forward_kernel,
@@ -693,7 +778,7 @@
             shape((rows, hidden_width), F32),
             shape((rows, hidden_width), BF),
         ],
-        [ranks, *x, both, xor(both, "mp", 1), ffn_gain_row, gate_weight, up_weight],
+        [RANKS, *x, both, xor(both, "mp", 1), ffn_gain_row, gate_weight, up_weight],
         name="ffn_forward",
     )
     hidden_there = xor(hidden, "ctx", 1)
@@ -708,11 +793,12 @@
         [gate_pre, up_proj, grad_hidden, gate_weight, up_weight, act_select],
         name="ffn_backward",
     )
-    kept, gate_packet = add(kept, xor(sent, "mp", 1), BF, "grad_act_core", carry=[gate_packet])
+    kept, gate_packet = add(kept, xor(sent, "mp", 1), BF, "grad_act_core", after=[there],
+        carry=[gate_packet])
     gate_there = xor(gate_packet, "ctx", 1)
     both = add(kept, xor(kept, "mp", 2), BF, "grad_act_chip", kernel=flipped_add_kernel)
     down_kept, down_sent = weight_grad(
-        ranks, [(cot, cot_there, hidden, hidden_there, (0, 0), hidden_width)], "down_grad",
+        [(cot, there, hidden, hidden_there, (0, 0), 0, hidden_width)], "down_grad",
         after=[both],
     )
 
@@ -725,56 +811,48 @@
             shape((1, width), F32),
             shape((rows, query_width), F32),
         ]
-        + [shape((rows, 2 * key_width), BF if d else F32) for d in range(count)],
-        [ranks, cot, resid, both, xor(both, "mp", 1), ffn_gain_row, out_weight, attn_rows,
+        + [shape((rows, 2 * key_width), BF if d else F32) for d in range(slots)]
+        + [shape((slots * rows, 2 * key_width), BF)],
+        [RANKS, cot, resid, both, xor(both, "mp", 1), ffn_gain_row, out_weight, attn_rows,
          log_sums, query_rot, position_row, *blocks],
         name="attention_backward",
         after=[down_sent],
     )
     grad_resid, grad_resid_b, grad_select, ffn_gain_part, grad_query = outs[:5]
-    terms = outs[5:]
-
-    arrived = [xor(terms[2 * j + 1], "ctx", 1) for j in range(slots)]
+    terms, odd_terms = outs[5:-1], outs[-1]
+
+    arrived = xor(odd_terms, "ctx", 1)
     gate_kept, gate_sent = weight_grad(
-        ranks,
-        [(act_ffn, gate_there, gate_packet, gate_there, (chosen, chosen), hidden_width)],
+        [(act_ffn, gate_there, gate_packet, gate_there, (chosen, chosen), 0, hidden_width)],
         "gate_grad",
         after=[grad_query],
     )
-    down_kept, down_arrived, back = halve(
-        down_kept, xor(down_sent, "ctx", 2), "down_fold", after=[gate_sent]
-    )
-    shifted = []
+    totals = launch(
+        functools.partial(pair_sum_kernel, slots),
+        [shape(terms[0].shape, BF if k else F32) for k in range(slots + 1)],
+        [RANKS, *terms, arrived],
+        name="pair_sums",
+        after=[gate_sent],
+        carry=[grad_up],
+    )
+    grad_up = totals[-1]
+    up_there = xor(grad_up, "ctx", 1)
+    shifted = [down(totals[k], 2 * k) for k in range(slots - 1, 0, -1)]
     if 2 * slots < n_ctx:
         pairs = [(i, i - 2 * slots) for i in range(2 * slots, n_ctx) if i % 2 == 1]
-        shifted.append(lax.ppermute(arrived[slots - 1], "ctx", pairs))
-    for k in range(slots - 1, 0, -1):
-        carried = [grad_up] if k == 1 else []
-        total = launch(
-            pair_sum_kernel,
-            [shape(terms[0].shape, BF)],
-            [ranks, terms[2 * k], arrived[k - 1], arrived[k]],
-            name="pair_sum",
-            after=[back],
-            carry=carried,
-        )
-        if carried:
-            grad_up = total[1]
-        shifted.append(down(total[0], 2 * k))
-    up_there = xor(grad_up, "ctx", 1)
-
-    late, query_gain_part, query_partial = launch(
+        shifted.append(lax.ppermute(totals[slots], "ctx", pairs))
+
+    grad_query_b, query_gain_part, query_partial = launch(
         query_backward_kernel,
         [
-            shape((rows, chosen + query_width), BF),
+            shape((rows, query_width), BF),
             shape((1, query_width), F32),
             shape((rows, width), F32),
         ],
-        [queries, query_gain_row, grad_query, cos, sin, query_weight, grad_select],
+        [queries, query_gain_row, grad_query, cos, sin, query_weight],
         name="query_backward",
-        after=[grad_up],
-    )
-    late_there = xor(late, "ctx", 1)
+        after=[totals[0]],
+    )
     out_kept, out_sent = launch(
         down_kernel,
         [shape((half, width), F32), shape((half, width), BF)],
@@ -782,83 +860,99 @@
         name="down",
         after=[query_partial],
     )
+    (down_kept, gate_kept), first_arrived, back = fold(
+        [(down_kept, xor(down_sent, "ctx", 2)), (gate_kept, xor(gate_sent, "ctx", 2))],
+        "first_fold",
+        after=[out_sent],
+    )
     up_kept, up_sent = weight_grad(
-        ranks, [(act_ffn, gate_there, grad_up, up_there, (0, 0), hidden_width)], "up_grad",
-        after=[out_sent],
-    )
-    pair_b, gains, kept, sent = launch(
+        [(act_ffn, gate_there, grad_up, up_there, (0, 0), 0, hidden_width)], "up_grad",
+        after=[back],
+    )
+    late, gains, kept, sent = launch(
         key_backward_kernel,
         [
-            shape((rows, 2 * key_width), BF),
+            shape((rows, chosen + query_width + 2 * key_width), BF),
             shape((2 * width // 128 + 2, 128), F32),
             shape((half, width), F32),
-            shape((half, width), BF),
+            shape((rows + 16, width), BF),
         ],
-        [ranks, keys_pre, key_gain_row, cos, sin, key_weight, value_weight, query_partial, *x,
-         ffn_gain_part, query_gain_part, terms[0], arrived[0], *shifted],
+        [keys_pre, key_gain_row, cos, sin, key_weight, value_weight, query_partial, *x,
+         ffn_gain_part, query_gain_part, out_sent, grad_select, grad_query_b, totals[0],
+         *shifted],
         name="key_backward",
         after=[up_sent],
     )
-    pair_there = xor(pair_b, "ctx", 1)
-    gate_kept, gate_arrived, back = halve(
-        gate_kept, xor(gate_sent, "ctx", 2), "gate_fold", after=[kept]
-    )
-    gains = add(gains, xor(gains, "mp", 1), F32, "gains", after=[back])
-    kept, across = mp_reduce_start(kept, sent, "grad_input_core", after=[gains])
-    gains = add(gains, xor(gains, "mp", 2), F32, "gains", after=[kept])
+    late_there = xor(late, "ctx", 1)
+    core_arrived = xor(sent, "mp", 1)
+    query_at = chosen
+    pair_at = chosen + query_width
+    input_kept, out_kept, gains, back = launch(
+        mp_fold_kernel,
+        [
+            shape((own_rows, width), F32),
+            shape((own_rows, width), F32),
+            shape(gains.shape, F32),
+            shape((half + 16, width), BF),
+        ],
+        [kept, out_kept, gains, core_arrived],
+        name="mp_fold",
+    )
     attn_kept, attn_sent = weight_grad(
-        ranks,
         [
-            (grad_resid_b, late_there, early, early_there, (chosen, chosen), query_width),
-            (act_attn, early_there, late, late_there, (chosen, chosen), query_width),
-            (act_attn, early_there, pair_b, pair_there, (0, 0), 2 * key_width),
+            (grad_resid_b, late_there, attn_b, there, (0, 2 * chosen), 0, query_width),
+            (act_attn, there, late, late_there, (query_at, query_at), chosen, query_width),
+            (act_attn, there, late, late_there, (pair_at, pair_at), chosen, 2 * key_width),
         ],
         "attention_grads",
-        after=[gains],
-    )
-    gains = add(gains, xor(gains, "ctx", 1), F32, "gains", after=[attn_sent])
-    up_kept, up_arrived, back = halve(
-        up_kept, xor(up_sent, "ctx", 2), "up_fold", after=[gains]
-    )
-    out_kept, out_across = mp_reduce_start(out_kept, out_sent, "block_out_core", after=[back])
-    grad_input = launch(
-        grad_input_kernel,
-        [shape((own_rows, width), F32)],
-        [x[0], attn_gain_row, grad_resid, kept, across],
-        name="grad_input",
-        after=[out_kept],
-    )[0]
-    block_out = launch(
-        block_out_kernel,
-        [shape((own_rows, width), BF)],
-        [resid, out_kept, out_across],
-        name="block_out",
-        after=[grad_input],
-    )[0]
-
-    def finish(kept, arrived, name, after, kernel=add_kernel, turned=False):
-        dims = kept.shape[::-1] if turned else kept.shape
-        return launch(kernel, [shape(dims, F32)], [kept, arrived], name=name, after=after)[0]
-
-    down_grad = finish(
-        down_kept, down_arrived, "down_last", [block_out], turned_add_kernel, True
-    )
-    gate_grad = finish(gate_kept, gate_arrived, "gate_last", [down_grad])
-    attn_kept, attn_arrived, back = halve(
-        attn_kept, xor(attn_sent, "ctx", 2), "attention_fold", after=[gate_grad]
+        after=[back],
+    )
+    grad_input, block_out, gains = launch(
+        outputs_kernel,
+        [
+            shape((own_rows, width), F32),
+            shape((own_rows, width), BF),
+            shape(gains.shape, F32),
+        ],
+        [x[0], attn_gain_row, grad_resid, resid, input_kept, out_kept, gains,
+         xor(back, "mp", 2)],
+        name="outputs",
+        after=[attn_sent],
+    )
+    gains = add(gains, xor(gains, "ctx", 1), F32, "gains")
+    (up_kept,), up_arrived, back = fold(
+        [(up_kept, xor(up_sent, "ctx", 2))], "up_fold", after=[gains]
+    )
+    token = shape((8, 128), F32)
+    down_grad, gate_grad, done = launch(
+        functools.partial(last_kernel, (True, False)),
+        [shape(down_kept.shape[::-1], F32), shape(gate_kept.shape, F32), token],
+        [down_kept, gate_kept, first_arrived],
+        name="first_last",
+        after=[back],
+    )
+    (attn_kept,), attn_arrived, back = fold(
+        [(attn_kept, xor(attn_sent, "ctx", 2))], "attention_fold", after=[done]
     )
     mask = 2
-    while mask < n_ctx:
+    while mask < n_ctx // 2:
         gains = add(gains, xor(gains, "ctx", mask), F32, "gains", after=[back])
         mask *= 2
-    up_grad = finish(up_kept, up_arrived, "up_last", [gains])
+    up_grad, done = launch(
+        functools.partial(last_kernel, (False,)),
+        [shape(up_kept.shape, F32), token],
+        [up_kept, up_arrived],
+        name="up_last",
+        after=[gains],
+    )
+    gains = add(gains, xor(gains, "ctx", mask), F32, "gains", after=[done])
     out_grad, query_grad, key_grad, value_grad = launch(
         attention_last_kernel,
         [shape((query_width, attn_kept.shape[0]), F32)]
         + [shape((attn_kept.shape[0], w), F32) for w in (query_width, key_width, key_width)],
         [attn_kept, attn_arrived],
         name="attention_last",
-        after=[up_grad],
+        after=[gains],
     )
     gains = gains.reshape(-1)
     heads = gains[2 * width :].reshape(2, -1, HD).sum(axis=1)

time: 215 us -> 183 us (0.85)
  waiting for transfers between devices: 98.9 us -> 87.8 us
  local copies, waits for them, and re-layouts: 12.8 us -> 4.91 us
  Pallas kernels: 36 us -> 29.8 us
  starting transfers between devices: 64.9 us -> 59.2 us
    pallas_call x36 -> x28, Pallas kernels: 36 us -> 26.5 us  [launch(): pl.pallas_call(run, out_shape=list(outs) + [shape(c.shape, c.dtype) for c...]
    unnamed x52 -> x36, local copies, waits for them, and re-layouts: 11.6 us -> 3.71 us
    ppermute x39 -> x30, waiting for transfers between devices: 92.8 us -> 85.2 us  [xor(): return lax.ppermute(values, axis, [(i, i ^ mask) for i in range(n)])]
    ppermute x39 -> x30, starting transfers between devices: 38.7 us -> 34.6 us  [xor(): return lax.ppermute(values, axis, [(i, i ^ mask) for i in range(n)])]
    ppermute x6 -> x5, waiting for transfers between devices: 6.04 us -> 2.65 us  [cross(): lax.ppermute(values, 'ctx', [(i, i ^ 1) for i in range(odd, n_ctx, 2)])]
    pallas_call x0 -> x1, Pallas kernels: none -> 3.31 us  [body(): pl.pallas_call(qkv_kernel, out_shape=outs, in_specs=[pl.BlockSpec(memory_...]
    ppermute x6 -> x5, starting transfers between devices: 14 us -> 12.7 us  [cross(): lax.ppermute(values, 'ctx', [(i, i ^ 1) for i in range(odd, n_ctx, 2)])]
  transfers between devices with their start and end apart: 51 -> 41, of which waited for: 27 -> 20; matrix products, arithmetic and copies ran while one was open for 1% -> 1% of each run, Pallas kernels for 12% -> 14%
where the time goes in v3:
time: 183 us
  waiting for transfers between devices  87.8 us (48%)
  starting transfers between devices  59.2 us (32%)
  Pallas kernels  29.8 us (16%)
  local copies, waits for them, and re-layouts  4.91 us (3%)
    ppermute x30, waiting for transfers between devices, xor(): return lax.ppermute(values, axis, [(i, i ^ mask) for i in range(n)])  85.2 us
    ppermute x30, starting transfers between devices, xor(): return lax.ppermute(values, axis, [(i, i ^ mask) for i in range(n)])  34.6 us
    pallas_call x28, Pallas kernels, launch(): pl.pallas_call(run, out_shape=list(outs) + [shape(c.shape, c.dtype) for c...  26.5 us
    ppermute x5, starting transfers between devices, cross(): lax.ppermute(values, 'ctx', [(i, i ^ 1) for i in range(odd, n_ctx, 2)])  12.7 us
    ppermute x3, starting transfers between devices, climb(): return lax.ppermute(pair, 'ctx', pairs) if pairs else jnp.zeros_like(pair)  8.65 us
    unnamed x36, local copies, waits for them, and re-layouts  3.71 us
  transfers between devices with their start and end apart: 41, of which 20 were waited for; matrix products, arithmetic and copies ran while one was open for 1% of the time, Pallas kernels for 14%

profile of v3, /device:TPU:0, one launch (start us, length us, event | category | flops | bytes accessed | tf_op | source)
XLA Modules:
  0.0 182.9 jit_solution(11390943135864526458)
XLA Ops:
  0.7 3.0 %collective-permute-start.3 = (bf16[64,1024]{1,0:T(8,128)(2,1)}, bf16[64,1024]{1,0:T(8,128)(2,1)S(1)}, u32[]{:S(2)}, u32[]{:S(2)}) collective-permute-start(bf16[64,1024]{1,0:T(8,128)(2,1)} %refs_0_.5), channel_id=1, source_target_pairs={{0,2},{1,3},{2,0},{3,1},{4,6},{5,7},{6,4},{7,5},{8,10},{9,11},{10,... | collective-permute-start | bytes 393224 | tf_op jit(solution)/shard_map/ppermute | solution.py:32
  3.7 3.7 %collective-permute-done.3.x1.refs_1_.refs_8_ = bf16[64,1024]{1,0:T(8,128)(2,1)S(1)} collective-permute-done((bf16[64,1024]{1,0:T(8,128)(2,1)}, bf16[64,1024]{1,0:T(8,128)(2,1)S(1)}, u32[]{:S(2)}, u32[]{:S(2)}) %collective-permute-start.3) | collective-permute-done | bytes 131104 | tf_op jit(solution)/shard_map/ppermute | solution.py:32
  7.4 1.7 collective-permute-start
  12.7 3.3 %qkv.1 = (bf16[256,1024]{1,0:T(8,128)(2,1)}, bf16[256,512]{1,0:T(8,128)(2,1)S(1)}, bf16[256,256]{1,0:T(8,128)(2,1)S(1)}, bf16[256,256]{1,0:T(8,128)(2,1)S(1)}, f...) custom-call(bf16[64,1024]{1,0:T(8,128)(2,1)S(1)} %collective-permute, ...), custom_call_target="tpu_custom_call" | custom-call | tf_op jit(solution)/shard_map/qkv/pallas_call | solution.py:705
  16.0 4.5 %collective-permute-start.7 = (bf16[256,256]{1,0:T(8,128)(2,1)S(1)}, bf16[256,256]{1,0:T(8,128)(2,1)S(1)}, u32[]{:S(2)}, u32[]{:S(2)}) collective-permute-start(bf16[256,256]{1,0:T(8,128)(2,1)S(1)} %get-tuple-element.103.refs_3_.refs_10_), channel_id=1, source_target_pairs={{0,16},{4,20},{8,24},{12,28},{1,17},{5,21},{9,25},{13,29},{2,18},{... | collective-permute-start | bytes 393224 | tf_op jit(solution)/shard_map/ppermute | solution.py:722
  20.6 3.5 %collective-permute-start.6 = (bf16[256,256]{1,0:T(8,128)(2,1)S(1)}, bf16[256,256]{1,0:T(8,128)(2,1)S(1)}, u32[]{:S(2)}, u32[]{:S(2)}) collective-permute-start(bf16[256,256]{1,0:T(8,128)(2,1)S(1)} %get-tuple-element.103.refs_3_.refs_10_), channel_id=1, source_target_pairs={{0,8},{4,12},{8,16},{12,20},{16,24},{20,28},{1,9},{5,13},{9,17},{1... | collective-permute-start | bytes 393224 | tf_op jit(solution)/shard_map/ppermute | solution.py:722
  24.8 4.1 %collective-permute-start.8 = (bf16[256,256]{1,0:T(8,128)(2,1)S(1)}, bf16[256,256]{1,0:T(8,128)(2,1)S(1)}, u32[]{:S(2)}, u32[]{:S(2)}) collective-permute-start(bf16[256,256]{1,0:T(8,128)(2,1)S(1)} %get-tuple-element.103.refs_3_.refs_10_), channel_id=1, source_target_pairs={{0,4},{8,12},{16,20},{24,28},{1,5},{9,13},{17,21},{25,29},{2,6},{1... | collective-permute-start | bytes 393224 | tf_op jit(solution)/shard_map/ppermute | solution.py:718
  28.9 1.3 collective-permute-start.10
  30.2 1.3 collective-permute-start.12
  31.5 1.3 collective-permute-start.11
  32.8 4.7 %collective-permute-start.9 = (bf16[256,256]{1,0:T(8,128)(2,1)S(1)}, bf16[256,256]{1,0:T(8,128)(2,1)S(1)}, u32[]{:S(2)}, u32[]{:S(2)}) collective-permute-start(bf16[256,256]{1,0:T(8,128)(2,1)S(1)} %collective-permute-done.6.refs_4_.refs_12_), channel_id=1, source_target_pairs={{0,4},{8,12},{16,20},{24,28},{1,5},{9,13},{17,21},{25,29},{2,6},{1... | collective-permute-start | bytes 393224 | tf_op jit(solution)/shard_map/ppermute | solution.py:718
  37.6 2.6 %collective-permute-done.11.refs_9_ = bf16[256,256]{1,0:T(8,128)(2,1)S(1)} collective-permute-done((bf16[256,256]{1,0:T(8,128)(2,1)S(1)}, bf16[256,256]{1,0:T(8,128)(2,1)S(1)}, u32[]{:S(2)}, u32[]{:S(2)}) %collective-permute-start.11) | collective-permute-done | bytes 131104 | tf_op jit(solution)/shard_map/ppermute | solution.py:718
  40.2 3.4 %attention.1 = (f32[256,256]{1,0:T(8,128)S(1)}, bf16[256,256]{1,0:T(8,128)(2,1)S(1)}, f32[2,512]{1,0:T(2,128)S(1)}, f32[128,1024]{1,0:T(8,128)S(1)}, bf16[128,10...) custom-call(bf16[256,256]{1,0:T(8,128)(2,1)S(1)} %get-tuple-element., ...), custom_call_target="tpu_custom_call" | custom-call | tf_op jit(solution)/shard_map/attention/pallas_call | solution.py:561
  43.7 1.5 collective-permute-done.14.refs_1_
  45.3 1.4 collective-permute-start.15
  46.7 1.3 collective-permute-done.2.refs_3_
  49.0 2.2 %collective-permute-start.18 = (bf16[256,1280]{1,0:T(8,128)(2,1)S(1)}, bf16[256,1280]{1,0:T(8,128)(2,1)S(1)}, u32[]{:S(2)}, u32[]{:S(2)}) collective-permute-start(bf16[256,1280]{1,0:T(8,128)(2,1)S(1)} %get-tuple-element.115), channel_id=1, source_target_pairs={{0,4},{4,0},{8,12},{12,8},{16,20},{20,16},{24,28},{28,24},{1,5},{5... | collective-permute-start | bytes 1966088 | tf_op jit(solution)/shard_map/ppermute | solution.py:32
  51.2 2.5 %collective-permute-done.15.refs_1_ = bf16[128,1024]{1,0:T(8,128)(2,1)S(1)} collective-permute-done((bf16[128,1024]{1,0:T(8,128)(2,1)S(1)}, bf16[128,1024]{1,0:T(8,128)(2,1)S(1)}, u32[]{:S(2)}, u32[]{:S(2)}) %collective-permute-start.15) | collective-permute-done | bytes 262176 | tf_op jit(solution)/shard_map/ppermute | solution.py:32
  53.8 1.5 collective-permute-done.16.refs_5_
  55.4 1.9 %ffn_forward.1 = (f32[256,1024]{1,0:T(8,128)S(1)}, bf16[256,1024]{1,0:T(8,128)(2,1)S(1)}, bf16[256,512]{1,0:T(8,128)(2,1)S(1)}, f32[256,1152]{1,0:T(8,128)S(1)},...) custom-call(bf16[64,1024]{1,0:T(8,128)(2,1)S(1)} %copy-done.6, ...), custom_call_target="tpu_custom_call" | custom-call | tf_op jit(solution)/shard_map/ffn_forward/pallas_call | solution.py:561
  57.3 3.2 %ffn_backward.1 = (bf16[256,1664]{1,0:T(8,128)(2,1)S(1)}, bf16[256,1152]{1,0:T(8,128)(2,1)S(1)}, f32[128,1024]{1,0:T(8,128)S(1)}, bf16[128,1024]{1,0:T(8,128)(2,1)S(1)}) custom-call(f32[256,1152]{1,0:T(8,128)S(1)} %get-tuple-element.110.refs_0_, f32[256,1152]{1,0:T(8,128)S(1)} %get-tuple-element.111.refs_1_, f32[256,1152]{1,0:T(8,128)S(1)} %get-tuple-element.108.refs_2_, ...), custom_call_target="tpu_custom_call" | custom-call | tf_op jit(solution)/shard_map/ffn_backward/pallas_call | solution.py:561
  60.6 2.2 %collective-permute-start.21 = (bf16[256,1152]{1,0:T(8,128)(2,1)S(1)}, bf16[256,1152]{1,0:T(8,128)(2,1)S(1)}, u32[]{:S(2)}, u32[]{:S(2)}) collective-permute-start(bf16[256,1152]{1,0:T(8,128)(2,1)S(1)} %get-tuple-element.124.refs_2_.refs_0_), channel_id=1, source_target_pairs={{0,4},{4,0},{8,12},{12,8},{16,20},{20,16},{24,28},{28,24},{1,5},{5... | collective-permute-start | bytes 1769480 | tf_op jit(solution)/shard_map/ppermute | solution.py:32
  62.8 3.9 %collective-permute-done.18.refs_2_.refs_1_.refs_3_.refs_5_.refs_9_ = bf16[256,1280]{1,0:T(8,128)(2,1)S(1)} collective-permute-done((bf16[256,1280]{1,0:T(8,128)(2,1)S(1)}, bf16[256,1280]{1,0:T(8,128)(2,1)S(1)}, u32[]{:S(2)}, u32[]{:S(2)}) %collective-permute-start.18) | collective-permute-done | bytes 655392 | tf_op jit(solution)/shard_map/ppermute | solution.py:32
  67.5 2.1 %collective-permute-start.23 = (bf16[256,1664]{1,0:T(8,128)(2,1)S(1)}, bf16[256,1664]{1,0:T(8,128)(2,1)S(1)}, u32[]{:S(2)}, u32[]{:S(2)}) collective-permute-start(bf16[256,1664]{1,0:T(8,128)(2,1)S(1)} %get-tuple-element.137.refs_2_), channel_id=1, source_target_pairs={{0,4},{4,0},{8,12},{12,8},{16,20},{20,16},{24,28},{28,24},{1,5},{5... | collective-permute-start | bytes 2555912 | tf_op jit(solution)/shard_map/ppermute | solution.py:32
  69.6 4.6 %collective-permute-done.19.refs_1_ = bf16[128,1024]{1,0:T(8,128)(2,1)S(1)} collective-permute-done((bf16[128,1024]{1,0:T(8,128)(2,1)S(1)}, bf16[128,1024]{1,0:T(8,128)(2,1)S(1)}, u32[]{:S(2)}, u32[]{:S(2)}) %collective-permute-start.19) | collective-permute-done | bytes 262176 | tf_op jit(solution)/shard_map/ppermute | solution.py:32
  74.4 5.0 %collective-permute-done.21.refs_3_ = bf16[256,1152]{1,0:T(8,128)(2,1)S(1)} collective-permute-done((bf16[256,1152]{1,0:T(8,128)(2,1)S(1)}, bf16[256,1152]{1,0:T(8,128)(2,1)S(1)}, u32[]{:S(2)}, u32[]{:S(2)}) %collective-permute-start.21) | collective-permute-done | bytes 589856 | tf_op jit(solution)/shard_map/ppermute | solution.py:32
  80.3 6.5 %attention_backward.1 = (f32[64,1024]{1,0:T(8,128)S(1)}, bf16[256,1024]{1,0:T(8,128)(2,1)S(1)}, bf16[256,512]{1,0:T(8,128)(2,1)S(1)}, f32[1,1024]{1,0:T(1,128)S(...) custom-call(bf16[256,1024]{1,0:T(8,128)(2,1)S(1)} %get-tuple-element, ...), custom_call_target="tpu_custom_call" | custom-call | tf_op jit(solution)/shard_map/attention_backward/pallas_call | solution.py:561
  86.8 2.1 %collective-permute-start.22 = (bf16[768,256]{1,0:T(8,128)(2,1)S(1)}, bf16[768,256]{1,0:T(8,128)(2,1)S(1)}, u32[]{:S(2)}, u32[]{:S(2)}) collective-permute-start(bf16[768,256]{1,0:T(8,128)(2,1)S(1)} %get-tuple-element.135), channel_id=1, source_target_pairs={{0,4},{4,0},{8,12},{12,8},{16,20},{20,16},{24,28},{28,24},{1,5},{5... | collective-permute-start | bytes 1179656 | tf_op jit(solution)/shard_map/ppermute | solution.py:32
  89.0 1.3 collective-permute-start.28
  90.2 7.4 %collective-permute-done.23.refs_1_.refs_3_ = bf16[256,1664]{1,0:T(8,128)(2,1)S(1)} collective-permute-done((bf16[256,1664]{1,0:T(8,128)(2,1)S(1)}, bf16[256,1664]{1,0:T(8,128)(2,1)S(1)}, u32[]{:S(2)}, u32[]{:S(2)}) %collective-permute-start.23) | collective-permute-done | bytes 852000 | tf_op jit(solution)/shard_map/ppermute | solution.py:32
  98.6 1.3 collective-permute-start.29
  99.9 5.7 %collective-permute-done.22.refs_3_ = bf16[768,256]{1,0:T(8,128)(2,1)S(1)} collective-permute-done((bf16[768,256]{1,0:T(8,128)(2,1)S(1)}, bf16[768,256]{1,0:T(8,128)(2,1)S(1)}, u32[]{:S(2)}, u32[]{:S(2)}) %collective-permute-start.22) | collective-permute-done | bytes 393248 | tf_op jit(solution)/shard_map/ppermute | solution.py:32
  105.7 1.8 collective-permute-start.27
  107.5 1.3 collective-permute-start.24
  108.8 1.3 collective-permute-start.25
  112.4 6.9 %collective-permute-done.29.refs_3_ = bf16[256,1152]{1,0:T(8,128)(2,1)S(1)} collective-permute-done((bf16[256,1152]{1,0:T(8,128)(2,1)S(1)}, bf16[256,1152]{1,0:T(8,128)(2,1)S(1)}, u32[]{:S(2)}, u32[]{:S(2)}) %collective-permute-start.29) | collective-permute-done | bytes 589856 | tf_op jit(solution)/shard_map/ppermute | solution.py:32
  122.6 5.1 %collective-permute-start.32 = (bf16[256,1024]{1,0:T(8,128)(2,1)S(1)}, bf16[256,1024]{1,0:T(8,128)(2,1)S(1)}, u32[]{:S(2)}, u32[]{:S(2)}) collective-permute-start(bf16[256,1024]{1,0:T(8,128)(2,1)S(1)} %get-tuple-element.164.refs_6_.refs_10_), channel_id=1, source_target_pairs={{0,4},{4,0},{8,12},{12,8},{16,20},{20,16},{24,28},{28,24},{1,5},{5... | collective-permute-start | bytes 1572872 | tf_op jit(solution)/shard_map/ppermute | solution.py:32
  129.6 10.7 %collective-permute-done.32.refs_1_.refs_7_.refs_11_ = bf16[256,1024]{1,0:T(8,128)(2,1)S(1)} collective-permute-done((bf16[256,1024]{1,0:T(8,128)(2,1)S(1)}, bf16[256,1024]{1,0:T(8,128)(2,1)S(1)}, u32[]{:S(2)}, u32[]{:S(2)}) %collective-permute-start.32) | collective-permute-done | bytes 524320 | tf_op jit(solution)/shard_map/ppermute | solution.py:32
  142.0 1.8 collective-permute-start.36
  143.8 1.9 %collective-permute-done.36.refs_1_ = f32[18,128]{1,0:T(8,128)S(1)} collective-permute-done((f32[18,128]{1,0:T(8,128)S(1)}, f32[18,128]{1,0:T(8,128)S(1)}, u32[]{:S(2)}, u32[]{:S(2)}) %collective-permute-start.36) | collective-permute-done | bytes 9248 | tf_op jit(solution)/shard_map/ppermute | solution.py:32
  145.7 8.3 %collective-permute-done.35.refs_1_ = bf16[256,1152]{1,0:T(8,128)(2,1)S(1)} collective-permute-done((bf16[256,1152]{1,0:T(8,128)(2,1)S(1)}, bf16[256,1152]{1,0:T(8,128)(2,1)S(1)}, u32[]{:S(2)}, u32[]{:S(2)}) %collective-permute-start.35) | collective-permute-done | bytes 589856 | tf_op jit(solution)/shard_map/ppermute | solution.py:32
  154.2 2.5 %collective-permute-start.38 = (f32[18,128]{1,0:T(8,128)S(1)}, f32[18,128]{1,0:T(8,128)S(1)}, u32[]{:S(2)}, u32[]{:S(2)}) collective-permute-start(f32[18,128]{1,0:T(8,128)S(1)} %gains.3.refs_2_.refs_0_), channel_id=1, source_target_pairs={{0,8},{4,12},{8,0},{12,4},{16,24},{20,28},{24,16},{28,20},{1,9},{5... | collective-permute-start | bytes 27656 | tf_op jit(solution)/shard_map/ppermute | solution.py:32
  156.6 2.0 %collective-permute-done.34.refs_2_ = bf16[128,2304]{1,0:T(8,128)(2,1)S(1)} collective-permute-done((bf16[128,2304]{1,0:T(8,128)(2,1)S(1)}, bf16[128,2304]{1,0:T(8,128)(2,1)S(1)}, u32[]{:S(2)}, u32[]{:S(2)}) %collective-permute-start.34) | collective-permute-done | bytes 589856 | tf_op jit(solution)/shard_map/ppermute | solution.py:32
  158.6 1.3 first_last.1
  159.9 10.8 %collective-permute-done.33.refs_1_ = bf16[256,768]{1,0:T(8,128)(2,1)S(1)} collective-permute-done((bf16[256,768]{1,0:T(8,128)(2,1)S(1)}, bf16[256,768]{1,0:T(8,128)(2,1)S(1)}, u32[]{:S(2)}, u32[]{:S(2)}) %collective-permute-start.33) | collective-permute-done | bytes 393248 | tf_op jit(solution)/shard_map/ppermute | solution.py:32
  170.9 2.9 %collective-permute-start.37 = (bf16[128,768]{1,0:T(8,128)(2,1)S(1)}, bf16[128,768]{1,0:T(8,128)(2,1)S(1)}, u32[]{:S(2)}, u32[]{:S(2)}) collective-permute-start(bf16[128,768]{1,0:T(8,128)(2,1)S(1)} %get-tuple-element.177.refs_2_), channel_id=1, source_target_pairs={{0,16},{4,20},{8,24},{12,28},{16,0},{20,4},{24,8},{28,12},{1,17},{... | collective-permute-start | bytes 589832 | tf_op jit(solution)/shard_map/ppermute | solution.py:32
  174.6 3.6 %collective-permute-done.39.refs_1_ = f32[18,128]{1,0:T(8,128)S(1)} collective-permute-done((f32[18,128]{1,0:T(8,128)S(1)}, f32[18,128]{1,0:T(8,128)S(1)}, u32[]{:S(2)}, u32[]{:S(2)}) %collective-permute-start.39) | collective-permute-done | bytes 9248 | tf_op jit(solution)/shard_map/ppermute | solution.py:32
  179.5 2.7 %collective-permute-done.37.refs_1_ = bf16[128,768]{1,0:T(8,128)(2,1)S(1)} collective-permute-done((bf16[128,768]{1,0:T(8,128)(2,1)S(1)}, bf16[128,768]{1,0:T(8,128)(2,1)S(1)}, u32[]{:S(2)}, u32[]{:S(2)}) %collective-permute-start.37) | collective-permute-done | bytes 196640 | tf_op jit(solution)/shard_map/ppermute | solution.py:32
  (104 shorter events, 21.1 us)
Async XLA Ops:
  0.6 39.6 %copy-start.3 = (bf16[256,1024]{1,0:T(8,128)(2,1)S(1)}, bf16[256,1024]{1,0:T(8,128)(2,1)}, u32[]{:S(2)}) copy-start(bf16[256,1024]{1,0:T(8,128)(2,1)} %refs_5_.3) | copy-start | bytes 1572868
  0.7 6.7 %collective-permute-start.3 = (bf16[64,1024]{1,0:T(8,128)(2,1)}, bf16[64,1024]{1,0:T(8,128)(2,1)S(1)}, u32[]{:S(2)}, u32[]{:S(2)}) collective-permute-start(bf16[64,1024]{1,0:T(8,128)(2,1)} %refs_0_.5), channel_id=1, source_target_pairs={{0,2},{1,3},{2,0},{3,1},{4,6},{5,7},{6,4},{7,5},{8,10},{9,11},{10,... | collective-permute-start | bytes 393224 | tf_op jit(solution)/shard_map/ppermute | solution.py:32
  3.7 5.5 %collective-permute-start.4 = (bf16[64,1024]{1,0:T(8,128)(2,1)}, bf16[64,1024]{1,0:T(8,128)(2,1)S(1)}, u32[]{:S(2)}, u32[]{:S(2)}) collective-permute-start(bf16[64,1024]{1,0:T(8,128)(2,1)} %refs_0_.5), channel_id=1, source_target_pairs={{0,1},{1,0},{2,3},{3,2},{4,5},{5,4},{6,7},{7,6},{8,9},{9,8},{10,11... | collective-permute-start | bytes 393224 | tf_op jit(solution)/shard_map/ppermute | solution.py:32
  7.4 1.8 collective-permute-start.5
  7.4 17.4 %collective-permute-start = (bf16[64,1024]{1,0:T(8,128)(2,1)}, bf16[64,1024]{1,0:T(8,128)(2,1)S(1)}, u32[]{:S(2)}, u32[]{:S(2)}) collective-permute-start(bf16[64,1024]{1,0:T(8,128)(2,1)} %refs_0_.3), channel_id=1, source_target_pairs={{0,2},{1,3},{2,0},{3,1},{4,6},{5,7},{6,4},{7,5},{8,10},{9,11},{10,... | collective-permute-start | bytes 393224 | tf_op jit(solution)/shard_map/ppermute | solution.py:32
  12.7 7.8 %copy-start.9 = (bf16[64,1024]{1,0:T(8,128)(2,1)S(1)}, bf16[64,1024]{1,0:T(8,128)(2,1)}, u32[]{:S(2)}) copy-start(bf16[64,1024]{1,0:T(8,128)(2,1)} %refs_0_.3) | copy-start | bytes 393220
  16.0 12.8 %collective-permute-start.7 = (bf16[256,256]{1,0:T(8,128)(2,1)S(1)}, bf16[256,256]{1,0:T(8,128)(2,1)S(1)}, u32[]{:S(2)}, u32[]{:S(2)}) collective-permute-start(bf16[256,256]{1,0:T(8,128)(2,1)S(1)} %get-tuple-element.103.refs_3_.refs_10_), channel_id=1, source_target_pairs={{0,16},{4,20},{8,24},{12,28},{1,17},{5,21},{9,25},{13,29},{2,18},{... | collective-permute-start | bytes 393224 | tf_op jit(solution)/shard_map/ppermute | solution.py:722
  20.5 9.6 %collective-permute-start.1 = (bf16[64,1024]{1,0:T(8,128)(2,1)S(1)}, bf16[64,1024]{1,0:T(8,128)(2,1)S(1)}, u32[]{:S(2)}, u32[]{:S(2)}) collective-permute-start(bf16[64,1024]{1,0:T(8,128)(2,1)S(1)} %copy-done.9), channel_id=1, source_target_pairs={{0,1},{1,0},{2,3},{3,2},{4,5},{5,4},{6,7},{7,6},{8,9},{9,8},{10,11... | collective-permute-start | bytes 393224 | tf_op jit(solution)/shard_map/ppermute | solution.py:32
  20.6 10.9 %collective-permute-start.6 = (bf16[256,256]{1,0:T(8,128)(2,1)S(1)}, bf16[256,256]{1,0:T(8,128)(2,1)S(1)}, u32[]{:S(2)}, u32[]{:S(2)}) collective-permute-start(bf16[256,256]{1,0:T(8,128)(2,1)S(1)} %get-tuple-element.103.refs_3_.refs_10_), channel_id=1, source_target_pairs={{0,8},{4,12},{8,16},{12,20},{16,24},{20,28},{1,9},{5,13},{9,17},{1... | collective-permute-start | bytes 393224 | tf_op jit(solution)/shard_map/ppermute | solution.py:722
  24.1 8.7 %collective-permute-start.13 = (bf16[256,256]{1,0:T(8,128)(2,1)S(1)}, bf16[256,256]{1,0:T(8,128)(2,1)S(1)}, u32[]{:S(2)}, u32[]{:S(2)}) collective-permute-start(bf16[256,256]{1,0:T(8,128)(2,1)S(1)} %get-tuple-element.103.refs_3_.refs_10_), channel_id=1, source_target_pairs={{4,24},{5,25},{6,26},{7,27}} | collective-permute-start | bytes 393224 | tf_op jit(solution)/shard_map/ppermute | solution.py:722
  24.8 12.8 %collective-permute-start.8 = (bf16[256,256]{1,0:T(8,128)(2,1)S(1)}, bf16[256,256]{1,0:T(8,128)(2,1)S(1)}, u32[]{:S(2)}, u32[]{:S(2)}) collective-permute-start(bf16[256,256]{1,0:T(8,128)(2,1)S(1)} %get-tuple-element.103.refs_3_.refs_10_), channel_id=1, source_target_pairs={{0,4},{8,12},{16,20},{24,28},{1,5},{9,13},{17,21},{25,29},{2,6},{1... | collective-permute-start | bytes 393224 | tf_op jit(solution)/shard_map/ppermute | solution.py:718
  28.9 8.7 %collective-permute-start.10 = (bf16[256,256]{1,0:T(8,128)(2,1)S(1)}, bf16[256,256]{1,0:T(8,128)(2,1)S(1)}, u32[]{:S(2)}, u32[]{:S(2)}) collective-permute-start(bf16[256,256]{1,0:T(8,128)(2,1)S(1)} %collective-permute-done.7.refs_5_.refs_14_), channel_id=1, source_target_pairs={{0,4},{8,12},{16,20},{24,28},{1,5},{9,13},{17,21},{25,29},{2,6},{1... | collective-permute-start | bytes 393224 | tf_op jit(solution)/shard_map/ppermute | solution.py:718
  30.2 10.0 %collective-permute-start.12 = (bf16[256,256]{1,0:T(8,128)(2,1)S(1)}, bf16[256,256]{1,0:T(8,128)(2,1)S(1)}, u32[]{:S(2)}, u32[]{:S(2)}) collective-permute-start(bf16[256,256]{1,0:T(8,128)(2,1)S(1)} %collective-permute-done.7.refs_5_.refs_14_), channel_id=1, source_target_pairs={{4,0},{12,8},{20,16},{28,24},{5,1},{13,9},{21,17},{29,25},{6,2},{1... | collective-permute-start | bytes 393224 | tf_op jit(solution)/shard_map/ppermute | solution.py:718
  31.5 8.7 %collective-permute-start.11 = (bf16[256,256]{1,0:T(8,128)(2,1)S(1)}, bf16[256,256]{1,0:T(8,128)(2,1)S(1)}, u32[]{:S(2)}, u32[]{:S(2)}) collective-permute-start(bf16[256,256]{1,0:T(8,128)(2,1)S(1)} %collective-permute-done.6.refs_4_.refs_12_), channel_id=1, source_target_pairs={{4,0},{12,8},{20,16},{28,24},{5,1},{13,9},{21,17},{29,25},{6,2},{1... | collective-permute-start | bytes 393224 | tf_op jit(solution)/shard_map/ppermute | solution.py:718
  32.8 7.4 %collective-permute-start.9 = (bf16[256,256]{1,0:T(8,128)(2,1)S(1)}, bf16[256,256]{1,0:T(8,128)(2,1)S(1)}, u32[]{:S(2)}, u32[]{:S(2)}) collective-permute-start(bf16[256,256]{1,0:T(8,128)(2,1)S(1)} %collective-permute-done.6.refs_4_.refs_12_), channel_id=1, source_target_pairs={{0,4},{8,12},{16,20},{24,28},{1,5},{9,13},{17,21},{25,29},{2,6},{1... | collective-permute-start | bytes 393224 | tf_op jit(solution)/shard_map/ppermute | solution.py:718
  40.2 7.8 %copy-start = (bf16[1152,1024]{1,0:T(8,128)(2,1)S(1)}, bf16[1152,1024]{1,0:T(8,128)(2,1)}, u32[]{:S(2)}) copy-start(bf16[1152,1024]{1,0:T(8,128)(2,1)} %refs_1_.1) | copy-start | bytes 7077892
  43.6 1.6 collective-permute-start.14
  45.3 8.4 %collective-permute-start.15 = (bf16[128,1024]{1,0:T(8,128)(2,1)S(1)}, bf16[128,1024]{1,0:T(8,128)(2,1)S(1)}, u32[]{:S(2)}, u32[]{:S(2)}) collective-permute-start(bf16[128,1024]{1,0:T(8,128)(2,1)S(1)} %resid_core.1.refs_7_.refs_0_), channel_id=1, source_target_pairs={{0,2},{1,3},{2,0},{3,1},{4,6},{5,7},{6,4},{7,5},{8,10},{9,11},{10,... | collective-permute-start | bytes 786440 | tf_op jit(solution)/shard_map/ppermute | solution.py:32
  46.7 1.3 collective-permute-start.2
  48.0 7.3 %copy-start.2 = (bf16[1024,1152]{1,0:T(8,128)(2,1)S(1)}, bf16[1024,1152]{1,0:T(8,128)(2,1)}, u32[]{:S(2)}) copy-start(bf16[1024,1152]{1,0:T(8,128)(2,1)} %refs_4_.4) | copy-start | bytes 7077892
  49.0 17.7 %collective-permute-start.18 = (bf16[256,1280]{1,0:T(8,128)(2,1)S(1)}, bf16[256,1280]{1,0:T(8,128)(2,1)S(1)}, u32[]{:S(2)}, u32[]{:S(2)}) collective-permute-start(bf16[256,1280]{1,0:T(8,128)(2,1)S(1)} %get-tuple-element.115), channel_id=1, source_target_pairs={{0,4},{4,0},{8,12},{12,8},{16,20},{20,16},{24,28},{28,24},{1,5},{5... | collective-permute-start | bytes 1966088 | tf_op jit(solution)/shard_map/ppermute | solution.py:32
  53.8 1.6 collective-permute-start.16
  60.4 6.3 %collective-permute-start.17 = (bf16[128,1024]{1,0:T(8,128)(2,1)S(1)}, bf16[128,1024]{1,0:T(8,128)(2,1)S(1)}, u32[]{:S(2)}, u32[]{:S(2)}) collective-permute-start(bf16[128,1024]{1,0:T(8,128)(2,1)S(1)} %get-tuple-element.114), channel_id=1, source_target_pairs={{0,1},{1,0},{2,3},{3,2},{4,5},{5,4},{6,7},{7,6},{8,9},{9,8},{10,11... | collective-permute-start | bytes 786440 | tf_op jit(solution)/shard_map/ppermute | solution.py:32
  60.6 18.7 %collective-permute-start.21 = (bf16[256,1152]{1,0:T(8,128)(2,1)S(1)}, bf16[256,1152]{1,0:T(8,128)(2,1)S(1)}, u32[]{:S(2)}, u32[]{:S(2)}) collective-permute-start(bf16[256,1152]{1,0:T(8,128)(2,1)S(1)} %get-tuple-element.124.refs_2_.refs_0_), channel_id=1, source_target_pairs={{0,4},{4,0},{8,12},{12,8},{16,20},{20,16},{24,28},{28,24},{1,5},{5... | collective-permute-start | bytes 1769480 | tf_op jit(solution)/shard_map/ppermute | solution.py:32
  66.8 7.4 %collective-permute-start.19 = (bf16[128,1024]{1,0:T(8,128)(2,1)S(1)}, bf16[128,1024]{1,0:T(8,128)(2,1)S(1)}, u32[]{:S(2)}, u32[]{:S(2)}) collective-permute-start(bf16[128,1024]{1,0:T(8,128)(2,1)S(1)} %get-tuple-element.117.refs_0_), channel_id=1, source_target_pairs={{0,2},{1,3},{2,0},{3,1},{4,6},{5,7},{6,4},{7,5},{8,10},{9,11},{10,... | collective-permute-start | bytes 786440 | tf_op jit(solution)/shard_map/ppermute | solution.py:32
  67.5 30.1 %collective-permute-start.23 = (bf16[256,1664]{1,0:T(8,128)(2,1)S(1)}, bf16[256,1664]{1,0:T(8,128)(2,1)S(1)}, u32[]{:S(2)}, u32[]{:S(2)}) collective-permute-start(bf16[256,1664]{1,0:T(8,128)(2,1)S(1)} %get-tuple-element.137.refs_2_), channel_id=1, source_target_pairs={{0,4},{4,0},{8,12},{12,8},{16,20},{20,16},{24,28},{28,24},{1,5},{5... | collective-permute-start | bytes 2555912 | tf_op jit(solution)/shard_map/ppermute | solution.py:32
  74.3 6.0 %collective-permute-start.20 = (bf16[128,1024]{1,0:T(8,128)(2,1)S(1)}, bf16[128,1024]{1,0:T(8,128)(2,1)S(1)}, u32[]{:S(2)}, u32[]{:S(2)}) collective-permute-start(bf16[128,1024]{1,0:T(8,128)(2,1)S(1)} %grad_act_chip.1.refs_4_.refs_2_), channel_id=1, source_target_pairs={{0,1},{1,0},{2,3},{3,2},{4,5},{5,4},{6,7},{7,6},{8,9},{9,8},{10,11... | collective-permute-start | bytes 786440 | tf_op jit(solution)/shard_map/ppermute | solution.py:32
  86.8 18.7 %collective-permute-start.22 = (bf16[768,256]{1,0:T(8,128)(2,1)S(1)}, bf16[768,256]{1,0:T(8,128)(2,1)S(1)}, u32[]{:S(2)}, u32[]{:S(2)}) collective-permute-start(bf16[768,256]{1,0:T(8,128)(2,1)S(1)} %get-tuple-element.135), channel_id=1, source_target_pairs={{0,4},{4,0},{8,12},{12,8},{16,20},{20,16},{24,28},{28,24},{1,5},{5... | collective-permute-start | bytes 1179656 | tf_op jit(solution)/shard_map/ppermute | solution.py:32
  89.0 21.2 %collective-permute-start.28 = (bf16[256,1152]{1,0:T(8,128)(2,1)S(1)}, bf16[256,1152]{1,0:T(8,128)(2,1)S(1)}, u32[]{:S(2)}, u32[]{:S(2)}) collective-permute-start(bf16[256,1152]{1,0:T(8,128)(2,1)S(1)} %get-tuple-element.125.refs_16_), channel_id=1, source_target_pairs={{0,8},{4,12},{8,0},{12,4},{16,24},{20,28},{24,16},{28,20},{1,9},{5... | collective-permute-start | bytes 1769480 | tf_op jit(solution)/shard_map/ppermute | solution.py:32
  98.6 12.3 %copy-start.5 = (bf16[1024,256]{1,0:T(8,128)(2,1)S(1)}, bf16[1024,256]{1,0:T(8,128)(2,1)}, u32[]{:S(2)}) copy-start(bf16[1024,256]{1,0:T(8,128)(2,1)} %refs_5_.4) | copy-start | bytes 1572868
  98.6 12.2 %copy-start.14 = (f32[64]{0:T(128)S(1)}, f32[64]{0:T(128)}, u32[]{:S(2)}) copy-start(f32[64]{0:T(128)} %param.21) | copy-start | bytes 772
  98.6 20.7 %collective-permute-start.29 = (bf16[256,1152]{1,0:T(8,128)(2,1)S(1)}, bf16[256,1152]{1,0:T(8,128)(2,1)S(1)}, u32[]{:S(2)}, u32[]{:S(2)}) collective-permute-start(bf16[256,1152]{1,0:T(8,128)(2,1)S(1)} %get-tuple-element.138.refs_4_), channel_id=1, source_target_pairs={{0,8},{4,12},{8,0},{12,4},{16,24},{20,28},{24,16},{28,20},{1,9},{5... | collective-permute-start | bytes 1769480 | tf_op jit(solution)/shard_map/ppermute | solution.py:32
  105.7 14.9 %collective-permute-start.27 = (bf16[256,1152]{1,0:T(8,128)(2,1)S(1)}, bf16[256,1152]{1,0:T(8,128)(2,1)S(1)}, u32[]{:S(2)}, u32[]{:S(2)}) collective-permute-start(bf16[256,1152]{1,0:T(8,128)(2,1)S(1)} %get-tuple-element.150.refs_2_), channel_id=1, source_target_pairs={{0,4},{4,0},{8,12},{12,8},{16,20},{20,16},{24,28},{28,24},{1,5},{5... | collective-permute-start | bytes 1769480 | tf_op jit(solution)/shard_map/ppermute | solution.py:32
  107.5 14.1 %collective-permute-start.24 = (bf16[256,256]{1,0:T(8,128)(2,1)S(1)}, bf16[256,256]{1,0:T(8,128)(2,1)S(1)}, u32[]{:S(2)}, u32[]{:S(2)}) collective-permute-start(bf16[256,256]{1,0:T(8,128)(2,1)S(1)} %get-tuple-element.147), channel_id=1, source_target_pairs={{16,0},{20,4},{24,8},{28,12},{17,1},{21,5},{25,9},{29,13},{18,2},{... | collective-permute-start | bytes 393224 | tf_op jit(solution)/shard_map/ppermute | solution.py:42
  108.8 12.8 %collective-permute-start.25 = (bf16[256,256]{1,0:T(8,128)(2,1)S(1)}, bf16[256,256]{1,0:T(8,128)(2,1)S(1)}, u32[]{:S(2)}, u32[]{:S(2)}) collective-permute-start(bf16[256,256]{1,0:T(8,128)(2,1)S(1)} %get-tuple-element.148), channel_id=1, source_target_pairs={{8,0},{12,4},{16,8},{20,12},{24,16},{28,20},{9,1},{13,5},{17,9},{2... | collective-permute-start | bytes 393224 | tf_op jit(solution)/shard_map/ppermute | solution.py:42
  110.1 11.5 %collective-permute-start.26 = (bf16[256,256]{1,0:T(8,128)(2,1)S(1)}, bf16[256,256]{1,0:T(8,128)(2,1)S(1)}, u32[]{:S(2)}, u32[]{:S(2)}) collective-permute-start(bf16[256,256]{1,0:T(8,128)(2,1)S(1)} %get-tuple-element.149), channel_id=1, source_target_pairs={{28,4},{29,5},{30,6},{31,7}} | collective-permute-start | bytes 393224 | tf_op jit(solution)/shard_map/ppermute | solution.py:843
  122.5 17.7 %copy-start.4 = (bf16[256,1024]{1,0:T(8,128)(2,1)S(1)}, bf16[256,1024]{1,0:T(8,128)(2,1)}, u32[]{:S(2)}) copy-start(bf16[256,1024]{1,0:T(8,128)(2,1)} %get-tuple-element.165.refs_4_.refs_8_) | copy-start | bytes 1572868
  122.5 5.2 %collective-permute-start.30 = (bf16[272,1024]{1,0:T(8,128)(2,1)S(1)}, bf16[272,1024]{1,0:T(8,128)(2,1)S(1)}, u32[]{:S(2)}, u32[]{:S(2)}) collective-permute-start(bf16[272,1024]{1,0:T(8,128)(2,1)S(1)} %get-tuple-element.158), channel_id=1, source_target_pairs={{0,1},{1,0},{2,3},{3,2},{4,5},{5,4},{6,7},{7,6},{8,9},{9,8},{10,11... | collective-permute-start | bytes 1671176 | tf_op jit(solution)/shard_map/ppermute | solution.py:32
  122.6 17.6 %collective-permute-start.32 = (bf16[256,1024]{1,0:T(8,128)(2,1)S(1)}, bf16[256,1024]{1,0:T(8,128)(2,1)S(1)}, u32[]{:S(2)}, u32[]{:S(2)}) collective-permute-start(bf16[256,1024]{1,0:T(8,128)(2,1)S(1)} %get-tuple-element.164.refs_6_.refs_10_), channel_id=1, source_target_pairs={{0,4},{4,0},{8,12},{12,8},{16,20},{20,16},{24,28},{28,24},{1,5},{5... | collective-permute-start | bytes 1572872 | tf_op jit(solution)/shard_map/ppermute | solution.py:32
  127.7 26.2 %collective-permute-start.35 = (bf16[256,1152]{1,0:T(8,128)(2,1)S(1)}, bf16[256,1152]{1,0:T(8,128)(2,1)S(1)}, u32[]{:S(2)}, u32[]{:S(2)}) collective-permute-start(bf16[256,1152]{1,0:T(8,128)(2,1)S(1)} %get-tuple-element.154.refs_20_), channel_id=1, source_target_pairs={{0,8},{4,12},{8,0},{12,4},{16,24},{20,28},{24,16},{28,20},{1,9},{5... | collective-permute-start | bytes 1769480 | tf_op jit(solution)/shard_map/ppermute | solution.py:32
  127.9 13.1 %collective-permute-start.31 = (bf16[144,1024]{1,0:T(8,128)(2,1)S(1)}, bf16[144,1024]{1,0:T(8,128)(2,1)S(1)}, u32[]{:S(2)}, u32[]{:S(2)}) collective-permute-start(bf16[144,1024]{1,0:T(8,128)(2,1)S(1)} %get-tuple-element.162.refs_12_), channel_id=1, source_target_pairs={{0,2},{1,3},{2,0},{3,1},{4,6},{5,7},{6,4},{7,5},{8,10},{9,11},{10,... | collective-permute-start | bytes 884744 | tf_op jit(solution)/shard_map/ppermute | solution.py:32
  128.8 29.8 %collective-permute-start.34 = (bf16[128,2304]{1,0:T(8,128)(2,1)S(1)}, bf16[128,2304]{1,0:T(8,128)(2,1)S(1)}, u32[]{:S(2)}, u32[]{:S(2)}) collective-permute-start(bf16[128,2304]{1,0:T(8,128)(2,1)S(1)} %get-tuple-element.153.refs_4_), channel_id=1, source_target_pairs={{0,16},{4,20},{8,24},{12,28},{16,0},{20,4},{24,8},{28,12},{1,17},{... | collective-permute-start | bytes 1769480 | tf_op jit(solution)/shard_map/ppermute | solution.py:32
  140.9 29.7 %collective-permute-start.33 = (bf16[256,768]{1,0:T(8,128)(2,1)S(1)}, bf16[256,768]{1,0:T(8,128)(2,1)S(1)}, u32[]{:S(2)}, u32[]{:S(2)}) collective-permute-start(bf16[256,768]{1,0:T(8,128)(2,1)S(1)} %get-tuple-element.166.refs_8_), channel_id=1, source_target_pairs={{0,8},{4,12},{8,0},{12,4},{16,24},{20,28},{24,16},{28,20},{1,9},{5... | collective-permute-start | bytes 1179656 | tf_op jit(solution)/shard_map/ppermute | solution.py:32
  142.0 3.7 %collective-permute-start.36 = (f32[18,128]{1,0:T(8,128)S(1)}, f32[18,128]{1,0:T(8,128)S(1)}, u32[]{:S(2)}, u32[]{:S(2)}) collective-permute-start(f32[18,128]{1,0:T(8,128)S(1)} %get-tuple-element.173.refs_0_), channel_id=1, source_target_pairs={{0,4},{4,0},{8,12},{12,8},{16,20},{20,16},{24,28},{28,24},{1,5},{5... | collective-permute-start | bytes 27656 | tf_op jit(solution)/shard_map/ppermute | solution.py:32
  154.1 19.7 %collective-permute-start.40 = (bf16[128,1152]{1,0:T(8,128)(2,1)S(1)}, bf16[128,1152]{1,0:T(8,128)(2,1)S(1)}, u32[]{:S(2)}, u32[]{:S(2)}) collective-permute-start(bf16[128,1152]{1,0:T(8,128)(2,1)S(1)} %get-tuple-element.174.refs_3_), channel_id=1, source_target_pairs={{0,16},{4,20},{8,24},{12,28},{16,0},{20,4},{24,8},{28,12},{1,17},{... | collective-permute-start | bytes 884744 | tf_op jit(solution)/shard_map/ppermute | solution.py:32
  154.2 16.6 %collective-permute-start.38 = (f32[18,128]{1,0:T(8,128)S(1)}, f32[18,128]{1,0:T(8,128)S(1)}, u32[]{:S(2)}, u32[]{:S(2)}) collective-permute-start(f32[18,128]{1,0:T(8,128)S(1)} %gains.3.refs_2_.refs_0_), channel_id=1, source_target_pairs={{0,8},{4,12},{8,0},{12,4},{16,24},{20,28},{24,16},{28,20},{1,9},{5... | collective-permute-start | bytes 27656 | tf_op jit(solution)/shard_map/ppermute | solution.py:32
  170.8 7.5 %collective-permute-start.39 = (f32[18,128]{1,0:T(8,128)S(1)}, f32[18,128]{1,0:T(8,128)S(1)}, u32[]{:S(2)}, u32[]{:S(2)}) collective-permute-start(f32[18,128]{1,0:T(8,128)S(1)} %gains.4.refs_2_.refs_0_), channel_id=1, source_target_pairs={{0,16},{4,20},{8,24},{12,28},{16,0},{20,4},{24,8},{28,12},{1,17},{... | collective-permute-start | bytes 27656 | tf_op jit(solution)/shard_map/ppermute | solution.py:32
  170.9 11.3 %collective-permute-start.37 = (bf16[128,768]{1,0:T(8,128)(2,1)S(1)}, bf16[128,768]{1,0:T(8,128)(2,1)S(1)}, u32[]{:S(2)}, u32[]{:S(2)}) collective-permute-start(bf16[128,768]{1,0:T(8,128)(2,1)S(1)} %get-tuple-element.177.refs_2_), channel_id=1, source_target_pairs={{0,16},{4,20},{8,24},{12,28},{16,0},{20,4},{24,8},{28,12},{1,17},{... | collective-permute-start | bytes 589832 | tf_op jit(solution)/shard_map/ppermute | solution.py:32
  (11 other events, 21.1 us)

commit v4 on v3

--- a/solution.py
+++ b/solution.py
@@ -165,6 +165,11 @@
     select_columns(ranks, act_out, select_out)
 
 
+def pack_kernel(cot, there_cot, packet_out):
+    packet_out[:, : cot.shape[1]] = cot[...]
+    packet_out[:, cot.shape[1] :] = there_cot[...]
+
+
 def select_columns(ranks, source, target):
     columns = target.shape[1]
     blocks = columns // 128
@@ -176,30 +181,36 @@
         target[:, b * 128 : (b + 1) * 128] = source[:, pl.ds(start, 128)]
 
 
-def cotangent_kernel(
-    ranks, c0, c1, c2, c3, wd, act_select, attn_b, cot_out, packet_out, grad_hidden_out
-):
-    cot = jnp.concatenate([c0[...], c1[...], c2[...], c3[...]], axis=0)
+def cotangent_kernel(ranks, p0, p1, p2, p3, wd, cot_out, there_out, grad_hidden_out):
+    packet = jnp.concatenate([p0[...], p1[...], p2[...], p3[...]], axis=0)
+    width = cot_out.shape[1]
+    cot = packet[:, :width]
     cot_out[...] = cot
-    chosen = act_select.shape[1]
-    select_columns(ranks, cot_out, packet_out.at[:, :chosen])
-    packet_out[:, chosen : 2 * chosen] = act_select[...]
-    packet_out[:, 2 * chosen :] = attn_b[...]
     grad_hidden_out[...] = dot(cot, wd[...], COLS)
-
-
-def attention_kernel(count, ranks, query_rot, positions, wo, *refs):
+    if width // lax.axis_size("ctx") != 128:
+        there_out[...] = jnp.zeros(there_out.shape, BF)
+        return
+    source = packet[:, width:].astype(F32)
+    for b in range(width // 256):
+        low = source[:, 256 * b : 256 * b + 128]
+        high = source[:, 256 * b + 128 : 256 * b + 256]
+        there_out[:, 128 * b : 128 * (b + 1)] = jnp.where(ranks[0] % 2 == 1, high, low).astype(BF)
+
+
+def attention_kernel(count, ranks, query_rot, positions, wo, act_select, *refs):
     slots = count // 2
     even = refs[:slots]
-    low_odd, high_odd = refs[slots : 2 * slots], refs[2 * slots : 3 * slots]
-    out_f32, out_b, sums_out, kept_out, sent_out = refs[3 * slots : 3 * slots + 5]
-    odd = refs[3 * slots + 5 : -1]
+    crossed = refs[slots : 2 * slots]
+    out_f32, out_b, sums_out, kept_out, sent_out = refs[2 * slots : 2 * slots + 5]
+    odd = refs[2 * slots + 5 : -1]
     scores = refs[-1]
     rows = query_rot.shape[0]
     key_width = even[0].shape[1] // 2
     for j in range(slots):
         odd[j][...] = jnp.where(
-            ranks[0] % 2 == 1, low_odd[j][...].astype(F32), high_odd[j][...].astype(F32)
+            ranks[0] % 2 == 1,
+            crossed[j][...].astype(F32),
+            crossed[(j + 1) % slots][...].astype(F32),
         ).astype(BF)
     blocks = [(even, odd)[d % 2][d // 2] for d in range(count)]
     query_index = ranks[0] * rows + place_of(
@@ -233,7 +244,9 @@
         sums_out[head : head + 1, :] = jnp.transpose(sums)[:1]
         out_f32[:, head * 128 : (head + 1) * 128] = unstack(mixed / total, head)
     attn_b = out_f32[...].astype(BF)
-    out_b[...] = attn_b
+    chosen = act_select.shape[1]
+    out_b[:, :chosen] = act_select[...]
+    out_b[:, chosen:] = attn_b
     half = rows // 2
     kept_out[...] = dot(attn_b[:half], wo[...])
     sent_out[...] = dot(attn_b[half:], wo[...]).astype(BF)
@@ -359,36 +372,27 @@
     )
 
 
-def ffn_forward_kernel(
-    ranks, x0, x1, x2, x3, half0, half1, gain, wg, wu,
-    resid_out, act_out, select_out, gate_out, up_out, hidden_out,
+def ffn_kernel(
+    ranks, x0, x1, x2, x3, half0, half1, gain, wg, wu, grad_hidden,
+    resid_out, act_out, hidden_out, gate_packet, grad_up_out, kept_out, sent_out,
 ):
     x = jnp.concatenate([x0[...], x1[...], x2[...], x3[...]], axis=0).astype(F32)
     resid = x + jnp.concatenate([half0[...], half1[...]], axis=0).astype(F32)
     resid_out[...] = resid
     act = (resid * row_norm(resid) * gain[...]).astype(BF)
     act_out[...] = act
-    gate = dot(act, wg[...])
+    values = dot(act, wg[...])
     upper = dot(act, wu[...])
-    gate_out[...] = gate
-    up_out[...] = upper
-    hidden_out[...] = (gate * jax.nn.sigmoid(gate) * upper).astype(BF)
-    select_columns(ranks, act_out, select_out)
-
-
-def ffn_backward_kernel(
-    gate, upper, grad_hidden, wg, wu, select, gate_packet, grad_up_out, kept_out, sent_out
-):
+    sigmoid = jax.nn.sigmoid(values)
+    hidden_out[...] = (values * sigmoid * upper).astype(BF)
     grads = grad_hidden[...]
-    values = gate[...]
-    sigmoid = jax.nn.sigmoid(values)
-    grad_gate = (grads * upper[...] * sigmoid * (1.0 + values * (1.0 - sigmoid))).astype(BF)
+    grad_gate = (grads * upper * sigmoid * (1.0 + values * (1.0 - sigmoid))).astype(BF)
     grad_up = (grads * values * sigmoid).astype(BF)
-    chosen = select.shape[1]
-    gate_packet[:, :chosen] = select[...]
+    chosen = act.shape[1] // 2
+    select_columns(ranks, act_out, gate_packet.at[:, :chosen])
     gate_packet[:, chosen:] = grad_gate
     grad_up_out[...] = grad_up
-    half = values.shape[0] // 2
+    half = resid.shape[0] // 2
     sent_out[...] = (
         dot(grad_gate[half:], wg[...], COLS) + dot(grad_up[half:], wu[...], COLS)
     ).astype(BF)
@@ -714,91 +718,82 @@
         name="qkv",
     )(*x[1:], *copied)
 
-    def cross(values, odd):
-        return lax.ppermute(values, "ctx", [(i, i ^ 1) for i in range(odd, n_ctx, 2)])
-
-    def climb(step, pairs):
-        pairs = [(i, i + step) for i in pairs if i + step < n_ctx]
+    def climb(step):
+        pairs = [(i, i + step) for i in range(n_ctx - step)]
         return lax.ppermute(pair, "ctx", pairs) if pairs else jnp.zeros_like(pair)
 
-    items = [pair] + [climb(2 * k, range(n_ctx)) for k in range(1, slots)]
-    farthest = climb(2 * slots - 1, range(1, n_ctx, 2))
-    low_odd = [cross(items[j], 0) for j in range(slots)]
-    high_odd = [cross(items[j + 1], 1) for j in range(slots - 1)] + [farthest]
-    even = items[:slots]
-    cot_chip = xor(cotangent, "mp", 2)
-    cot_core = xor(cotangent, "mp", 1)
+    even = [pair] + [climb(2 * k) for k in range(1, slots)]
+    farthest = 2 * slots - 1
+    pairs = [(i, i + 1) for i in range(0, n_ctx, 2)]
+    pairs += [(i, i + farthest) for i in range(1, n_ctx - farthest, 2)]
+    crossed = [lax.ppermute(pair, "ctx", pairs)] + [xor(e, "ctx", 1) for e in even[1:]]
+    packet = launch(
+        pack_kernel,
+        [shape((own_rows, 2 * width), BF)],
+        [cotangent, xor(cotangent, "ctx", 1)],
+        name="pack",
+        after=[pair],
+    )[0]
+    packets = mp_gather(packet)
 
     outs = launch(
         functools.partial(attention_kernel, count),
         [
             shape((rows, query_width), F32),
-            shape((rows, query_width), BF),
+            shape((rows, width // 2 + query_width), BF),
             shape((2, 2 * rows), F32),
             shape((half, width), F32),
             shape((half, width), BF),
         ]
         + [shape((rows, 2 * key_width), BF) for _ in range(slots)],
-        [RANKS, query_rot, position_column, out_weight,
-         *even, *low_odd, *high_odd],
+        [RANKS, query_rot, position_column, out_weight, act_attn_select,
+         *even, *crossed],
         scratch=[pltpu.VMEM((2 * rows, count * rows), F32)],
         name="attention",
-        after=[cot_chip, cot_core],
-    )
-    attn_rows, attn_b, log_sums, kept, sent = outs[:5]
+        after=packets[1:3],
+    )
+    attn_rows, early, log_sums, kept, sent = outs[:5]
     blocks = [(even, outs[5:])[d % 2][d // 2] for d in range(count)]
     chosen = width // 2
 
     kept = add(kept, xor(sent, "mp", 1), BF, "resid_core")
-    cot, packet, grad_hidden = launch(
+    cot, cot_there, grad_hidden = launch(
         cotangent_kernel,
         [
             shape((rows, width), BF),
-            shape((rows, 2 * chosen + query_width), BF),
+            shape((rows, chosen), BF),
             shape((rows, hidden_width), F32),
         ],
-        [RANKS, cotangent, cot_chip, cot_core, xor(cot_chip, "mp", 1), down_weight,
-         act_attn_select, attn_b],
+        [RANKS, *packets, down_weight],
         name="cotangent",
         after=[kept],
     )
-    there = xor(packet, "ctx", 1)
+    early_there = xor(early, "ctx", 1)
     both = add(
         kept, xor(kept, "mp", 2), BF, "resid_chip", kernel=flipped_add_kernel,
         after=[grad_hidden],
     )
 
-    resid, act_ffn, act_select, gate_pre, up_proj, hidden = launch(
-        ffn_forward_kernel,
+    resid, act_ffn, hidden, gate_packet, grad_up, kept, sent = launch(
+        ffn_kernel,
         [
             shape((rows, width), F32),
             shape((rows, width), BF),
-            shape((rows, chosen), BF),
-            shape((rows, hidden_width), F32),
-            shape((rows, hidden_width), F32),
             shape((rows, hidden_width), BF),
-        ],
-        [RANKS, *x, both, xor(both, "mp", 1), ffn_gain_row, gate_weight, up_weight],
-        name="ffn_forward",
-    )
-    hidden_there = xor(hidden, "ctx", 1)
-    gate_packet, grad_up, kept, sent = launch(
-        ffn_backward_kernel,
-        [
             shape((rows, chosen + hidden_width), BF),
             shape((rows, hidden_width), BF),
             shape((half, width), F32),
             shape((half, width), BF),
         ],
-        [gate_pre, up_proj, grad_hidden, gate_weight, up_weight, act_select],
-        name="ffn_backward",
-    )
-    kept, gate_packet = add(kept, xor(sent, "mp", 1), BF, "grad_act_core", after=[there],
-        carry=[gate_packet])
+        [RANKS, *x, both, xor(both, "mp", 1), ffn_gain_row, gate_weight, up_weight, grad_hidden],
+        name="ffn",
+    )
+    hidden_there = xor(hidden, "ctx", 1)
+    kept, gate_packet = add(kept, xor(sent, "mp", 1), BF, "grad_act_core", carry=[gate_packet])
     gate_there = xor(gate_packet, "ctx", 1)
     both = add(kept, xor(kept, "mp", 2), BF, "grad_act_chip", kernel=flipped_add_kernel)
     down_kept, down_sent = weight_grad(
-        [(cot, there, hidden, hidden_there, (0, 0), 0, hidden_width)], "down_grad",
+        [(cot, cot_there, hidden, hidden_there, (0, 0), 0, hidden_width)], "down_grad",
         after=[both],
     )
 
@@ -822,10 +817,11 @@
     terms, odd_terms = outs[5:-1], outs[-1]
 
     arrived = xor(odd_terms, "ctx", 1)
+    down_arrived = xor(down_sent, "ctx", 2)
     gate_kept, gate_sent = weight_grad(
         [(act_ffn, gate_there, gate_packet, gate_there, (chosen, chosen), 0, hidden_width)],
         "gate_grad",
-        after=[grad_query],
+        after=[grad_query, down_arrived],
     )
     totals = launch(
         functools.partial(pair_sum_kernel, slots),
@@ -861,7 +857,7 @@
         after=[query_partial],
     )
     (down_kept, gate_kept), first_arrived, back = fold(
-        [(down_kept, xor(down_sent, "ctx", 2)), (gate_kept, xor(gate_sent, "ctx", 2))],
+        [(down_kept, down_arrived), (gate_kept, xor(gate_sent, "ctx", 2))],
         "first_fold",
         after=[out_sent],
     )
@@ -898,15 +894,6 @@
         [kept, out_kept, gains, core_arrived],
         name="mp_fold",
     )
-    attn_kept, attn_sent = weight_grad(
-        [
-            (grad_resid_b, late_there, attn_b, there, (0, 2 * chosen), 0, query_width),
-            (act_attn, there, late, late_there, (query_at, query_at), chosen, query_width),
-            (act_attn, there, late, late_there, (pair_at, pair_at), chosen, 2 * key_width),
-        ],
-        "attention_grads",
-        after=[back],
-    )
     grad_input, block_out, gains = launch(
         outputs_kernel,
         [
@@ -917,9 +904,18 @@
         [x[0], attn_gain_row, grad_resid, resid, input_kept, out_kept, gains,
          xor(back, "mp", 2)],
         name="outputs",
-        after=[attn_sent],
-    )
-    gains = add(gains, xor(gains, "ctx", 1), F32, "gains")
+        after=[early_there],
+    )
+    attn_kept, attn_sent = weight_grad(
+        [
+            (grad_resid_b, late_there, early, early_there, (chosen, chosen), 0, query_width),
+            (act_attn, early_there, late, late_there, (query_at, query_at), 0, query_width),
+            (act_attn, early_there, late, late_there, (pair_at, pair_at), 0, 2 * key_width),
+        ],
+        "attention_grads",
+        after=[gains],
+    )
+    gains = add(gains, xor(gains, "ctx", 1), F32, "gains", after=[attn_sent])
     (up_kept,), up_arrived, back = fold(
         [(up_kept, xor(up_sent, "ctx", 2))], "up_fold", after=[gains]
     )
@@ -931,19 +927,19 @@
         name="first_last",
         after=[back],
     )
+    mask = 2
+    while mask < n_ctx // 2:
+        gains = add(gains, xor(gains, "ctx", mask), F32, "gains", after=[done])
+        mask *= 2
     (attn_kept,), attn_arrived, back = fold(
         [(attn_kept, xor(attn_sent, "ctx", 2))], "attention_fold", after=[done]
     )
-    mask = 2
-    while mask < n_ctx // 2:
-        gains = add(gains, xor(gains, "ctx", mask), F32, "gains", after=[back])
-        mask *= 2
     up_grad, done = launch(
         functools.partial(last_kernel, (False,)),
         [shape(up_kept.shape, F32), token],
         [up_kept, up_arrived],
         name="up_last",
-        after=[gains],
+        after=[back],
     )
     gains = add(gains, xor(gains, "ctx", mask), F32, "gains", after=[done])
     out_grad, query_grad, key_grad, value_grad = launch(

time: 183 us -> 178 us (0.973)
  starting transfers between devices: 59.2 us -> 47.1 us
  waiting for transfers between devices: 87.8 us -> 94.4 us
    ppermute x5 -> x1, starting transfers between devices: 12.7 us -> 3.42 us  [body(): lax.ppermute(pair, 'ctx', pairs)]
    ppermute x30 -> x33, waiting for transfers between devices: 85.2 us -> 92.8 us  [xor(): return lax.ppermute(values, axis, [(i, i ^ mask) for i in range(n)])]
    ppermute x30 -> x33, starting transfers between devices: 34.6 us -> 32.5 us  [xor(): return lax.ppermute(values, axis, [(i, i ^ mask) for i in range(n)])]
    ppermute x3 -> x2, starting transfers between devices: 8.65 us -> 7.98 us  [climb(): return lax.ppermute(pair, 'ctx', pairs) if pairs else jnp.zeros_like(pair)]
  transfers between devices with their start and end apart: 41 -> 39, of which waited for: 20 -> 19; matrix products, arithmetic and copies ran while one was open for 1% -> 1% of each run, Pallas kernels for 14% -> 11%
where the time goes in v4:
time: 178 us
  waiting for transfers between devices  94.4 us (53%)
  starting transfers between devices  47.1 us (26%)
  Pallas kernels  30.1 us (17%)
  local copies, waits for them, and re-layouts  4.95 us (3%)
    ppermute x33, waiting for transfers between devices, xor(): return lax.ppermute(values, axis, [(i, i ^ mask) for i in range(n)])  92.8 us
    ppermute x33, starting transfers between devices, xor(): return lax.ppermute(values, axis, [(i, i ^ mask) for i in range(n)])  32.5 us
    pallas_call x28, Pallas kernels, launch(): pl.pallas_call(run, out_shape=list(outs) + [shape(c.shape, c.dtype) for c...  26.8 us
    ppermute x2, starting transfers between devices, climb(): return lax.ppermute(pair, 'ctx', pairs) if pairs else jnp.zeros_like(pair)  7.98 us
    unnamed x36, local copies, waits for them, and re-layouts  3.75 us
  transfers between devices with their start and end apart: 39, of which 19 were waited for; matrix products, arithmetic and copies ran while one was open for 1% of the time, Pallas kernels for 11%

profile of v4, /device:TPU:0, one launch (start us, length us, event | category | flops | bytes accessed | tf_op | source)
XLA Modules:
  0.0 177.6 jit_solution(7892319100562145563)
XLA Ops:
  0.7 3.0 %collective-permute-start.1 = (bf16[64,1024]{1,0:T(8,128)(2,1)}, bf16[64,1024]{1,0:T(8,128)(2,1)S(1)}, u32[]{:S(2)}, u32[]{:S(2)}) collective-permute-start(bf16[64,1024]{1,0:T(8,128)(2,1)} %refs_0_.5), channel_id=1, source_target_pairs={{0,2},{1,3},{2,0},{3,1},{4,6},{5,7},{6,4},{7,5},{8,10},{9,11},{10,... | collective-permute-start | bytes 393224 | tf_op jit(solution)/shard_map/ppermute | solution.py:32
  3.7 3.7 %collective-permute-done.1.x1.refs_1_.refs_8_ = bf16[64,1024]{1,0:T(8,128)(2,1)S(1)} collective-permute-done((bf16[64,1024]{1,0:T(8,128)(2,1)}, bf16[64,1024]{1,0:T(8,128)(2,1)S(1)}, u32[]{:S(2)}, u32[]{:S(2)}) %collective-permute-start.1) | collective-permute-done | bytes 131104 | tf_op jit(solution)/shard_map/ppermute | solution.py:32
  7.4 1.8 collective-permute-start
  12.7 3.3 %qkv.1 = (bf16[256,1024]{1,0:T(8,128)(2,1)}, bf16[256,512]{1,0:T(8,128)(2,1)S(1)}, bf16[256,256]{1,0:T(8,128)(2,1)S(1)}, bf16[256,256]{1,0:T(8,128)(2,1)S(1)}, f...) custom-call(bf16[64,1024]{1,0:T(8,128)(2,1)S(1)} %collective-permute, ...), custom_call_target="tpu_custom_call" | custom-call | tf_op jit(solution)/shard_map/qkv/pallas_call | solution.py:709
  16.0 3.5 %collective-permute-start.7 = (bf16[256,256]{1,0:T(8,128)(2,1)S(1)}, bf16[256,256]{1,0:T(8,128)(2,1)S(1)}, u32[]{:S(2)}, u32[]{:S(2)}) collective-permute-start(bf16[256,256]{1,0:T(8,128)(2,1)S(1)} %get-tuple-element.97.refs_2_.refs_4_.refs_10_), channel_id=1, source_target_pairs={{0,8},{4,12},{8,16},{12,20},{16,24},{20,28},{1,9},{5,13},{9,17},{1... | collective-permute-start | bytes 393224 | tf_op jit(solution)/shard_map/ppermute | solution.py:723
  19.6 1.6 collective-permute-start.4
  21.1 4.5 %collective-permute-start.8 = (bf16[256,256]{1,0:T(8,128)(2,1)S(1)}, bf16[256,256]{1,0:T(8,128)(2,1)S(1)}, u32[]{:S(2)}, u32[]{:S(2)}) collective-permute-start(bf16[256,256]{1,0:T(8,128)(2,1)S(1)} %get-tuple-element.97.refs_2_.refs_4_.refs_10_), channel_id=1, source_target_pairs={{0,16},{4,20},{8,24},{12,28},{1,17},{5,21},{9,25},{13,29},{2,18},{... | collective-permute-start | bytes 393224 | tf_op jit(solution)/shard_map/ppermute | solution.py:723
  25.6 3.4 %collective-permute-start.9 = (bf16[256,256]{1,0:T(8,128)(2,1)S(1)}, bf16[256,256]{1,0:T(8,128)(2,1)S(1)}, u32[]{:S(2)}, u32[]{:S(2)}) collective-permute-start(bf16[256,256]{1,0:T(8,128)(2,1)S(1)} %get-tuple-element.97.refs_2_.refs_4_.refs_10_), channel_id=1, source_target_pairs={{0,4},{8,12},{16,20},{24,28},{4,24},{1,5},{9,13},{17,21},{25,29},{... | collective-permute-start | bytes 393224 | tf_op jit(solution)/shard_map/ppermute | solution.py:729
  29.2 2.0 %collective-permute-start.11 = (bf16[256,256]{1,0:T(8,128)(2,1)S(1)}, bf16[256,256]{1,0:T(8,128)(2,1)S(1)}, u32[]{:S(2)}, u32[]{:S(2)}) collective-permute-start(bf16[256,256]{1,0:T(8,128)(2,1)S(1)} %collective-permute-done.8.refs_6_.refs_14_), channel_id=1, source_target_pairs={{0,4},{4,0},{8,12},{12,8},{16,20},{20,16},{24,28},{28,24},{1,5},{5... | collective-permute-start | bytes 393224 | tf_op jit(solution)/shard_map/ppermute | solution.py:32
  31.2 1.5 collective-permute-done.9.refs_7_
  32.7 2.8 %collective-permute-done.10.refs_8_ = bf16[256,256]{1,0:T(8,128)(2,1)S(1)} collective-permute-done((bf16[256,256]{1,0:T(8,128)(2,1)S(1)}, bf16[256,256]{1,0:T(8,128)(2,1)S(1)}, u32[]{:S(2)}, u32[]{:S(2)}) %collective-permute-start.10) | collective-permute-done | bytes 131104 | tf_op jit(solution)/shard_map/ppermute | solution.py:32
  35.5 2.1 %collective-permute-done.11.refs_9_ = bf16[256,256]{1,0:T(8,128)(2,1)S(1)} collective-permute-done((bf16[256,256]{1,0:T(8,128)(2,1)S(1)}, bf16[256,256]{1,0:T(8,128)(2,1)S(1)}, u32[]{:S(2)}, u32[]{:S(2)}) %collective-permute-start.11) | collective-permute-done | bytes 131104 | tf_op jit(solution)/shard_map/ppermute | solution.py:32
  37.6 3.4 %attention.1 = (f32[256,256]{1,0:T(8,128)S(1)}, bf16[256,768]{1,0:T(8,128)(2,1)S(1)}, f32[2,512]{1,0:T(2,128)S(1)}, f32[128,1024]{1,0:T(8,128)S(1)}, bf16[128,10...) custom-call(bf16[256,256]{1,0:T(8,128)(2,1)S(1)} %get-tuple-element., ...), custom_call_target="tpu_custom_call" | custom-call | tf_op jit(solution)/shard_map/attention/pallas_call | solution.py:565
  41.6 1.0 collective-permute-done.12.refs_1_
  43.3 0.9 cotangent.1
  44.3 6.8 %collective-permute-done.13.refs_1_ = bf16[128,1024]{1,0:T(8,128)(2,1)S(1)} collective-permute-done((bf16[128,1024]{1,0:T(8,128)(2,1)S(1)}, bf16[128,1024]{1,0:T(8,128)(2,1)S(1)}, u32[]{:S(2)}, u32[]{:S(2)}) %collective-permute-start.13) | collective-permute-done | bytes 262176 | tf_op jit(solution)/shard_map/ppermute | solution.py:32
  51.2 1.5 collective-permute-done.14.refs_5_
  52.8 5.2 %ffn.1 = (f32[256,1024]{1,0:T(8,128)S(1)}, bf16[256,1024]{1,0:T(8,128)(2,1)S(1)}, bf16[256,1152]{1,0:T(8,128)(2,1)S(1)}, bf16[256,1664]{1,0:T(8,128)(2,1)S(1)}, ...) custom-call(bf16[64,1024]{1,0:T(8,128)(2,1)S(1)} %copy-done.6, ...), custom_call_target="tpu_custom_call" | custom-call | tf_op jit(solution)/shard_map/ffn/pallas_call | solution.py:565
  58.2 2.5 %collective-permute-start.18 = (bf16[256,1152]{1,0:T(8,128)(2,1)S(1)}, bf16[256,1152]{1,0:T(8,128)(2,1)S(1)}, u32[]{:S(2)}, u32[]{:S(2)}) collective-permute-start(bf16[256,1152]{1,0:T(8,128)(2,1)S(1)} %get-tuple-element.117.refs_2_.refs_0_), channel_id=1, source_target_pairs={{0,4},{4,0},{8,12},{12,8},{16,20},{20,16},{24,28},{28,24},{1,5},{5... | collective-permute-start | bytes 1769480 | tf_op jit(solution)/shard_map/ppermute | solution.py:32
  61.3 1.4 collective-permute-start.20
  62.7 6.4 %collective-permute-done.16.refs_1_ = bf16[128,1024]{1,0:T(8,128)(2,1)S(1)} collective-permute-done((bf16[128,1024]{1,0:T(8,128)(2,1)S(1)}, bf16[128,1024]{1,0:T(8,128)(2,1)S(1)}, u32[]{:S(2)}, u32[]{:S(2)}) %collective-permute-start.16) | collective-permute-done | bytes 262176 | tf_op jit(solution)/shard_map/ppermute | solution.py:32
  69.2 5.6 %collective-permute-done.18.refs_3_ = bf16[256,1152]{1,0:T(8,128)(2,1)S(1)} collective-permute-done((bf16[256,1152]{1,0:T(8,128)(2,1)S(1)}, bf16[256,1152]{1,0:T(8,128)(2,1)S(1)}, u32[]{:S(2)}, u32[]{:S(2)}) %collective-permute-start.18) | collective-permute-done | bytes 589856 | tf_op jit(solution)/shard_map/ppermute | solution.py:32
  74.8 0.9 down_grad.1
  76.1 6.6 %attention_backward.1 = (f32[64,1024]{1,0:T(8,128)S(1)}, bf16[256,1024]{1,0:T(8,128)(2,1)S(1)}, bf16[256,512]{1,0:T(8,128)(2,1)S(1)}, f32[1,1024]{1,0:T(1,128)S(...) custom-call(bf16[256,1024]{1,0:T(8,128)(2,1)S(1)} %get-tuple-element, ...), custom_call_target="tpu_custom_call" | custom-call | tf_op jit(solution)/shard_map/attention_backward/pallas_call | solution.py:565
  82.6 2.0 %collective-permute-start.19 = (bf16[768,256]{1,0:T(8,128)(2,1)S(1)}, bf16[768,256]{1,0:T(8,128)(2,1)S(1)}, u32[]{:S(2)}, u32[]{:S(2)}) collective-permute-start(bf16[768,256]{1,0:T(8,128)(2,1)S(1)} %get-tuple-element.128), channel_id=1, source_target_pairs={{0,4},{4,0},{8,12},{12,8},{16,20},{20,16},{24,28},{28,24},{1,5},{5... | collective-permute-start | bytes 1179656 | tf_op jit(solution)/shard_map/ppermute | solution.py:32
  84.7 8.4 %collective-permute-done.20.refs_1_.refs_3_ = bf16[256,1664]{1,0:T(8,128)(2,1)S(1)} collective-permute-done((bf16[256,1664]{1,0:T(8,128)(2,1)S(1)}, bf16[256,1664]{1,0:T(8,128)(2,1)S(1)}, u32[]{:S(2)}, u32[]{:S(2)}) %collective-permute-start.20) | collective-permute-done | bytes 852000 | tf_op jit(solution)/shard_map/ppermute | solution.py:32
  93.1 0.9 gate_grad.1
  94.3 6.9 %collective-permute-done.19.refs_3_ = bf16[768,256]{1,0:T(8,128)(2,1)S(1)} collective-permute-done((bf16[768,256]{1,0:T(8,128)(2,1)S(1)}, bf16[768,256]{1,0:T(8,128)(2,1)S(1)}, u32[]{:S(2)}, u32[]{:S(2)}) %collective-permute-start.19) | collective-permute-done | bytes 393248 | tf_op jit(solution)/shard_map/ppermute | solution.py:32
  101.4 1.8 %collective-permute-start.25 = (bf16[256,1152]{1,0:T(8,128)(2,1)S(1)}, bf16[256,1152]{1,0:T(8,128)(2,1)S(1)}, u32[]{:S(2)}, u32[]{:S(2)}) collective-permute-start(bf16[256,1152]{1,0:T(8,128)(2,1)S(1)} %get-tuple-element.143.refs_2_), channel_id=1, source_target_pairs={{0,4},{4,0},{8,12},{12,8},{16,20},{20,16},{24,28},{28,24},{1,5},{5... | collective-permute-start | bytes 1769480 | tf_op jit(solution)/shard_map/ppermute | solution.py:32
  103.2 1.3 collective-permute-start.22
  104.5 1.3 collective-permute-start.23
  108.1 3.7 %collective-permute-done.26.refs_3_ = bf16[256,1152]{1,0:T(8,128)(2,1)S(1)} collective-permute-done((bf16[256,1152]{1,0:T(8,128)(2,1)S(1)}, bf16[256,1152]{1,0:T(8,128)(2,1)S(1)}, u32[]{:S(2)}, u32[]{:S(2)}) %collective-permute-start.26) | collective-permute-done | bytes 589856 | tf_op jit(solution)/shard_map/ppermute | solution.py:32
  112.0 4.5 %collective-permute-done.25.refs_3_ = bf16[256,1152]{1,0:T(8,128)(2,1)S(1)} collective-permute-done((bf16[256,1152]{1,0:T(8,128)(2,1)S(1)}, bf16[256,1152]{1,0:T(8,128)(2,1)S(1)}, u32[]{:S(2)}, u32[]{:S(2)}) %collective-permute-start.25) | collective-permute-done | bytes 589856 | tf_op jit(solution)/shard_map/ppermute | solution.py:32
  116.5 0.9 up_grad.1
  118.5 2.8 %collective-permute-start.30 = (bf16[256,1024]{1,0:T(8,128)(2,1)S(1)}, bf16[256,1024]{1,0:T(8,128)(2,1)S(1)}, u32[]{:S(2)}, u32[]{:S(2)}) collective-permute-start(bf16[256,1024]{1,0:T(8,128)(2,1)S(1)} %get-tuple-element.160.refs_6_.refs_10_), channel_id=1, source_target_pairs={{0,4},{4,0},{8,12},{12,8},{16,20},{20,16},{24,28},{28,24},{1,5},{5... | collective-permute-start | bytes 1572872 | tf_op jit(solution)/shard_map/ppermute | solution.py:32
  122.2 2.7 %collective-permute-start.32 = (bf16[128,2304]{1,0:T(8,128)(2,1)S(1)}, bf16[128,2304]{1,0:T(8,128)(2,1)S(1)}, u32[]{:S(2)}, u32[]{:S(2)}) collective-permute-start(bf16[128,2304]{1,0:T(8,128)(2,1)S(1)} %get-tuple-element.146.refs_4_), channel_id=1, source_target_pairs={{0,16},{4,20},{8,24},{12,28},{16,0},{20,4},{24,8},{28,12},{1,17},{... | collective-permute-start | bytes 1769480 | tf_op jit(solution)/shard_map/ppermute | solution.py:32
  124.9 17.4 %collective-permute-done.29.refs_8_.refs_3_.refs_5_.refs_9_ = bf16[256,768]{1,0:T(8,128)(2,1)S(1)} collective-permute-done((bf16[256,768]{1,0:T(8,128)(2,1)S(1)}, bf16[256,768]{1,0:T(8,128)(2,1)S(1)}, u32[]{:S(2)}, u32[]{:S(2)}) %collective-permute-start.29) | collective-permute-done | bytes 393248 | tf_op jit(solution)/shard_map/ppermute | solution.py:32
  142.2 1.0 outputs.1
  144.0 1.8 %collective-permute-start.34 = (f32[18,128]{1,0:T(8,128)S(1)}, f32[18,128]{1,0:T(8,128)S(1)}, u32[]{:S(2)}, u32[]{:S(2)}) collective-permute-start(f32[18,128]{1,0:T(8,128)S(1)} %get-tuple-element.162.refs_12_.refs_0_), channel_id=1, source_target_pairs={{0,4},{4,0},{8,12},{12,8},{16,20},{20,16},{24,28},{28,24},{1,5},{5... | collective-permute-start | bytes 27656 | tf_op jit(solution)/shard_map/ppermute | solution.py:32
  145.9 1.9 %collective-permute-done.34.refs_1_ = f32[18,128]{1,0:T(8,128)S(1)} collective-permute-done((f32[18,128]{1,0:T(8,128)S(1)}, f32[18,128]{1,0:T(8,128)S(1)}, u32[]{:S(2)}, u32[]{:S(2)}) %collective-permute-start.34) | collective-permute-done | bytes 9248 | tf_op jit(solution)/shard_map/ppermute | solution.py:32
  147.8 1.1 collective-permute-done.33.refs_1_
  149.1 1.4 collective-permute-start.38
  150.5 1.0 collective-permute-start.36
  151.5 1.3 first_last.1
  152.8 11.6 %collective-permute-done.36.refs_1_ = f32[18,128]{1,0:T(8,128)S(1)} collective-permute-done((f32[18,128]{1,0:T(8,128)S(1)}, f32[18,128]{1,0:T(8,128)S(1)}, u32[]{:S(2)}, u32[]{:S(2)}) %collective-permute-start.36) | collective-permute-done | bytes 9248 | tf_op jit(solution)/shard_map/ppermute | solution.py:32
  165.2 2.2 %collective-permute-start.35 = (bf16[128,768]{1,0:T(8,128)(2,1)S(1)}, bf16[128,768]{1,0:T(8,128)(2,1)S(1)}, u32[]{:S(2)}, u32[]{:S(2)}) collective-permute-start(bf16[128,768]{1,0:T(8,128)(2,1)S(1)} %get-tuple-element.171.refs_2_), channel_id=1, source_target_pairs={{0,16},{4,20},{8,24},{12,28},{16,0},{20,4},{24,8},{28,12},{1,17},{... | collective-permute-start | bytes 589832 | tf_op jit(solution)/shard_map/ppermute | solution.py:32
  168.3 4.9 %collective-permute-done.37.refs_1_ = f32[18,128]{1,0:T(8,128)S(1)} collective-permute-done((f32[18,128]{1,0:T(8,128)S(1)}, f32[18,128]{1,0:T(8,128)S(1)}, u32[]{:S(2)}, u32[]{:S(2)}) %collective-permute-start.37) | collective-permute-done | bytes 9248 | tf_op jit(solution)/shard_map/ppermute | solution.py:32
  174.5 2.4 %collective-permute-done.35.refs_1_ = bf16[128,768]{1,0:T(8,128)(2,1)S(1)} collective-permute-done((bf16[128,768]{1,0:T(8,128)(2,1)S(1)}, bf16[128,768]{1,0:T(8,128)(2,1)S(1)}, u32[]{:S(2)}, u32[]{:S(2)}) %collective-permute-start.35) | collective-permute-done | bytes 196640 | tf_op jit(solution)/shard_map/ppermute | solution.py:32
  (100 shorter events, 16.0 us)
Async XLA Ops:
  0.6 37.0 %copy-start.4 = (bf16[256,1024]{1,0:T(8,128)(2,1)S(1)}, bf16[256,1024]{1,0:T(8,128)(2,1)}, u32[]{:S(2)}) copy-start(bf16[256,1024]{1,0:T(8,128)(2,1)} %refs_5_.3) | copy-start | bytes 1572868
  0.7 6.7 %collective-permute-start.1 = (bf16[64,1024]{1,0:T(8,128)(2,1)}, bf16[64,1024]{1,0:T(8,128)(2,1)S(1)}, u32[]{:S(2)}, u32[]{:S(2)}) collective-permute-start(bf16[64,1024]{1,0:T(8,128)(2,1)} %refs_0_.5), channel_id=1, source_target_pairs={{0,2},{1,3},{2,0},{3,1},{4,6},{5,7},{6,4},{7,5},{8,10},{9,11},{10,... | collective-permute-start | bytes 393224 | tf_op jit(solution)/shard_map/ppermute | solution.py:32
  3.7 5.5 %collective-permute-start.2 = (bf16[64,1024]{1,0:T(8,128)(2,1)}, bf16[64,1024]{1,0:T(8,128)(2,1)S(1)}, u32[]{:S(2)}, u32[]{:S(2)}) collective-permute-start(bf16[64,1024]{1,0:T(8,128)(2,1)} %refs_0_.5), channel_id=1, source_target_pairs={{0,1},{1,0},{2,3},{3,2},{4,5},{5,4},{6,7},{7,6},{8,9},{9,8},{10,11... | collective-permute-start | bytes 393224 | tf_op jit(solution)/shard_map/ppermute | solution.py:32
  7.4 1.8 %collective-permute-start.3 = (bf16[64,1024]{1,0:T(8,128)(2,1)S(1)}, bf16[64,1024]{1,0:T(8,128)(2,1)S(1)}, u32[]{:S(2)}, u32[]{:S(2)}) collective-permute-start(bf16[64,1024]{1,0:T(8,128)(2,1)S(1)} %collective-permute-done.1.x1.refs_1_.refs_8_), channel_id=1, source_target_pairs={{0,1},{1,0},{2,3},{3,2},{4,5},{5,4},{6,7},{7,6},{8,9},{9,8},{10,11... | collective-permute-start | bytes 393224 | tf_op jit(solution)/shard_map/ppermute | solution.py:32
  7.4 12.2 %collective-permute-start = (bf16[64,1024]{1,0:T(8,128)(2,1)}, bf16[64,1024]{1,0:T(8,128)(2,1)S(1)}, u32[]{:S(2)}, u32[]{:S(2)}) collective-permute-start(bf16[64,1024]{1,0:T(8,128)(2,1)} %refs_0_.3), channel_id=1, source_target_pairs={{0,4},{4,0},{8,12},{12,8},{16,20},{20,16},{24,28},{28,24},{1,5},{5... | collective-permute-start | bytes 393224 | tf_op jit(solution)/shard_map/ppermute | solution.py:32
  12.7 6.8 %copy-start.9 = (bf16[64,1024]{1,0:T(8,128)(2,1)S(1)}, bf16[64,1024]{1,0:T(8,128)(2,1)}, u32[]{:S(2)}) copy-start(bf16[64,1024]{1,0:T(8,128)(2,1)} %refs_0_.3) | copy-start | bytes 393220
  16.0 13.0 %collective-permute-start.7 = (bf16[256,256]{1,0:T(8,128)(2,1)S(1)}, bf16[256,256]{1,0:T(8,128)(2,1)S(1)}, u32[]{:S(2)}, u32[]{:S(2)}) collective-permute-start(bf16[256,256]{1,0:T(8,128)(2,1)S(1)} %get-tuple-element.97.refs_2_.refs_4_.refs_10_), channel_id=1, source_target_pairs={{0,8},{4,12},{8,16},{12,20},{16,24},{20,28},{1,9},{5,13},{9,17},{1... | collective-permute-start | bytes 393224 | tf_op jit(solution)/shard_map/ppermute | solution.py:723
  19.6 13.1 %collective-permute-start.4 = (bf16[64,2048]{1,0:T(8,128)(2,1)S(1)}, bf16[64,2048]{1,0:T(8,128)(2,1)S(1)}, u32[]{:S(2)}, u32[]{:S(2)}) collective-permute-start(bf16[64,2048]{1,0:T(8,128)(2,1)S(1)} %pack.1.refs_0_), channel_id=1, source_target_pairs={{0,2},{1,3},{2,0},{3,1},{4,6},{5,7},{6,4},{7,5},{8,10},{9,11},{10,... | collective-permute-start | bytes 786440 | tf_op jit(solution)/shard_map/ppermute | solution.py:32
  21.1 11.6 %collective-permute-start.5 = (bf16[64,2048]{1,0:T(8,128)(2,1)S(1)}, bf16[64,2048]{1,0:T(8,128)(2,1)S(1)}, u32[]{:S(2)}, u32[]{:S(2)}) collective-permute-start(bf16[64,2048]{1,0:T(8,128)(2,1)S(1)} %pack.1.refs_0_), channel_id=1, source_target_pairs={{0,1},{1,0},{2,3},{3,2},{4,5},{5,4},{6,7},{7,6},{8,9},{9,8},{10,11... | collective-permute-start | bytes 786440 | tf_op jit(solution)/shard_map/ppermute | solution.py:32
  21.1 8.0 %collective-permute-start.8 = (bf16[256,256]{1,0:T(8,128)(2,1)S(1)}, bf16[256,256]{1,0:T(8,128)(2,1)S(1)}, u32[]{:S(2)}, u32[]{:S(2)}) collective-permute-start(bf16[256,256]{1,0:T(8,128)(2,1)S(1)} %get-tuple-element.97.refs_2_.refs_4_.refs_10_), channel_id=1, source_target_pairs={{0,16},{4,20},{8,24},{12,28},{1,17},{5,21},{9,25},{13,29},{2,18},{... | collective-permute-start | bytes 393224 | tf_op jit(solution)/shard_map/ppermute | solution.py:723
  25.6 7.1 %collective-permute-start.9 = (bf16[256,256]{1,0:T(8,128)(2,1)S(1)}, bf16[256,256]{1,0:T(8,128)(2,1)S(1)}, u32[]{:S(2)}, u32[]{:S(2)}) collective-permute-start(bf16[256,256]{1,0:T(8,128)(2,1)S(1)} %get-tuple-element.97.refs_2_.refs_4_.refs_10_), channel_id=1, source_target_pairs={{0,4},{8,12},{16,20},{24,28},{4,24},{1,5},{9,13},{17,21},{25,29},{... | collective-permute-start | bytes 393224 | tf_op jit(solution)/shard_map/ppermute | solution.py:729
  29.1 6.4 %collective-permute-start.10 = (bf16[256,256]{1,0:T(8,128)(2,1)S(1)}, bf16[256,256]{1,0:T(8,128)(2,1)S(1)}, u32[]{:S(2)}, u32[]{:S(2)}) collective-permute-start(bf16[256,256]{1,0:T(8,128)(2,1)S(1)} %collective-permute-done.7.refs_5_.refs_12_), channel_id=1, source_target_pairs={{0,4},{4,0},{8,12},{12,8},{16,20},{20,16},{24,28},{28,24},{1,5},{5... | collective-permute-start | bytes 393224 | tf_op jit(solution)/shard_map/ppermute | solution.py:32
  29.2 8.5 %collective-permute-start.11 = (bf16[256,256]{1,0:T(8,128)(2,1)S(1)}, bf16[256,256]{1,0:T(8,128)(2,1)S(1)}, u32[]{:S(2)}, u32[]{:S(2)}) collective-permute-start(bf16[256,256]{1,0:T(8,128)(2,1)S(1)} %collective-permute-done.8.refs_6_.refs_14_), channel_id=1, source_target_pairs={{0,4},{4,0},{8,12},{12,8},{16,20},{20,16},{24,28},{28,24},{1,5},{5... | collective-permute-start | bytes 393224 | tf_op jit(solution)/shard_map/ppermute | solution.py:32
  37.6 5.7 %copy-start = (bf16[1152,1024]{1,0:T(8,128)(2,1)S(1)}, bf16[1152,1024]{1,0:T(8,128)(2,1)}, u32[]{:S(2)}) copy-start(bf16[1152,1024]{1,0:T(8,128)(2,1)} %refs_1_.1) | copy-start | bytes 7077892
  41.0 1.6 collective-permute-start.12
  41.1 2.2 %collective-permute-start.6 = (bf16[64,2048]{1,0:T(8,128)(2,1)S(1)}, bf16[64,2048]{1,0:T(8,128)(2,1)S(1)}, u32[]{:S(2)}, u32[]{:S(2)}) collective-permute-start(bf16[64,2048]{1,0:T(8,128)(2,1)S(1)} %collective-permute-done.4.refs_10_.refs_1_), channel_id=1, source_target_pairs={{0,1},{1,0},{2,3},{3,2},{4,5},{5,4},{6,7},{7,6},{8,9},{9,8},{10,11... | collective-permute-start | bytes 786440 | tf_op jit(solution)/shard_map/ppermute | solution.py:32
  42.7 8.4 %collective-permute-start.13 = (bf16[128,1024]{1,0:T(8,128)(2,1)S(1)}, bf16[128,1024]{1,0:T(8,128)(2,1)S(1)}, u32[]{:S(2)}, u32[]{:S(2)}) collective-permute-start(bf16[128,1024]{1,0:T(8,128)(2,1)S(1)} %resid_core.1.refs_5_.refs_0_), channel_id=1, source_target_pairs={{0,2},{1,3},{2,0},{3,1},{4,6},{5,7},{6,4},{7,5},{8,10},{9,11},{10,... | collective-permute-start | bytes 786440 | tf_op jit(solution)/shard_map/ppermute | solution.py:32
  43.3 9.5 %copy-start.1 = (bf16[1024,1152]{1,0:T(8,128)(2,1)S(1)}, bf16[1024,1152]{1,0:T(8,128)(2,1)}, u32[]{:S(2)}) copy-start(bf16[1024,1152]{1,0:T(8,128)(2,1)} %refs_7_.2) | copy-start | bytes 7077892
  43.3 9.5 %copy-start.2 = (bf16[1024,1152]{1,0:T(8,128)(2,1)S(1)}, bf16[1024,1152]{1,0:T(8,128)(2,1)}, u32[]{:S(2)}) copy-start(bf16[1024,1152]{1,0:T(8,128)(2,1)} %refs_8_.1) | copy-start | bytes 7077892
  44.2 8.5 %copy-start.10 = (f32[1024]{0:T(1024)S(1)}, f32[1024]{0:T(1024)}, u32[]{:S(2)}) copy-start(f32[1024]{0:T(1024)} %param.23) | copy-start | bytes 12292
  51.2 1.6 collective-permute-start.14
  58.0 2.7 %collective-permute-start.15 = (bf16[128,1024]{1,0:T(8,128)(2,1)S(1)}, bf16[128,1024]{1,0:T(8,128)(2,1)S(1)}, u32[]{:S(2)}, u32[]{:S(2)}) collective-permute-start(bf16[128,1024]{1,0:T(8,128)(2,1)S(1)} %get-tuple-element.107), channel_id=1, source_target_pairs={{0,1},{1,0},{2,3},{3,2},{4,5},{5,4},{6,7},{7,6},{8,9},{9,8},{10,11... | collective-permute-start | bytes 786440 | tf_op jit(solution)/shard_map/ppermute | solution.py:32
  58.2 16.7 %collective-permute-start.18 = (bf16[256,1152]{1,0:T(8,128)(2,1)S(1)}, bf16[256,1152]{1,0:T(8,128)(2,1)S(1)}, u32[]{:S(2)}, u32[]{:S(2)}) collective-permute-start(bf16[256,1152]{1,0:T(8,128)(2,1)S(1)} %get-tuple-element.117.refs_2_.refs_0_), channel_id=1, source_target_pairs={{0,4},{4,0},{8,12},{12,8},{16,20},{20,16},{24,28},{28,24},{1,5},{5... | collective-permute-start | bytes 1769480 | tf_op jit(solution)/shard_map/ppermute | solution.py:32
  60.7 8.4 %collective-permute-start.16 = (bf16[128,1024]{1,0:T(8,128)(2,1)S(1)}, bf16[128,1024]{1,0:T(8,128)(2,1)S(1)}, u32[]{:S(2)}, u32[]{:S(2)}) collective-permute-start(bf16[128,1024]{1,0:T(8,128)(2,1)S(1)} %get-tuple-element.109.refs_0_), channel_id=1, source_target_pairs={{0,2},{1,3},{2,0},{3,1},{4,6},{5,7},{6,4},{7,5},{8,10},{9,11},{10,... | collective-permute-start | bytes 786440 | tf_op jit(solution)/shard_map/ppermute | solution.py:32
  61.3 31.8 %collective-permute-start.20 = (bf16[256,1664]{1,0:T(8,128)(2,1)S(1)}, bf16[256,1664]{1,0:T(8,128)(2,1)S(1)}, u32[]{:S(2)}, u32[]{:S(2)}) collective-permute-start(bf16[256,1664]{1,0:T(8,128)(2,1)S(1)} %get-tuple-element.130.refs_2_), channel_id=1, source_target_pairs={{0,4},{4,0},{8,12},{12,8},{16,20},{20,16},{24,28},{28,24},{1,5},{5... | collective-permute-start | bytes 2555912 | tf_op jit(solution)/shard_map/ppermute | solution.py:32
  69.2 6.9 %collective-permute-start.17 = (bf16[128,1024]{1,0:T(8,128)(2,1)S(1)}, bf16[128,1024]{1,0:T(8,128)(2,1)S(1)}, u32[]{:S(2)}, u32[]{:S(2)}) collective-permute-start(bf16[128,1024]{1,0:T(8,128)(2,1)S(1)} %grad_act_chip.1.refs_4_.refs_2_), channel_id=1, source_target_pairs={{0,1},{1,0},{2,3},{3,2},{4,5},{5,4},{6,7},{7,6},{8,9},{9,8},{10,11... | collective-permute-start | bytes 786440 | tf_op jit(solution)/shard_map/ppermute | solution.py:32
  75.8 17.3 %collective-permute-start.21 = (bf16[256,1152]{1,0:T(8,128)(2,1)S(1)}, bf16[256,1152]{1,0:T(8,128)(2,1)S(1)}, u32[]{:S(2)}, u32[]{:S(2)}) collective-permute-start(bf16[256,1152]{1,0:T(8,128)(2,1)S(1)} %get-tuple-element.118.refs_16_), channel_id=1, source_target_pairs={{0,8},{4,12},{8,0},{12,4},{16,24},{20,28},{24,16},{28,20},{1,9},{5... | collective-permute-start | bytes 1769480 | tf_op jit(solution)/shard_map/ppermute | solution.py:32
  82.6 18.6 %collective-permute-start.19 = (bf16[768,256]{1,0:T(8,128)(2,1)S(1)}, bf16[768,256]{1,0:T(8,128)(2,1)S(1)}, u32[]{:S(2)}, u32[]{:S(2)}) collective-permute-start(bf16[768,256]{1,0:T(8,128)(2,1)S(1)} %get-tuple-element.128), channel_id=1, source_target_pairs={{0,4},{4,0},{8,12},{12,8},{16,20},{20,16},{24,28},{28,24},{1,5},{5... | collective-permute-start | bytes 1179656 | tf_op jit(solution)/shard_map/ppermute | solution.py:32
  94.0 12.4 %copy-start.5 = (bf16[1024,256]{1,0:T(8,128)(2,1)S(1)}, bf16[1024,256]{1,0:T(8,128)(2,1)}, u32[]{:S(2)}) copy-start(bf16[1024,256]{1,0:T(8,128)(2,1)} %refs_5_.4) | copy-start | bytes 1572868
  94.0 12.4 %copy-start.14 = (f32[64]{0:T(128)S(1)}, f32[64]{0:T(128)}, u32[]{:S(2)}) copy-start(f32[64]{0:T(128)} %param.21) | copy-start | bytes 772
  94.1 17.7 %collective-permute-start.26 = (bf16[256,1152]{1,0:T(8,128)(2,1)S(1)}, bf16[256,1152]{1,0:T(8,128)(2,1)S(1)}, u32[]{:S(2)}, u32[]{:S(2)}) collective-permute-start(bf16[256,1152]{1,0:T(8,128)(2,1)S(1)} %get-tuple-element.131.refs_4_), channel_id=1, source_target_pairs={{0,8},{4,12},{8,0},{12,4},{16,24},{20,28},{24,16},{28,20},{1,9},{5... | collective-permute-start | bytes 1769480 | tf_op jit(solution)/shard_map/ppermute | solution.py:32
  101.4 15.1 %collective-permute-start.25 = (bf16[256,1152]{1,0:T(8,128)(2,1)S(1)}, bf16[256,1152]{1,0:T(8,128)(2,1)S(1)}, u32[]{:S(2)}, u32[]{:S(2)}) collective-permute-start(bf16[256,1152]{1,0:T(8,128)(2,1)S(1)} %get-tuple-element.143.refs_2_), channel_id=1, source_target_pairs={{0,4},{4,0},{8,12},{12,8},{16,20},{20,16},{24,28},{28,24},{1,5},{5... | collective-permute-start | bytes 1769480 | tf_op jit(solution)/shard_map/ppermute | solution.py:32
  103.2 14.2 %collective-permute-start.22 = (bf16[256,256]{1,0:T(8,128)(2,1)S(1)}, bf16[256,256]{1,0:T(8,128)(2,1)S(1)}, u32[]{:S(2)}, u32[]{:S(2)}) collective-permute-start(bf16[256,256]{1,0:T(8,128)(2,1)S(1)} %get-tuple-element.140), channel_id=1, source_target_pairs={{16,0},{20,4},{24,8},{28,12},{17,1},{21,5},{25,9},{29,13},{18,2},{... | collective-permute-start | bytes 393224 | tf_op jit(solution)/shard_map/ppermute | solution.py:42
  104.5 13.0 %collective-permute-start.23 = (bf16[256,256]{1,0:T(8,128)(2,1)S(1)}, bf16[256,256]{1,0:T(8,128)(2,1)S(1)}, u32[]{:S(2)}, u32[]{:S(2)}) collective-permute-start(bf16[256,256]{1,0:T(8,128)(2,1)S(1)} %get-tuple-element.141), channel_id=1, source_target_pairs={{8,0},{12,4},{16,8},{20,12},{24,16},{28,20},{9,1},{13,5},{17,9},{2... | collective-permute-start | bytes 393224 | tf_op jit(solution)/shard_map/ppermute | solution.py:42
  105.8 11.7 %collective-permute-start.24 = (bf16[256,256]{1,0:T(8,128)(2,1)S(1)}, bf16[256,256]{1,0:T(8,128)(2,1)S(1)}, u32[]{:S(2)}, u32[]{:S(2)}) collective-permute-start(bf16[256,256]{1,0:T(8,128)(2,1)S(1)} %get-tuple-element.142), channel_id=1, source_target_pairs={{28,4},{29,5},{30,6},{31,7}} | collective-permute-start | bytes 393224 | tf_op jit(solution)/shard_map/ppermute | solution.py:839
  118.4 23.9 %copy-start.12 = (f32[1024]{0:T(1024)S(1)}, f32[1024]{0:T(1024)}, u32[]{:S(2)}) copy-start(f32[1024]{0:T(1024)} %param.16) | copy-start | bytes 12292
  118.4 3.1 %collective-permute-start.27 = (bf16[272,1024]{1,0:T(8,128)(2,1)S(1)}, bf16[272,1024]{1,0:T(8,128)(2,1)S(1)}, u32[]{:S(2)}, u32[]{:S(2)}) collective-permute-start(bf16[272,1024]{1,0:T(8,128)(2,1)S(1)} %get-tuple-element.151), channel_id=1, source_target_pairs={{0,1},{1,0},{2,3},{3,2},{4,5},{5,4},{6,7},{7,6},{8,9},{9,8},{10,11... | collective-permute-start | bytes 1671176 | tf_op jit(solution)/shard_map/ppermute | solution.py:32
  118.5 24.8 %collective-permute-start.30 = (bf16[256,1024]{1,0:T(8,128)(2,1)S(1)}, bf16[256,1024]{1,0:T(8,128)(2,1)S(1)}, u32[]{:S(2)}, u32[]{:S(2)}) collective-permute-start(bf16[256,1024]{1,0:T(8,128)(2,1)S(1)} %get-tuple-element.160.refs_6_.refs_10_), channel_id=1, source_target_pairs={{0,4},{4,0},{8,12},{12,8},{16,20},{20,16},{24,28},{28,24},{1,5},{5... | collective-permute-start | bytes 1572872 | tf_op jit(solution)/shard_map/ppermute | solution.py:32
  121.3 27.7 %collective-permute-start.33 = (bf16[256,1152]{1,0:T(8,128)(2,1)S(1)}, bf16[256,1152]{1,0:T(8,128)(2,1)S(1)}, u32[]{:S(2)}, u32[]{:S(2)}) collective-permute-start(bf16[256,1152]{1,0:T(8,128)(2,1)S(1)} %get-tuple-element.147.refs_20_), channel_id=1, source_target_pairs={{0,8},{4,12},{8,0},{12,4},{16,24},{20,28},{24,16},{28,20},{1,9},{5... | collective-permute-start | bytes 1769480 | tf_op jit(solution)/shard_map/ppermute | solution.py:32
  121.3 20.9 %collective-permute-start.29 = (bf16[256,768]{1,0:T(8,128)(2,1)S(1)}, bf16[256,768]{1,0:T(8,128)(2,1)S(1)}, u32[]{:S(2)}, u32[]{:S(2)}) collective-permute-start(bf16[256,768]{1,0:T(8,128)(2,1)S(1)} %get-tuple-element.156.refs_2_), channel_id=1, source_target_pairs={{0,4},{4,0},{8,12},{12,8},{16,20},{20,16},{24,28},{28,24},{1,5},{5... | collective-permute-start | bytes 1179656 | tf_op jit(solution)/shard_map/ppermute | solution.py:32
  121.6 20.6 %collective-permute-start.28 = (bf16[144,1024]{1,0:T(8,128)(2,1)S(1)}, bf16[144,1024]{1,0:T(8,128)(2,1)S(1)}, u32[]{:S(2)}, u32[]{:S(2)}) collective-permute-start(bf16[144,1024]{1,0:T(8,128)(2,1)S(1)} %get-tuple-element.155), channel_id=1, source_target_pairs={{0,2},{1,3},{2,0},{3,1},{4,6},{5,7},{6,4},{7,5},{8,10},{9,11},{10,... | collective-permute-start | bytes 884744 | tf_op jit(solution)/shard_map/ppermute | solution.py:32
  122.2 29.3 %collective-permute-start.32 = (bf16[128,2304]{1,0:T(8,128)(2,1)S(1)}, bf16[128,2304]{1,0:T(8,128)(2,1)S(1)}, u32[]{:S(2)}, u32[]{:S(2)}) collective-permute-start(bf16[128,2304]{1,0:T(8,128)(2,1)S(1)} %get-tuple-element.146.refs_4_), channel_id=1, source_target_pairs={{0,16},{4,20},{8,24},{12,28},{16,0},{20,4},{24,8},{28,12},{1,17},{... | collective-permute-start | bytes 1769480 | tf_op jit(solution)/shard_map/ppermute | solution.py:32
  144.0 21.2 %collective-permute-start.31 = (bf16[256,768]{1,0:T(8,128)(2,1)S(1)}, bf16[256,768]{1,0:T(8,128)(2,1)S(1)}, u32[]{:S(2)}, u32[]{:S(2)}) collective-permute-start(bf16[256,768]{1,0:T(8,128)(2,1)S(1)} %get-tuple-element.164.refs_2_), channel_id=1, source_target_pairs={{0,8},{4,12},{8,0},{12,4},{16,24},{20,28},{24,16},{28,20},{1,9},{5... | collective-permute-start | bytes 1179656 | tf_op jit(solution)/shard_map/ppermute | solution.py:32
  144.0 3.8 %collective-permute-start.34 = (f32[18,128]{1,0:T(8,128)S(1)}, f32[18,128]{1,0:T(8,128)S(1)}, u32[]{:S(2)}, u32[]{:S(2)}) collective-permute-start(f32[18,128]{1,0:T(8,128)S(1)} %get-tuple-element.162.refs_12_.refs_0_), channel_id=1, source_target_pairs={{0,4},{4,0},{8,12},{12,8},{16,20},{20,16},{24,28},{28,24},{1,5},{5... | collective-permute-start | bytes 27656 | tf_op jit(solution)/shard_map/ppermute | solution.py:32
  149.1 18.3 %collective-permute-start.38 = (bf16[128,1152]{1,0:T(8,128)(2,1)S(1)}, bf16[128,1152]{1,0:T(8,128)(2,1)S(1)}, u32[]{:S(2)}, u32[]{:S(2)}) collective-permute-start(bf16[128,1152]{1,0:T(8,128)(2,1)S(1)} %get-tuple-element.168.refs_3_), channel_id=1, source_target_pairs={{0,16},{4,20},{8,24},{12,28},{16,0},{20,4},{24,8},{28,12},{1,17},{... | collective-permute-start | bytes 884744 | tf_op jit(solution)/shard_map/ppermute | solution.py:32
  150.5 13.8 %collective-permute-start.36 = (f32[18,128]{1,0:T(8,128)S(1)}, f32[18,128]{1,0:T(8,128)S(1)}, u32[]{:S(2)}, u32[]{:S(2)}) collective-permute-start(f32[18,128]{1,0:T(8,128)S(1)} %gains.3.refs_2_.refs_0_), channel_id=1, source_target_pairs={{0,8},{4,12},{8,0},{12,4},{16,24},{20,28},{24,16},{28,20},{1,9},{5... | collective-permute-start | bytes 27656 | tf_op jit(solution)/shard_map/ppermute | solution.py:32
  164.3 8.9 %collective-permute-start.37 = (f32[18,128]{1,0:T(8,128)S(1)}, f32[18,128]{1,0:T(8,128)S(1)}, u32[]{:S(2)}, u32[]{:S(2)}) collective-permute-start(f32[18,128]{1,0:T(8,128)S(1)} %gains.4.refs_0_), channel_id=1, source_target_pairs={{0,16},{4,20},{8,24},{12,28},{16,0},{20,4},{24,8},{28,12},{1,17},{... | collective-permute-start | bytes 27656 | tf_op jit(solution)/shard_map/ppermute | solution.py:32
  165.2 11.6 %collective-permute-start.35 = (bf16[128,768]{1,0:T(8,128)(2,1)S(1)}, bf16[128,768]{1,0:T(8,128)(2,1)S(1)}, u32[]{:S(2)}, u32[]{:S(2)}) collective-permute-start(bf16[128,768]{1,0:T(8,128)(2,1)S(1)} %get-tuple-element.171.refs_2_), channel_id=1, source_target_pairs={{0,16},{4,20},{8,24},{12,28},{16,0},{20,4},{24,8},{28,12},{1,17},{... | collective-permute-start | bytes 589832 | tf_op jit(solution)/shard_map/ppermute | solution.py:32
  (9 other events, 7.6 us)

commit v5 on v4

--- a/solution.py
+++ b/solution.py
@@ -252,6 +252,19 @@
     sent_out[...] = dot(attn_b[half:], wo[...]).astype(BF)
 
 
+def piece_kernel(packet, out):
+    out[...] = packet[:, packet.shape[1] - 128 :]
+
+
+def join_kernel(p0, p1, p2, p3, out):
+    own = p0.shape[0] // 4
+    for quarter, piece in enumerate((p0, p1, p2, p3)):
+        for b in range(4):
+            out[quarter * own : (quarter + 1) * own, 128 * b : 128 * (b + 1)] = piece[
+                b * own : (b + 1) * own, :
+            ]
+
+
 def add_kernel(kept, arrived, out):
     out[...] = (kept[...].astype(F32) + arrived[...].astype(F32)).astype(out.dtype)
 
@@ -350,8 +363,9 @@
 
 def down_kernel(hidden, wd, kept_out, sent_out):
     half = hidden.shape[0] // 2
-    sent_out[...] = dot(hidden[half:, :], wd[...]).astype(BF)
-    kept_out[...] = dot(hidden[:half, :], wd[...])
+    columns = wd.shape[0]
+    sent_out[...] = dot(hidden[half:, :columns], wd[...]).astype(BF)
+    kept_out[...] = dot(hidden[:half, :columns], wd[...])
 
 
 def outputs_kernel(
@@ -374,7 +388,7 @@
 
 def ffn_kernel(
     ranks, x0, x1, x2, x3, half0, half1, gain, wg, wu, grad_hidden,
-    resid_out, act_out, hidden_out, gate_packet, grad_up_out, kept_out, sent_out,
+    resid_out, act_out, hidden_out, grad_gate_out, grad_up_out, kept_out, sent_out, select,
 ):
     x = jnp.concatenate([x0[...], x1[...], x2[...], x3[...]], axis=0).astype(F32)
     resid = x + jnp.concatenate([half0[...], half1[...]], axis=0).astype(F32)
@@ -384,13 +398,16 @@
     values = dot(act, wg[...])
     upper = dot(act, wu[...])
     sigmoid = jax.nn.sigmoid(values)
-    hidden_out[...] = (values * sigmoid * upper).astype(BF)
+    columns = values.shape[1]
+    hidden_out[:, :columns] = (values * sigmoid * upper).astype(BF)
     grads = grad_hidden[...]
     grad_gate = (grads * upper * sigmoid * (1.0 + values * (1.0 - sigmoid))).astype(BF)
     grad_up = (grads * values * sigmoid).astype(BF)
-    chosen = act.shape[1] // 2
-    select_columns(ranks, act_out, gate_packet.at[:, :chosen])
-    gate_packet[:, chosen:] = grad_gate
+    own = select.shape[0]
+    select_columns(ranks, act_out.at[:own, :], select)
+    for b in range(4):
+        hidden_out[b * own : (b + 1) * own, columns:] = select[:, 128 * b : 128 * (b + 1)]
+    grad_gate_out[...] = grad_gate
     grad_up_out[...] = grad_up
     half = resid.shape[0] // 2
     sent_out[...] = (
@@ -774,27 +791,31 @@
         after=[grad_hidden],
     )
 
-    resid, act_ffn, hidden, gate_packet, grad_up, kept, sent = launch(
+    resid, act_ffn, hidden, grad_gate, grad_up, kept, sent = launch(
         ffn_kernel,
         [
             shape((rows, width), F32),
             shape((rows, width), BF),
+            shape((rows, hidden_width + 128), BF),
             shape((rows, hidden_width), BF),
-            shape((rows, chosen + hidden_width), BF),
             shape((rows, hidden_width), BF),
             shape((half, width), F32),
             shape((half, width), BF),
         ],
         [RANKS, *x, both, xor(both, "mp", 1), ffn_gain_row, gate_weight, up_weight, grad_hidden],
+        scratch=[pltpu.VMEM((own_rows, chosen), BF)],
         name="ffn",
     )
     hidden_there = xor(hidden, "ctx", 1)
-    kept, gate_packet = add(kept, xor(sent, "mp", 1), BF, "grad_act_core", carry=[gate_packet])
-    gate_there = xor(gate_packet, "ctx", 1)
+    kept, grad_gate = add(kept, xor(sent, "mp", 1), BF, "grad_act_core", carry=[grad_gate])
+    gate_there = xor(grad_gate, "ctx", 1)
     both = add(kept, xor(kept, "mp", 2), BF, "grad_act_chip", kernel=flipped_add_kernel)
+    act_piece = launch(
+        piece_kernel, [shape((rows, 128), BF)], [hidden_there], name="piece", after=[both]
+    )[0]
     down_kept, down_sent = weight_grad(
         [(cot, cot_there, hidden, hidden_there, (0, 0), 0, hidden_width)], "down_grad",
-        after=[both],
+        after=[act_piece],
     )
 
     outs = launch(
@@ -818,8 +839,15 @@
 
     arrived = xor(odd_terms, "ctx", 1)
     down_arrived = xor(down_sent, "ctx", 2)
+    act_there = launch(
+        join_kernel,
+        [shape((rows, chosen), BF)],
+        mp_gather(act_piece),
+        name="join",
+        after=[grad_query],
+    )[0]
     gate_kept, gate_sent = weight_grad(
-        [(act_ffn, gate_there, gate_packet, gate_there, (chosen, chosen), 0, hidden_width)],
+        [(act_ffn, act_there, grad_gate, gate_there, (0, 0), 0, hidden_width)],
         "gate_grad",
         after=[grad_query, down_arrived],
     )
@@ -862,7 +890,7 @@
         after=[out_sent],
     )
     up_kept, up_sent = weight_grad(
-        [(act_ffn, gate_there, grad_up, up_there, (0, 0), 0, hidden_width)], "up_grad",
+        [(act_ffn, act_there, grad_up, up_there, (0, 0), 0, hidden_width)], "up_grad",
         after=[back],
     )
     late, gains, kept, sent = launch(

time: 178 us -> 176 us (0.989)
  waiting for transfers between devices: 94.4 us -> 91.7 us
    ppermute x33 -> x36, waiting for transfers between devices: 92.8 us -> 89.3 us  [xor(): return lax.ppermute(values, axis, [(i, i ^ mask) for i in range(n)])]
    ppermute x33 -> x36, starting transfers between devices: 32.5 us -> 33.5 us  [xor(): return lax.ppermute(values, axis, [(i, i ^ mask) for i in range(n)])]
    pallas_call x28 -> x30, Pallas kernels: 26.8 us -> 26.9 us  [launch(): pl.pallas_call(run, out_shape=list(outs) + [shape(c.shape, c.dtype) for c...]
  transfers between devices with their start and end apart: 39 -> 42, of which waited for: 19 -> 21; matrix products, arithmetic and copies ran while one was open for 1% -> 1% of each run, Pallas kernels for 11% -> 11%
where the time goes in v5:
time: 176 us
  waiting for transfers between devices  91.7 us (52%)
  starting transfers between devices  48.2 us (27%)
  Pallas kernels  30.2 us (17%)
  local copies, waits for them, and re-layouts  4.9 us (3%)
    ppermute x36, waiting for transfers between devices, xor(): return lax.ppermute(values, axis, [(i, i ^ mask) for i in range(n)])  89.3 us
    ppermute x36, starting transfers between devices, xor(): return lax.ppermute(values, axis, [(i, i ^ mask) for i in range(n)])  33.5 us
    pallas_call x30, Pallas kernels, launch(): pl.pallas_call(run, out_shape=list(outs) + [shape(c.shape, c.dtype) for c...  26.9 us
    ppermute x2, starting transfers between devices, climb(): return lax.ppermute(pair, 'ctx', pairs) if pairs else jnp.zeros_like(pair)  7.98 us
    unnamed x36, local copies, waits for them, and re-layouts  3.7 us
  transfers between devices with their start and end apart: 42, of which 21 were waited for; matrix products, arithmetic and copies ran while one was open for 1% of the time, Pallas kernels for 11%

profile of v5, /device:TPU:0, one launch (start us, length us, event | category | flops | bytes accessed | tf_op | source)
XLA Modules:
  0.0 176.1 jit_solution(17548135676214889975)
XLA Ops:
  0.7 3.0 %collective-permute-start.1 = (bf16[64,1024]{1,0:T(8,128)(2,1)}, bf16[64,1024]{1,0:T(8,128)(2,1)S(1)}, u32[]{:S(2)}, u32[]{:S(2)}) collective-permute-start(bf16[64,1024]{1,0:T(8,128)(2,1)} %refs_0_.5), channel_id=1, source_target_pairs={{0,2},{1,3},{2,0},{3,1},{4,6},{5,7},{6,4},{7,5},{8,10},{9,11},{10,... | collective-permute-start | bytes 393224 | tf_op jit(solution)/shard_map/ppermute | solution.py:32
  3.7 3.7 %collective-permute-done.1.x1.refs_1_.refs_8_ = bf16[64,1024]{1,0:T(8,128)(2,1)S(1)} collective-permute-done((bf16[64,1024]{1,0:T(8,128)(2,1)}, bf16[64,1024]{1,0:T(8,128)(2,1)S(1)}, u32[]{:S(2)}, u32[]{:S(2)}) %collective-permute-start.1) | collective-permute-done | bytes 131104 | tf_op jit(solution)/shard_map/ppermute | solution.py:32
  7.4 1.8 %collective-permute-start = (bf16[64,1024]{1,0:T(8,128)(2,1)}, bf16[64,1024]{1,0:T(8,128)(2,1)S(1)}, u32[]{:S(2)}, u32[]{:S(2)}) collective-permute-start(bf16[64,1024]{1,0:T(8,128)(2,1)} %refs_0_.3), channel_id=1, source_target_pairs={{0,4},{4,0},{8,12},{12,8},{16,20},{20,16},{24,28},{28,24},{1,5},{5... | collective-permute-start | bytes 393224 | tf_op jit(solution)/shard_map/ppermute | solution.py:32
  9.2 0.9 copy-done.6
  12.7 3.3 %qkv.1 = (bf16[256,1024]{1,0:T(8,128)(2,1)}, bf16[256,512]{1,0:T(8,128)(2,1)S(1)}, bf16[256,256]{1,0:T(8,128)(2,1)S(1)}, bf16[256,256]{1,0:T(8,128)(2,1)S(1)}, f...) custom-call(bf16[64,1024]{1,0:T(8,128)(2,1)S(1)} %collective-permute, ...), custom_call_target="tpu_custom_call" | custom-call | tf_op jit(solution)/shard_map/qkv/pallas_call | solution.py:726
  16.0 3.5 %collective-permute-start.7 = (bf16[256,256]{1,0:T(8,128)(2,1)S(1)}, bf16[256,256]{1,0:T(8,128)(2,1)S(1)}, u32[]{:S(2)}, u32[]{:S(2)}) collective-permute-start(bf16[256,256]{1,0:T(8,128)(2,1)S(1)} %get-tuple-element.97.refs_2_.refs_4_.refs_10_), channel_id=1, source_target_pairs={{0,8},{4,12},{8,16},{12,20},{16,24},{20,28},{1,9},{5,13},{9,17},{1... | collective-permute-start | bytes 393224 | tf_op jit(solution)/shard_map/ppermute | solution.py:740
  19.6 1.6 collective-permute-start.4
  21.1 4.5 %collective-permute-start.8 = (bf16[256,256]{1,0:T(8,128)(2,1)S(1)}, bf16[256,256]{1,0:T(8,128)(2,1)S(1)}, u32[]{:S(2)}, u32[]{:S(2)}) collective-permute-start(bf16[256,256]{1,0:T(8,128)(2,1)S(1)} %get-tuple-element.97.refs_2_.refs_4_.refs_10_), channel_id=1, source_target_pairs={{0,16},{4,20},{8,24},{12,28},{1,17},{5,21},{9,25},{13,29},{2,18},{... | collective-permute-start | bytes 393224 | tf_op jit(solution)/shard_map/ppermute | solution.py:740
  25.6 3.4 %collective-permute-start.9 = (bf16[256,256]{1,0:T(8,128)(2,1)S(1)}, bf16[256,256]{1,0:T(8,128)(2,1)S(1)}, u32[]{:S(2)}, u32[]{:S(2)}) collective-permute-start(bf16[256,256]{1,0:T(8,128)(2,1)S(1)} %get-tuple-element.97.refs_2_.refs_4_.refs_10_), channel_id=1, source_target_pairs={{0,4},{8,12},{16,20},{24,28},{4,24},{1,5},{9,13},{17,21},{25,29},{... | collective-permute-start | bytes 393224 | tf_op jit(solution)/shard_map/ppermute | solution.py:746
  29.2 2.0 %collective-permute-start.11 = (bf16[256,256]{1,0:T(8,128)(2,1)S(1)}, bf16[256,256]{1,0:T(8,128)(2,1)S(1)}, u32[]{:S(2)}, u32[]{:S(2)}) collective-permute-start(bf16[256,256]{1,0:T(8,128)(2,1)S(1)} %collective-permute-done.8.refs_6_.refs_14_), channel_id=1, source_target_pairs={{0,4},{4,0},{8,12},{12,8},{16,20},{20,16},{24,28},{28,24},{1,5},{5... | collective-permute-start | bytes 393224 | tf_op jit(solution)/shard_map/ppermute | solution.py:32
  31.2 1.5 collective-permute-done.9.refs_7_
  32.7 2.8 %collective-permute-done.10.refs_8_ = bf16[256,256]{1,0:T(8,128)(2,1)S(1)} collective-permute-done((bf16[256,256]{1,0:T(8,128)(2,1)S(1)}, bf16[256,256]{1,0:T(8,128)(2,1)S(1)}, u32[]{:S(2)}, u32[]{:S(2)}) %collective-permute-start.10) | collective-permute-done | bytes 131104 | tf_op jit(solution)/shard_map/ppermute | solution.py:32
  35.5 2.1 %collective-permute-done.11.refs_9_ = bf16[256,256]{1,0:T(8,128)(2,1)S(1)} collective-permute-done((bf16[256,256]{1,0:T(8,128)(2,1)S(1)}, bf16[256,256]{1,0:T(8,128)(2,1)S(1)}, u32[]{:S(2)}, u32[]{:S(2)}) %collective-permute-start.11) | collective-permute-done | bytes 131104 | tf_op jit(solution)/shard_map/ppermute | solution.py:32
  37.6 3.4 %attention.1 = (f32[256,256]{1,0:T(8,128)S(1)}, bf16[256,768]{1,0:T(8,128)(2,1)S(1)}, f32[2,512]{1,0:T(2,128)S(1)}, f32[128,1024]{1,0:T(8,128)S(1)}, bf16[128,10...) custom-call(bf16[256,256]{1,0:T(8,128)(2,1)S(1)} %get-tuple-element., ...), custom_call_target="tpu_custom_call" | custom-call | tf_op jit(solution)/shard_map/attention/pallas_call | solution.py:582
  41.6 1.0 collective-permute-done.12.refs_1_
  43.3 0.9 cotangent.1
  44.3 6.8 %collective-permute-done.13.refs_1_ = bf16[128,1024]{1,0:T(8,128)(2,1)S(1)} collective-permute-done((bf16[128,1024]{1,0:T(8,128)(2,1)S(1)}, bf16[128,1024]{1,0:T(8,128)(2,1)S(1)}, u32[]{:S(2)}, u32[]{:S(2)}) %collective-permute-start.13) | collective-permute-done | bytes 262176 | tf_op jit(solution)/shard_map/ppermute | solution.py:32
  51.2 1.5 collective-permute-done.14.refs_5_
  52.8 5.1 %ffn.1 = (f32[256,1024]{1,0:T(8,128)S(1)}, bf16[256,1024]{1,0:T(8,128)(2,1)S(1)}, bf16[256,1280]{1,0:T(8,128)(2,1)S(1)}, bf16[256,1152]{1,0:T(8,128)(2,1)S(1)}, ...) custom-call(bf16[64,1024]{1,0:T(8,128)(2,1)S(1)} %copy-done.6, ...), custom_call_target="tpu_custom_call" | custom-call | tf_op jit(solution)/shard_map/ffn/pallas_call | solution.py:582
  57.9 2.5 %collective-permute-start.18 = (bf16[256,1280]{1,0:T(8,128)(2,1)S(1)}, bf16[256,1280]{1,0:T(8,128)(2,1)S(1)}, u32[]{:S(2)}, u32[]{:S(2)}) collective-permute-start(bf16[256,1280]{1,0:T(8,128)(2,1)S(1)} %get-tuple-element.117.refs_2_.refs_0_), channel_id=1, source_target_pairs={{0,4},{4,0},{8,12},{12,8},{16,20},{20,16},{24,28},{28,24},{1,5},{5... | collective-permute-start | bytes 1966088 | tf_op jit(solution)/shard_map/ppermute | solution.py:32
  60.5 1.5 collective-permute-done.15.refs_1_
  62.7 7.8 %collective-permute-done.16.refs_1_ = bf16[128,1024]{1,0:T(8,128)(2,1)S(1)} collective-permute-done((bf16[128,1024]{1,0:T(8,128)(2,1)S(1)}, bf16[128,1024]{1,0:T(8,128)(2,1)S(1)}, u32[]{:S(2)}, u32[]{:S(2)}) %collective-permute-start.16) | collective-permute-done | bytes 262176 | tf_op jit(solution)/shard_map/ppermute | solution.py:32
  70.8 5.2 %collective-permute-done.18.refs_0_.refs_3_ = bf16[256,1280]{1,0:T(8,128)(2,1)S(1)} collective-permute-done((bf16[256,1280]{1,0:T(8,128)(2,1)S(1)}, bf16[256,1280]{1,0:T(8,128)(2,1)S(1)}, u32[]{:S(2)}, u32[]{:S(2)}) %collective-permute-start.18) | collective-permute-done | bytes 655392 | tf_op jit(solution)/shard_map/ppermute | solution.py:32
  76.0 0.9 down_grad.1
  77.2 6.6 %attention_backward.1 = (f32[64,1024]{1,0:T(8,128)S(1)}, bf16[256,1024]{1,0:T(8,128)(2,1)S(1)}, bf16[256,512]{1,0:T(8,128)(2,1)S(1)}, f32[1,1024]{1,0:T(1,128)S(...) custom-call(bf16[256,1024]{1,0:T(8,128)(2,1)S(1)} %get-tuple-element, ...), custom_call_target="tpu_custom_call" | custom-call | tf_op jit(solution)/shard_map/attention_backward/pallas_call | solution.py:582
  83.8 2.1 %collective-permute-start.19 = (bf16[768,256]{1,0:T(8,128)(2,1)S(1)}, bf16[768,256]{1,0:T(8,128)(2,1)S(1)}, u32[]{:S(2)}, u32[]{:S(2)}) collective-permute-start(bf16[768,256]{1,0:T(8,128)(2,1)S(1)} %get-tuple-element.128), channel_id=1, source_target_pairs={{0,4},{4,0},{8,12},{12,8},{16,20},{20,16},{24,28},{28,24},{1,5},{5... | collective-permute-start | bytes 1179656 | tf_op jit(solution)/shard_map/ppermute | solution.py:32
  86.5 3.7 %collective-permute-done.20.refs_1_ = bf16[256,128]{1,0:T(8,128)(2,1)S(1)} collective-permute-done((bf16[256,128]{1,0:T(8,128)(2,1)S(1)}, bf16[256,128]{1,0:T(8,128)(2,1)S(1)}, u32[]{:S(2)}, u32[]{:S(2)}) %collective-permute-start.20) | collective-permute-done | bytes 65568 | tf_op jit(solution)/shard_map/ppermute | solution.py:32
  90.2 1.2 collective-permute-done.22.refs_3_
  91.5 0.9 gate_grad.1
  92.5 1.9 %collective-permute-start.29 = (bf16[256,1152]{1,0:T(8,128)(2,1)S(1)}, bf16[256,1152]{1,0:T(8,128)(2,1)S(1)}, u32[]{:S(2)}, u32[]{:S(2)}) collective-permute-start(bf16[256,1152]{1,0:T(8,128)(2,1)S(1)} %get-tuple-element.131.refs_4_), channel_id=1, source_target_pairs={{0,8},{4,12},{8,0},{12,4},{16,24},{20,28},{24,16},{28,20},{1,9},{5... | collective-permute-start | bytes 1769480 | tf_op jit(solution)/shard_map/ppermute | solution.py:32
  94.3 2.2 %collective-permute-done.19.refs_3_ = bf16[768,256]{1,0:T(8,128)(2,1)S(1)} collective-permute-done((bf16[768,256]{1,0:T(8,128)(2,1)S(1)}, bf16[768,256]{1,0:T(8,128)(2,1)S(1)}, u32[]{:S(2)}, u32[]{:S(2)}) %collective-permute-start.19) | collective-permute-done | bytes 393248 | tf_op jit(solution)/shard_map/ppermute | solution.py:32
  96.7 1.8 %collective-permute-start.28 = (bf16[256,1152]{1,0:T(8,128)(2,1)S(1)}, bf16[256,1152]{1,0:T(8,128)(2,1)S(1)}, u32[]{:S(2)}, u32[]{:S(2)}) collective-permute-start(bf16[256,1152]{1,0:T(8,128)(2,1)S(1)} %get-tuple-element.143.refs_2_), channel_id=1, source_target_pairs={{0,4},{4,0},{8,12},{12,8},{16,20},{20,16},{24,28},{28,24},{1,5},{5... | collective-permute-start | bytes 1769480 | tf_op jit(solution)/shard_map/ppermute | solution.py:32
  98.5 1.3 collective-permute-start.25
  99.8 1.3 collective-permute-start.26
  103.4 8.1 %collective-permute-done.29.refs_3_ = bf16[256,1152]{1,0:T(8,128)(2,1)S(1)} collective-permute-done((bf16[256,1152]{1,0:T(8,128)(2,1)S(1)}, bf16[256,1152]{1,0:T(8,128)(2,1)S(1)}, u32[]{:S(2)}, u32[]{:S(2)}) %collective-permute-start.29) | collective-permute-done | bytes 589856 | tf_op jit(solution)/shard_map/ppermute | solution.py:32
  111.8 0.9 up_grad.1
  114.6 6.1 %collective-permute-start.33 = (bf16[256,1024]{1,0:T(8,128)(2,1)S(1)}, bf16[256,1024]{1,0:T(8,128)(2,1)S(1)}, u32[]{:S(2)}, u32[]{:S(2)}) collective-permute-start(bf16[256,1024]{1,0:T(8,128)(2,1)S(1)} %get-tuple-element.160.refs_6_.refs_10_), channel_id=1, source_target_pairs={{0,4},{4,0},{8,12},{12,8},{16,20},{20,16},{24,28},{28,24},{1,5},{5... | collective-permute-start | bytes 1572872 | tf_op jit(solution)/shard_map/ppermute | solution.py:32
  121.6 20.0 %collective-permute-done.32.refs_8_.refs_3_.refs_5_.refs_9_ = bf16[256,768]{1,0:T(8,128)(2,1)S(1)} collective-permute-done((bf16[256,768]{1,0:T(8,128)(2,1)S(1)}, bf16[256,768]{1,0:T(8,128)(2,1)S(1)}, u32[]{:S(2)}, u32[]{:S(2)}) %collective-permute-start.32) | collective-permute-done | bytes 393248 | tf_op jit(solution)/shard_map/ppermute | solution.py:32
  141.6 1.0 outputs.1
  143.4 1.8 %collective-permute-start.37 = (f32[18,128]{1,0:T(8,128)S(1)}, f32[18,128]{1,0:T(8,128)S(1)}, u32[]{:S(2)}, u32[]{:S(2)}) collective-permute-start(f32[18,128]{1,0:T(8,128)S(1)} %get-tuple-element.162.refs_12_.refs_0_), channel_id=1, source_target_pairs={{0,4},{4,0},{8,12},{12,8},{16,20},{20,16},{24,28},{28,24},{1,5},{5... | collective-permute-start | bytes 27656 | tf_op jit(solution)/shard_map/ppermute | solution.py:32
  145.2 1.9 %collective-permute-done.37.refs_1_ = f32[18,128]{1,0:T(8,128)S(1)} collective-permute-done((f32[18,128]{1,0:T(8,128)S(1)}, f32[18,128]{1,0:T(8,128)S(1)}, u32[]{:S(2)}, u32[]{:S(2)}) %collective-permute-start.37) | collective-permute-done | bytes 9248 | tf_op jit(solution)/shard_map/ppermute | solution.py:32
  147.4 2.0 %collective-permute-start.39 = (f32[18,128]{1,0:T(8,128)S(1)}, f32[18,128]{1,0:T(8,128)S(1)}, u32[]{:S(2)}, u32[]{:S(2)}) collective-permute-start(f32[18,128]{1,0:T(8,128)S(1)} %gains.3.refs_2_.refs_0_), channel_id=1, source_target_pairs={{0,8},{4,12},{8,0},{12,4},{16,24},{20,28},{24,16},{28,20},{1,9},{5... | collective-permute-start | bytes 27656 | tf_op jit(solution)/shard_map/ppermute | solution.py:32
  149.4 1.0 collective-permute-done.35.refs_2_
  150.4 1.3 first_last.1
  151.7 12.5 %collective-permute-done.39.refs_1_ = f32[18,128]{1,0:T(8,128)S(1)} collective-permute-done((f32[18,128]{1,0:T(8,128)S(1)}, f32[18,128]{1,0:T(8,128)S(1)}, u32[]{:S(2)}, u32[]{:S(2)}) %collective-permute-start.39) | collective-permute-done | bytes 9248 | tf_op jit(solution)/shard_map/ppermute | solution.py:32
  164.3 3.0 %collective-permute-start.38 = (bf16[128,768]{1,0:T(8,128)(2,1)S(1)}, bf16[128,768]{1,0:T(8,128)(2,1)S(1)}, u32[]{:S(2)}, u32[]{:S(2)}) collective-permute-start(bf16[128,768]{1,0:T(8,128)(2,1)S(1)} %get-tuple-element.171.refs_2_), channel_id=1, source_target_pairs={{0,16},{4,20},{8,24},{12,28},{16,0},{20,4},{24,8},{28,12},{1,17},{... | collective-permute-start | bytes 589832 | tf_op jit(solution)/shard_map/ppermute | solution.py:32
  168.2 3.0 %collective-permute-done.40.refs_1_ = f32[18,128]{1,0:T(8,128)S(1)} collective-permute-done((f32[18,128]{1,0:T(8,128)S(1)}, f32[18,128]{1,0:T(8,128)S(1)}, u32[]{:S(2)}, u32[]{:S(2)}) %collective-permute-start.40) | collective-permute-done | bytes 9248 | tf_op jit(solution)/shard_map/ppermute | solution.py:32
  172.4 2.9 %collective-permute-done.38.refs_1_ = bf16[128,768]{1,0:T(8,128)(2,1)S(1)} collective-permute-done((bf16[128,768]{1,0:T(8,128)(2,1)S(1)}, bf16[128,768]{1,0:T(8,128)(2,1)S(1)}, u32[]{:S(2)}, u32[]{:S(2)}) %collective-permute-start.38) | collective-permute-done | bytes 196640 | tf_op jit(solution)/shard_map/ppermute | solution.py:32
  (108 shorter events, 15.5 us)
Async XLA Ops:
  0.6 37.0 %copy-start.4 = (bf16[256,1024]{1,0:T(8,128)(2,1)S(1)}, bf16[256,1024]{1,0:T(8,128)(2,1)}, u32[]{:S(2)}) copy-start(bf16[256,1024]{1,0:T(8,128)(2,1)} %refs_5_.3) | copy-start | bytes 1572868
  0.7 6.7 %collective-permute-start.1 = (bf16[64,1024]{1,0:T(8,128)(2,1)}, bf16[64,1024]{1,0:T(8,128)(2,1)S(1)}, u32[]{:S(2)}, u32[]{:S(2)}) collective-permute-start(bf16[64,1024]{1,0:T(8,128)(2,1)} %refs_0_.5), channel_id=1, source_target_pairs={{0,2},{1,3},{2,0},{3,1},{4,6},{5,7},{6,4},{7,5},{8,10},{9,11},{10,... | collective-permute-start | bytes 393224 | tf_op jit(solution)/shard_map/ppermute | solution.py:32
  3.7 5.5 %collective-permute-start.2 = (bf16[64,1024]{1,0:T(8,128)(2,1)}, bf16[64,1024]{1,0:T(8,128)(2,1)S(1)}, u32[]{:S(2)}, u32[]{:S(2)}) collective-permute-start(bf16[64,1024]{1,0:T(8,128)(2,1)} %refs_0_.5), channel_id=1, source_target_pairs={{0,1},{1,0},{2,3},{3,2},{4,5},{5,4},{6,7},{7,6},{8,9},{9,8},{10,11... | collective-permute-start | bytes 393224 | tf_op jit(solution)/shard_map/ppermute | solution.py:32
  7.4 1.8 %collective-permute-start.3 = (bf16[64,1024]{1,0:T(8,128)(2,1)S(1)}, bf16[64,1024]{1,0:T(8,128)(2,1)S(1)}, u32[]{:S(2)}, u32[]{:S(2)}) collective-permute-start(bf16[64,1024]{1,0:T(8,128)(2,1)S(1)} %collective-permute-done.1.x1.refs_1_.refs_8_), channel_id=1, source_target_pairs={{0,1},{1,0},{2,3},{3,2},{4,5},{5,4},{6,7},{7,6},{8,9},{9,8},{10,11... | collective-permute-start | bytes 393224 | tf_op jit(solution)/shard_map/ppermute | solution.py:32
  7.4 12.2 %collective-permute-start = (bf16[64,1024]{1,0:T(8,128)(2,1)}, bf16[64,1024]{1,0:T(8,128)(2,1)S(1)}, u32[]{:S(2)}, u32[]{:S(2)}) collective-permute-start(bf16[64,1024]{1,0:T(8,128)(2,1)} %refs_0_.3), channel_id=1, source_target_pairs={{0,4},{4,0},{8,12},{12,8},{16,20},{20,16},{24,28},{28,24},{1,5},{5... | collective-permute-start | bytes 393224 | tf_op jit(solution)/shard_map/ppermute | solution.py:32
  16.0 13.0 %collective-permute-start.7 = (bf16[256,256]{1,0:T(8,128)(2,1)S(1)}, bf16[256,256]{1,0:T(8,128)(2,1)S(1)}, u32[]{:S(2)}, u32[]{:S(2)}) collective-permute-start(bf16[256,256]{1,0:T(8,128)(2,1)S(1)} %get-tuple-element.97.refs_2_.refs_4_.refs_10_), channel_id=1, source_target_pairs={{0,8},{4,12},{8,16},{12,20},{16,24},{20,28},{1,9},{5,13},{9,17},{1... | collective-permute-start | bytes 393224 | tf_op jit(solution)/shard_map/ppermute | solution.py:740
  19.6 13.1 %collective-permute-start.4 = (bf16[64,2048]{1,0:T(8,128)(2,1)S(1)}, bf16[64,2048]{1,0:T(8,128)(2,1)S(1)}, u32[]{:S(2)}, u32[]{:S(2)}) collective-permute-start(bf16[64,2048]{1,0:T(8,128)(2,1)S(1)} %pack.1.refs_0_), channel_id=1, source_target_pairs={{0,2},{1,3},{2,0},{3,1},{4,6},{5,7},{6,4},{7,5},{8,10},{9,11},{10,... | collective-permute-start | bytes 786440 | tf_op jit(solution)/shard_map/ppermute | solution.py:32
  21.1 11.6 %collective-permute-start.5 = (bf16[64,2048]{1,0:T(8,128)(2,1)S(1)}, bf16[64,2048]{1,0:T(8,128)(2,1)S(1)}, u32[]{:S(2)}, u32[]{:S(2)}) collective-permute-start(bf16[64,2048]{1,0:T(8,128)(2,1)S(1)} %pack.1.refs_0_), channel_id=1, source_target_pairs={{0,1},{1,0},{2,3},{3,2},{4,5},{5,4},{6,7},{7,6},{8,9},{9,8},{10,11... | collective-permute-start | bytes 786440 | tf_op jit(solution)/shard_map/ppermute | solution.py:32
  21.1 8.0 %collective-permute-start.8 = (bf16[256,256]{1,0:T(8,128)(2,1)S(1)}, bf16[256,256]{1,0:T(8,128)(2,1)S(1)}, u32[]{:S(2)}, u32[]{:S(2)}) collective-permute-start(bf16[256,256]{1,0:T(8,128)(2,1)S(1)} %get-tuple-element.97.refs_2_.refs_4_.refs_10_), channel_id=1, source_target_pairs={{0,16},{4,20},{8,24},{12,28},{1,17},{5,21},{9,25},{13,29},{2,18},{... | collective-permute-start | bytes 393224 | tf_op jit(solution)/shard_map/ppermute | solution.py:740
  25.6 7.1 %collective-permute-start.9 = (bf16[256,256]{1,0:T(8,128)(2,1)S(1)}, bf16[256,256]{1,0:T(8,128)(2,1)S(1)}, u32[]{:S(2)}, u32[]{:S(2)}) collective-permute-start(bf16[256,256]{1,0:T(8,128)(2,1)S(1)} %get-tuple-element.97.refs_2_.refs_4_.refs_10_), channel_id=1, source_target_pairs={{0,4},{8,12},{16,20},{24,28},{4,24},{1,5},{9,13},{17,21},{25,29},{... | collective-permute-start | bytes 393224 | tf_op jit(solution)/shard_map/ppermute | solution.py:746
  29.1 6.4 %collective-permute-start.10 = (bf16[256,256]{1,0:T(8,128)(2,1)S(1)}, bf16[256,256]{1,0:T(8,128)(2,1)S(1)}, u32[]{:S(2)}, u32[]{:S(2)}) collective-permute-start(bf16[256,256]{1,0:T(8,128)(2,1)S(1)} %collective-permute-done.7.refs_5_.refs_12_), channel_id=1, source_target_pairs={{0,4},{4,0},{8,12},{12,8},{16,20},{20,16},{24,28},{28,24},{1,5},{5... | collective-permute-start | bytes 393224 | tf_op jit(solution)/shard_map/ppermute | solution.py:32
  29.2 8.5 %collective-permute-start.11 = (bf16[256,256]{1,0:T(8,128)(2,1)S(1)}, bf16[256,256]{1,0:T(8,128)(2,1)S(1)}, u32[]{:S(2)}, u32[]{:S(2)}) collective-permute-start(bf16[256,256]{1,0:T(8,128)(2,1)S(1)} %collective-permute-done.8.refs_6_.refs_14_), channel_id=1, source_target_pairs={{0,4},{4,0},{8,12},{12,8},{16,20},{20,16},{24,28},{28,24},{1,5},{5... | collective-permute-start | bytes 393224 | tf_op jit(solution)/shard_map/ppermute | solution.py:32
  41.0 1.6 collective-permute-start.12
  41.1 2.2 %collective-permute-start.6 = (bf16[64,2048]{1,0:T(8,128)(2,1)S(1)}, bf16[64,2048]{1,0:T(8,128)(2,1)S(1)}, u32[]{:S(2)}, u32[]{:S(2)}) collective-permute-start(bf16[64,2048]{1,0:T(8,128)(2,1)S(1)} %collective-permute-done.4.refs_10_.refs_1_), channel_id=1, source_target_pairs={{0,1},{1,0},{2,3},{3,2},{4,5},{5,4},{6,7},{7,6},{8,9},{9,8},{10,11... | collective-permute-start | bytes 786440 | tf_op jit(solution)/shard_map/ppermute | solution.py:32
  42.7 8.4 %collective-permute-start.13 = (bf16[128,1024]{1,0:T(8,128)(2,1)S(1)}, bf16[128,1024]{1,0:T(8,128)(2,1)S(1)}, u32[]{:S(2)}, u32[]{:S(2)}) collective-permute-start(bf16[128,1024]{1,0:T(8,128)(2,1)S(1)} %resid_core.1.refs_5_.refs_0_), channel_id=1, source_target_pairs={{0,2},{1,3},{2,0},{3,1},{4,6},{5,7},{6,4},{7,5},{8,10},{9,11},{10,... | collective-permute-start | bytes 786440 | tf_op jit(solution)/shard_map/ppermute | solution.py:32
  43.3 9.5 %copy-start.1 = (bf16[1024,1152]{1,0:T(8,128)(2,1)S(1)}, bf16[1024,1152]{1,0:T(8,128)(2,1)}, u32[]{:S(2)}) copy-start(bf16[1024,1152]{1,0:T(8,128)(2,1)} %refs_7_.2) | copy-start | bytes 7077892
  43.3 9.5 %copy-start.2 = (bf16[1024,1152]{1,0:T(8,128)(2,1)S(1)}, bf16[1024,1152]{1,0:T(8,128)(2,1)}, u32[]{:S(2)}) copy-start(bf16[1024,1152]{1,0:T(8,128)(2,1)} %refs_8_.1) | copy-start | bytes 7077892
  51.2 1.6 collective-permute-start.14
  57.9 18.1 %collective-permute-start.18 = (bf16[256,1280]{1,0:T(8,128)(2,1)S(1)}, bf16[256,1280]{1,0:T(8,128)(2,1)S(1)}, u32[]{:S(2)}, u32[]{:S(2)}) collective-permute-start(bf16[256,1280]{1,0:T(8,128)(2,1)S(1)} %get-tuple-element.117.refs_2_.refs_0_), channel_id=1, source_target_pairs={{0,4},{4,0},{8,12},{12,8},{16,20},{20,16},{24,28},{28,24},{1,5},{5... | collective-permute-start | bytes 1966088 | tf_op jit(solution)/shard_map/ppermute | solution.py:32
  60.5 1.5 collective-permute-start.15
  62.1 8.4 %collective-permute-start.16 = (bf16[128,1024]{1,0:T(8,128)(2,1)S(1)}, bf16[128,1024]{1,0:T(8,128)(2,1)S(1)}, u32[]{:S(2)}, u32[]{:S(2)}) collective-permute-start(bf16[128,1024]{1,0:T(8,128)(2,1)S(1)} %get-tuple-element.109.refs_0_), channel_id=1, source_target_pairs={{0,2},{1,3},{2,0},{3,1},{4,6},{5,7},{6,4},{7,5},{8,10},{9,11},{10,... | collective-permute-start | bytes 786440 | tf_op jit(solution)/shard_map/ppermute | solution.py:32
  70.5 6.7 %collective-permute-start.17 = (bf16[128,1024]{1,0:T(8,128)(2,1)S(1)}, bf16[128,1024]{1,0:T(8,128)(2,1)S(1)}, u32[]{:S(2)}, u32[]{:S(2)}) collective-permute-start(bf16[128,1024]{1,0:T(8,128)(2,1)S(1)} %grad_act_chip.1.refs_1_.refs_2_), channel_id=1, source_target_pairs={{0,1},{1,0},{2,3},{3,2},{4,5},{5,4},{6,7},{7,6},{8,9},{9,8},{10,11... | collective-permute-start | bytes 786440 | tf_op jit(solution)/shard_map/ppermute | solution.py:32
  70.6 20.9 %collective-permute-start.23 = (bf16[256,1152]{1,0:T(8,128)(2,1)S(1)}, bf16[256,1152]{1,0:T(8,128)(2,1)S(1)}, u32[]{:S(2)}, u32[]{:S(2)}) collective-permute-start(bf16[256,1152]{1,0:T(8,128)(2,1)S(1)} %get-tuple-element.130.refs_2_), channel_id=1, source_target_pairs={{0,4},{4,0},{8,12},{12,8},{16,20},{20,16},{24,28},{28,24},{1,5},{5... | collective-permute-start | bytes 1769480 | tf_op jit(solution)/shard_map/ppermute | solution.py:32
  76.9 14.6 %collective-permute-start.24 = (bf16[256,1152]{1,0:T(8,128)(2,1)S(1)}, bf16[256,1152]{1,0:T(8,128)(2,1)S(1)}, u32[]{:S(2)}, u32[]{:S(2)}) collective-permute-start(bf16[256,1152]{1,0:T(8,128)(2,1)S(1)} %get-tuple-element.118.refs_16_), channel_id=1, source_target_pairs={{0,8},{4,12},{8,0},{12,4},{16,24},{20,28},{24,16},{28,20},{1,9},{5... | collective-permute-start | bytes 1769480 | tf_op jit(solution)/shard_map/ppermute | solution.py:32
  83.8 12.8 %collective-permute-start.19 = (bf16[768,256]{1,0:T(8,128)(2,1)S(1)}, bf16[768,256]{1,0:T(8,128)(2,1)S(1)}, u32[]{:S(2)}, u32[]{:S(2)}) collective-permute-start(bf16[768,256]{1,0:T(8,128)(2,1)S(1)} %get-tuple-element.128), channel_id=1, source_target_pairs={{0,4},{4,0},{8,12},{12,8},{16,20},{20,16},{24,28},{28,24},{1,5},{5... | collective-permute-start | bytes 1179656 | tf_op jit(solution)/shard_map/ppermute | solution.py:32
  85.9 4.3 %collective-permute-start.20 = (bf16[256,128]{1,0:T(8,128)(2,1)S(1)}, bf16[256,128]{1,0:T(8,128)(2,1)S(1)}, u32[]{:S(2)}, u32[]{:S(2)}) collective-permute-start(bf16[256,128]{1,0:T(8,128)(2,1)S(1)} %piece.1.refs_4_.refs_0_), channel_id=1, source_target_pairs={{0,2},{1,3},{2,0},{3,1},{4,6},{5,7},{6,4},{7,5},{8,10},{9,11},{10,... | collective-permute-start | bytes 196616 | tf_op jit(solution)/shard_map/ppermute | solution.py:32
  86.5 3.7 %collective-permute-start.21 = (bf16[256,128]{1,0:T(8,128)(2,1)S(1)}, bf16[256,128]{1,0:T(8,128)(2,1)S(1)}, u32[]{:S(2)}, u32[]{:S(2)}) collective-permute-start(bf16[256,128]{1,0:T(8,128)(2,1)S(1)} %piece.1.refs_4_.refs_0_), channel_id=1, source_target_pairs={{0,1},{1,0},{2,3},{3,2},{4,5},{5,4},{6,7},{7,6},{8,9},{9,8},{10,11... | collective-permute-start | bytes 196616 | tf_op jit(solution)/shard_map/ppermute | solution.py:32
  90.2 1.3 collective-permute-start.22
  92.4 9.3 %copy-start.5 = (bf16[1024,256]{1,0:T(8,128)(2,1)S(1)}, bf16[1024,256]{1,0:T(8,128)(2,1)}, u32[]{:S(2)}) copy-start(bf16[1024,256]{1,0:T(8,128)(2,1)} %refs_5_.4) | copy-start | bytes 1572868
  92.5 9.3 %copy-start.14 = (f32[64]{0:T(128)S(1)}, f32[64]{0:T(128)}, u32[]{:S(2)}) copy-start(f32[64]{0:T(128)} %param.21) | copy-start | bytes 772
  92.5 19.0 %collective-permute-start.29 = (bf16[256,1152]{1,0:T(8,128)(2,1)S(1)}, bf16[256,1152]{1,0:T(8,128)(2,1)S(1)}, u32[]{:S(2)}, u32[]{:S(2)}) collective-permute-start(bf16[256,1152]{1,0:T(8,128)(2,1)S(1)} %get-tuple-element.131.refs_4_), channel_id=1, source_target_pairs={{0,8},{4,12},{8,0},{12,4},{16,24},{20,28},{24,16},{28,20},{1,9},{5... | collective-permute-start | bytes 1769480 | tf_op jit(solution)/shard_map/ppermute | solution.py:32
  96.7 15.0 %collective-permute-start.28 = (bf16[256,1152]{1,0:T(8,128)(2,1)S(1)}, bf16[256,1152]{1,0:T(8,128)(2,1)S(1)}, u32[]{:S(2)}, u32[]{:S(2)}) collective-permute-start(bf16[256,1152]{1,0:T(8,128)(2,1)S(1)} %get-tuple-element.143.refs_2_), channel_id=1, source_target_pairs={{0,4},{4,0},{8,12},{12,8},{16,20},{20,16},{24,28},{28,24},{1,5},{5... | collective-permute-start | bytes 1769480 | tf_op jit(solution)/shard_map/ppermute | solution.py:32
  98.5 14.2 %collective-permute-start.25 = (bf16[256,256]{1,0:T(8,128)(2,1)S(1)}, bf16[256,256]{1,0:T(8,128)(2,1)S(1)}, u32[]{:S(2)}, u32[]{:S(2)}) collective-permute-start(bf16[256,256]{1,0:T(8,128)(2,1)S(1)} %get-tuple-element.140), channel_id=1, source_target_pairs={{16,0},{20,4},{24,8},{28,12},{17,1},{21,5},{25,9},{29,13},{18,2},{... | collective-permute-start | bytes 393224 | tf_op jit(solution)/shard_map/ppermute | solution.py:42
  99.8 13.8 %collective-permute-start.26 = (bf16[256,256]{1,0:T(8,128)(2,1)S(1)}, bf16[256,256]{1,0:T(8,128)(2,1)S(1)}, u32[]{:S(2)}, u32[]{:S(2)}) collective-permute-start(bf16[256,256]{1,0:T(8,128)(2,1)S(1)} %get-tuple-element.141), channel_id=1, source_target_pairs={{8,0},{12,4},{16,8},{20,12},{24,16},{28,20},{9,1},{13,5},{17,9},{2... | collective-permute-start | bytes 393224 | tf_op jit(solution)/shard_map/ppermute | solution.py:42
  101.1 12.5 %collective-permute-start.27 = (bf16[256,256]{1,0:T(8,128)(2,1)S(1)}, bf16[256,256]{1,0:T(8,128)(2,1)S(1)}, u32[]{:S(2)}, u32[]{:S(2)}) collective-permute-start(bf16[256,256]{1,0:T(8,128)(2,1)S(1)} %get-tuple-element.142), channel_id=1, source_target_pairs={{28,4},{29,5},{30,6},{31,7}} | collective-permute-start | bytes 393224 | tf_op jit(solution)/shard_map/ppermute | solution.py:867
  114.5 27.1 %copy-start.12 = (f32[1024]{0:T(1024)S(1)}, f32[1024]{0:T(1024)}, u32[]{:S(2)}) copy-start(f32[1024]{0:T(1024)} %param.16) | copy-start | bytes 12292
  114.5 6.3 %collective-permute-start.30 = (bf16[272,1024]{1,0:T(8,128)(2,1)S(1)}, bf16[272,1024]{1,0:T(8,128)(2,1)S(1)}, u32[]{:S(2)}, u32[]{:S(2)}) collective-permute-start(bf16[272,1024]{1,0:T(8,128)(2,1)S(1)} %get-tuple-element.151), channel_id=1, source_target_pairs={{0,1},{1,0},{2,3},{3,2},{4,5},{5,4},{6,7},{7,6},{8,9},{9,8},{10,11... | collective-permute-start | bytes 1671176 | tf_op jit(solution)/shard_map/ppermute | solution.py:32
  114.6 28.0 %collective-permute-start.33 = (bf16[256,1024]{1,0:T(8,128)(2,1)S(1)}, bf16[256,1024]{1,0:T(8,128)(2,1)S(1)}, u32[]{:S(2)}, u32[]{:S(2)}) collective-permute-start(bf16[256,1024]{1,0:T(8,128)(2,1)S(1)} %get-tuple-element.160.refs_6_.refs_10_), channel_id=1, source_target_pairs={{0,4},{4,0},{8,12},{12,8},{16,20},{20,16},{24,28},{28,24},{1,5},{5... | collective-permute-start | bytes 1572872 | tf_op jit(solution)/shard_map/ppermute | solution.py:32
  120.6 26.5 %collective-permute-start.36 = (bf16[256,1152]{1,0:T(8,128)(2,1)S(1)}, bf16[256,1152]{1,0:T(8,128)(2,1)S(1)}, u32[]{:S(2)}, u32[]{:S(2)}) collective-permute-start(bf16[256,1152]{1,0:T(8,128)(2,1)S(1)} %get-tuple-element.147.refs_20_), channel_id=1, source_target_pairs={{0,8},{4,12},{8,0},{12,4},{16,24},{20,28},{24,16},{28,20},{1,9},{5... | collective-permute-start | bytes 1769480 | tf_op jit(solution)/shard_map/ppermute | solution.py:32
  120.6 20.9 %collective-permute-start.32 = (bf16[256,768]{1,0:T(8,128)(2,1)S(1)}, bf16[256,768]{1,0:T(8,128)(2,1)S(1)}, u32[]{:S(2)}, u32[]{:S(2)}) collective-permute-start(bf16[256,768]{1,0:T(8,128)(2,1)S(1)} %get-tuple-element.156.refs_2_), channel_id=1, source_target_pairs={{0,4},{4,0},{8,12},{12,8},{16,20},{20,16},{24,28},{28,24},{1,5},{5... | collective-permute-start | bytes 1179656 | tf_op jit(solution)/shard_map/ppermute | solution.py:32
  121.0 20.6 %collective-permute-start.31 = (bf16[144,1024]{1,0:T(8,128)(2,1)S(1)}, bf16[144,1024]{1,0:T(8,128)(2,1)S(1)}, u32[]{:S(2)}, u32[]{:S(2)}) collective-permute-start(bf16[144,1024]{1,0:T(8,128)(2,1)S(1)} %get-tuple-element.155), channel_id=1, source_target_pairs={{0,2},{1,3},{2,0},{3,1},{4,6},{5,7},{6,4},{7,5},{8,10},{9,11},{10,... | collective-permute-start | bytes 884744 | tf_op jit(solution)/shard_map/ppermute | solution.py:32
  121.6 28.9 %collective-permute-start.35 = (bf16[128,2304]{1,0:T(8,128)(2,1)S(1)}, bf16[128,2304]{1,0:T(8,128)(2,1)S(1)}, u32[]{:S(2)}, u32[]{:S(2)}) collective-permute-start(bf16[128,2304]{1,0:T(8,128)(2,1)S(1)} %get-tuple-element.146.refs_4_), channel_id=1, source_target_pairs={{0,16},{4,20},{8,24},{12,28},{16,0},{20,4},{24,8},{28,12},{1,17},{... | collective-permute-start | bytes 1769480 | tf_op jit(solution)/shard_map/ppermute | solution.py:32
  143.3 20.9 %collective-permute-start.34 = (bf16[256,768]{1,0:T(8,128)(2,1)S(1)}, bf16[256,768]{1,0:T(8,128)(2,1)S(1)}, u32[]{:S(2)}, u32[]{:S(2)}) collective-permute-start(bf16[256,768]{1,0:T(8,128)(2,1)S(1)} %get-tuple-element.164.refs_2_), channel_id=1, source_target_pairs={{0,8},{4,12},{8,0},{12,4},{16,24},{20,28},{24,16},{28,20},{1,9},{5... | collective-permute-start | bytes 1179656 | tf_op jit(solution)/shard_map/ppermute | solution.py:32
  143.4 3.8 %collective-permute-start.37 = (f32[18,128]{1,0:T(8,128)S(1)}, f32[18,128]{1,0:T(8,128)S(1)}, u32[]{:S(2)}, u32[]{:S(2)}) collective-permute-start(f32[18,128]{1,0:T(8,128)S(1)} %get-tuple-element.162.refs_12_.refs_0_), channel_id=1, source_target_pairs={{0,4},{4,0},{8,12},{12,8},{16,20},{20,16},{24,28},{28,24},{1,5},{5... | collective-permute-start | bytes 27656 | tf_op jit(solution)/shard_map/ppermute | solution.py:32
  147.3 20.0 %collective-permute-start.41 = (bf16[128,1152]{1,0:T(8,128)(2,1)S(1)}, bf16[128,1152]{1,0:T(8,128)(2,1)S(1)}, u32[]{:S(2)}, u32[]{:S(2)}) collective-permute-start(bf16[128,1152]{1,0:T(8,128)(2,1)S(1)} %get-tuple-element.168.refs_3_), channel_id=1, source_target_pairs={{0,16},{4,20},{8,24},{12,28},{16,0},{20,4},{24,8},{28,12},{1,17},{... | collective-permute-start | bytes 884744 | tf_op jit(solution)/shard_map/ppermute | solution.py:32
  147.4 16.8 %collective-permute-start.39 = (f32[18,128]{1,0:T(8,128)S(1)}, f32[18,128]{1,0:T(8,128)S(1)}, u32[]{:S(2)}, u32[]{:S(2)}) collective-permute-start(f32[18,128]{1,0:T(8,128)S(1)} %gains.3.refs_2_.refs_0_), channel_id=1, source_target_pairs={{0,8},{4,12},{8,0},{12,4},{16,24},{20,28},{24,16},{28,20},{1,9},{5... | collective-permute-start | bytes 27656 | tf_op jit(solution)/shard_map/ppermute | solution.py:32
  164.2 7.0 %collective-permute-start.40 = (f32[18,128]{1,0:T(8,128)S(1)}, f32[18,128]{1,0:T(8,128)S(1)}, u32[]{:S(2)}, u32[]{:S(2)}) collective-permute-start(f32[18,128]{1,0:T(8,128)S(1)} %gains.4.refs_0_), channel_id=1, source_target_pairs={{0,16},{4,20},{8,24},{12,28},{16,0},{20,4},{24,8},{28,12},{1,17},{... | collective-permute-start | bytes 27656 | tf_op jit(solution)/shard_map/ppermute | solution.py:32
  164.3 11.0 %collective-permute-start.38 = (bf16[128,768]{1,0:T(8,128)(2,1)S(1)}, bf16[128,768]{1,0:T(8,128)(2,1)S(1)}, u32[]{:S(2)}, u32[]{:S(2)}) collective-permute-start(bf16[128,768]{1,0:T(8,128)(2,1)S(1)} %get-tuple-element.171.refs_2_), channel_id=1, source_target_pairs={{0,16},{4,20},{8,24},{12,28},{16,0},{20,4},{24,8},{28,12},{1,17},{... | collective-permute-start | bytes 589832 | tf_op jit(solution)/shard_map/ppermute | solution.py:32
  (12 other events, 31.2 us)
